TPU v7x, 32 devices: a whole 2x2x4 slice. The times are simulated.
32 devices in a mesh: chan: 4 (over z), rows: 8 (over y, x, core).
Axes of the slice: x: 2, y: 2, z: 4, core: 2. Of those that a mesh axis runs over, the one named last changes fastest.
Arguments:
- estimate: float32 [4, 2048, 2048], P('chan', 'rows'), may hold values from -3 to 3
- dirty_image: float32 [4, 2048, 2048], P('chan', 'rows'), may hold values from -40 to 40
- psf_weights: float32 [4, 2048, 2048], P('chan', None, 'rows'), may hold values from 0.05 to 2
Outputs:
- new_estimate: float32 [4, 2048, 2048], P('chan', 'rows')
- residual: float32 [4, 2048, 2048], P('chan', 'rows')
All inputs are finite; a program needn't handle non-finite values.
Results may differ from a plain program's by a relative error of at most 0.0001.
Values sent between devices are 32-bit elements; how exact they have to be, the bound alone decides.
No kernel may reach another device: no remote copies, remote signals or barrier semaphores. Data moves between devices by JAX's collectives and lax.ppermute only.
A program may use at most 128 MiB of HBM per device.

v0:
```python
import functools
import math

import jax
import jax.numpy as jnp
import ml_dtypes
import numpy as np
from jax import lax
from jax.experimental import pallas as pl
from jax.experimental.pallas import tpu as pltpu
from jax.sharding import PartitionSpec as P

fractions = (0.03, 0.02, 0.015)
taps = (0.0625, 0.25, 0.375, 0.25, 0.0625)
step_size = 0.9
inner_length = 128
highest = lax.Precision.HIGHEST
lane_count = 128
vmem_bytes = 56 * 1024 * 1024


def with_halo(cells, sides, width):
    for axis, dim in sides:
        count = lax.axis_size(axis)
        ends = count - 1
        head = lax.slice_in_dim(cells, 0, width, axis=dim)
        tail = lax.slice_in_dim(cells, cells.shape[dim] - width, cells.shape[dim], axis=dim)
        cells = jnp.concatenate(
            [
                lax.ppermute(tail, axis, [(i, (i + 1) % count) for i in range(ends)]),
                cells,
                lax.ppermute(head, axis, [((i + 1) % count, i) for i in range(ends)]),
            ],
            axis=dim,
        )
    return cells


def phase_table(first_count, second_count, length, sign):
    first_ids = lax.iota(jnp.int32, first_count)
    second_ids = lax.iota(jnp.int32, second_count)
    angles = (first_ids[:, None] * second_ids[None, :] % length).astype(jnp.float32) * (
        2.0 * math.pi / length
    )
    return (jnp.cos(angles), sign * jnp.sin(angles))


def dft_last(real_in, imag_in, sign):
    batch, length = real_in.shape
    outer = length // inner_length
    real_part = real_in.reshape(batch, outer, inner_length)
    imag_part = imag_in.reshape(batch, outer, inner_length)
    cos_small, sin_small = phase_table(outer, outer, outer, sign)
    first_real = jnp.einsum("kn,bnm->bkm", cos_small, real_part, precision=highest) - jnp.einsum(
        "kn,bnm->bkm", sin_small, imag_part, precision=highest
    )
    first_imag = jnp.einsum("kn,bnm->bkm", cos_small, imag_part, precision=highest) + jnp.einsum(
        "kn,bnm->bkm", sin_small, real_part, precision=highest
    )
    cos_twist, sin_twist = phase_table(outer, inner_length, length, sign)
    twist_real = first_real * cos_twist - first_imag * sin_twist
    twist_imag = first_imag * cos_twist + first_real * sin_twist
    cos_large, sin_large = phase_table(inner_length, inner_length, inner_length, sign)
    last_real = jnp.einsum("bkm,mj->bkj", twist_real, cos_large, precision=highest) - jnp.einsum(
        "bkm,mj->bkj", twist_imag, sin_large, precision=highest
    )
    last_imag = jnp.einsum("bkm,mj->bkj", twist_imag, cos_large, precision=highest) + jnp.einsum(
        "bkm,mj->bkj", twist_real, sin_large, precision=highest
    )
    return (
        jnp.transpose(last_real, (0, 2, 1)).reshape(batch, length),
        jnp.transpose(last_imag, (0, 2, 1)).reshape(batch, length),
    )


def dft_first(real_in, imag_in, sign):
    length, width = real_in.shape
    outer = length // inner_length
    real_part = real_in.reshape(outer, inner_length, width)
    imag_part = imag_in.reshape(outer, inner_length, width)
    cos_small, sin_small = phase_table(outer, outer, outer, sign)
    first_real = jnp.einsum("kn,nmw->kmw", cos_small, real_part, precision=highest) - jnp.einsum(
        "kn,nmw->kmw", sin_small, imag_part, precision=highest
    )
    first_imag = jnp.einsum("kn,nmw->kmw", cos_small, imag_part, precision=highest) + jnp.einsum(
        "kn,nmw->kmw", sin_small, real_part, precision=highest
    )
    cos_twist, sin_twist = phase_table(outer, inner_length, length, sign)
    cos_twist = cos_twist[:, :, None]
    sin_twist = sin_twist[:, :, None]
    twist_real = first_real * cos_twist - first_imag * sin_twist
    twist_imag = first_imag * cos_twist + first_real * sin_twist
    cos_large, sin_large = phase_table(inner_length, inner_length, inner_length, sign)
    last_real = jnp.einsum("kmw,mj->kjw", twist_real, cos_large, precision=highest) - jnp.einsum(
        "kmw,mj->kjw", twist_imag, sin_large, precision=highest
    )
    last_imag = jnp.einsum("kmw,mj->kjw", twist_imag, cos_large, precision=highest) + jnp.einsum(
        "kmw,mj->kjw", twist_real, sin_large, precision=highest
    )
    return (
        jnp.transpose(last_real, (1, 0, 2)).reshape(length, width),
        jnp.transpose(last_imag, (1, 0, 2)).reshape(length, width),
    )


def columns_forward(pieces):
    real_out, imag_out = dft_first(pieces[0][:, 0, :], pieces[1][:, 0, :], -1.0)
    return (real_out[:, None, :], imag_out[:, None, :])


def rows_inverse(pieces):
    real_in = pieces[0][0]
    imag_in = pieces[1][0]
    length = real_in.shape[1]
    real_out, imag_out = dft_last(real_in, imag_in, 1.0)
    return (real_out * (1.0 / (length * length)))[None]


def max_over(cells, axis):
    count = lax.axis_size(axis)
    if count & (count - 1):
        return lax.pmax(cells, axis)
    distance = 1
    while distance < count:
        other = lax.ppermute(cells, axis, [(i, i ^ distance) for i in range(count)])
        cells = jnp.maximum(cells, other)
        distance *= 2
    return cells


def smooth_both(values, spacing):
    for dim in (2, 1):
        count = values.shape[dim] - 4 * spacing
        total = taps[0] * lax.slice_in_dim(values, 0, count, axis=dim)
        for tap_index in range(1, 5):
            start = tap_index * spacing
            total = total + taps[tap_index] * lax.slice_in_dim(
                values, start, start + count, axis=dim
            )
        values = total
    return values


def real_dft(parts):
    count = len(parts)
    if count == 1:
        return [(parts[0], None)]
    if count == 2:
        return [(parts[0] + parts[1], None), (parts[0] - parts[1], None)]
    even = real_dft(parts[0::2])
    odd = real_dft(parts[1::2])
    out = [None] * (count // 2 + 1)
    for k in range(count // 4 + 1):
        turned = spin(odd[k], -2.0 * math.pi * k / count)
        out[k] = pair_add(even[k], turned)
        low = pair_sub(even[k], turned)
        out[count // 2 - k] = (low[0], None if low[1] is None else -low[1])
    out[0] = (out[0][0], None)
    out[count // 2] = (out[count // 2][0], None)
    return out


def real_inverse_dft(pairs):
    count = 2 * (len(pairs) - 1)
    if count == 2:
        return [pairs[0][0] + pairs[1][0], pairs[0][0] - pairs[1][0]]
    even, odd = [], []
    for k in range(count // 4 + 1):
        low = pairs[k]
        high = pairs[count // 2 - k]
        high = (high[0], None if high[1] is None else -high[1])
        even.append(pair_add(low, high))
        odd.append(spin(pair_sub(low, high), 2.0 * math.pi * k / count))
    for half in (even, odd):
        half[0] = (half[0][0], None)
        half[-1] = (half[-1][0], None)
    even = real_inverse_dft(even)
    odd = real_inverse_dft(odd)
    return [cells for both in zip(even, odd) for cells in both]


def complex_dft(pairs, sign):
    count = len(pairs)
    if count == 1:
        return pairs
    even = complex_dft(pairs[0::2], sign)
    odd = complex_dft(pairs[1::2], sign)
    turned = [spin(odd[k], sign * 2.0 * math.pi * k / count) for k in range(count // 2)]
    return [pair_add(a, b) for a, b in zip(even, turned)] + [
        pair_sub(a, b) for a, b in zip(even, turned)
    ]


def pair_add(a, b):
    if a[1] is None or b[1] is None:
        return (a[0] + b[0], a[1] if b[1] is None else b[1])
    return (a[0] + b[0], a[1] + b[1])


def pair_sub(a, b):
    if b[1] is None:
        return (a[0] - b[0], a[1])
    return (a[0] - b[0], -b[1] if a[1] is None else a[1] - b[1])


def spin(pair, angle):
    quarter = angle / (0.5 * math.pi)
    turns = round(quarter)
    real, imag = pair
    if abs(quarter - turns) < 1e-9:
        turns %= 4
        if turns == 0:
            return pair
        if turns == 2:
            return (-real, None if imag is None else -imag)
        if imag is None:
            return (jnp.zeros_like(real), real if turns == 1 else -real)
        return (-imag, real) if turns == 1 else (imag, -real)
    cosine, sine = math.cos(angle), math.sin(angle)
    if imag is None:
        return (real * cosine, real * sine)
    if abs(abs(cosine) - abs(sine)) < 1e-9:
        a, b = math.copysign(1.0, cosine), math.copysign(1.0, sine)
        root = abs(cosine)
        first = real if a > 0 else -real
        second = imag if b > 0 else -imag
        third = real if b > 0 else -real
        fourth = imag if a > 0 else -imag
        return ((first - second) * root, (third + fourth) * root)
    return (real * cosine - imag * sine, real * sine + imag * cosine)


def split(cells):
    high = cells.astype(jnp.bfloat16)
    return high, (cells - high.astype(jnp.float32)).astype(jnp.bfloat16)


def dot(a, b):
    return jnp.dot(a, b, preferred_element_type=jnp.float32)


def split_table(table):
    high = table.astype(np.float32).astype(ml_dtypes.bfloat16)
    low = (table - high.astype(np.float64)).astype(np.float32).astype(ml_dtypes.bfloat16)
    return np.stack([high, low], axis=-3)


def group_columns(length, count, group):
    radix = 2 * count
    lanes = length // radix
    spots = np.arange(lanes)
    if group:
        return group + radix * spots
    half = lanes // 2
    return np.where(spots < half, radix * spots, count + radix * (spots - half))


def row_tables(length, count):
    radix = 2 * count
    lanes = length // radix
    half = lanes // 2
    spots = np.arange(lanes)
    there, back = [], []
    for group in range(count):
        columns = group_columns(length, count, group)
        angles = 2.0 * np.pi * (np.outer(spots, columns) % length) / length
        cosine, sine = np.cos(angles), np.sin(angles)
        ahead = np.zeros((2, lanes, 2, lanes))
        behind = np.zeros((2, lanes, 2, lanes))
        if group:
            ahead[0, :, 0], ahead[0, :, 1] = cosine, -sine
            ahead[1, :, 0], ahead[1, :, 1] = sine, cosine
            behind[0, :, 0], behind[0, :, 1] = cosine.T, sine.T
            behind[1, :, 0], behind[1, :, 1] = -sine.T, cosine.T
        else:
            for part, where in enumerate((slice(0, half), slice(half, lanes))):
                ahead[part, :, 0, where] = cosine[:, where]
                ahead[part, :, 1, where] = -sine[:, where]
                behind[0, where, part] = 2.0 * cosine[:, where].T
                behind[1, where, part] = -2.0 * sine[:, where].T
            ahead[0, :, 1, 0] = (-1.0) ** spots
            behind[0, 0, 0] = 1.0
            behind[1, 0, 0] = (-1.0) ** spots
        there.append(ahead.reshape(2 * lanes, 2 * lanes))
        back.append(behind.reshape(2 * lanes, 2 * lanes) / float(length) ** 2)
    return split_table(np.stack(there)), split_table(np.stack(back))


def column_tables(length, steps):
    size = length // steps
    spots = np.arange(size)
    there = []
    for step in range(steps):
        angles = 2.0 * np.pi * ((np.outer(spots, steps * spots + step)) % length) / length
        cosine, sine = np.cos(angles), np.sin(angles)
        there.append(np.block([[cosine, sine], [-sine, cosine]]))
    there = np.stack(there)
    return split_table(there), split_table(np.swapaxes(there, 1, 2))


def weight_tables(length, count):
    width = length // count
    lanes = length // (2 * count)
    per_class = width // (2 * count)
    packs = lanes // (2 * per_class)
    radix = 2 * count

    def classes(group):
        return (group, radix - group) if group else (0, count)

    pick = np.zeros((packs, width, count, lanes))
    for group in range(count):
        for which, kind in enumerate(classes(group)):
            for q in range(per_class):
                for pack in range(packs):
                    lane = pack * 2 * per_class + which * per_class + q
                    pick[pack, radix * q + kind, group, lane] = 1.0
    place = np.zeros((2, count, lanes, packs * 2 + 1, lanes))

    def slot(group, column, pack):
        column %= length
        source, rest = divmod(column, width)
        which = classes(group).index(rest % radix)
        return source, pack * 2 * per_class + which * per_class + rest // radix

    for version, group in ((0, 0), (1, 1)):
        columns = group_columns(length, count, group)
        for pack in range(packs):
            for lane in range(lanes):
                column = int(columns[lane])
                mates = [(column, 0, 0.5), (-column, 1, 0.5)]
                if group == 0 and lane == 0:
                    mates = [(c, s, 0.25) for c in (0, length // 2) for s in (0, 1)]
                for mate, side, value in mates:
                    source, where = slot(group, mate, pack)
                    place[version, source, where, pack * 2 + side, lane] += value
            if group == 0:
                for mate, value in ((0, 0.25), (length // 2, -0.25)):
                    source, where = slot(group, mate, pack)
                    place[version, source, where, packs * 2, pack] += value
    flip = np.zeros((lanes, 2 * lanes))
    flip[np.arange(1, lanes), lanes - np.arange(1, lanes)] = 1.0
    flip[0, lanes] = 1.0
    as_half = lambda table: table.astype(np.float32).astype(ml_dtypes.bfloat16)
    return (
        as_half(pick.reshape(packs * width, count * lanes)),
        as_half(place.reshape(2, count * lanes, (packs * 2 + 1) * lanes)),
        as_half(flip),
    )


def whole_call(body, out_shapes, scratch, name):
    return pl.pallas_call(
        body,
        out_shape=out_shapes,
        scratch_shapes=scratch,
        compiler_params=pltpu.CompilerParams(vmem_limit_bytes=vmem_bytes),
        name=name,
    )


def row_forward_body(steps, x_ref, table_ref, out_ref, held):
    groups, _, height, lanes = out_ref.shape
    each = height // steps
    for start in range(0, height, 16):
        rows = pl.ds(start, 16)
        tiles = [x_ref[rows, pl.ds(lanes * t, lanes)] for t in range(2 * groups)]
        pairs = real_dft(tiles)
        pairs = [(pairs[0][0], pairs[groups][0])] + pairs[1:groups]
        for group in range(groups):
            high, low = split(jnp.concatenate(pairs[group], axis=1))
            held[0, group, rows, :] = high
            held[1, group, rows, :] = low
    for group in range(groups):
        done = (
            dot(held[0, group], table_ref[group, 0])
            + dot(held[1, group], table_ref[group, 0])
            + dot(held[0, group], table_ref[group, 1])
        )
        for start in range(0, height, 8):
            spread = pl.ds(start % steps * each + start // steps, 8, stride=each)
            out_ref[group, 0, spread, :] = done[start : start + 8, :lanes]
            out_ref[group, 1, spread, :] = done[start : start + 8, lanes:]


def row_inverse_body(steps, in_ref, table_ref, est_ref, dirty_ref, res_ref, half_ref, held):
    groups, _, height, lanes = in_ref.shape
    each = height // steps
    for group in range(groups):
        parts = []
        for part in range(2):
            pieces = [
                in_ref[
                    group,
                    part,
                    pl.ds(start % steps * each + start // steps, 8, stride=each),
                    :,
                ]
                for start in range(0, height, 8)
            ]
            parts.append(jnp.concatenate(pieces, axis=0))
        high, low = split(jnp.concatenate(parts, axis=1))
        held[group] = (
            dot(high, table_ref[group, 0])
            + dot(low, table_ref[group, 0])
            + dot(high, table_ref[group, 1])
        )
    for start in range(0, height, 8):
        rows = pl.ds(start, 8)
        pairs = [
            (held[group, rows, pl.ds(0, lanes)], held[group, rows, pl.ds(lanes, lanes)])
            for group in range(groups)
        ]
        pairs = [(pairs[0][0], None)] + pairs[1:] + [(pairs[0][1], None)]
        tiles = real_inverse_dft(pairs)
        for t in range(2 * groups):
            where = pl.ds(lanes * t, lanes)
            residual = dirty_ref[rows, where] - tiles[t]
            res_ref[rows, where] = residual
            half_ref[rows, where] = est_ref[rows, where] + step_size * residual


def column_body(
    steps, in_ref, there_ref, back_ref, weight_ref, mirror_ref, flip_ref, out_ref, held, made
):
    count, _, height, lanes = in_ref.shape
    each = height // steps
    size = each * count
    for step in range(steps):
        rows = pl.ds(step * each, each)
        block = jnp.concatenate(
            [in_ref[source, part, rows, :] for part in range(2) for source in range(count)],
            axis=0,
        )
        high, low = split(block)
        done = (
            dot(there_ref[step, 0], high)
            + dot(there_ref[step, 1], high)
            + dot(there_ref[step, 0], low)
        )
        held[0, step] = done[:size]
        held[1, step] = done[size:]

    def forward(chunk, carry):
        rows = pl.ds(pl.multiple_of(chunk * 8, 8), 8)
        pairs = [(held[0, step, rows, :], held[1, step, rows, :]) for step in range(steps)]
        for step, pair in enumerate(complex_dft(pairs, -1.0)):
            held[0, step, rows, :] = pair[0]
            held[1, step, rows, :] = pair[1]
        return carry

    lax.fori_loop(0, size // 8, forward, 0)
    for step in range(steps):
        facing = [
            jnp.concatenate([held[0, other], held[1, other]], axis=1)
            for other in (steps - 1 - step, (steps - step) % steps)
        ]
        high, low = split(jnp.concatenate(facing, axis=0))
        turned = dot(flip_ref[...], high) + dot(flip_ref[...], low)
        weight = weight_ref[step]
        mirror = mirror_ref[step]
        made[0, step] = weight * held[0, step] + mirror * turned[:, :lanes]
        made[1, step] = weight * held[1, step] - mirror * turned[:, lanes:]

    def backward(chunk, carry):
        rows = pl.ds(pl.multiple_of(chunk * 8, 8), 8)
        pairs = [(made[0, step, rows, :], made[1, step, rows, :]) for step in range(steps)]
        for step, pair in enumerate(complex_dft(pairs, 1.0)):
            made[0, step, rows, :] = pair[0]
            made[1, step, rows, :] = pair[1]
        return carry

    lax.fori_loop(0, size // 8, backward, 0)
    for step in range(steps):
        high, low = split(jnp.concatenate([made[0, step], made[1, step]], axis=0))
        done = (
            dot(back_ref[step, 0], high)
            + dot(back_ref[step, 1], high)
            + dot(back_ref[step, 0], low)
        )
        rows = pl.ds(step * each, each)
        for part in range(2):
            for target in range(count):
                start = part * size + target * each
                out_ref[target, part, rows, :] = done[start : start + each]


def weight_pick_body(w_ref, pick_ref, out_ref):
    count, _, lanes = out_ref.shape
    packs, _, width = w_ref.shape
    total = 0.0
    for pack in range(packs):
        high, low = split(w_ref[pack])
        chosen = pick_ref[pl.ds(pack * width, width), :]
        total = total + dot(high, chosen) + dot(low, chosen)
    for target in range(count):
        out_ref[target] = total[:, target * lanes : (target + 1) * lanes]


def weight_place_body(in_ref, place_ref, flip_ref, weight_ref, mirror_ref, held):
    count, depth, lanes = in_ref.shape
    steps, size, _ = weight_ref.shape
    packs = steps * size // depth
    total = 0.0
    for source in range(count):
        high, low = split(in_ref[source])
        chosen = place_ref[pl.ds(source * lanes, lanes), :]
        total = total + dot(high, chosen) + dot(low, chosen)
    inner = depth // size
    extra = total[:, 2 * packs * lanes :]
    first = lax.broadcasted_iota(jnp.int32, (size, lanes), 1) == 0
    for step in range(steps):
        pack, rest = divmod(step, inner)
        rows = slice(rest * size, (rest + 1) * size)
        lone = extra[rows]
        if pack:
            lone = pltpu.roll(lone, lanes - pack, 1)
        lone = jnp.where(first, lone, 0.0)
        mirror_ref[step] = lone
        weight_ref[step] = total[rows, 2 * pack * lanes : (2 * pack + 1) * lanes]
        held[step] = jnp.concatenate(
            [total[rows, (2 * pack + 1) * lanes : (2 * pack + 2) * lanes], lone], axis=1
        )
    for step in range(steps):
        high, low = split(
            jnp.concatenate([held[steps - 1 - step], held[(steps - step) % steps]], axis=0)
        )
        turned = dot(flip_ref[...], high) + dot(flip_ref[...], low)
        weight_ref[step] += turned[:, :lanes]
        mirror_ref[step] += turned[:, lanes:]


def filtered(values, dirty, weights):
    height, length = values.shape
    count = lax.axis_size("rows")
    lanes = length // (2 * count)
    steps = height // 16
    size = length // steps
    width = weights.shape[1]
    f32 = jnp.float32
    pick, place, flip = [jnp.asarray(table) for table in weight_tables(length, count)]
    there, back = [jnp.asarray(table) for table in row_tables(length, count)]
    down, up = [jnp.asarray(table) for table in column_tables(length, steps)]
    shape = lambda *dims: jax.ShapeDtypeStruct(dims, f32)
    packs = length * width // (count * lanes) // (length // count)
    packs = pick.shape[0] // width
    depth = length // packs

    sent = whole_call(weight_pick_body, shape(count, depth, lanes), [], "weight_pick")(
        weights.reshape(packs, depth, width), pick
    )
    sent = lax.all_to_all(sent, "rows", 0, 0, tiled=True)
    ahead = whole_call(
        functools.partial(row_forward_body, steps),
        shape(count, 2, height, lanes),
        [pltpu.VMEM((2, count, height, 2 * lanes), jnp.bfloat16)],
        "row_forward",
    )(values, there)
    ahead = lax.all_to_all(ahead, "rows", 0, 0, tiled=True)
    mine = jnp.where(lax.axis_index("rows") == 0, place[0], place[1])
    weight, mirror = whole_call(
        weight_place_body,
        [shape(steps, size, lanes)] * 2,
        [pltpu.VMEM((steps, size, 2 * lanes), f32)],
        "weight_place",
    )(sent, mine, flip)
    behind = whole_call(
        functools.partial(column_body, steps),
        shape(count, 2, height, lanes),
        [pltpu.VMEM((2, steps, size, lanes), f32)] * 2,
        "column_filter",
    )(ahead, down, up, weight, mirror, flip)
    behind = lax.all_to_all(behind, "rows", 0, 0, tiled=True)
    return whole_call(
        functools.partial(row_inverse_body, steps),
        [shape(height, length)] * 2,
        [pltpu.VMEM((count, height, 2 * lanes), f32)],
        "row_inverse",
    )(behind, back, values, dirty)


def filtered_plain(values, dirty, weights):
    height, length = values.shape
    row_count = lax.axis_size("rows")
    narrow = length // row_count
    spec_real, spec_imag = dft_last(values, jnp.zeros_like(values), -1.0)
    spec_real = spec_real.reshape(height, row_count, narrow)
    spec_imag = spec_imag.reshape(height, row_count, narrow)
    col_real, col_imag = columns_forward(
        (
            lax.all_to_all(spec_real, "rows", split_axis=1, concat_axis=0, tiled=True),
            lax.all_to_all(spec_imag, "rows", split_axis=1, concat_axis=0, tiled=True),
        )
    )
    prod_real = weights * col_real[:, 0, :]
    prod_imag = weights * col_imag[:, 0, :]
    back_real, back_imag = dft_first(prod_real, prod_imag, 1.0)
    back_real = back_real.reshape(row_count, height, narrow)
    back_imag = back_imag.reshape(row_count, height, narrow)
    blurred = rows_inverse(
        (
            lax.all_to_all(back_real, "rows", split_axis=0, concat_axis=2, tiled=True),
            lax.all_to_all(back_imag, "rows", split_axis=0, concat_axis=2, tiled=True),
        )
    )[0]
    residual = dirty - blurred
    return residual, values + step_size * residual


def shards(estimate, dirty_image, psf_weights):
    values = estimate[0]
    height, length = values.shape
    row_count = lax.axis_size("rows")
    if length == 2 * row_count * lane_count:
        residual, halfway = filtered(values, dirty_image[0], psf_weights[0])
    else:
        residual, halfway = filtered_plain(values, dirty_image[0], psf_weights[0])
    depth = 14
    chan_count = lax.axis_size("chan")
    part = length // chan_count
    padded = with_halo(halfway, (("rows", 0),), depth)
    padded = jnp.pad(padded, ((0, 0), (depth, depth)))
    pieces = jnp.stack(
        [padded[:, q * part : (q + 1) * part + 2 * depth] for q in range(chan_count)]
    )
    current = lax.all_to_all(pieces, "chan", split_axis=0, concat_axis=0, tiled=True)
    row_ids = lax.axis_index("rows") * height - depth + lax.iota(jnp.int32, height + 2 * depth)
    col_ids = lax.axis_index("chan") * part - depth + lax.iota(jnp.int32, part + 2 * depth)
    margin = depth
    details = []
    for scale_level in range(3):
        reach = 2 << scale_level
        smoother = smooth_both(current, 1 << scale_level)
        row_ids = row_ids[reach:-reach]
        col_ids = col_ids[reach:-reach]
        inside = ((row_ids >= 0) & (row_ids < length))[:, None] & (
            (col_ids >= 0) & (col_ids < length)
        )[None, :]
        smoother = jnp.where(inside[None], smoother, 0.0)
        new_margin = margin - reach
        details.append(
            current[:, margin : margin + height, margin : margin + part]
            - smoother[:, new_margin : new_margin + height, new_margin : new_margin + part]
        )
        current = smoother
        margin = new_margin
    energies = [jnp.sum(detail * detail, axis=0) for detail in details]
    peaks = jnp.stack([jnp.broadcast_to(jnp.max(energy), (128,)) for energy in energies])
    peaks = max_over(max_over(peaks, "rows"), "chan")
    output = current
    for scale_level in range(3):
        threshold = fractions[scale_level] * jnp.sqrt(peaks[scale_level, 0])
        factor = 1.0 - threshold / jnp.maximum(jnp.sqrt(energies[scale_level]), threshold)
        output = output + factor[None] * details[scale_level]
    output = lax.all_to_all(output, "chan", split_axis=0, concat_axis=2, tiled=True)[0]
    new_estimate = output[None]
    return (new_estimate, residual[None])


def solution(mesh):
    return jax.shard_map(
        shards,
        mesh=mesh,
        in_specs=(P("chan", "rows", None), P("chan", "rows", None), P("chan", None, "rows")),
        out_specs=(P("chan", "rows", None), P("chan", "rows", None)),
        check_vma=False,
    )
```

profile of v0, /device:TPU:0, one launch (start us, length us, event | category | flops | bytes accessed | tf_op | source)
XLA Modules:
  0.0 305.8 jit_solution(13022831751476686806)
XLA Ops:
  0.6 5.9 %weight_pick.1 = f32[8,512,128]{2,1,0:T(8,128)} custom-call(f32[4,512,256]{2,1,0:T(8,128)} %bitcast.28, bf16[1024,1024]{1,0:T(8,128)(2,1)} %constant.39.clone.pick_ref), custom_call_target="tpu_custom_call" | custom-call | tf_op jit(solution)/shard_map/weight_pick/pallas_call | solution.py:549
  6.5 5.2 %all-to-all-start.1 = ((f32[8,512,128]{2,1,0:T(8,128)}), f32[8,512,128]{2,1,0:T(8,128)S(1)}, u32[]{:S(2)}, u32[]{:S(2)}) async-start(f32[8,512,128]{2,1,0:T(8,128)} %weight_pick.1), calls=%async_computation.1 | async-start | bytes 4194304 | tf_op jit(solution)/shard_map/all_to_all | solution.py:552
  11.7 5.7 %row_forward.1 = f32[8,2,256,128]{3,2,1,0:T(8,128)} custom-call(f32[256,2048]{1,0:T(8,128)} %bitcast.24, bf16[8,2,256,256]{3,2,1,0:T(8,128)(2,1)} %constant.42.clone.table_ref), custom_call_target="tpu_custom_call" | custom-call | tf_op jit(solution)/shard_map/row_forward/pallas_call | solution.py:553
  17.4 21.0 %all-to-all-done.1.in_ref = f32[8,512,128]{2,1,0:T(8,128)S(1)} async-done(((f32[8,512,128]{2,1,0:T(8,128)}), f32[8,512,128]{2,1,0:T(8,128)S(1)}, u32[]{:S(2)}, u32[]{:S(2)}) %all-to-all-start.1) | async-done | bytes 2097184 | tf_op jit(solution)/shard_map/all_to_all | solution.py:552
  38.3 1.3 copy-done.4
  39.7 3.8 %all-to-all-start = ((f32[8,2,256,128]{3,2,1,0:T(8,128)}), f32[8,2,256,128]{3,2,1,0:T(8,128)S(1)}, u32[]{:S(2)}, u32[]{:S(2)}) async-start(f32[8,2,256,128]{3,2,1,0:T(8,128)} %row_forward.1), calls=%async_computation | async-start | bytes 4194304 | tf_op jit(solution)/shard_map/all_to_all | solution.py:559
  43.5 3.4 %select_bitcast_fusion.place_ref = bf16[1024,1152]{1,0:T(8,128)(2,1)} fusion(bf16[1,1024,1152]{2,1,0:T(8,128)(2,1)} %constant.21, bf16[1,1024,1152]{2,1,0:T(8,128)(2,1)} %constant.22, pred[]{:T(512)S(6)} %eq.3), kind=kLoop, calls=%fused_computation.42 | loop fusion | flops 1179648 | bytes 7077889 | tf_op jit(solution)/shard_map/jit(_where)/select_n | solution.py:560
  46.8 10.5 %weight_place.1 = (f32[16,128,128]{2,1,0:T(8,128)}, f32[16,128,128]{2,1,0:T(8,128)}) custom-call(f32[8,512,128]{2,1,0:T(8,128)} %copy-done.4, bf16[1024,1152]{1,0:T(8,128)(2,1)} %select_bitcast_fusion.place_ref, bf16[128,256]{1,0:T(8,128)(2,1)} %constant.41.clone.flip_ref), custom_call_target="tpu_custom_call" | custom-call | tf_op jit(solution)/shard_map/weight_place/pallas_call | solution.py:561
  57.3 12.5 %all-to-all-done.in_ref = f32[8,2,256,128]{3,2,1,0:T(8,128)S(1)} async-done(((f32[8,2,256,128]{3,2,1,0:T(8,128)}), f32[8,2,256,128]{3,2,1,0:T(8,128)S(1)}, u32[]{:S(2)}, u32[]{:S(2)}) %all-to-all-start) | async-done | bytes 2097184 | tf_op jit(solution)/shard_map/all_to_all | solution.py:559
  69.8 1.3 copy-done.3
  71.2 11.8 %column_filter.1 = f32[8,2,256,128]{3,2,1,0:T(8,128)} custom-call(f32[8,2,256,128]{3,2,1,0:T(8,128)} %copy-done.3, bf16[16,2,256,256]{3,2,1,0:T(8,128)(2,1)} %constant.44.clone.there_ref, bf16[16,2,256,256]{3,2,1,0:T(8,128)(2,1)} %constant.45.clone.back_ref, f32[16,128,128]{2,1,0:T(8,128)} %get-tuple-element.6.weight_ref, ...), custom_call_target="tpu_custom_call" | custom-call | tf_op jit(solution)/shard_map/column_filter/pallas_call | solution.py:567
  82.9 30.9 %all_to_all.38.in_ref = f32[8,2,256,128]{3,2,1,0:T(8,128)} all-to-all(f32[8,2,256,128]{3,2,1,0:T(8,128)} %column_filter.1), channel_id=1, replica_groups=mesh['chan'=4,'rows'=8] {'rows'}, dimensions={0} | all-to-all | bytes 4194304 | tf_op jit(solution)/shard_map/all_to_all | solution.py:573
  113.9 7.4 %row_inverse.1 = (f32[256,2048]{1,0:T(8,128)}, f32[256,2048]{1,0:T(8,128)}) custom-call(f32[8,2,256,128]{3,2,1,0:T(8,128)} %all_to_all.38.in_ref, bf16[8,2,256,256]{3,2,1,0:T(8,128)(2,1)} %constant.43.clone.table_ref, f32[256,2048]{1,0:T(8,128)} %bitcast.25, f32[256,2048]{1,0:T(8,128)} %bitcast.29), custom_call_target="tpu_custom_call" | custom-call | tf_op jit(solution)/shard_map/row_inverse/pallas_call | solution.py:574
  121.3 1.0 fusion.30
  122.3 1.3 collective-permute-start
  123.6 1.5 collective-permute-start.1
  125.1 2.5 collective-permute-done.1
  127.6 1.9 pad_maximum_fusion.1
  129.5 0.8 fusion.27
  130.3 1.8 pad_maximum_fusion
  132.1 4.9 %all-to-all-start.3 = ((f32[4,284,540]{2,1,0:T(8,128)}), f32[4,284,540]{2,1,0:T(8,128)S(1)}, u32[]{:S(2)}, u32[]{:S(2)}) async-start(f32[4,284,540]{2,1,0:T(8,128)} %pad_maximum_fusion), calls=%async_computation.3 | async-start | bytes 5898240 | tf_op jit(solution)/shard_map/all_to_all | solution.py:626
  137.5 0.8 broadcast_and_fusion.2
  138.6 65.2 %all-to-all-done.3 = f32[4,284,540]{2,1,0:T(8,128)S(1)} async-done(((f32[4,284,540]{2,1,0:T(8,128)}), f32[4,284,540]{2,1,0:T(8,128)S(1)}, u32[]{:S(2)}, u32[]{:S(2)}) %all-to-all-start.3) | async-done | bytes 2453792 | tf_op jit(solution)/shard_map/all_to_all | solution.py:626
  203.8 3.1 %fusion = f32[4,284,536]{2,1,0:T(8,128)S(1)} fusion(f32[4,284,540]{2,1,0:T(8,128)S(1)} %all-to-all-done.3), kind=kLoop, calls=%fused_computation.1 | loop fusion | flops 5480064 | bytes 14613504 | tf_op jit(solution)/shard_map/add | solution.py:137
  206.9 1.7 fusion.9
  208.6 3.0 fusion.4
  211.7 1.4 fusion.14
  213.1 2.4 fusion.18
  215.5 5.0 %multiply_reduce_fusion.2 = (f32[256,512]{1,0:T(8,128)S(1)}, f32[256,512]{1,0:T(8,128)}, f32[256,512]{1,0:T(8,128)}, f32[4,256,512]{2,1,0:T(8,128)}) fusion(f32[4,280,536]{2,1,0:T(8,128)S(1)} %fusion.9, f32[4,284,540]{2,1,0:T(8,128)S(1)} %all-to-all-done.3, f32[4,272,528]{2,1,0:T(8,128)S(1)} %fusion.14, f32[4,272,512]{2,1,0:T(8,128)S(1)} %fusion.18, ...), kind=kLoop, calls=%fused_computation.66 | loop fusion | flops 9568256 | bytes 20578304 | tf_op jit(solution)/shard_map/reduce_sum | solution.py:647
  220.5 1.8 reduce_max.29
  222.3 1.8 reduce_max.28
  224.1 0.7 reduce_max.27
  224.8 2.1 maximum_maximum_fusion
  227.0 0.9 collective-permute-start.2
  227.9 0.8 collective-permute-done.2
  228.8 3.3 %collective-permute-start.3 = (f32[3,128]{1,0:T(4,128)S(1)}, f32[3,128]{1,0:T(4,128)S(1)}, u32[]{:S(2)}, u32[]{:S(2)}) collective-permute-start(f32[3,128]{1,0:T(4,128)S(1)} %broadcast_maximum_fusion), channel_id=1, source_target_pairs={{0,2},{1,3},{2,0},{3,1},{4,6},{5,7},{6,4},{7,5},{8,10},{9,11},{10,... | collective-permute-start | bytes 4616 | tf_op jit(solution)/shard_map/ppermute | solution.py:125
  232.1 1.6 collective-permute-done.3
  233.7 2.1 collective-permute-start.4
  235.8 1.6 collective-permute-done.4
  237.4 3.6 %collective-permute-done.5 = f32[3,128]{1,0:T(4,128)S(1)} collective-permute-done((f32[3,128]{1,0:T(4,128)S(1)}, f32[3,128]{1,0:T(4,128)S(1)}, u32[]{:S(2)}, u32[]{:S(2)}) %collective-permute-start.5) | collective-permute-done | bytes 1568 | tf_op jit(solution)/shard_map/ppermute | solution.py:125
  241.0 4.5 %collective-permute-done.6 = f32[3,128]{1,0:T(4,128)S(1)} collective-permute-done((f32[3,128]{1,0:T(4,128)S(1)}, f32[3,128]{1,0:T(4,128)S(1)}, u32[]{:S(2)}, u32[]{:S(2)}) %collective-permute-start.6) | collective-permute-done | bytes 1568 | tf_op jit(solution)/shard_map/ppermute | solution.py:125
  245.5 0.6 fusion.31
  248.0 0.2 divide_subtract_fusion.2
  248.2 1.6 divide_subtract_fusion
  249.8 4.2 %multiply_add_fusion = f32[4,256,512]{2,1,0:T(8,128)S(1)} fusion(f32[4,256,512]{2,1,0:T(8,128)} %get-tuple-element.15, f32[4,272,528]{2,1,0:T(8,128)} %copy-done.2, f32[256,512]{1,0:T(8,128)S(1)} %get-tuple-element.25, f32[256,512]{1,0:T(8,128)S(1)} %get-tuple-element.26, f32[256,512]{1,0:T(8,128)S(1)} %divide_subtract_fusion.2, ...), kind=kLoop, calls=%fused_computation.63 | loop fusion | flops 4718592 | bytes 12058624 | tf_op jit(solution)/shard_map/add | solution.py:654
  254.0 47.1 %all_to_all.39 = f32[4,256,512]{2,1,0:T(8,128)S(1)} all-to-all(f32[4,256,512]{2,1,0:T(8,128)S(1)} %multiply_add_fusion), channel_id=1, replica_groups=mesh['chan'=4,'rows'=8] {'chan'}, dimensions={0} | all-to-all | bytes 4194304 | tf_op jit(solution)/shard_map/all_to_all | solution.py:655
  301.1 1.9 copy.12
  302.9 2.9 copy.13
  (29 shorter events, 1.0 us)
Async XLA Ops:
  6.5 31.8 %all-to-all-start.1 = ((f32[8,512,128]{2,1,0:T(8,128)}), f32[8,512,128]{2,1,0:T(8,128)S(1)}, u32[]{:S(2)}, u32[]{:S(2)}) async-start(f32[8,512,128]{2,1,0:T(8,128)} %weight_pick.1), calls=%async_computation.1 | async-start | bytes 4194304 | tf_op jit(solution)/shard_map/all_to_all | solution.py:552
  38.3 1.3 copy-start.4
  39.7 30.2 %all-to-all-start = ((f32[8,2,256,128]{3,2,1,0:T(8,128)}), f32[8,2,256,128]{3,2,1,0:T(8,128)S(1)}, u32[]{:S(2)}, u32[]{:S(2)}) async-start(f32[8,2,256,128]{3,2,1,0:T(8,128)} %row_forward.1), calls=%async_computation | async-start | bytes 4194304 | tf_op jit(solution)/shard_map/all_to_all | solution.py:559
  69.8 1.3 copy-start.3
  122.3 2.8 collective-permute-start
  123.6 4.0 %collective-permute-start.1 = (f32[14,2048]{1,0:T(8,128)S(1)}, f32[14,2048]{1,0:T(8,128)S(1)}, u32[]{:S(2)}, u32[]{:S(2)}) collective-permute-start(f32[14,2048]{1,0:T(8,128)S(1)} %get-tuple-element.21), channel_id=1, source_target_pairs={{1,0},{2,1},{3,2},{4,3},{5,4},{6,5},{7,6},{9,8},{10,9},{11,10},{12... | collective-permute-start | bytes 344072 | tf_op jit(solution)/shard_map/ppermute | solution.py:32
  132.1 71.7 %all-to-all-start.3 = ((f32[4,284,540]{2,1,0:T(8,128)}), f32[4,284,540]{2,1,0:T(8,128)S(1)}, u32[]{:S(2)}, u32[]{:S(2)}) async-start(f32[4,284,540]{2,1,0:T(8,128)} %pad_maximum_fusion), calls=%async_computation.3 | async-start | bytes 5898240 | tf_op jit(solution)/shard_map/all_to_all | solution.py:626
  208.6 6.8 %copy-start = (f32[4,280,536]{2,1,0:T(8,128)}, f32[4,280,536]{2,1,0:T(8,128)S(1)}, u32[]{:S(2)}) copy-start(f32[4,280,536]{2,1,0:T(8,128)S(1)} %fusion.9) | copy-start | bytes 7203844
  213.1 2.4 copy-start.2
  213.1 2.4 copy-start.5
  224.8 25.0 %copy-start.1 = (f32[4,280,536]{2,1,0:T(8,128)S(1)}, f32[4,280,536]{2,1,0:T(8,128)}, u32[]{:S(2)}) copy-start(f32[4,280,536]{2,1,0:T(8,128)} %copy-done) | copy-start | bytes 7203844
  227.0 1.7 collective-permute-start.2
  228.8 4.9 %collective-permute-start.3 = (f32[3,128]{1,0:T(4,128)S(1)}, f32[3,128]{1,0:T(4,128)S(1)}, u32[]{:S(2)}, u32[]{:S(2)}) collective-permute-start(f32[3,128]{1,0:T(4,128)S(1)} %broadcast_maximum_fusion), channel_id=1, source_target_pairs={{0,2},{1,3},{2,0},{3,1},{4,6},{5,7},{6,4},{7,5},{8,10},{9,11},{10,... | collective-permute-start | bytes 4616 | tf_op jit(solution)/shard_map/ppermute | solution.py:125
  233.7 3.7 %collective-permute-start.4 = (f32[3,128]{1,0:T(4,128)S(1)}, f32[3,128]{1,0:T(4,128)S(1)}, u32[]{:S(2)}, u32[]{:S(2)}) collective-permute-start(f32[3,128]{1,0:T(4,128)S(1)} %fusion.32), channel_id=1, source_target_pairs={{0,4},{1,5},{2,6},{3,7},{4,0},{5,1},{6,2},{7,3},{8,12},{9,13},{10,... | collective-permute-start | bytes 4616 | tf_op jit(solution)/shard_map/ppermute | solution.py:125
  237.4 3.6 %collective-permute-start.5 = (f32[3,128]{1,0:T(4,128)S(1)}, f32[3,128]{1,0:T(4,128)S(1)}, u32[]{:S(2)}, u32[]{:S(2)}) collective-permute-start(f32[3,128]{1,0:T(4,128)S(1)} %max.41), channel_id=1, source_target_pairs={{0,8},{8,0},{16,24},{24,16},{1,9},{9,1},{17,25},{25,17},{2,10},{10... | collective-permute-start | bytes 4616 | tf_op jit(solution)/shard_map/ppermute | solution.py:125
  241.0 4.5 %collective-permute-start.6 = (f32[3,128]{1,0:T(4,128)S(1)}, f32[3,128]{1,0:T(4,128)S(1)}, u32[]{:S(2)}, u32[]{:S(2)}) collective-permute-start(f32[3,128]{1,0:T(4,128)S(1)} %max.42), channel_id=1, source_target_pairs={{0,16},{8,24},{16,0},{24,8},{1,17},{9,25},{17,1},{25,9},{2,18},{10... | collective-permute-start | bytes 4616 | tf_op jit(solution)/shard_map/ppermute | solution.py:125
where the time goes:
time: 307 us; the launch traced here: 306 us
  waiting for transfers between devices  113 us (37%)
  blocking collectives  78 us (25%)
  Pallas kernels  41.2 us (13%)
  other arithmetic  37.8 us (12%)
  starting transfers between devices  22.9 us (7%)
  local copies, waits for them, and re-layouts  9.86 us (3%)
    all_to_all x1, waiting for transfers between devices, shards(): lax.all_to_all(pieces, 'chan', split_axis=0, concat_axis=0, tiled=True)  65.2 us
    all_to_all x1, blocking collectives, shards(): lax.all_to_all(output, 'chan', split_axis=0, concat_axis=2, tiled=True)[0]  47.1 us
    all_to_all x1, blocking collectives, filtered(): behind = lax.all_to_all(behind, 'rows', 0, 0, tiled=True)  30.9 us
    all_to_all x1, waiting for transfers between devices, filtered(): sent = lax.all_to_all(sent, 'rows', 0, 0, tiled=True)  21 us
    all_to_all x1, waiting for transfers between devices, filtered(): ahead = lax.all_to_all(ahead, 'rows', 0, 0, tiled=True)  12.5 us
    ppermute x5, waiting for transfers between devices, max_over(): other = lax.ppermute(cells, axis, [(i, i ^ distance) for i in range(count)])  12 us
    pallas_call x1, Pallas kernels, filtered(): whole_call(functools.partial(column_body, steps), shape(count, 2, height,...  11.8 us
    pallas_call x1, Pallas kernels, filtered(): whole_call(weight_place_body, [shape(steps, size, lanes)] * 2, [pltpu.VME...  10.5 us
  transfers between devices with their start and end apart: 10, of which 9 were waited for; matrix products, arithmetic and copies ran while one was open for 2% of the time, Pallas kernels for 5%

commit v1 on v0

--- a/solution.py
+++ b/solution.py
@@ -17,6 +17,8 @@
 highest = lax.Precision.HIGHEST
 lane_count = 128
 vmem_bytes = 56 * 1024 * 1024
+rim = 16
+halo_rows = 16
 
 
 def with_halo(cells, sides, width):
@@ -286,8 +288,13 @@
     return split_table(np.stack(there)), split_table(np.stack(back))
 
 
-def column_tables(length, steps):
+def column_tables(length, count, steps):
     size = length // steps
+    each = size // count
+    quarter = each // 4
+    order = np.r_[0:quarter, each - quarter : each, quarter : each - quarter]
+    order = (np.arange(count)[:, None] * each + order[None]).reshape(-1)
+    order = np.concatenate([order, size + order])
     spots = np.arange(size)
     there = []
     for step in range(steps):
@@ -295,7 +302,7 @@
         cosine, sine = np.cos(angles), np.sin(angles)
         there.append(np.block([[cosine, sine], [-sine, cosine]]))
     there = np.stack(there)
-    return split_table(there), split_table(np.swapaxes(there, 1, 2))
+    return split_table(there), split_table(np.swapaxes(there, 1, 2)[:, order])
 
 
 def weight_tables(length, count):
@@ -349,13 +356,20 @@
     )
 
 
-def whole_call(body, out_shapes, scratch, name):
+def busy(microseconds):
+    return pl.CostEstimate(
+        flops=0, bytes_accessed=int(microseconds * 3.5e6), transcendentals=0
+    )
+
+
+def whole_call(body, out_shapes, scratch, name, microseconds):
     return pl.pallas_call(
         body,
         out_shape=out_shapes,
         scratch_shapes=scratch,
         compiler_params=pltpu.CompilerParams(vmem_limit_bytes=vmem_bytes),
         name=name,
+        cost_estimate=busy(microseconds),
     )
 
 
@@ -383,32 +397,46 @@
             out_ref[group, 1, spread, :] = done[start : start + 8, lanes:]
 
 
-def row_inverse_body(steps, in_ref, table_ref, est_ref, dirty_ref, res_ref, half_ref, held):
-    groups, _, height, lanes = in_ref.shape
-    each = height // steps
-    for group in range(groups):
-        parts = []
-        for part in range(2):
-            pieces = [
-                in_ref[
-                    group,
-                    part,
-                    pl.ds(start % steps * each + start // steps, 8, stride=each),
-                    :,
+def row_inverse_body(
+    steps, in_ref, table_ref, est_ref, dirty_ref, old_ref, res_ref, half_ref, held
+):
+    del old_ref
+    groups, _, chunk, lanes = in_ref.shape
+    parts, _, wide = half_ref.shape
+    each = chunk // steps
+    block = est_ref.shape[0]
+    turn = pl.program_id(0)
+
+    @pl.when(turn == 0)
+    def _():
+        for group in range(groups):
+            halves = []
+            for part in range(2):
+                pieces = [
+                    in_ref[
+                        group,
+                        part,
+                        pl.ds(start % steps * each + start // steps, 8, stride=each),
+                        :,
+                    ]
+                    for start in range(0, chunk, 8)
                 ]
-                for start in range(0, height, 8)
-            ]
-            parts.append(jnp.concatenate(pieces, axis=0))
-        high, low = split(jnp.concatenate(parts, axis=1))
-        held[group] = (
-            dot(high, table_ref[group, 0])
-            + dot(low, table_ref[group, 0])
-            + dot(high, table_ref[group, 1])
-        )
-    for start in range(0, height, 8):
+                halves.append(jnp.concatenate(pieces, axis=0))
+            high, low = split(jnp.concatenate(halves, axis=1))
+            held[group] = (
+                dot(high, table_ref[group, 0])
+                + dot(low, table_ref[group, 0])
+                + dot(high, table_ref[group, 1])
+            )
+
+    per = wide // lanes
+    lane_ids = lax.broadcasted_iota(jnp.int32, (8, lanes), 1)
+    sides = [None] * parts
+    for start in range(0, block, 8):
         rows = pl.ds(start, 8)
+        chunk_rows = pl.ds(pl.multiple_of(turn * block + start, 8), 8)
         pairs = [
-            (held[group, rows, pl.ds(0, lanes)], held[group, rows, pl.ds(lanes, lanes)])
+            (held[group, chunk_rows, pl.ds(0, lanes)], held[group, chunk_rows, pl.ds(lanes, lanes)])
             for group in range(groups)
         ]
         pairs = [(pairs[0][0], None)] + pairs[1:] + [(pairs[0][1], None)]
@@ -417,11 +445,144 @@
             where = pl.ds(lanes * t, lanes)
             residual = dirty_ref[rows, where] - tiles[t]
             res_ref[rows, where] = residual
-            half_ref[rows, where] = est_ref[rows, where] + step_size * residual
+            tiles[t] = est_ref[rows, where] + step_size * residual
+            half_ref[t // per, chunk_rows, pl.ds(lanes * (t % per), lanes)] = tiles[t]
+        offset = start // 8 * 2 * rim % lanes
+        for part in range(parts):
+            done = jnp.zeros_like(tiles[0]) if offset == 0 else sides[part]
+            if part > 0:
+                turned = pltpu.roll(tiles[part * per - 1], (offset + rim) % lanes, 1)
+                done = jnp.where((lane_ids >= offset) & (lane_ids < offset + rim), turned, done)
+            if part < parts - 1:
+                turned = pltpu.roll(tiles[(part + 1) * per], (offset + rim) % lanes, 1)
+                done = jnp.where(
+                    (lane_ids >= offset + rim) & (lane_ids < offset + 2 * rim), turned, done
+                )
+            sides[part] = done
+            if offset + 2 * rim == lanes:
+                spot = turn * (block // 8 * 2 * rim // lanes) + start // 8 * 2 * rim // lanes
+                where = pl.ds(pl.multiple_of(spot * lanes, lanes), lanes)
+                half_ref[part, pl.ds(chunk, 8), where] = done
+
+
+def starlet_body(chans, q_ref, *refs):
+    edges, cores = refs[:chans], refs[chans : 2 * chans]
+    above, below = refs[2 * chans : 3 * chans], refs[3 * chans : 4 * chans]
+    detail_ref, energy_ref, peak_ref, cells, across = refs[4 * chans :]
+    _, _, height, part = detail_ref.shape
+    margin = 8
+    base = margin + halo_rows
+    lanes = lane_count
+    chunk = height // 2
+    quarter = height // 4
+    total = part + lanes
+    no_left, no_right = q_ref[0] > 0, q_ref[1] > 0
+    no_top, no_bottom = q_ref[2] > 0, q_ref[3] > 0
+    lane_ids = lax.broadcasted_iota(jnp.int32, (8, total), 1)
+    outside = ((lane_ids >= total - lanes // 2) & no_left) | (
+        (lane_ids >= part) & (lane_ids < total - lanes // 2) & no_right
+    )
+
+    def fill(target, source, source_row, count, pack_row, group):
+        cells[pl.ds(target, count), pl.ds(0, part)] = source[pl.ds(source_row, count), :]
+        for i in range(count // 8):
+            spot = (group + i) * 2 * rim
+            tile = source[pl.ds(pack_row, 8), pl.ds(spot // lanes * lanes, lanes)]
+            shift = (lanes - spot % lanes - rim) % lanes
+            cells[pl.ds(target + 8 * i, 8), pl.ds(part, lanes)] = pltpu.roll(tile, shift, 1)
+
+    for chan in range(chans):
+        edge, core = edges[chan], cores[chan]
+        fill(margin, above[chan], 0, halo_rows, halo_rows, (chunk - halo_rows) // 8)
+        fill(base, edge, 0, quarter, chunk, 0)
+        fill(base + quarter, core, 0, chunk, chunk, 0)
+        fill(base + 3 * quarter, edge, quarter, quarter, chunk, quarter // 8)
+        fill(base + height, below[chan], 0, halo_rows, halo_rows, 0)
+        for level in range(3):
+            gap = 1 << level
+            blocks = (height + 2 * halo_rows) // 8
+
+            def sweep(i, carry):
+                rows = pl.ds(pl.multiple_of(margin + 8 * i, 8), 8)
+                row = cells[rows, :]
+                near = pltpu.roll(row, gap, 1) + pltpu.roll(row, total - gap, 1)
+                far = pltpu.roll(row, 2 * gap, 1) + pltpu.roll(row, total - 2 * gap, 1)
+                across[rows, :] = (far + 4.0 * near) + 6.0 * row
+                return carry
+
+            lax.fori_loop(0, blocks, sweep, 0, unroll=6)
+
+            def down(i, carry, inner):
+                start = margin + 8 * i
+                if not isinstance(start, int):
+                    start = pl.multiple_of(start, 8)
+                rows = pl.ds(start, 8)
+                window = across[pl.ds(start - 8, 24), :]
+                near = window[8 - gap : 16 - gap] + window[8 + gap : 16 + gap]
+                far = window[8 - 2 * gap : 16 - 2 * gap] + window[8 + 2 * gap : 16 + 2 * gap]
+                smooth = ((far + 4.0 * near) + 6.0 * window[8:16]) * (1.0 / 256.0)
+                if not inner:
+                    gone = no_top if i < halo_rows // 8 else no_bottom
+                    cells[rows, :] = jnp.where(gone | outside, 0.0, smooth)
+                    return carry
+                smooth = jnp.where(outside, 0.0, smooth)
+                detail = cells[rows, pl.ds(0, part)] - smooth[:, :part]
+                cells[rows, :] = smooth
+                to = pl.ds(pl.multiple_of(8 * i - halo_rows, 8), 8)
+                detail_ref[chan, level, to, :] = detail
+                if level == 2:
+                    detail_ref[chan, 3, to, :] = smooth[:, :part]
+                square = detail * detail
+                if chan:
+                    square = square + energy_ref[level, to, :]
+                energy_ref[level, to, :] = square
+                if chan == chans - 1:
+                    return jnp.maximum(carry, square)
+                return carry
+
+            skirt = halo_rows // 8
+            if level < 2:
+                for i in range(skirt):
+                    down(i, 0, False)
+                    down(blocks - 1 - i, 0, False)
+            peak = lax.fori_loop(
+                skirt,
+                blocks - skirt,
+                functools.partial(down, inner=True),
+                jnp.zeros((8, part), jnp.float32),
+                unroll=8,
+            )
+            if chan == chans - 1:
+                most = peak[:, :lanes]
+                for t in range(1, part // lanes):
+                    most = jnp.maximum(most, peak[:, t * lanes : (t + 1) * lanes])
+                peak_ref[level] = most
+
+
+def shrink_body(chans, detail_ref, energy_ref, peak_ref, *out_refs):
+    factors = []
+    for level in range(3):
+        threshold = fractions[level] * jnp.sqrt(jnp.max(peak_ref[level], keepdims=True))
+        energy = jnp.sqrt(energy_ref[level])
+        threshold = jnp.broadcast_to(threshold, energy.shape)
+        factors.append(1.0 - threshold / jnp.maximum(energy, threshold))
+    for chan in range(chans):
+        total = detail_ref[chan, 3]
+        for level in range(3):
+            total = total + factors[level] * detail_ref[chan, level]
+        out_refs[chan][...] = total
+
+
+def join_body(me_ref, *refs):
+    chans = len(refs) - 1
+    part = refs[0].shape[1]
+    for chan in range(chans):
+        start = pl.multiple_of((me_ref[0] ^ chan) * part, part)
+        refs[-1][:, pl.ds(start, part)] = refs[chan][...]
 
 
 def column_body(
-    steps, in_ref, there_ref, back_ref, weight_ref, mirror_ref, flip_ref, out_ref, held, made
+    steps, in_ref, there_ref, back_ref, weight_ref, mirror_ref, flip_ref, edge_ref, core_ref, held, made
 ):
     count, _, height, lanes = in_ref.shape
     each = height // steps
@@ -478,11 +639,13 @@
             + dot(back_ref[step, 1], high)
             + dot(back_ref[step, 0], low)
         )
-        rows = pl.ds(step * each, each)
+        half = each // 2
+        rows = pl.ds(step * half, half)
         for part in range(2):
             for target in range(count):
                 start = part * size + target * each
-                out_ref[target, part, rows, :] = done[start : start + each]
+                edge_ref[target, part, rows, :] = done[start : start + half]
+                core_ref[target, part, rows, :] = done[start + half : start + each]
 
 
 def weight_pick_body(w_ref, pick_ref, out_ref):
@@ -540,13 +703,13 @@
     f32 = jnp.float32
     pick, place, flip = [jnp.asarray(table) for table in weight_tables(length, count)]
     there, back = [jnp.asarray(table) for table in row_tables(length, count)]
-    down, up = [jnp.asarray(table) for table in column_tables(length, steps)]
+    down, up = [jnp.asarray(table) for table in column_tables(length, count, steps)]
     shape = lambda *dims: jax.ShapeDtypeStruct(dims, f32)
     packs = length * width // (count * lanes) // (length // count)
     packs = pick.shape[0] // width
     depth = length // packs
 
-    sent = whole_call(weight_pick_body, shape(count, depth, lanes), [], "weight_pick")(
+    sent = whole_call(weight_pick_body, shape(count, depth, lanes), [], "weight_pick", 6)(
         weights.reshape(packs, depth, width), pick
     )
     sent = lax.all_to_all(sent, "rows", 0, 0, tiled=True)
@@ -555,6 +718,7 @@
         shape(count, 2, height, lanes),
         [pltpu.VMEM((2, count, height, 2 * lanes), jnp.bfloat16)],
         "row_forward",
+        6,
     )(values, there)
     ahead = lax.all_to_all(ahead, "rows", 0, 0, tiled=True)
     mine = jnp.where(lax.axis_index("rows") == 0, place[0], place[1])
@@ -563,20 +727,120 @@
         [shape(steps, size, lanes)] * 2,
         [pltpu.VMEM((steps, size, 2 * lanes), f32)],
         "weight_place",
+        10,
     )(sent, mine, flip)
-    behind = whole_call(
+    half = height // 2
+    edge, core = whole_call(
         functools.partial(column_body, steps),
-        shape(count, 2, height, lanes),
+        [shape(count, 2, half, lanes)] * 2,
         [pltpu.VMEM((2, steps, size, lanes), f32)] * 2,
         "column_filter",
+        12,
     )(ahead, down, up, weight, mirror, flip)
-    behind = lax.all_to_all(behind, "rows", 0, 0, tiled=True)
-    return whole_call(
-        functools.partial(row_inverse_body, steps),
-        [shape(height, length)] * 2,
-        [pltpu.VMEM((count, height, 2 * lanes), f32)],
-        "row_inverse",
-    )(behind, back, values, dirty)
+    edge = lax.all_to_all(edge, "rows", 0, 0, tiled=True)
+    core = lax.all_to_all(core, "rows", 0, 0, tiled=True)
+    chans = lax.axis_size("chan")
+    part = length // chans
+    quarter = height // 4
+
+    def row_inverse(cells, old, blocks):
+        rows_spec = pl.BlockSpec((quarter, length), lambda i: (blocks[0] + i * blocks[1], 0))
+        whole = lambda *dims: pl.BlockSpec(dims, lambda i: (0,) * len(dims))
+        return pl.pallas_call(
+            functools.partial(row_inverse_body, steps),
+            grid=(2,),
+            in_specs=[
+                whole(*cells.shape),
+                whole(*back.shape),
+                rows_spec,
+                rows_spec,
+                pl.BlockSpec(memory_space=pl.ANY),
+            ],
+            out_specs=[rows_spec, whole(chans, half + 8, part)],
+            out_shape=[shape(height, length), shape(chans, half + 8, part)],
+            scratch_shapes=[pltpu.VMEM((count, half, 2 * lanes), f32)],
+            input_output_aliases={4: 0} if old is not dirty else {},
+            compiler_params=pltpu.CompilerParams(vmem_limit_bytes=vmem_bytes),
+            name="row_inverse",
+        cost_estimate=busy(5),
+        )(cells, back, values, dirty, old)
+
+    def over_chans(cells):
+        me = lax.axis_index("chan")
+        got = []
+        for turn in range(chans):
+            mine = lax.dynamic_index_in_dim(cells, me ^ turn, 0, keepdims=False)
+            if turn:
+                mine = lax.ppermute(mine, "chan", [(i, i ^ turn) for i in range(chans)])
+            got.append(mine)
+        return got
+
+    residual, outer = row_inverse(edge, dirty, (0, 3))
+    outer = over_chans(outer)
+    core, *outer = lax.optimization_barrier((core, *outer))
+    residual, inner = row_inverse(core, residual, (1, 1))
+    inner = over_chans(inner)
+    ahead_pairs = [(i, i + 1) for i in range(count - 1)]
+    back_pairs = [(i + 1, i) for i in range(count - 1)]
+    last = jnp.stack([cells[half - halo_rows :] for cells in outer])
+    first = jnp.stack(
+        [jnp.concatenate([cells[:halo_rows], cells[half:]], axis=0) for cells in outer]
+    )
+    last = lax.ppermute(last, "rows", ahead_pairs)
+    first = lax.ppermute(first, "rows", back_pairs)
+    above = [last[c] for c in range(chans)]
+    below = [first[c] for c in range(chans)]
+    chan_id, row_id = lax.axis_index("chan"), lax.axis_index("rows")
+    at_end = jnp.stack(
+        [chan_id == 0, chan_id == chans - 1, row_id == 0, row_id == count - 1]
+    ).astype(jnp.int32)
+    vmem = pl.BlockSpec(memory_space=pltpu.VMEM)
+    details, energy, peaks = pl.pallas_call(
+        functools.partial(starlet_body, chans),
+        in_specs=[pl.BlockSpec(memory_space=pltpu.SMEM)] + [vmem] * (4 * chans),
+        out_specs=[vmem] * 3,
+        out_shape=[shape(chans, 4, height, part), shape(3, height, part), shape(3, 8, lanes)],
+        scratch_shapes=[
+            pltpu.VMEM((height + 2 * halo_rows + 16, part + lanes), f32),
+            pltpu.VMEM((height + 2 * halo_rows + 16, part + lanes), f32),
+        ],
+        compiler_params=pltpu.CompilerParams(vmem_limit_bytes=vmem_bytes),
+        name="starlet",
+        cost_estimate=busy(25),
+    )(at_end, *outer, *inner, *above, *below)
+    peaks = max_over(max_over(peaks, "rows"), "chan")
+    thick = height // 4
+    shrunk = pl.pallas_call(
+        functools.partial(shrink_body, chans),
+        grid=(4,),
+        in_specs=[
+            pl.BlockSpec((chans, 4, thick, part), lambda i: (0, 0, i, 0)),
+            pl.BlockSpec((3, thick, part), lambda i: (0, i, 0)),
+            pl.BlockSpec((3, 8, lanes), lambda i: (0, 0, 0)),
+        ],
+        out_specs=[pl.BlockSpec((thick, part), lambda i: (i, 0))] * chans,
+        out_shape=[shape(height, part)] * chans,
+        compiler_params=pltpu.CompilerParams(vmem_limit_bytes=vmem_bytes),
+        name="shrink",
+        cost_estimate=busy(6),
+    )(details, energy, peaks)
+    shrunk = [shrunk[0]] + [
+        lax.ppermute(shrunk[turn], "chan", [(i, i ^ turn) for i in range(chans)])
+        for turn in range(1, chans)
+    ]
+    new_estimate = pl.pallas_call(
+        join_body,
+        grid_spec=pltpu.PrefetchScalarGridSpec(
+            num_scalar_prefetch=1,
+            grid=(4,),
+            in_specs=[pl.BlockSpec((thick, part), lambda i, me: (i, 0))] * chans,
+            out_specs=pl.BlockSpec((thick, length), lambda i, me: (i, 0)),
+        ),
+        out_shape=shape(height, length),
+        name="join",
+        cost_estimate=busy(4),
+    )(jnp.reshape(chan_id, (1,)).astype(jnp.int32), *shrunk)
+    return new_estimate, residual
 
 
 def filtered_plain(values, dirty, weights):
@@ -607,14 +871,8 @@
     return residual, values + step_size * residual
 
 
-def shards(estimate, dirty_image, psf_weights):
-    values = estimate[0]
-    height, length = values.shape
-    row_count = lax.axis_size("rows")
-    if length == 2 * row_count * lane_count:
-        residual, halfway = filtered(values, dirty_image[0], psf_weights[0])
-    else:
-        residual, halfway = filtered_plain(values, dirty_image[0], psf_weights[0])
+def joined_plain(halfway):
+    height, length = halfway.shape
     depth = 14
     chan_count = lax.axis_size("chan")
     part = length // chan_count
@@ -653,8 +911,20 @@
         factor = 1.0 - threshold / jnp.maximum(jnp.sqrt(energies[scale_level]), threshold)
         output = output + factor[None] * details[scale_level]
     output = lax.all_to_all(output, "chan", split_axis=0, concat_axis=2, tiled=True)[0]
-    new_estimate = output[None]
-    return (new_estimate, residual[None])
+    return output
+
+
+def shards(estimate, dirty_image, psf_weights):
+    values, dirty, weights = estimate[0], dirty_image[0], psf_weights[0]
+    height, length = values.shape
+    row_count, chan_count = lax.axis_size("rows"), lax.axis_size("chan")
+    whole_tiles = length == 2 * row_count * lane_count and length % (chan_count * lane_count) == 0
+    if whole_tiles and chan_count & (chan_count - 1) == 0:
+        new_estimate, residual = filtered(values, dirty, weights)
+    else:
+        residual, halfway = filtered_plain(values, dirty, weights)
+        new_estimate = joined_plain(halfway)
+    return (new_estimate[None], residual[None])
 
 
 def solution(mesh):

time: 307 us -> 276 us (0.90); the launches traced: 306 us -> 271 us
  blocking collectives: 78 us -> 19.6 us
  Pallas kernels: 41.2 us -> 79.9 us
  other arithmetic: 37.8 us -> 5.36 us
  starting transfers between devices: 22.9 us -> 37.2 us
  waiting for transfers between devices: 113 us -> 122 us
  local copies, waits for them, and re-layouts: 9.86 us -> 6.53 us
    ppermute x2 -> x11, waiting for transfers between devices: 2.5 us -> 71.4 us  [the longest x6 37.2 us: over_chans(): mine = lax.ppermute(mine, 'chan', [(i, i ^ turn) for i in range(chans)])]
    all_to_all x1, waiting for transfers between devices: 65.2 us -> 4.4 us  [filtered(): core = lax.all_to_all(core, 'rows', 0, 0, tiled=True)]
    all_to_all x2 -> x1, blocking collectives: 78 us -> 19.6 us  [filtered(): edge = lax.all_to_all(edge, 'rows', 0, 0, tiled=True)]
    pallas_call x3 -> x7, Pallas kernels: 25.1 us -> 63.7 us  [the longest x1 27.2 us: filtered(): pl.pallas_call(functools.partial(starlet_body, chans), in_specs=[pl.Block...]
    ppermute x2 -> x11, starting transfers between devices: 2.81 us -> 16.2 us  [the longest x6 8.85 us: over_chans(): mine = lax.ppermute(mine, 'chan', [(i, i ^ turn) for i in range(chans)])]
    add x6 -> x0, other arithmetic: 12.7 us -> none  [the longest x3 8.47 us: smooth_both(): total + taps[tap_index] * lax.slice_in_dim(values, start, start + count,...]
    reduce_sum x1 -> x0, other arithmetic: 5.01 us -> none  [shards(): energies = [jnp.sum(detail * detail, axis=0) for detail in details]]
    squeeze x0 -> x4, local copies, waits for them, and re-layouts: none -> 4.66 us  [the longest x2 3.29 us: over_chans(): mine = lax.dynamic_index_in_dim(cells, me ^ turn, 0, keepdims=False)]
  transfers between devices with their start and end apart: 10 -> 19, of which waited for: 9 -> 14; matrix products, arithmetic and copies ran while one was open for 2% -> 3% of each run, Pallas kernels for 5% -> 9%
where the time goes in v1:
time: 276 us; the launch traced here: 271 us
  waiting for transfers between devices  122 us (44%)
  Pallas kernels  79.9 us (29%)
  starting transfers between devices  37.2 us (13%)
  blocking collectives  19.6 us (7%)
  local copies, waits for them, and re-layouts  6.53 us (2%)
  other arithmetic  5.36 us (2%)
    ppermute x6, waiting for transfers between devices, over_chans(): mine = lax.ppermute(mine, 'chan', [(i, i ^ turn) for i in range(chans)])  37.2 us
    ppermute x3, waiting for transfers between devices, filtered(): lax.ppermute(shrunk[turn], 'chan', [(i, i ^ turn) for i in range(chans)])  34.2 us
    pallas_call x1, Pallas kernels, filtered(): pl.pallas_call(functools.partial(starlet_body, chans), in_specs=[pl.Block...  27.2 us
    all_to_all x1, waiting for transfers between devices, filtered(): sent = lax.all_to_all(sent, 'rows', 0, 0, tiled=True)  21 us
    all_to_all x1, blocking collectives, filtered(): edge = lax.all_to_all(edge, 'rows', 0, 0, tiled=True)  19.6 us
    ppermute x5, waiting for transfers between devices, max_over(): other = lax.ppermute(cells, axis, [(i, i ^ distance) for i in range(count)])  12.7 us
    all_to_all x1, waiting for transfers between devices, filtered(): ahead = lax.all_to_all(ahead, 'rows', 0, 0, tiled=True)  12.5 us
    pallas_call x1, Pallas kernels, filtered(): whole_call(functools.partial(column_body, steps), [shape(count, 2, half,...  12 us
  transfers between devices with their start and end apart: 19, of which 14 were waited for; matrix products, arithmetic and copies ran while one was open for 3% of the time, Pallas kernels for 9%

profile of v1, /device:TPU:0, one launch (start us, length us, event | category | flops | bytes accessed | tf_op | source)
XLA Modules:
  0.0 271.5 jit_solution(3867723401745636560)
XLA Ops:
  0.6 5.9 %weight_pick.1 = f32[8,512,128]{2,1,0:T(8,128)} custom-call(f32[4,512,256]{2,1,0:T(8,128)} %bitcast.66, bf16[1024,1024]{1,0:T(8,128)(2,1)} %constant.51.clone.pick_ref), custom_call_target="tpu_custom_call" | custom-call | bytes 21000000 | tf_op jit(solution)/shard_map/weight_pick/pallas_call | solution.py:712
  6.5 5.2 %all-to-all-start.1 = ((f32[8,512,128]{2,1,0:T(8,128)}), f32[8,512,128]{2,1,0:T(8,128)S(1)}, u32[]{:S(2)}, u32[]{:S(2)}) async-start(f32[8,512,128]{2,1,0:T(8,128)} %weight_pick.1), calls=%async_computation.1 | async-start | bytes 4194304 | tf_op jit(solution)/shard_map/all_to_all | solution.py:715
  11.7 5.7 %row_forward.1 = f32[8,2,256,128]{3,2,1,0:T(8,128)} custom-call(f32[256,2048]{1,0:T(8,128)} %bitcast.60, bf16[8,2,256,256]{3,2,1,0:T(8,128)(2,1)} %constant.54.clone.table_ref), custom_call_target="tpu_custom_call" | custom-call | bytes 21000000 | tf_op jit(solution)/shard_map/row_forward/pallas_call | solution.py:716
  17.4 21.0 %all-to-all-done.1.in_ref = f32[8,512,128]{2,1,0:T(8,128)S(1)} async-done(((f32[8,512,128]{2,1,0:T(8,128)}), f32[8,512,128]{2,1,0:T(8,128)S(1)}, u32[]{:S(2)}, u32[]{:S(2)}) %all-to-all-start.1) | async-done | bytes 2097184 | tf_op jit(solution)/shard_map/all_to_all | solution.py:715
  38.3 4.5 %all-to-all-start = ((f32[8,2,256,128]{3,2,1,0:T(8,128)}), f32[8,2,256,128]{3,2,1,0:T(8,128)}, u32[]{:S(2)}, u32[]{:S(2)}) async-start(f32[8,2,256,128]{3,2,1,0:T(8,128)} %row_forward.1), calls=%async_computation | async-start | bytes 4194304 | tf_op jit(solution)/shard_map/all_to_all | solution.py:723
  42.9 3.4 %select_bitcast_fusion.place_ref = bf16[1024,1152]{1,0:T(8,128)(2,1)} fusion(bf16[1,1024,1152]{2,1,0:T(8,128)(2,1)} %constant.61, bf16[1,1024,1152]{2,1,0:T(8,128)(2,1)} %constant.62, pred[]{:T(512)} %eq.15), kind=kLoop, calls=%fused_computation | loop fusion | flops 1179648 | bytes 7077889 | tf_op jit(solution)/shard_map/jit(_where)/select_n | solution.py:724
  46.3 10.5 %weight_place.1 = (f32[16,128,128]{2,1,0:T(8,128)}, f32[16,128,128]{2,1,0:T(8,128)}) custom-call(f32[8,512,128]{2,1,0:T(8,128)} %copy-done, bf16[1024,1152]{1,0:T(8,128)(2,1)} %select_bitcast_fusion.place_ref, bf16[128,256]{1,0:T(8,128)(2,1)} %constant.53.clone.flip_ref), custom_call_target="tpu_custom_call" | custom-call | bytes 35000000 | tf_op jit(solution)/shard_map/weight_place/pallas_call | solution.py:725
  56.8 12.5 %all-to-all-done.in_ref = f32[8,2,256,128]{3,2,1,0:T(8,128)} async-done(((f32[8,2,256,128]{3,2,1,0:T(8,128)}), f32[8,2,256,128]{3,2,1,0:T(8,128)}, u32[]{:S(2)}, u32[]{:S(2)}) %all-to-all-start) | async-done | bytes 2097184 | tf_op jit(solution)/shard_map/all_to_all | solution.py:723
  69.4 12.0 %column_filter.1 = (f32[8,2,128,128]{3,2,1,0:T(8,128)}, f32[8,2,128,128]{3,2,1,0:T(8,128)}) custom-call(f32[8,2,256,128]{3,2,1,0:T(8,128)} %all-to-all-done.in_ref, bf16[16,2,256,256]{3,2,1,0:T(8,128)(2,1)} %constant.56.clone.there_ref, bf16[16,2,256,256]{3,2,1,0:T(8,128)(2,1)} %constant.57.clone.back_ref, f32[16,128,128]{2,1,0:T(8,128)} %get-tuple-element.22.weight_ref, ...), custom_call_target="tpu_custom_call" | custom-call | bytes 42000000 | tf_op jit(solution)/shard_map/column_filter/pallas_call | solution.py:733
  81.4 19.6 %all_to_all.20.in_ref = f32[8,2,128,128]{3,2,1,0:T(8,128)} all-to-all(f32[8,2,128,128]{3,2,1,0:T(8,128)} %get-tuple-element.25), channel_id=1, replica_groups=mesh['chan'=4,'rows'=8] {'rows'}, dimensions={0} | all-to-all | bytes 2097152 | tf_op jit(solution)/shard_map/all_to_all | solution.py:740
  100.9 3.6 %all-to-all-start.2 = ((f32[8,2,128,128]{3,2,1,0:T(8,128)}), f32[8,2,128,128]{3,2,1,0:T(8,128)S(1)}, u32[]{:S(2)}, u32[]{:S(2)}) async-start(f32[8,2,128,128]{3,2,1,0:T(8,128)} %get-tuple-element.24), calls=%async_computation.2 | async-start | bytes 2097152 | tf_op jit(solution)/shard_map/all_to_all | solution.py:741
  104.5 4.5 %row_inverse.2 = (f32[256,2048]{1,0:T(8,128)}, f32[4,136,512]{2,1,0:T(8,128)}) custom-call(f32[8,2,128,128]{3,2,1,0:T(8,128)} %all_to_all.20.in_ref, bf16[8,2,256,256]{3,2,1,0:T(8,128)(2,1)} %constant.55.clone.table_ref, f32[256,2048]{1,0:T(8,128)} %bitcast.61, f32[256,2048]{1,0:T(8,128)} %bitcast.63, f32[256,2048]{1,0:T(8,128)} %bitcast.64), custom_call_target="tpu_custom_call" | custom-call | bytes 17500000 | tf_op jit(solution)/shard_map/row_inverse/pallas_call | solution.py:749
  109.0 1.3 dynamic-slice_bitcast_fusion.4
  110.3 3.7 %collective-permute-start.2 = (f32[136,512]{1,0:T(8,128)S(1)}, f32[136,512]{1,0:T(8,128)S(1)}, u32[]{:S(2)}, u32[]{:S(2)}) collective-permute-start(f32[136,512]{1,0:T(8,128)S(1)} %get-tuple-element.46), channel_id=1, source_target_pairs={{0,24},{8,16},{16,8},{24,0},{1,25},{9,17},{17,9},{25,1},{2,26},{10... | collective-permute-start | bytes 835592 | tf_op jit(solution)/shard_map/ppermute | solution.py:774
  114.0 0.8 collective-permute-start
  114.8 0.6 add_convert_fusion.q_ref
  115.4 4.4 %all-to-all-done.2.in_ref = f32[8,2,128,128]{3,2,1,0:T(8,128)S(1)} async-done(((f32[8,2,128,128]{3,2,1,0:T(8,128)}), f32[8,2,128,128]{3,2,1,0:T(8,128)S(1)}, u32[]{:S(2)}, u32[]{:S(2)}) %all-to-all-start.2) | async-done | bytes 1048608 | tf_op jit(solution)/shard_map/all_to_all | solution.py:741
  119.8 2.0 collective-permute-done.2.refs_3_
  121.8 16.4 %collective-permute-done.1.refs_2_ = f32[136,512]{1,0:T(8,128)S(1)} collective-permute-done((f32[136,512]{1,0:T(8,128)S(1)}, f32[136,512]{1,0:T(8,128)S(1)}, u32[]{:S(2)}, u32[]{:S(2)}) %collective-permute-start.1) | collective-permute-done | bytes 278560 | tf_op jit(solution)/shard_map/ppermute | solution.py:774
  138.4 1.5 collective-permute-start.6
  140.0 1.5 collective-permute-start.7
  141.5 4.5 %row_inverse.3 = (f32[256,2048]{1,0:T(8,128)}, f32[4,136,512]{2,1,0:T(8,128)}) custom-call(f32[8,2,128,128]{3,2,1,0:T(8,128)} %copy-done.1, bf16[8,2,256,256]{3,2,1,0:T(8,128)(2,1)} %constant.55.clone.table_ref, f32[256,2048]{1,0:T(8,128)} %bitcast.62, f32[256,2048]{1,0:T(8,128)} %bitcast.65, ...), custom_call_target="tpu_custom_call", output_to_operand_aliasing={{0}: (4, {})} | custom-call | bytes 17500000 | tf_op jit(solution)/shard_map/row_inverse/pallas_call | solution.py:749
  146.0 2.0 dynamic-slice_bitcast_fusion
  148.0 2.5 collective-permute-start.5
  150.5 1.9 collective-permute-start.3
  152.4 0.7 slice_bitcast_fusion.4
  153.1 0.7 slice_bitcast_fusion
  153.8 3.9 %collective-permute-done.5.refs_7_ = f32[136,512]{1,0:T(8,128)S(1)} collective-permute-done((f32[136,512]{1,0:T(8,128)S(1)}, f32[136,512]{1,0:T(8,128)S(1)}, u32[]{:S(2)}, u32[]{:S(2)}) %collective-permute-start.5) | collective-permute-done | bytes 278560 | tf_op jit(solution)/shard_map/ppermute | solution.py:774
  157.7 15.0 %collective-permute-done.4.refs_6_ = f32[136,512]{1,0:T(8,128)S(1)} collective-permute-done((f32[136,512]{1,0:T(8,128)S(1)}, f32[136,512]{1,0:T(8,128)S(1)}, u32[]{:S(2)}, u32[]{:S(2)}) %collective-permute-start.4) | collective-permute-done | bytes 278560 | tf_op jit(solution)/shard_map/ppermute | solution.py:774
  172.6 0.7 copy-done.10
  173.4 27.2 %starlet.1 = (f32[4,4,256,512]{3,2,1,0:T(8,128)}, f32[3,256,512]{2,1,0:T(8,128)}, f32[3,8,128]{2,1,0:T(8,128)}) custom-call(s32[4]{0:T(128)} %add_convert_fusion.q_ref, f32[136,512]{1,0:T(8,128)} %copy-done.2, f32[136,512]{1,0:T(8,128)} %copy-done.8, f32[136,512]{1,0:T(8,128)} %copy-done.7, f32[136,512]{1,0:T(8,128)} %copy-done.6, ...), custom_call_target="tpu_custom_call" | custom-call | bytes 87500000 | tf_op jit(solution)/shard_map/starlet/pallas_call | solution.py:798
  200.6 1.8 collective-permute-start.8
  202.4 1.0 collective-permute-done.8
  203.4 0.7 max.15
  204.1 3.9 %collective-permute-start.9 = (f32[3,8,128]{2,1,0:T(8,128)S(1)}, f32[3,8,128]{2,1,0:T(8,128)S(1)}, u32[]{:S(2)}, u32[]{:S(2)}) collective-permute-start(f32[3,8,128]{2,1,0:T(8,128)S(1)} %max.15), channel_id=1, source_target_pairs={{0,2},{1,3},{2,0},{3,1},{4,6},{5,7},{6,4},{7,5},{8,10},{9,11},{10,... | collective-permute-start | bytes 36872 | tf_op jit(solution)/shard_map/ppermute | solution.py:127
  208.0 1.7 collective-permute-done.9
  209.7 2.0 collective-permute-start.10
  211.7 1.7 collective-permute-done.10
  213.4 3.7 %collective-permute-done.11 = f32[3,8,128]{2,1,0:T(8,128)S(1)} collective-permute-done((f32[3,8,128]{2,1,0:T(8,128)S(1)}, f32[3,8,128]{2,1,0:T(8,128)S(1)}, u32[]{:S(2)}, u32[]{:S(2)}) %collective-permute-start.11) | collective-permute-done | bytes 12320 | tf_op jit(solution)/shard_map/ppermute | solution.py:127
  217.1 4.6 %collective-permute-done.12 = f32[3,8,128]{2,1,0:T(8,128)S(1)} collective-permute-done((f32[3,8,128]{2,1,0:T(8,128)S(1)}, f32[3,8,128]{2,1,0:T(8,128)S(1)}, u32[]{:S(2)}, u32[]{:S(2)}) %collective-permute-start.12) | collective-permute-done | bytes 12320 | tf_op jit(solution)/shard_map/ppermute | solution.py:127
  221.7 0.6 max.19.peak_ref
  222.3 5.8 %shrink.1 = (f32[256,512]{1,0:T(8,128)}, f32[256,512]{1,0:T(8,128)}, f32[256,512]{1,0:T(8,128)}, f32[256,512]{1,0:T(8,128)}) custom-call(f32[4,4,256,512]{3,2,1,0:T(8,128)} %get-tuple-element.34.detail_ref, f32[3,256,512]{2,1,0:T(8,128)} %get-tuple-element.35.energy_ref, f32[3,8,128]{2,1,0:T(8,128)} %max.19.peak_ref), custom_call_target="tpu_custom_call" | custom-call | bytes 21000000 | tf_op jit(solution)/shard_map/shrink/pallas_call | solution.py:813
  228.2 1.8 collective-permute-start.14
  230.0 2.5 collective-permute-start.15
  232.5 15.3 %collective-permute-done.13.refs_1_ = f32[256,512]{1,0:T(8,128)S(1)} collective-permute-done((f32[256,512]{1,0:T(8,128)}, f32[256,512]{1,0:T(8,128)S(1)}, u32[]{:S(2)}, u32[]{:S(2)}) %collective-permute-start.13) | collective-permute-done | bytes 524320 | tf_op jit(solution)/shard_map/ppermute | solution.py:828
  247.8 18.9 %collective-permute-done.14.refs_2_ = f32[256,512]{1,0:T(8,128)S(1)} collective-permute-done((f32[256,512]{1,0:T(8,128)}, f32[256,512]{1,0:T(8,128)S(1)}, u32[]{:S(2)}, u32[]{:S(2)}) %collective-permute-start.14) | collective-permute-done | bytes 524320 | tf_op jit(solution)/shard_map/ppermute | solution.py:828
  266.7 0.8 copy-done.4
  267.6 3.8 %join.1 = f32[256,2048]{1,0:T(8,128)} custom-call(s32[1]{0:T(128)} %bitcast.me_ref, f32[256,512]{1,0:T(8,128)} %get-tuple-element.37.refs_0_, f32[256,512]{1,0:T(8,128)} %copy-done.3, f32[256,512]{1,0:T(8,128)} %copy-done.4, f32[256,512]{1,0:T(8,128)} %copy-done.5), custom_call_target="tpu_custom_call" | custom-call | bytes 14000000 | tf_op jit(solution)/shard_map/join/pallas_call | solution.py:831
  (49 shorter events, 0.6 us)
Async XLA Ops:
  6.5 31.8 %all-to-all-start.1 = ((f32[8,512,128]{2,1,0:T(8,128)}), f32[8,512,128]{2,1,0:T(8,128)S(1)}, u32[]{:S(2)}, u32[]{:S(2)}) async-start(f32[8,512,128]{2,1,0:T(8,128)} %weight_pick.1), calls=%async_computation.1 | async-start | bytes 4194304 | tf_op jit(solution)/shard_map/all_to_all | solution.py:715
  38.3 4.6 %copy-start = (f32[8,512,128]{2,1,0:T(8,128)}, f32[8,512,128]{2,1,0:T(8,128)S(1)}, u32[]{:S(2)}) copy-start(f32[8,512,128]{2,1,0:T(8,128)S(1)} %all-to-all-done.1.in_ref) | copy-start | bytes 6291460
  38.3 31.0 %all-to-all-start = ((f32[8,2,256,128]{3,2,1,0:T(8,128)}), f32[8,2,256,128]{3,2,1,0:T(8,128)}, u32[]{:S(2)}, u32[]{:S(2)}) async-start(f32[8,2,256,128]{3,2,1,0:T(8,128)} %row_forward.1), calls=%async_computation | async-start | bytes 4194304 | tf_op jit(solution)/shard_map/all_to_all | solution.py:723
  100.9 18.9 %all-to-all-start.2 = ((f32[8,2,128,128]{3,2,1,0:T(8,128)}), f32[8,2,128,128]{3,2,1,0:T(8,128)S(1)}, u32[]{:S(2)}, u32[]{:S(2)}) async-start(f32[8,2,128,128]{3,2,1,0:T(8,128)} %get-tuple-element.24), calls=%async_computation.2 | async-start | bytes 2097152 | tf_op jit(solution)/shard_map/all_to_all | solution.py:741
  110.3 35.7 %copy-start.2 = (f32[136,512]{1,0:T(8,128)}, f32[136,512]{1,0:T(8,128)S(1)}, u32[]{:S(2)}) copy-start(f32[136,512]{1,0:T(8,128)S(1)} %get-tuple-element.27.refs_0_) | copy-start | bytes 835588
  110.3 11.5 %collective-permute-start.2 = (f32[136,512]{1,0:T(8,128)S(1)}, f32[136,512]{1,0:T(8,128)S(1)}, u32[]{:S(2)}, u32[]{:S(2)}) collective-permute-start(f32[136,512]{1,0:T(8,128)S(1)} %get-tuple-element.46), channel_id=1, source_target_pairs={{0,24},{8,16},{16,8},{24,0},{1,25},{9,17},{17,9},{25,1},{2,26},{10... | collective-permute-start | bytes 835592 | tf_op jit(solution)/shard_map/ppermute | solution.py:774
  114.0 24.2 %collective-permute-start.1 = (f32[136,512]{1,0:T(8,128)S(1)}, f32[136,512]{1,0:T(8,128)S(1)}, u32[]{:S(2)}, u32[]{:S(2)}) collective-permute-start(f32[136,512]{1,0:T(8,128)S(1)} %get-tuple-element.47), channel_id=1, source_target_pairs={{0,16},{8,24},{16,0},{24,8},{1,17},{9,25},{17,1},{25,9},{2,18},{10... | collective-permute-start | bytes 835592 | tf_op jit(solution)/shard_map/ppermute | solution.py:774
  114.0 24.2 %collective-permute-start = (f32[136,512]{1,0:T(8,128)S(1)}, f32[136,512]{1,0:T(8,128)S(1)}, u32[]{:S(2)}, u32[]{:S(2)}) collective-permute-start(f32[136,512]{1,0:T(8,128)S(1)} %get-tuple-element.48), channel_id=1, source_target_pairs={{0,8},{8,0},{16,24},{24,16},{1,9},{9,1},{17,25},{25,17},{2,10},{10... | collective-permute-start | bytes 835592 | tf_op jit(solution)/shard_map/ppermute | solution.py:774
  119.8 21.6 %copy-start.1 = (f32[8,2,128,128]{3,2,1,0:T(8,128)}, f32[8,2,128,128]{3,2,1,0:T(8,128)S(1)}, u32[]{:S(2)}) copy-start(f32[8,2,128,128]{3,2,1,0:T(8,128)S(1)} %all-to-all-done.2.in_ref) | copy-start | bytes 3145732
  121.8 24.2 %copy-start.6 = (f32[136,512]{1,0:T(8,128)}, f32[136,512]{1,0:T(8,128)S(1)}, u32[]{:S(2)}) copy-start(f32[136,512]{1,0:T(8,128)S(1)} %collective-permute-done.2.refs_3_) | copy-start | bytes 835588
  138.3 7.8 %copy-start.7 = (f32[136,512]{1,0:T(8,128)}, f32[136,512]{1,0:T(8,128)S(1)}, u32[]{:S(2)}) copy-start(f32[136,512]{1,0:T(8,128)S(1)} %collective-permute-done.1.refs_2_) | copy-start | bytes 835588
  138.3 7.8 %copy-start.8 = (f32[136,512]{1,0:T(8,128)}, f32[136,512]{1,0:T(8,128)S(1)}, u32[]{:S(2)}) copy-start(f32[136,512]{1,0:T(8,128)S(1)} %collective-permute-done.refs_1_) | copy-start | bytes 835588
  138.4 14.0 %collective-permute-start.6 = (f32[4,24,512]{2,1,0:T(8,128)S(1)}, f32[4,24,512]{2,1,0:T(8,128)S(1)}, u32[]{:S(2)}, u32[]{:S(2)}) collective-permute-start(f32[4,24,512]{2,1,0:T(8,128)S(1)} %pad_maximum_fusion), channel_id=1, source_target_pairs={{0,1},{1,2},{2,3},{3,4},{4,5},{5,6},{6,7},{8,9},{9,10},{10,11},{11... | collective-permute-start | bytes 589832 | tf_op jit(solution)/shard_map/ppermute | solution.py:789
  140.0 13.2 %collective-permute-start.7 = (f32[4,24,512]{2,1,0:T(8,128)S(1)}, f32[4,24,512]{2,1,0:T(8,128)S(1)}, u32[]{:S(2)}, u32[]{:S(2)}) collective-permute-start(f32[4,24,512]{2,1,0:T(8,128)S(1)} %pad_maximum_fusion.1), channel_id=1, source_target_pairs={{1,0},{2,1},{3,2},{4,3},{5,4},{6,5},{7,6},{9,8},{10,9},{11,10},{12... | collective-permute-start | bytes 589832 | tf_op jit(solution)/shard_map/ppermute | solution.py:790
  148.0 9.6 %collective-permute-start.5 = (f32[136,512]{1,0:T(8,128)S(1)}, f32[136,512]{1,0:T(8,128)S(1)}, u32[]{:S(2)}, u32[]{:S(2)}) collective-permute-start(f32[136,512]{1,0:T(8,128)S(1)} %get-tuple-element.42), channel_id=1, source_target_pairs={{0,24},{8,16},{16,8},{24,0},{1,25},{9,17},{17,9},{25,1},{2,26},{10... | collective-permute-start | bytes 835592 | tf_op jit(solution)/shard_map/ppermute | solution.py:774
  150.5 22.1 %collective-permute-start.4 = (f32[136,512]{1,0:T(8,128)S(1)}, f32[136,512]{1,0:T(8,128)S(1)}, u32[]{:S(2)}, u32[]{:S(2)}) collective-permute-start(f32[136,512]{1,0:T(8,128)S(1)} %get-tuple-element.43), channel_id=1, source_target_pairs={{0,16},{8,24},{16,0},{24,8},{1,17},{9,25},{17,1},{25,9},{2,18},{10... | collective-permute-start | bytes 835592 | tf_op jit(solution)/shard_map/ppermute | solution.py:774
  150.5 22.1 %collective-permute-start.3 = (f32[136,512]{1,0:T(8,128)S(1)}, f32[136,512]{1,0:T(8,128)S(1)}, u32[]{:S(2)}, u32[]{:S(2)}) collective-permute-start(f32[136,512]{1,0:T(8,128)S(1)} %get-tuple-element.44), channel_id=1, source_target_pairs={{0,8},{8,0},{16,24},{24,16},{1,9},{9,1},{17,25},{25,17},{2,10},{10... | collective-permute-start | bytes 835592 | tf_op jit(solution)/shard_map/ppermute | solution.py:774
  157.7 15.0 %copy-start.9 = (f32[136,512]{1,0:T(8,128)}, f32[136,512]{1,0:T(8,128)S(1)}, u32[]{:S(2)}) copy-start(f32[136,512]{1,0:T(8,128)S(1)} %collective-permute-done.5.refs_7_) | copy-start | bytes 835588
  172.6 0.7 copy-start.10
  172.6 0.8 copy-start.11
  200.6 2.8 %collective-permute-start.8 = (f32[3,8,128]{2,1,0:T(8,128)}, f32[3,8,128]{2,1,0:T(8,128)S(1)}, u32[]{:S(2)}, u32[]{:S(2)}) collective-permute-start(f32[3,8,128]{2,1,0:T(8,128)} %get-tuple-element.36), channel_id=1, source_target_pairs={{0,1},{1,0},{2,3},{3,2},{4,5},{5,4},{6,7},{7,6},{8,9},{9,8},{10,11... | collective-permute-start | bytes 36872 | tf_op jit(solution)/shard_map/ppermute | solution.py:127
  204.1 5.6 %collective-permute-start.9 = (f32[3,8,128]{2,1,0:T(8,128)S(1)}, f32[3,8,128]{2,1,0:T(8,128)S(1)}, u32[]{:S(2)}, u32[]{:S(2)}) collective-permute-start(f32[3,8,128]{2,1,0:T(8,128)S(1)} %max.15), channel_id=1, source_target_pairs={{0,2},{1,3},{2,0},{3,1},{4,6},{5,7},{6,4},{7,5},{8,10},{9,11},{10,... | collective-permute-start | bytes 36872 | tf_op jit(solution)/shard_map/ppermute | solution.py:127
  209.7 3.7 %collective-permute-start.10 = (f32[3,8,128]{2,1,0:T(8,128)S(1)}, f32[3,8,128]{2,1,0:T(8,128)S(1)}, u32[]{:S(2)}, u32[]{:S(2)}) collective-permute-start(f32[3,8,128]{2,1,0:T(8,128)S(1)} %max.16), channel_id=1, source_target_pairs={{0,4},{1,5},{2,6},{3,7},{4,0},{5,1},{6,2},{7,3},{8,12},{9,13},{10,... | collective-permute-start | bytes 36872 | tf_op jit(solution)/shard_map/ppermute | solution.py:127
  213.4 3.7 %collective-permute-start.11 = (f32[3,8,128]{2,1,0:T(8,128)S(1)}, f32[3,8,128]{2,1,0:T(8,128)S(1)}, u32[]{:S(2)}, u32[]{:S(2)}) collective-permute-start(f32[3,8,128]{2,1,0:T(8,128)S(1)} %max.17), channel_id=1, source_target_pairs={{0,8},{8,0},{16,24},{24,16},{1,9},{9,1},{17,25},{25,17},{2,10},{10... | collective-permute-start | bytes 36872 | tf_op jit(solution)/shard_map/ppermute | solution.py:127
  217.1 4.6 %collective-permute-start.12 = (f32[3,8,128]{2,1,0:T(8,128)S(1)}, f32[3,8,128]{2,1,0:T(8,128)S(1)}, u32[]{:S(2)}, u32[]{:S(2)}) collective-permute-start(f32[3,8,128]{2,1,0:T(8,128)S(1)} %max.18), channel_id=1, source_target_pairs={{0,16},{8,24},{16,0},{24,8},{1,17},{9,25},{17,1},{25,9},{2,18},{10... | collective-permute-start | bytes 36872 | tf_op jit(solution)/shard_map/ppermute | solution.py:127
  228.1 19.7 %collective-permute-start.13 = (f32[256,512]{1,0:T(8,128)}, f32[256,512]{1,0:T(8,128)S(1)}, u32[]{:S(2)}, u32[]{:S(2)}) collective-permute-start(f32[256,512]{1,0:T(8,128)} %get-tuple-element.38), channel_id=1, source_target_pairs={{0,8},{8,0},{16,24},{24,16},{1,9},{9,1},{17,25},{25,17},{2,10},{10... | collective-permute-start | bytes 1572872 | tf_op jit(solution)/shard_map/ppermute | solution.py:828
  228.2 38.4 %collective-permute-start.14 = (f32[256,512]{1,0:T(8,128)}, f32[256,512]{1,0:T(8,128)S(1)}, u32[]{:S(2)}, u32[]{:S(2)}) collective-permute-start(f32[256,512]{1,0:T(8,128)} %get-tuple-element.39), channel_id=1, source_target_pairs={{0,16},{8,24},{16,0},{24,8},{1,17},{9,25},{17,1},{25,9},{2,18},{10... | collective-permute-start | bytes 1572872 | tf_op jit(solution)/shard_map/ppermute | solution.py:828
  230.0 36.7 %collective-permute-start.15 = (f32[256,512]{1,0:T(8,128)}, f32[256,512]{1,0:T(8,128)S(1)}, u32[]{:S(2)}, u32[]{:S(2)}) collective-permute-start(f32[256,512]{1,0:T(8,128)} %get-tuple-element.40), channel_id=1, source_target_pairs={{0,24},{8,16},{16,8},{24,0},{1,25},{9,17},{17,9},{25,1},{2,26},{10... | collective-permute-start | bytes 1572872 | tf_op jit(solution)/shard_map/ppermute | solution.py:828
  247.8 18.9 %copy-start.3 = (f32[256,512]{1,0:T(8,128)}, f32[256,512]{1,0:T(8,128)S(1)}, u32[]{:S(2)}) copy-start(f32[256,512]{1,0:T(8,128)S(1)} %collective-permute-done.13.refs_1_) | copy-start | bytes 1572868
  266.7 0.8 copy-start.4
  266.7 1.0 copy-start.5

commit v2 on v1

--- a/solution.py
+++ b/solution.py
@@ -19,6 +19,7 @@
 vmem_bytes = 56 * 1024 * 1024
 rim = 16
 halo_rows = 16
+unroll = 2
 
 
 def with_halo(cells, sides, width):
@@ -118,15 +119,14 @@
     return (real_out * (1.0 / (length * length)))[None]
 
 
-def max_over(cells, axis):
+def max_over(cells, axis, distances):
     count = lax.axis_size(axis)
-    if count & (count - 1):
-        return lax.pmax(cells, axis)
-    distance = 1
-    while distance < count:
-        other = lax.ppermute(cells, axis, [(i, i ^ distance) for i in range(count)])
+    others = [
+        lax.ppermute(cells, axis, [(i, i ^ distance) for i in range(count)])
+        for distance in distances
+    ]
+    for other in others:
         cells = jnp.maximum(cells, other)
-        distance *= 2
     return cells
 
 
@@ -465,105 +465,91 @@
                 half_ref[part, pl.ds(chunk, 8), where] = done
 
 
-def starlet_body(chans, q_ref, *refs):
-    edges, cores = refs[:chans], refs[chans : 2 * chans]
-    above, below = refs[2 * chans : 3 * chans], refs[3 * chans : 4 * chans]
-    detail_ref, energy_ref, peak_ref, cells, across = refs[4 * chans :]
-    _, _, height, part = detail_ref.shape
-    margin = 8
-    base = margin + halo_rows
+def starlet_body(chans, spans, fills, ends_ref, *refs):
+    sources, (detail_ref, peak_ref, ping, pong) = refs[:-4], refs[-4:]
+    part = detail_ref.shape[3]
     lanes = lane_count
-    chunk = height // 2
-    quarter = height // 4
+    tiles = part // lanes
     total = part + lanes
-    no_left, no_right = q_ref[0] > 0, q_ref[1] > 0
-    no_top, no_bottom = q_ref[2] > 0, q_ref[3] > 0
-    lane_ids = lax.broadcasted_iota(jnp.int32, (8, total), 1)
-    outside = ((lane_ids >= total - lanes // 2) & no_left) | (
-        (lane_ids >= part) & (lane_ids < total - lanes // 2) & no_right
-    )
-
-    def fill(target, source, source_row, count, pack_row, group):
-        cells[pl.ds(target, count), pl.ds(0, part)] = source[pl.ds(source_row, count), :]
-        for i in range(count // 8):
-            spot = (group + i) * 2 * rim
-            tile = source[pl.ds(pack_row, 8), pl.ds(spot // lanes * lanes, lanes)]
-            shift = (lanes - spot % lanes - rim) % lanes
-            cells[pl.ds(target + 8 * i, 8), pl.ds(part, lanes)] = pltpu.roll(tile, shift, 1)
-
+    no_left, no_right = ends_ref[0] > 0, ends_ref[1] > 0
+    no_top, no_bottom = ends_ref[2] > 0, ends_ref[3] > 0
+    lane_ids = lax.broadcasted_iota(jnp.int32, (8, lanes), 1)
+    outside = ((lane_ids >= lanes // 2) & no_left) | ((lane_ids < lanes // 2) & no_right)
     for chan in range(chans):
-        edge, core = edges[chan], cores[chan]
-        fill(margin, above[chan], 0, halo_rows, halo_rows, (chunk - halo_rows) // 8)
-        fill(base, edge, 0, quarter, chunk, 0)
-        fill(base + quarter, core, 0, chunk, chunk, 0)
-        fill(base + 3 * quarter, edge, quarter, quarter, chunk, quarter // 8)
-        fill(base + height, below[chan], 0, halo_rows, halo_rows, 0)
+        for target, index, source_row, count, pack_row, group in fills:
+            source = sources[index * chans + chan]
+            to = pl.ds(8 + target, count)
+            ping[chan, to, pl.ds(0, part)] = source[pl.ds(source_row, count), :]
+            for i in range(count // 8):
+                spot = (group + i) * 2 * rim
+                tile = source[pl.ds(pack_row, 8), pl.ds(spot // lanes * lanes, lanes)]
+                shift = (lanes - spot % lanes - rim) % lanes
+                to = pl.ds(8 + target + 8 * i, 8)
+                ping[chan, to, pl.ds(part, lanes)] = pltpu.roll(tile, shift, 1)
+
+    skirt = halo_rows // 8
+    peaks = [jnp.zeros((8, part), jnp.float32)] * 3
+    for start, blocks, out_start, top, bottom in spans:
         for level in range(3):
             gap = 1 << level
-            blocks = (height + 2 * halo_rows) // 8
-
-            def sweep(i, carry):
-                rows = pl.ds(pl.multiple_of(margin + 8 * i, 8), 8)
-                row = cells[rows, :]
-                near = pltpu.roll(row, gap, 1) + pltpu.roll(row, total - gap, 1)
-                far = pltpu.roll(row, 2 * gap, 1) + pltpu.roll(row, total - 2 * gap, 1)
-                across[rows, :] = (far + 4.0 * near) + 6.0 * row
-                return carry
-
-            lax.fori_loop(0, blocks, sweep, 0, unroll=6)
-
-            def down(i, carry, inner):
-                start = margin + 8 * i
-                if not isinstance(start, int):
-                    start = pl.multiple_of(start, 8)
-                rows = pl.ds(start, 8)
-                window = across[pl.ds(start - 8, 24), :]
-                near = window[8 - gap : 16 - gap] + window[8 + gap : 16 + gap]
-                far = window[8 - 2 * gap : 16 - 2 * gap] + window[8 + 2 * gap : 16 + 2 * gap]
-                smooth = ((far + 4.0 * near) + 6.0 * window[8:16]) * (1.0 / 256.0)
-                if not inner:
-                    gone = no_top if i < halo_rows // 8 else no_bottom
-                    cells[rows, :] = jnp.where(gone | outside, 0.0, smooth)
-                    return carry
-                smooth = jnp.where(outside, 0.0, smooth)
-                detail = cells[rows, pl.ds(0, part)] - smooth[:, :part]
-                cells[rows, :] = smooth
-                to = pl.ds(pl.multiple_of(8 * i - halo_rows, 8), 8)
-                detail_ref[chan, level, to, :] = detail
-                if level == 2:
-                    detail_ref[chan, 3, to, :] = smooth[:, :part]
-                square = detail * detail
-                if chan:
-                    square = square + energy_ref[level, to, :]
-                energy_ref[level, to, :] = square
-                if chan == chans - 1:
-                    return jnp.maximum(carry, square)
-                return carry
-
-            skirt = halo_rows // 8
-            if level < 2:
-                for i in range(skirt):
-                    down(i, 0, False)
-                    down(blocks - 1 - i, 0, False)
-            peak = lax.fori_loop(
-                skirt,
-                blocks - skirt,
-                functools.partial(down, inner=True),
-                jnp.zeros((8, part), jnp.float32),
-                unroll=8,
-            )
-            if chan == chans - 1:
-                most = peak[:, :lanes]
-                for t in range(1, part // lanes):
-                    most = jnp.maximum(most, peak[:, t * lanes : (t + 1) * lanes])
-                peak_ref[level] = most
-
-
-def shrink_body(chans, detail_ref, energy_ref, peak_ref, *out_refs):
+            before, after = (ping, pong) if level % 2 == 0 else (pong, ping)
+
+            def step(i, peak, level, gap, before, after):
+                base = 8 + start + 8 * i
+                if not isinstance(i, int):
+                    base = pl.multiple_of(base, 8)
+                inner = not isinstance(i, int)
+                energy = 0.0
+                for chan in range(chans):
+                    window = before[chan, pl.ds(base - 8, 24), :]
+                    near = window[8 - gap : 16 - gap] + window[8 + gap : 16 + gap]
+                    far = window[8 - 2 * gap : 16 - 2 * gap] + window[8 + 2 * gap : 16 + 2 * gap]
+                    row = (far + 4.0 * near) + 6.0 * window[8:16]
+                    near = pltpu.roll(row, gap, 1) + pltpu.roll(row, total - gap, 1)
+                    far = pltpu.roll(row, 2 * gap, 1) + pltpu.roll(row, total - 2 * gap, 1)
+                    smooth = ((far + 4.0 * near) + 6.0 * row) * (1.0 / 256.0)
+                    whole = smooth[:, :part]
+                    if level < 2:
+                        side = jnp.where(outside, 0.0, smooth[:, part:])
+                        if not inner and (top if i < skirt else bottom):
+                            gone = no_top if i < skirt else no_bottom
+                            side = jnp.where(gone, 0.0, side)
+                            after[chan, pl.ds(base, 8), pl.ds(0, part)] = jnp.where(
+                                gone, 0.0, whole
+                            )
+                        else:
+                            after[chan, pl.ds(base, 8), pl.ds(0, part)] = whole
+                        after[chan, pl.ds(base, 8), pl.ds(part, lanes)] = side
+                    if inner:
+                        to = pl.ds(pl.multiple_of(out_start + 8 * i - halo_rows, 8), 8)
+                        detail = window[8:16, :part] - whole
+                        detail_ref[chan, level, to, :] = detail
+                        if level == 2:
+                            detail_ref[chan, 3, to, :] = whole
+                        energy = energy + detail * detail
+                return jnp.maximum(peak, energy) if inner else peak
+
+            step = functools.partial(step, level=level, gap=gap, before=before, after=after)
+            for i in range(level, skirt):
+                step(i, None)
+                step(blocks - 1 - i, None)
+            peaks[level] = lax.fori_loop(skirt, blocks - skirt, step, peaks[level], unroll=unroll)
+    for level in range(3):
+        most = peaks[level][:, :lanes]
+        for t in range(1, tiles):
+            most = jnp.maximum(most, peaks[level][:, t * lanes : (t + 1) * lanes])
+        peak_ref[level] = most
+
+
+def shrink_body(chans, detail_ref, peak_ref, *out_refs):
     factors = []
     for level in range(3):
+        energy = 0.0
+        for chan in range(chans):
+            detail = detail_ref[chan, level]
+            energy = energy + detail * detail
+        energy = jnp.sqrt(energy)
         threshold = fractions[level] * jnp.sqrt(jnp.max(peak_ref[level], keepdims=True))
-        energy = jnp.sqrt(energy_ref[level])
         threshold = jnp.broadcast_to(threshold, energy.shape)
         factors.append(1.0 - threshold / jnp.maximum(energy, threshold))
     for chan in range(chans):
@@ -574,11 +560,18 @@
 
 
 def join_body(me_ref, *refs):
-    chans = len(refs) - 1
+    chans = (len(refs) - 1) // 2
+    out_ref = refs[-1]
     part = refs[0].shape[1]
+    outer_rows, inner_rows = refs[0].shape[0] // 2, refs[chans].shape[0]
     for chan in range(chans):
-        start = pl.multiple_of((me_ref[0] ^ chan) * part, part)
-        refs[-1][:, pl.ds(start, part)] = refs[chan][...]
+        outer, inner = refs[chan], refs[chans + chan]
+        columns = pl.ds(pl.multiple_of((me_ref[0] ^ chan) * part, part), part)
+        out_ref[pl.ds(0, outer_rows), columns] = outer[pl.ds(0, outer_rows), :]
+        out_ref[pl.ds(outer_rows, inner_rows), columns] = inner[...]
+        out_ref[pl.ds(outer_rows + inner_rows, outer_rows), columns] = outer[
+            pl.ds(outer_rows, outer_rows), :
+        ]
 
 
 def column_body(
@@ -765,20 +758,26 @@
         cost_estimate=busy(5),
         )(cells, back, values, dirty, old)
 
-    def over_chans(cells):
+    def pieces_for(cells):
         me = lax.axis_index("chan")
-        got = []
-        for turn in range(chans):
-            mine = lax.dynamic_index_in_dim(cells, me ^ turn, 0, keepdims=False)
-            if turn:
-                mine = lax.ppermute(mine, "chan", [(i, i ^ turn) for i in range(chans)])
-            got.append(mine)
-        return got
+        return [
+            lax.dynamic_index_in_dim(cells, me ^ turn, 0, keepdims=False) for turn in range(chans)
+        ]
+
+    def over_chans(pieces):
+        return [pieces[0]] + [
+            lax.ppermute(pieces[turn], "chan", [(i, i ^ turn) for i in range(chans)])
+            for turn in range(1, chans)
+        ]
+
+    def in_order(earlier, later):
+        both = lax.optimization_barrier((*earlier, *later))
+        return list(both[: len(earlier)]), list(both[len(earlier) :])
 
     residual, outer = row_inverse(edge, dirty, (0, 3))
-    outer = over_chans(outer)
-    core, *outer = lax.optimization_barrier((core, *outer))
+    outer = over_chans(pieces_for(outer))
     residual, inner = row_inverse(core, residual, (1, 1))
+    outer, inner = in_order(outer, pieces_for(inner))
     inner = over_chans(inner)
     ahead_pairs = [(i, i + 1) for i in range(count - 1)]
     back_pairs = [(i + 1, i) for i in range(count - 1)]
@@ -795,51 +794,84 @@
         [chan_id == 0, chan_id == chans - 1, row_id == 0, row_id == count - 1]
     ).astype(jnp.int32)
     vmem = pl.BlockSpec(memory_space=pltpu.VMEM)
-    details, energy, peaks = pl.pallas_call(
-        functools.partial(starlet_body, chans),
-        in_specs=[pl.BlockSpec(memory_space=pltpu.SMEM)] + [vmem] * (4 * chans),
-        out_specs=[vmem] * 3,
-        out_shape=[shape(chans, 4, height, part), shape(3, height, part), shape(3, 8, lanes)],
-        scratch_shapes=[
-            pltpu.VMEM((height + 2 * halo_rows + 16, part + lanes), f32),
-            pltpu.VMEM((height + 2 * halo_rows + 16, part + lanes), f32),
-        ],
-        compiler_params=pltpu.CompilerParams(vmem_limit_bytes=vmem_bytes),
-        name="starlet",
-        cost_estimate=busy(25),
-    )(at_end, *outer, *inner, *above, *below)
-    peaks = max_over(max_over(peaks, "rows"), "chan")
-    thick = height // 4
-    shrunk = pl.pallas_call(
-        functools.partial(shrink_body, chans),
-        grid=(4,),
-        in_specs=[
-            pl.BlockSpec((chans, 4, thick, part), lambda i: (0, 0, i, 0)),
-            pl.BlockSpec((3, thick, part), lambda i: (0, i, 0)),
-            pl.BlockSpec((3, 8, lanes), lambda i: (0, 0, 0)),
-        ],
-        out_specs=[pl.BlockSpec((thick, part), lambda i: (i, 0))] * chans,
-        out_shape=[shape(height, part)] * chans,
-        compiler_params=pltpu.CompilerParams(vmem_limit_bytes=vmem_bytes),
-        name="shrink",
-        cost_estimate=busy(6),
-    )(details, energy, peaks)
-    shrunk = [shrunk[0]] + [
-        lax.ppermute(shrunk[turn], "chan", [(i, i ^ turn) for i in range(chans)])
-        for turn in range(1, chans)
-    ]
+
+    def starlet(sources, rows, spans, fills, microseconds):
+        extent = max(fill[0] + fill[3] for fill in fills) + 16
+        cells = pltpu.VMEM((chans, extent, part + lanes), f32)
+        return pl.pallas_call(
+            functools.partial(starlet_body, chans, spans, fills),
+            in_specs=[pl.BlockSpec(memory_space=pltpu.SMEM)] + [vmem] * len(sources),
+            out_specs=[vmem] * 2,
+            out_shape=[shape(chans, 4, rows, part), shape(3, 8, lanes)],
+            scratch_shapes=[cells, cells],
+            compiler_params=pltpu.CompilerParams(vmem_limit_bytes=vmem_bytes),
+            name="starlet",
+            cost_estimate=busy(microseconds),
+        )(at_end, *sources)
+
+    reach = quarter + halo_rows
+    most = quarter - halo_rows
+    skirt = halo_rows // 8
+    outer_details, outer_peaks = starlet(
+        outer + above + below,
+        2 * most,
+        (
+            (0, reach // 8, 0, True, False),
+            (reach + 16, reach // 8, most, False, True),
+        ),
+        (
+            (0, 1, 0, halo_rows, halo_rows, (half - halo_rows) // 8),
+            (halo_rows, 0, 0, quarter, half, 0),
+            (reach + 16, 0, quarter, quarter, half, quarter // 8),
+            (reach + 16 + quarter, 2, 0, halo_rows, halo_rows, 0),
+        ),
+        12,
+    )
+    inner_details, inner_peaks = starlet(
+        outer + inner,
+        half + 2 * halo_rows,
+        ((0, half // 8 + 4 * skirt, 0, False, False),),
+        (
+            (0, 0, quarter - 2 * halo_rows, 2 * halo_rows, half, (quarter - 2 * halo_rows) // 8),
+            (2 * halo_rows, 1, 0, half, half, 0),
+            (2 * halo_rows + half, 0, quarter, 2 * halo_rows, half, quarter // 8),
+        ),
+        12,
+    )
+    peaks = jnp.maximum(outer_peaks, inner_peaks)
+    peaks = max_over(peaks, "rows", range(1, 2))
+    peaks = max_over(peaks, "rows", range(2, count, 2))
+    peaks = max_over(peaks, "chan", range(1, chans))
+
+    def shrink(details):
+        rows = details.shape[2]
+        thick = rows // 2
+        return pl.pallas_call(
+            functools.partial(shrink_body, chans),
+            grid=(2,),
+            in_specs=[
+                pl.BlockSpec((chans, 4, thick, part), lambda i: (0, 0, i, 0)),
+                pl.BlockSpec((3, 8, lanes), lambda i: (0, 0, 0)),
+            ],
+            out_specs=[pl.BlockSpec((thick, part), lambda i: (i, 0))] * chans,
+            out_shape=[shape(rows, part)] * chans,
+            compiler_params=pltpu.CompilerParams(vmem_limit_bytes=vmem_bytes),
+            name="shrink",
+            cost_estimate=busy(3),
+        )(details, peaks)
+
+    outer = over_chans(shrink(outer_details))
+    outer, inner = in_order(outer, shrink(inner_details))
+    inner = over_chans(inner)
     new_estimate = pl.pallas_call(
         join_body,
-        grid_spec=pltpu.PrefetchScalarGridSpec(
-            num_scalar_prefetch=1,
-            grid=(4,),
-            in_specs=[pl.BlockSpec((thick, part), lambda i, me: (i, 0))] * chans,
-            out_specs=pl.BlockSpec((thick, length), lambda i, me: (i, 0)),
-        ),
+        in_specs=[pl.BlockSpec(memory_space=pltpu.SMEM)] + [vmem] * (2 * chans),
+        out_specs=vmem,
         out_shape=shape(height, length),
+        compiler_params=pltpu.CompilerParams(vmem_limit_bytes=vmem_bytes),
         name="join",
         cost_estimate=busy(4),
-    )(jnp.reshape(chan_id, (1,)).astype(jnp.int32), *shrunk)
+    )(jnp.reshape(chan_id, (1,)).astype(jnp.int32), *outer, *inner)
     return new_estimate, residual
 
 
@@ -904,7 +936,8 @@
         margin = new_margin
     energies = [jnp.sum(detail * detail, axis=0) for detail in details]
     peaks = jnp.stack([jnp.broadcast_to(jnp.max(energy), (128,)) for energy in energies])
-    peaks = max_over(max_over(peaks, "rows"), "chan")
+    for axis in ("rows", "chan"):
+        peaks = lax.pmax(peaks, axis)
     output = current
     for scale_level in range(3):
         threshold = fractions[scale_level] * jnp.sqrt(peaks[scale_level, 0])

time: 276 us -> 253 us (0.917)
  waiting for transfers between devices: 122 us -> 91 us
  starting transfers between devices: 37.2 us -> 50.9 us
  Pallas kernels: 79.9 us -> 74.7 us
    ppermute x14 -> x19, waiting for transfers between devices: 84.1 us -> 52.7 us  [the longest x12 43.9 us: over_chans(): lax.ppermute(pieces[turn], 'chan', [(i, i ^ turn) for i in range(chans)])]
    ppermute x14 -> x19, starting transfers between devices: 20.9 us -> 33.6 us  [the longest x12 22.2 us: over_chans(): lax.ppermute(pieces[turn], 'chan', [(i, i ^ turn) for i in range(chans)])]
    pallas_call x3 -> x5, Pallas kernels: 36.8 us -> 31.6 us  [the longest x2 21.9 us: starlet(): pl.pallas_call(functools.partial(starlet_body, chans, spans, fills), in_s...]
  transfers between devices with their start and end apart: 19 -> 24, of which waited for: 14 -> 16; matrix products, arithmetic and copies ran while one was open for 3% -> 3% of each run, Pallas kernels for 9% -> 15%
where the time goes in v2:
time: 253 us; the launch traced here: 251 us
  waiting for transfers between devices  91 us (36%)
  Pallas kernels  74.7 us (30%)
  starting transfers between devices  50.9 us (20%)
  blocking collectives  19.6 us (8%)
  local copies, waits for them, and re-layouts  8.05 us (3%)
  other arithmetic  5.39 us (2%)
    ppermute x12, waiting for transfers between devices, over_chans(): lax.ppermute(pieces[turn], 'chan', [(i, i ^ turn) for i in range(chans)])  43.9 us
    ppermute x12, starting transfers between devices, over_chans(): lax.ppermute(pieces[turn], 'chan', [(i, i ^ turn) for i in range(chans)])  22.2 us
    pallas_call x2, Pallas kernels, starlet(): pl.pallas_call(functools.partial(starlet_body, chans, spans, fills), in_s...  21.9 us
    all_to_all x1, waiting for transfers between devices, filtered(): sent = lax.all_to_all(sent, 'rows', 0, 0, tiled=True)  21 us
    all_to_all x1, blocking collectives, filtered(): edge = lax.all_to_all(edge, 'rows', 0, 0, tiled=True)  19.6 us
    all_to_all x1, waiting for transfers between devices, filtered(): ahead = lax.all_to_all(ahead, 'rows', 0, 0, tiled=True)  12.6 us
    pallas_call x1, Pallas kernels, filtered(): whole_call(functools.partial(column_body, steps), [shape(count, 2, half,...  12 us
    ppermute x7, starting transfers between devices, max_over(): lax.ppermute(cells, axis, [(i, i ^ distance) for i in range(count)])  11.4 us
  transfers between devices with their start and end apart: 24, of which 16 were waited for; matrix products, arithmetic and copies ran while one was open for 3% of the time, Pallas kernels for 15%

profile of v2, /device:TPU:0, one launch (start us, length us, event | category | flops | bytes accessed | tf_op | source)
XLA Modules:
  0.0 250.5 jit_solution(10983295279305457626)
XLA Ops:
  0.6 5.9 %weight_pick.1 = f32[8,512,128]{2,1,0:T(8,128)} custom-call(f32[4,512,256]{2,1,0:T(8,128)} %bitcast.66, bf16[1024,1024]{1,0:T(8,128)(2,1)} %constant.51.clone.pick_ref), custom_call_target="tpu_custom_call" | custom-call | bytes 21000000 | tf_op jit(solution)/shard_map/weight_pick/pallas_call | solution.py:705
  6.5 5.2 %all-to-all-start.1 = ((f32[8,512,128]{2,1,0:T(8,128)}), f32[8,512,128]{2,1,0:T(8,128)S(1)}, u32[]{:S(2)}, u32[]{:S(2)}) async-start(f32[8,512,128]{2,1,0:T(8,128)} %weight_pick.1), calls=%async_computation.1 | async-start | bytes 4194304 | tf_op jit(solution)/shard_map/all_to_all | solution.py:708
  11.7 5.7 %row_forward.1 = f32[8,2,256,128]{3,2,1,0:T(8,128)} custom-call(f32[256,2048]{1,0:T(8,128)} %bitcast.60, bf16[8,2,256,256]{3,2,1,0:T(8,128)(2,1)} %constant.54.clone.table_ref), custom_call_target="tpu_custom_call" | custom-call | bytes 21000000 | tf_op jit(solution)/shard_map/row_forward/pallas_call | solution.py:709
  17.4 21.0 %all-to-all-done.1.in_ref = f32[8,512,128]{2,1,0:T(8,128)S(1)} async-done(((f32[8,512,128]{2,1,0:T(8,128)}), f32[8,512,128]{2,1,0:T(8,128)S(1)}, u32[]{:S(2)}, u32[]{:S(2)}) %all-to-all-start.1) | async-done | bytes 2097184 | tf_op jit(solution)/shard_map/all_to_all | solution.py:708
  38.3 4.5 %all-to-all-start = ((f32[8,2,256,128]{3,2,1,0:T(8,128)}), f32[8,2,256,128]{3,2,1,0:T(8,128)}, u32[]{:S(2)}, u32[]{:S(2)}) async-start(f32[8,2,256,128]{3,2,1,0:T(8,128)} %row_forward.1), calls=%async_computation | async-start | bytes 4194304 | tf_op jit(solution)/shard_map/all_to_all | solution.py:716
  42.9 3.3 %select_bitcast_fusion.place_ref = bf16[1024,1152]{1,0:T(8,128)(2,1)} fusion(bf16[1,1024,1152]{2,1,0:T(8,128)(2,1)} %constant.61, bf16[1,1024,1152]{2,1,0:T(8,128)(2,1)} %constant.62, pred[]{:T(512)} %eq.15), kind=kLoop, calls=%fused_computation | loop fusion | flops 1179648 | bytes 7077889 | tf_op jit(solution)/shard_map/jit(_where)/select_n | solution.py:717
  46.2 10.5 %weight_place.1 = (f32[16,128,128]{2,1,0:T(8,128)}, f32[16,128,128]{2,1,0:T(8,128)}) custom-call(f32[8,512,128]{2,1,0:T(8,128)} %copy-done, bf16[1024,1152]{1,0:T(8,128)(2,1)} %select_bitcast_fusion.place_ref, bf16[128,256]{1,0:T(8,128)(2,1)} %constant.53.clone.flip_ref), custom_call_target="tpu_custom_call" | custom-call | bytes 35000000 | tf_op jit(solution)/shard_map/weight_place/pallas_call | solution.py:718
  56.7 12.6 %all-to-all-done.in_ref = f32[8,2,256,128]{3,2,1,0:T(8,128)} async-done(((f32[8,2,256,128]{3,2,1,0:T(8,128)}), f32[8,2,256,128]{3,2,1,0:T(8,128)}, u32[]{:S(2)}, u32[]{:S(2)}) %all-to-all-start) | async-done | bytes 2097184 | tf_op jit(solution)/shard_map/all_to_all | solution.py:716
  69.3 12.0 %column_filter.1 = (f32[8,2,128,128]{3,2,1,0:T(8,128)}, f32[8,2,128,128]{3,2,1,0:T(8,128)}) custom-call(f32[8,2,256,128]{3,2,1,0:T(8,128)} %all-to-all-done.in_ref, bf16[16,2,256,256]{3,2,1,0:T(8,128)(2,1)} %constant.56.clone.there_ref, bf16[16,2,256,256]{3,2,1,0:T(8,128)(2,1)} %constant.57.clone.back_ref, f32[16,128,128]{2,1,0:T(8,128)} %get-tuple-element.38.weight_ref, ...), custom_call_target="tpu_custom_call" | custom-call | bytes 42000000 | tf_op jit(solution)/shard_map/column_filter/pallas_call | solution.py:726
  81.3 19.6 %all_to_all.20.in_ref = f32[8,2,128,128]{3,2,1,0:T(8,128)} all-to-all(f32[8,2,128,128]{3,2,1,0:T(8,128)} %get-tuple-element.40), channel_id=1, replica_groups=mesh['chan'=4,'rows'=8] {'rows'}, dimensions={0} | all-to-all | bytes 2097152 | tf_op jit(solution)/shard_map/all_to_all | solution.py:733
  100.9 3.6 %all-to-all-start.3 = ((f32[8,2,128,128]{3,2,1,0:T(8,128)}), f32[8,2,128,128]{3,2,1,0:T(8,128)S(1)}, u32[]{:S(2)}, u32[]{:S(2)}) async-start(f32[8,2,128,128]{3,2,1,0:T(8,128)} %get-tuple-element.42), calls=%async_computation.3 | async-start | bytes 2097152 | tf_op jit(solution)/shard_map/all_to_all | solution.py:734
  104.5 4.5 %row_inverse.2 = (f32[256,2048]{1,0:T(8,128)}, f32[4,136,512]{2,1,0:T(8,128)}) custom-call(f32[8,2,128,128]{3,2,1,0:T(8,128)} %all_to_all.20.in_ref, bf16[8,2,256,256]{3,2,1,0:T(8,128)(2,1)} %constant.55.clone.table_ref, f32[256,2048]{1,0:T(8,128)} %bitcast.61, f32[256,2048]{1,0:T(8,128)} %bitcast.63, f32[256,2048]{1,0:T(8,128)} %bitcast.64), custom_call_target="tpu_custom_call" | custom-call | bytes 17500000 | tf_op jit(solution)/shard_map/row_inverse/pallas_call | solution.py:742
  109.0 1.3 dynamic-slice_bitcast_fusion.4
  110.3 1.7 collective-permute-start
  112.0 2.6 %collective-permute-start.1 = (f32[136,512]{1,0:T(8,128)S(1)}, f32[136,512]{1,0:T(8,128)S(1)}, u32[]{:S(2)}, u32[]{:S(2)}) collective-permute-start(f32[136,512]{1,0:T(8,128)S(1)} %get-tuple-element.79), channel_id=1, source_target_pairs={{0,16},{8,24},{16,0},{24,8},{1,17},{9,25},{17,1},{25,9},{2,18},{10... | collective-permute-start | bytes 835592 | tf_op jit(solution)/shard_map/ppermute | solution.py:769
  115.5 4.4 %all-to-all-done.3.in_ref = f32[8,2,128,128]{3,2,1,0:T(8,128)S(1)} async-done(((f32[8,2,128,128]{3,2,1,0:T(8,128)}), f32[8,2,128,128]{3,2,1,0:T(8,128)S(1)}, u32[]{:S(2)}, u32[]{:S(2)}) %all-to-all-start.3) | async-done | bytes 1048608 | tf_op jit(solution)/shard_map/all_to_all | solution.py:734
  119.8 1.0 copy-done.1
  120.8 4.5 %row_inverse.3 = (f32[256,2048]{1,0:T(8,128)}, f32[4,136,512]{2,1,0:T(8,128)}) custom-call(f32[8,2,128,128]{3,2,1,0:T(8,128)} %copy-done.1, bf16[8,2,256,256]{3,2,1,0:T(8,128)(2,1)} %constant.55.clone.table_ref, f32[256,2048]{1,0:T(8,128)} %bitcast.62, f32[256,2048]{1,0:T(8,128)} %bitcast.65, ...), custom_call_target="tpu_custom_call", output_to_operand_aliasing={{0}: (4, {})} | custom-call | bytes 17500000 | tf_op jit(solution)/shard_map/row_inverse/pallas_call | solution.py:742
  125.3 2.0 dynamic-slice_bitcast_fusion
  127.3 7.0 %collective-permute-done.1.refs_2_ = f32[136,512]{1,0:T(8,128)S(1)} collective-permute-done((f32[136,512]{1,0:T(8,128)S(1)}, f32[136,512]{1,0:T(8,128)S(1)}, u32[]{:S(2)}, u32[]{:S(2)}) %collective-permute-start.1) | collective-permute-done | bytes 278560 | tf_op jit(solution)/shard_map/ppermute | solution.py:769
  134.6 1.5 collective-permute-start.4
  136.1 5.7 %collective-permute-start.5 = (f32[136,512]{1,0:T(8,128)S(1)}, f32[136,512]{1,0:T(8,128)S(1)}, u32[]{:S(2)}, u32[]{:S(2)}) collective-permute-start(f32[136,512]{1,0:T(8,128)S(1)} %get-tuple-element.52), channel_id=1, source_target_pairs={{0,8},{8,0},{16,24},{24,16},{1,9},{9,1},{17,25},{25,17},{2,10},{10... | collective-permute-start | bytes 835592 | tf_op jit(solution)/shard_map/ppermute | solution.py:769
  141.8 1.1 collective-permute-start.6
  142.9 1.4 collective-permute-start.7
  144.3 2.5 collective-permute-start.3
  148.5 9.2 %starlet.2 = (f32[4,4,96,512]{3,2,1,0:T(8,128)}, f32[3,8,128]{2,1,0:T(8,128)}) custom-call(s32[4]{0:T(128)} %add_convert_fusion.ends_ref, f32[136,512]{1,0:T(8,128)} %copy-done.2, f32[136,512]{1,0:T(8,128)} %copy-done.3, f32[136,512]{1,0:T(8,128)} %copy-done.4, f32[136,512]{1,0:T(8,128)} %copy-done.5, f32[24,512]{1,0:T(8,128)} %get-tuple-element.89.refs_4_, ...), custom_call_target="tpu_custom_call" | custom-call | bytes 42000000 | tf_op jit(solution)/shard_map/starlet/pallas_call | solution.py:801
  157.8 6.5 %collective-permute-done.6.refs_6_ = f32[136,512]{1,0:T(8,128)S(1)} collective-permute-done((f32[136,512]{1,0:T(8,128)S(1)}, f32[136,512]{1,0:T(8,128)S(1)}, u32[]{:S(2)}, u32[]{:S(2)}) %collective-permute-start.6) | collective-permute-done | bytes 278560 | tf_op jit(solution)/shard_map/ppermute | solution.py:769
  165.7 12.6 %starlet.3 = (f32[4,4,160,512]{3,2,1,0:T(8,128)}, f32[3,8,128]{2,1,0:T(8,128)}) custom-call(s32[4]{0:T(128)} %add_convert_fusion.ends_ref, f32[136,512]{1,0:T(8,128)} %copy-done.2, f32[136,512]{1,0:T(8,128)} %copy-done.3, f32[136,512]{1,0:T(8,128)} %copy-done.4, f32[136,512]{1,0:T(8,128)} %copy-done.5, f32[136,512]{1,0:T(8,128)} %get-tuple-element.51.refs_4_, ...), custom_call_target="tpu_custom_call" | custom-call | bytes 42000000 | tf_op jit(solution)/shard_map/starlet/pallas_call | solution.py:801
  179.0 1.2 collective-permute-done.8
  180.2 2.4 collective-permute-start.10
  182.6 1.4 collective-permute-start.11
  184.2 3.0 %collective-permute-done.11 = f32[3,8,128]{2,1,0:T(8,128)S(1)} collective-permute-done((f32[3,8,128]{2,1,0:T(8,128)S(1)}, f32[3,8,128]{2,1,0:T(8,128)S(1)}, u32[]{:S(2)}, u32[]{:S(2)}) %collective-permute-start.11) | collective-permute-done | bytes 12320 | tf_op jit(solution)/shard_map/ppermute | solution.py:125
  187.6 5.1 %collective-permute-start.12 = (f32[3,8,128]{2,1,0:T(8,128)S(1)}, f32[3,8,128]{2,1,0:T(8,128)S(1)}, u32[]{:S(2)}, u32[]{:S(2)}) collective-permute-start(f32[3,8,128]{2,1,0:T(8,128)S(1)} %maximum_maximum_fusion.1), channel_id=1, source_target_pairs={{0,8},{8,0},{16,24},{24,16},{1,9},{9,1},{17,25},{25,17},{2,10},{10... | collective-permute-start | bytes 36872 | tf_op jit(solution)/shard_map/ppermute | solution.py:125
  192.7 1.1 collective-permute-start.13
  193.8 1.4 collective-permute-start.14
  195.2 2.1 collective-permute-done.13
  197.3 2.0 collective-permute-done.14
  199.9 2.9 %shrink.2 = (f32[96,512]{1,0:T(8,128)}, f32[96,512]{1,0:T(8,128)}, f32[96,512]{1,0:T(8,128)}, f32[96,512]{1,0:T(8,128)}) custom-call(f32[4,4,96,512]{3,2,1,0:T(8,128)} %get-tuple-element.49.detail_ref, f32[3,8,128]{2,1,0:T(8,128)} %maximum_maximum_fusion.peak_ref), custom_call_target="tpu_custom_call" | custom-call | bytes 10500000 | tf_op jit(solution)/shard_map/shrink/pallas_call | solution.py:849
  203.0 1.8 collective-permute-start.16
  204.8 2.4 collective-permute-start.17
  207.2 3.8 %shrink.3 = (f32[160,512]{1,0:T(8,128)}, f32[160,512]{1,0:T(8,128)}, f32[160,512]{1,0:T(8,128)}, f32[160,512]{1,0:T(8,128)}) custom-call(f32[4,4,160,512]{3,2,1,0:T(8,128)} %get-tuple-element.60.detail_ref, f32[3,8,128]{2,1,0:T(8,128)} %maximum_maximum_fusion.peak_ref), custom_call_target="tpu_custom_call" | custom-call | bytes 10500000 | tf_op jit(solution)/shard_map/shrink/pallas_call | solution.py:849
  211.0 1.1 collective-permute-done.15.refs_1_
  212.2 6.0 %collective-permute-done.16.refs_2_ = f32[96,512]{1,0:T(8,128)S(1)} collective-permute-done((f32[96,512]{1,0:T(8,128)}, f32[96,512]{1,0:T(8,128)S(1)}, u32[]{:S(2)}, u32[]{:S(2)}) %collective-permute-start.16) | collective-permute-done | bytes 196640 | tf_op jit(solution)/shard_map/ppermute | solution.py:769
  218.2 2.8 %collective-permute-start.18 = (f32[160,512]{1,0:T(8,128)}, f32[160,512]{1,0:T(8,128)S(1)}, u32[]{:S(2)}, u32[]{:S(2)}) collective-permute-start(f32[160,512]{1,0:T(8,128)} %get-tuple-element.70), channel_id=1, source_target_pairs={{0,8},{8,0},{16,24},{24,16},{1,9},{9,1},{17,25},{25,17},{2,10},{10... | collective-permute-start | bytes 983048 | tf_op jit(solution)/shard_map/ppermute | solution.py:769
  221.1 2.4 collective-permute-start.20
  223.4 8.8 %collective-permute-done.18.refs_5_ = f32[160,512]{1,0:T(8,128)S(1)} collective-permute-done((f32[160,512]{1,0:T(8,128)}, f32[160,512]{1,0:T(8,128)S(1)}, u32[]{:S(2)}, u32[]{:S(2)}) %collective-permute-start.18) | collective-permute-done | bytes 327712 | tf_op jit(solution)/shard_map/ppermute | solution.py:769
  232.2 14.4 %collective-permute-done.19.refs_6_ = f32[160,512]{1,0:T(8,128)S(1)} collective-permute-done((f32[160,512]{1,0:T(8,128)}, f32[160,512]{1,0:T(8,128)S(1)}, u32[]{:S(2)}, u32[]{:S(2)}) %collective-permute-start.19) | collective-permute-done | bytes 327712 | tf_op jit(solution)/shard_map/ppermute | solution.py:769
  247.5 3.0 %join.1 = f32[256,2048]{1,0:T(8,128)} custom-call(s32[1]{0:T(128)} %bitcast.me_ref, f32[96,512]{1,0:T(8,128)} %get-tuple-element.65.refs_0_, f32[96,512]{1,0:T(8,128)} %copy-done.12, f32[96,512]{1,0:T(8,128)} %copy-done.13, f32[96,512]{1,0:T(8,128)} %copy-done.14, f32[160,512]{1,0:T(8,128)} %get-tuple-element.69.refs_4_, f32[160,512]{1,0:T(8,128)} %copy-done.6, ...), custom_call_target="tpu_custom_call" | custom-call | bytes 14000000 | tf_op jit(solution)/shard_map/join/pallas_call | solution.py:866
  (68 shorter events, 7.2 us)
Async XLA Ops:
  6.5 31.8 %all-to-all-start.1 = ((f32[8,512,128]{2,1,0:T(8,128)}), f32[8,512,128]{2,1,0:T(8,128)S(1)}, u32[]{:S(2)}, u32[]{:S(2)}) async-start(f32[8,512,128]{2,1,0:T(8,128)} %weight_pick.1), calls=%async_computation.1 | async-start | bytes 4194304 | tf_op jit(solution)/shard_map/all_to_all | solution.py:708
  38.3 4.5 %copy-start = (f32[8,512,128]{2,1,0:T(8,128)}, f32[8,512,128]{2,1,0:T(8,128)S(1)}, u32[]{:S(2)}) copy-start(f32[8,512,128]{2,1,0:T(8,128)S(1)} %all-to-all-done.1.in_ref) | copy-start | bytes 6291460
  38.3 31.0 %all-to-all-start = ((f32[8,2,256,128]{3,2,1,0:T(8,128)}), f32[8,2,256,128]{3,2,1,0:T(8,128)}, u32[]{:S(2)}, u32[]{:S(2)}) async-start(f32[8,2,256,128]{3,2,1,0:T(8,128)} %row_forward.1), calls=%async_computation | async-start | bytes 4194304 | tf_op jit(solution)/shard_map/all_to_all | solution.py:716
  100.9 18.9 %all-to-all-start.3 = ((f32[8,2,128,128]{3,2,1,0:T(8,128)}), f32[8,2,128,128]{3,2,1,0:T(8,128)S(1)}, u32[]{:S(2)}, u32[]{:S(2)}) async-start(f32[8,2,128,128]{3,2,1,0:T(8,128)} %get-tuple-element.42), calls=%async_computation.3 | async-start | bytes 2097152 | tf_op jit(solution)/shard_map/all_to_all | solution.py:734
  110.3 24.2 %copy-start.2 = (f32[136,512]{1,0:T(8,128)}, f32[136,512]{1,0:T(8,128)S(1)}, u32[]{:S(2)}) copy-start(f32[136,512]{1,0:T(8,128)S(1)} %get-tuple-element.45.refs_0_) | copy-start | bytes 835588
  110.3 17.0 %collective-permute-start = (f32[136,512]{1,0:T(8,128)S(1)}, f32[136,512]{1,0:T(8,128)S(1)}, u32[]{:S(2)}, u32[]{:S(2)}) collective-permute-start(f32[136,512]{1,0:T(8,128)S(1)} %get-tuple-element.80), channel_id=1, source_target_pairs={{0,8},{8,0},{16,24},{24,16},{1,9},{9,1},{17,25},{25,17},{2,10},{10... | collective-permute-start | bytes 835592 | tf_op jit(solution)/shard_map/ppermute | solution.py:769
  112.0 22.4 %collective-permute-start.1 = (f32[136,512]{1,0:T(8,128)S(1)}, f32[136,512]{1,0:T(8,128)S(1)}, u32[]{:S(2)}, u32[]{:S(2)}) collective-permute-start(f32[136,512]{1,0:T(8,128)S(1)} %get-tuple-element.79), channel_id=1, source_target_pairs={{0,16},{8,24},{16,0},{24,8},{1,17},{9,25},{17,1},{25,9},{2,18},{10... | collective-permute-start | bytes 835592 | tf_op jit(solution)/shard_map/ppermute | solution.py:769
  114.6 19.8 %collective-permute-start.2 = (f32[136,512]{1,0:T(8,128)S(1)}, f32[136,512]{1,0:T(8,128)S(1)}, u32[]{:S(2)}, u32[]{:S(2)}) collective-permute-start(f32[136,512]{1,0:T(8,128)S(1)} %get-tuple-element.78), channel_id=1, source_target_pairs={{0,24},{8,16},{16,8},{24,0},{1,25},{9,17},{17,9},{25,1},{2,26},{10... | collective-permute-start | bytes 835592 | tf_op jit(solution)/shard_map/ppermute | solution.py:769
  119.8 1.0 copy-start.1
  127.3 21.2 %copy-start.3 = (f32[136,512]{1,0:T(8,128)}, f32[136,512]{1,0:T(8,128)S(1)}, u32[]{:S(2)}) copy-start(f32[136,512]{1,0:T(8,128)S(1)} %collective-permute-done.refs_1_) | copy-start | bytes 835588
  134.4 14.1 %copy-start.4 = (f32[136,512]{1,0:T(8,128)}, f32[136,512]{1,0:T(8,128)S(1)}, u32[]{:S(2)}) copy-start(f32[136,512]{1,0:T(8,128)S(1)} %collective-permute-done.1.refs_2_) | copy-start | bytes 835588
  134.4 14.1 %copy-start.5 = (f32[136,512]{1,0:T(8,128)}, f32[136,512]{1,0:T(8,128)S(1)}, u32[]{:S(2)}) copy-start(f32[136,512]{1,0:T(8,128)S(1)} %collective-permute-done.2.refs_3_) | copy-start | bytes 835588
  134.6 12.2 %collective-permute-start.4 = (f32[4,24,512]{2,1,0:T(8,128)S(1)}, f32[4,24,512]{2,1,0:T(8,128)S(1)}, u32[]{:S(2)}, u32[]{:S(2)}) collective-permute-start(f32[4,24,512]{2,1,0:T(8,128)S(1)} %pad_maximum_fusion.1), channel_id=1, source_target_pairs={{1,0},{2,1},{3,2},{4,3},{5,4},{6,5},{7,6},{9,8},{10,9},{11,10},{12... | collective-permute-start | bytes 589832 | tf_op jit(solution)/shard_map/ppermute | solution.py:789
  136.1 21.7 %collective-permute-start.5 = (f32[136,512]{1,0:T(8,128)S(1)}, f32[136,512]{1,0:T(8,128)S(1)}, u32[]{:S(2)}, u32[]{:S(2)}) collective-permute-start(f32[136,512]{1,0:T(8,128)S(1)} %get-tuple-element.52), channel_id=1, source_target_pairs={{0,8},{8,0},{16,24},{24,16},{1,9},{9,1},{17,25},{25,17},{2,10},{10... | collective-permute-start | bytes 835592 | tf_op jit(solution)/shard_map/ppermute | solution.py:769
  141.8 22.4 %collective-permute-start.6 = (f32[136,512]{1,0:T(8,128)S(1)}, f32[136,512]{1,0:T(8,128)S(1)}, u32[]{:S(2)}, u32[]{:S(2)}) collective-permute-start(f32[136,512]{1,0:T(8,128)S(1)} %get-tuple-element.53), channel_id=1, source_target_pairs={{0,16},{8,24},{16,0},{24,8},{1,17},{9,25},{17,1},{25,9},{2,18},{10... | collective-permute-start | bytes 835592 | tf_op jit(solution)/shard_map/ppermute | solution.py:769
  142.9 21.3 %collective-permute-start.7 = (f32[136,512]{1,0:T(8,128)S(1)}, f32[136,512]{1,0:T(8,128)S(1)}, u32[]{:S(2)}, u32[]{:S(2)}) collective-permute-start(f32[136,512]{1,0:T(8,128)S(1)} %get-tuple-element.54), channel_id=1, source_target_pairs={{0,24},{8,16},{16,8},{24,0},{1,25},{9,17},{17,9},{25,1},{2,26},{10... | collective-permute-start | bytes 835592 | tf_op jit(solution)/shard_map/ppermute | solution.py:769
  144.3 3.5 %collective-permute-start.3 = (f32[4,24,512]{2,1,0:T(8,128)S(1)}, f32[4,24,512]{2,1,0:T(8,128)S(1)}, u32[]{:S(2)}, u32[]{:S(2)}) collective-permute-start(f32[4,24,512]{2,1,0:T(8,128)S(1)} %pad_maximum_fusion), channel_id=1, source_target_pairs={{0,1},{1,2},{2,3},{3,4},{4,5},{5,6},{6,7},{8,9},{9,10},{10,11},{11... | collective-permute-start | bytes 589832 | tf_op jit(solution)/shard_map/ppermute | solution.py:788
  157.8 20.6 %copy-start.15 = (f32[3,8,128]{2,1,0:T(8,128)S(1)}, f32[3,8,128]{2,1,0:T(8,128)}, u32[]{:S(2)}) copy-start(f32[3,8,128]{2,1,0:T(8,128)} %get-tuple-element.50) | copy-start | bytes 36868
  157.8 6.5 %copy-start.9 = (f32[136,512]{1,0:T(8,128)}, f32[136,512]{1,0:T(8,128)S(1)}, u32[]{:S(2)}) copy-start(f32[136,512]{1,0:T(8,128)S(1)} %collective-permute-done.5.refs_5_) | copy-start | bytes 835588
  164.2 0.7 copy-start.10
  165.0 0.7 copy-start.11
  179.0 1.2 collective-permute-start.8
  180.2 4.0 %collective-permute-start.10 = (f32[3,8,128]{2,1,0:T(8,128)S(1)}, f32[3,8,128]{2,1,0:T(8,128)S(1)}, u32[]{:S(2)}, u32[]{:S(2)}) collective-permute-start(f32[3,8,128]{2,1,0:T(8,128)S(1)} %max.25), channel_id=1, source_target_pairs={{0,4},{1,5},{2,6},{3,7},{4,0},{5,1},{6,2},{7,3},{8,12},{9,13},{10,... | collective-permute-start | bytes 36872 | tf_op jit(solution)/shard_map/ppermute | solution.py:125
  182.6 4.7 %collective-permute-start.11 = (f32[3,8,128]{2,1,0:T(8,128)S(1)}, f32[3,8,128]{2,1,0:T(8,128)S(1)}, u32[]{:S(2)}, u32[]{:S(2)}) collective-permute-start(f32[3,8,128]{2,1,0:T(8,128)S(1)} %max.25), channel_id=1, source_target_pairs={{0,6},{1,7},{2,4},{3,5},{4,2},{5,3},{6,0},{7,1},{8,14},{9,15},{10,... | collective-permute-start | bytes 36872 | tf_op jit(solution)/shard_map/ppermute | solution.py:125
  183.9 3.7 %collective-permute-start.9 = (f32[3,8,128]{2,1,0:T(8,128)S(1)}, f32[3,8,128]{2,1,0:T(8,128)S(1)}, u32[]{:S(2)}, u32[]{:S(2)}) collective-permute-start(f32[3,8,128]{2,1,0:T(8,128)S(1)} %max.25), channel_id=1, source_target_pairs={{0,2},{1,3},{2,0},{3,1},{4,6},{5,7},{6,4},{7,5},{8,10},{9,11},{10,... | collective-permute-start | bytes 36872 | tf_op jit(solution)/shard_map/ppermute | solution.py:125
  187.6 7.6 %collective-permute-start.12 = (f32[3,8,128]{2,1,0:T(8,128)S(1)}, f32[3,8,128]{2,1,0:T(8,128)S(1)}, u32[]{:S(2)}, u32[]{:S(2)}) collective-permute-start(f32[3,8,128]{2,1,0:T(8,128)S(1)} %maximum_maximum_fusion.1), channel_id=1, source_target_pairs={{0,8},{8,0},{16,24},{24,16},{1,9},{9,1},{17,25},{25,17},{2,10},{10... | collective-permute-start | bytes 36872 | tf_op jit(solution)/shard_map/ppermute | solution.py:125
  192.7 4.6 %collective-permute-start.13 = (f32[3,8,128]{2,1,0:T(8,128)S(1)}, f32[3,8,128]{2,1,0:T(8,128)S(1)}, u32[]{:S(2)}, u32[]{:S(2)}) collective-permute-start(f32[3,8,128]{2,1,0:T(8,128)S(1)} %maximum_maximum_fusion.1), channel_id=1, source_target_pairs={{0,16},{8,24},{16,0},{24,8},{1,17},{9,25},{17,1},{25,9},{2,18},{10... | collective-permute-start | bytes 36872 | tf_op jit(solution)/shard_map/ppermute | solution.py:125
  193.8 5.5 %collective-permute-start.14 = (f32[3,8,128]{2,1,0:T(8,128)S(1)}, f32[3,8,128]{2,1,0:T(8,128)S(1)}, u32[]{:S(2)}, u32[]{:S(2)}) collective-permute-start(f32[3,8,128]{2,1,0:T(8,128)S(1)} %maximum_maximum_fusion.1), channel_id=1, source_target_pairs={{0,24},{8,16},{16,8},{24,0},{1,25},{9,17},{17,9},{25,1},{2,26},{10... | collective-permute-start | bytes 36872 | tf_op jit(solution)/shard_map/ppermute | solution.py:125
  202.8 9.4 %collective-permute-start.15 = (f32[96,512]{1,0:T(8,128)}, f32[96,512]{1,0:T(8,128)S(1)}, u32[]{:S(2)}, u32[]{:S(2)}) collective-permute-start(f32[96,512]{1,0:T(8,128)} %get-tuple-element.57), channel_id=1, source_target_pairs={{0,8},{8,0},{16,24},{24,16},{1,9},{9,1},{17,25},{25,17},{2,10},{10... | collective-permute-start | bytes 589832 | tf_op jit(solution)/shard_map/ppermute | solution.py:769
  203.0 15.3 %collective-permute-start.16 = (f32[96,512]{1,0:T(8,128)}, f32[96,512]{1,0:T(8,128)S(1)}, u32[]{:S(2)}, u32[]{:S(2)}) collective-permute-start(f32[96,512]{1,0:T(8,128)} %get-tuple-element.58), channel_id=1, source_target_pairs={{0,16},{8,24},{16,0},{24,8},{1,17},{9,25},{17,1},{25,9},{2,18},{10... | collective-permute-start | bytes 589832 | tf_op jit(solution)/shard_map/ppermute | solution.py:769
  204.8 13.5 %collective-permute-start.17 = (f32[96,512]{1,0:T(8,128)}, f32[96,512]{1,0:T(8,128)S(1)}, u32[]{:S(2)}, u32[]{:S(2)}) collective-permute-start(f32[96,512]{1,0:T(8,128)} %get-tuple-element.59), channel_id=1, source_target_pairs={{0,24},{8,16},{16,8},{24,0},{1,25},{9,17},{17,9},{25,1},{2,26},{10... | collective-permute-start | bytes 589832 | tf_op jit(solution)/shard_map/ppermute | solution.py:769
  212.2 34.5 %copy-start.12 = (f32[96,512]{1,0:T(8,128)}, f32[96,512]{1,0:T(8,128)S(1)}, u32[]{:S(2)}) copy-start(f32[96,512]{1,0:T(8,128)S(1)} %collective-permute-done.15.refs_1_) | copy-start | bytes 589828
  218.2 28.4 %copy-start.13 = (f32[96,512]{1,0:T(8,128)}, f32[96,512]{1,0:T(8,128)S(1)}, u32[]{:S(2)}) copy-start(f32[96,512]{1,0:T(8,128)S(1)} %collective-permute-done.16.refs_2_) | copy-start | bytes 589828
  218.2 28.4 %copy-start.14 = (f32[96,512]{1,0:T(8,128)}, f32[96,512]{1,0:T(8,128)S(1)}, u32[]{:S(2)}) copy-start(f32[96,512]{1,0:T(8,128)S(1)} %collective-permute-done.17.refs_3_) | copy-start | bytes 589828
  218.2 14.0 %collective-permute-start.18 = (f32[160,512]{1,0:T(8,128)}, f32[160,512]{1,0:T(8,128)S(1)}, u32[]{:S(2)}, u32[]{:S(2)}) collective-permute-start(f32[160,512]{1,0:T(8,128)} %get-tuple-element.70), channel_id=1, source_target_pairs={{0,8},{8,0},{16,24},{24,16},{1,9},{9,1},{17,25},{25,17},{2,10},{10... | collective-permute-start | bytes 983048 | tf_op jit(solution)/shard_map/ppermute | solution.py:769
  221.1 25.6 %collective-permute-start.19 = (f32[160,512]{1,0:T(8,128)}, f32[160,512]{1,0:T(8,128)S(1)}, u32[]{:S(2)}, u32[]{:S(2)}) collective-permute-start(f32[160,512]{1,0:T(8,128)} %get-tuple-element.71), channel_id=1, source_target_pairs={{0,16},{8,24},{16,0},{24,8},{1,17},{9,25},{17,1},{25,9},{2,18},{10... | collective-permute-start | bytes 983048 | tf_op jit(solution)/shard_map/ppermute | solution.py:769
  221.1 25.6 %collective-permute-start.20 = (f32[160,512]{1,0:T(8,128)}, f32[160,512]{1,0:T(8,128)S(1)}, u32[]{:S(2)}, u32[]{:S(2)}) collective-permute-start(f32[160,512]{1,0:T(8,128)} %get-tuple-element.72), channel_id=1, source_target_pairs={{0,24},{8,16},{16,8},{24,0},{1,25},{9,17},{17,9},{25,1},{2,26},{10... | collective-permute-start | bytes 983048 | tf_op jit(solution)/shard_map/ppermute | solution.py:769
  232.2 14.4 %copy-start.6 = (f32[160,512]{1,0:T(8,128)}, f32[160,512]{1,0:T(8,128)S(1)}, u32[]{:S(2)}) copy-start(f32[160,512]{1,0:T(8,128)S(1)} %collective-permute-done.18.refs_5_) | copy-start | bytes 983044
  246.6 0.7 copy-start.7
  246.6 0.8 copy-start.8

commit v3 on v2

--- a/solution.py
+++ b/solution.py
@@ -296,16 +296,16 @@
     order = (np.arange(count)[:, None] * each + order[None]).reshape(-1)
     order = np.concatenate([order, size + order])
     spots = np.arange(size)
-    there = []
-    for step in range(steps):
-        angles = 2.0 * np.pi * ((np.outer(spots, steps * spots + step)) % length) / length
-        cosine, sine = np.cos(angles), np.sin(angles)
-        there.append(np.block([[cosine, sine], [-sine, cosine]]))
-    there = np.stack(there)
-    return split_table(there), split_table(np.swapaxes(there, 1, 2)[:, order])
-
-
-def weight_tables(length, count):
+    angles = 2.0 * np.pi * (np.outer(spots, spots) % size) / size
+    cosine, sine = np.cos(angles), np.sin(angles)
+    there = np.block([[cosine, sine], [-sine, cosine]])
+    turns = np.zeros((2, size, lane_count), np.float32)
+    angles = 2.0 * np.pi * np.outer(spots, np.arange(steps)) / length
+    turns[0, :, :steps], turns[1, :, :steps] = np.cos(angles), np.sin(angles)
+    return split_table(there), split_table(there.T[order]), turns
+
+
+def weight_tables(length, count, steps):
     width = length // count
     lanes = length // (2 * count)
     per_class = width // (2 * count)
@@ -315,13 +315,11 @@
     def classes(group):
         return (group, radix - group) if group else (0, count)
 
-    pick = np.zeros((packs, width, count, lanes))
+    pick = np.zeros((width, count, 2, per_class))
     for group in range(count):
         for which, kind in enumerate(classes(group)):
             for q in range(per_class):
-                for pack in range(packs):
-                    lane = pack * 2 * per_class + which * per_class + q
-                    pick[pack, radix * q + kind, group, lane] = 1.0
+                pick[radix * q + kind, group, which, q] = 1.0
     place = np.zeros((2, count, lanes, packs * 2 + 1, lanes))
 
     def slot(group, column, pack):
@@ -345,12 +343,11 @@
                 for mate, value in ((0, 0.25), (length // 2, -0.25)):
                     source, where = slot(group, mate, pack)
                     place[version, source, where, packs * 2, pack] += value
-    flip = np.zeros((lanes, 2 * lanes))
-    flip[np.arange(1, lanes), lanes - np.arange(1, lanes)] = 1.0
-    flip[0, lanes] = 1.0
+    flip = np.zeros((length // steps, length // steps))
+    flip[np.arange(len(flip)), -np.arange(len(flip))] = 1.0
     as_half = lambda table: table.astype(np.float32).astype(ml_dtypes.bfloat16)
     return (
-        as_half(pick.reshape(packs * width, count * lanes)),
+        as_half(pick.reshape(width, width)),
         as_half(place.reshape(2, count * lanes, (packs * 2 + 1) * lanes)),
         as_half(flip),
     )
@@ -373,8 +370,10 @@
     )
 
 
-def row_forward_body(steps, x_ref, table_ref, out_ref, held):
-    groups, _, height, lanes = out_ref.shape
+def row_forward_body(steps, me_ref, x_ref, table_ref, *refs):
+    out_refs, held = refs[:-1], refs[-1]
+    groups = len(out_refs)
+    _, height, lanes = out_refs[0].shape
     each = height // steps
     for start in range(0, height, 16):
         rows = pl.ds(start, 16)
@@ -385,7 +384,8 @@
             high, low = split(jnp.concatenate(pairs[group], axis=1))
             held[0, group, rows, :] = high
             held[1, group, rows, :] = low
-    for group in range(groups):
+    for turn, out_ref in enumerate(out_refs):
+        group = me_ref[0] ^ turn
         done = (
             dot(held[0, group], table_ref[group, 0])
             + dot(held[1, group], table_ref[group, 0])
@@ -393,8 +393,8 @@
         )
         for start in range(0, height, 8):
             spread = pl.ds(start % steps * each + start // steps, 8, stride=each)
-            out_ref[group, 0, spread, :] = done[start : start + 8, :lanes]
-            out_ref[group, 1, spread, :] = done[start : start + 8, lanes:]
+            out_ref[0, spread, :] = done[start : start + 8, :lanes]
+            out_ref[1, spread, :] = done[start : start + 8, lanes:]
 
 
 def row_inverse_body(
@@ -574,116 +574,161 @@
         ]
 
 
-def column_body(
-    steps, in_ref, there_ref, back_ref, weight_ref, mirror_ref, flip_ref, edge_ref, core_ref, held, made
-):
-    count, _, height, lanes = in_ref.shape
+def facing(blocks, step):
+    rows = lax.broadcasted_iota(jnp.int32, blocks[0].shape, 0)
+    return jnp.where(rows == 0, blocks[-step % len(blocks)], blocks[len(blocks) - 1 - step])
+
+
+def column_body(steps, count, me_ref, *refs):
+    in_refs = refs[:count]
+    there_ref, back_ref, turn_ref, weight_ref, mirror_ref, flip_ref = refs[count : count + 6]
+    edge_ref, core_ref, gathered, held, made = refs[count + 6 :]
+    _, height, lanes = in_refs[0].shape
     each = height // steps
     size = each * count
-    for step in range(steps):
-        rows = pl.ds(step * each, each)
-        block = jnp.concatenate(
-            [in_ref[source, part, rows, :] for part in range(2) for source in range(count)],
-            axis=0,
-        )
-        high, low = split(block)
-        done = (
-            dot(there_ref[step, 0], high)
-            + dot(there_ref[step, 1], high)
-            + dot(there_ref[step, 0], low)
-        )
-        held[0, step] = done[:size]
-        held[1, step] = done[size:]
+    for turn, in_ref in enumerate(in_refs):
+        source = me_ref[0] ^ turn
+        for part in range(2):
+            to = pl.ds(pl.multiple_of(part * size + source * each, 8), each)
+            for step in range(steps):
+                gathered[to, pl.ds(step * lanes, lanes)] = in_ref[part, pl.ds(step * each, each), :]
+    for step in range(0, steps, 2):
+        high, low = split(gathered[:, pl.ds(step * lanes, 2 * lanes)])
+        done = dot(there_ref[0], high) + dot(there_ref[1], high) + dot(there_ref[0], low)
+        for k in range(2):
+            held[0, step + k] = done[:size, k * lanes : (k + 1) * lanes]
+            held[1, step + k] = done[size:, k * lanes : (k + 1) * lanes]
+
+    def turned(pairs, rows, sign):
+        cosines, sines = turn_ref[0, rows, :], turn_ref[1, rows, :]
+        out = [pairs[0]]
+        for step in range(1, steps):
+            real, imag = pairs[step]
+            cosine = jnp.broadcast_to(cosines[:, step : step + 1], real.shape)
+            sine = sign * jnp.broadcast_to(sines[:, step : step + 1], real.shape)
+            out.append((real * cosine - imag * sine, imag * cosine + real * sine))
+        return out
 
     def forward(chunk, carry):
         rows = pl.ds(pl.multiple_of(chunk * 8, 8), 8)
         pairs = [(held[0, step, rows, :], held[1, step, rows, :]) for step in range(steps)]
-        for step, pair in enumerate(complex_dft(pairs, -1.0)):
+        for step, pair in enumerate(complex_dft(turned(pairs, rows, -1.0), -1.0)):
             held[0, step, rows, :] = pair[0]
             held[1, step, rows, :] = pair[1]
         return carry
 
     lax.fori_loop(0, size // 8, forward, 0)
+    lane_ids = lax.broadcasted_iota(jnp.int32, (size, lanes), 1)
+    lone = jnp.zeros((size, lanes), jnp.float32)
     for step in range(steps):
-        facing = [
-            jnp.concatenate([held[0, other], held[1, other]], axis=1)
-            for other in (steps - 1 - step, (steps - step) % steps)
-        ]
-        high, low = split(jnp.concatenate(facing, axis=0))
-        turned = dot(flip_ref[...], high) + dot(flip_ref[...], low)
+        for part in range(2):
+            spot = 2 * step + part
+            moved = facing([held[part, other] for other in range(steps)], step)
+            if spot:
+                moved = pltpu.roll(moved, spot, 1)
+            lone = jnp.where(lane_ids == spot, moved, lone)
+    high, low = split(lone)
+    lone = (dot(flip_ref[...], high) + dot(flip_ref[...], low)) * mirror_ref[...]
+    for step in range(steps):
         weight = weight_ref[step]
-        mirror = mirror_ref[step]
-        made[0, step] = weight * held[0, step] + mirror * turned[:, :lanes]
-        made[1, step] = weight * held[1, step] - mirror * turned[:, lanes:]
+        for part in range(2):
+            spot = 2 * step + part
+            moved = pltpu.roll(lone, lanes - spot, 1) if spot else lone
+            made[part, step] = weight * held[part, step] + jnp.where(lane_ids == 0, moved, 0.0)
 
     def backward(chunk, carry):
         rows = pl.ds(pl.multiple_of(chunk * 8, 8), 8)
         pairs = [(made[0, step, rows, :], made[1, step, rows, :]) for step in range(steps)]
-        for step, pair in enumerate(complex_dft(pairs, 1.0)):
+        for step, pair in enumerate(turned(complex_dft(pairs, 1.0), rows, 1.0)):
             made[0, step, rows, :] = pair[0]
             made[1, step, rows, :] = pair[1]
         return carry
 
     lax.fori_loop(0, size // 8, backward, 0)
-    for step in range(steps):
-        high, low = split(jnp.concatenate([made[0, step], made[1, step]], axis=0))
-        done = (
-            dot(back_ref[step, 0], high)
-            + dot(back_ref[step, 1], high)
-            + dot(back_ref[step, 0], low)
-        )
-        half = each // 2
-        rows = pl.ds(step * half, half)
-        for part in range(2):
-            for target in range(count):
-                start = part * size + target * each
-                edge_ref[target, part, rows, :] = done[start : start + half]
-                core_ref[target, part, rows, :] = done[start + half : start + each]
+    half = each // 2
+    for step in range(0, steps, 2):
+        block = [
+            jnp.concatenate([made[part, step + k] for k in range(2)], axis=1) for part in range(2)
+        ]
+        high, low = split(jnp.concatenate(block, axis=0))
+        done = dot(back_ref[0], high) + dot(back_ref[1], high) + dot(back_ref[0], low)
+        for k in range(2):
+            rows = pl.ds((step + k) * half, half)
+            columns = slice(k * lanes, (k + 1) * lanes)
+            for part in range(2):
+                for target in range(count):
+                    start = part * size + target * each
+                    edge_ref[target, part, rows, :] = done[start : start + half, columns]
+                    core_ref[target, part, rows, :] = done[start + half : start + each, columns]
 
 
 def weight_pick_body(w_ref, pick_ref, out_ref):
-    count, _, lanes = out_ref.shape
+    count, thick, lanes = out_ref.shape
     packs, _, width = w_ref.shape
-    total = 0.0
+    piece = lanes // packs
+    chosen = []
     for pack in range(packs):
         high, low = split(w_ref[pack])
-        chosen = pick_ref[pl.ds(pack * width, width), :]
-        total = total + dot(high, chosen) + dot(low, chosen)
+        chosen.append(dot(high, pick_ref[...]) + dot(low, pick_ref[...]))
+    lane_ids = lax.broadcasted_iota(jnp.int32, (thick, lanes), 1)
     for target in range(count):
-        out_ref[target] = total[:, target * lanes : (target + 1) * lanes]
-
-
-def weight_place_body(in_ref, place_ref, flip_ref, weight_ref, mirror_ref, held):
+        start = target * piece // lanes * lanes
+        total = None
+        for pack in range(packs):
+            moved = chosen[pack][:, start : start + lanes]
+            shift = (pack - target) % packs * piece
+            if shift:
+                moved = pltpu.roll(moved, shift, 1)
+            total = moved if pack == 0 else jnp.where(lane_ids >= pack * piece, moved, total)
+        out_ref[target] = total
+
+
+def weight_place_body(in_ref, place_ref, flip_ref, weight_ref, mirror_ref):
     count, depth, lanes = in_ref.shape
     steps, size, _ = weight_ref.shape
     packs = steps * size // depth
+    inner = depth // size
     total = 0.0
     for source in range(count):
         high, low = split(in_ref[source])
         chosen = place_ref[pl.ds(source * lanes, lanes), :]
         total = total + dot(high, chosen) + dot(low, chosen)
-    inner = depth // size
-    extra = total[:, 2 * packs * lanes :]
-    first = lax.broadcasted_iota(jnp.int32, (size, lanes), 1) == 0
+
+    def block(step, side):
+        pack, rest = divmod(step, inner)
+        start = (2 * pack + side) * lanes if side < 2 else 2 * packs * lanes
+        return total[rest * size : (rest + 1) * size, start : start + lanes]
+
+    def flipped(cells):
+        high, low = split(cells)
+        return dot(flip_ref[...], high) + dot(flip_ref[...], low)
+
+    lane_ids = lax.broadcasted_iota(jnp.int32, (size, lanes), 1)
+    extra = [block(step, 2) for step in range(steps)]
+    extra = [
+        pltpu.roll(cells, lanes - step // inner, 1) if step // inner else cells
+        for step, cells in enumerate(extra)
+    ]
+    straight = jnp.zeros((size, lanes), jnp.float32)
+    opposite = straight
     for step in range(steps):
-        pack, rest = divmod(step, inner)
-        rows = slice(rest * size, (rest + 1) * size)
-        lone = extra[rows]
-        if pack:
-            lone = pltpu.roll(lone, lanes - pack, 1)
-        lone = jnp.where(first, lone, 0.0)
-        mirror_ref[step] = lone
-        weight_ref[step] = total[rows, 2 * pack * lanes : (2 * pack + 1) * lanes]
-        held[step] = jnp.concatenate(
-            [total[rows, (2 * pack + 1) * lanes : (2 * pack + 2) * lanes], lone], axis=1
-        )
-    for step in range(steps):
-        high, low = split(
-            jnp.concatenate([held[steps - 1 - step], held[(steps - step) % steps]], axis=0)
-        )
-        turned = dot(flip_ref[...], high) + dot(flip_ref[...], low)
-        weight_ref[step] += turned[:, :lanes]
-        mirror_ref[step] += turned[:, lanes:]
+        against = facing(extra, step)
+        for part in range(2):
+            spot = 2 * step + part
+            sign = 1.0 - 2.0 * part
+            straight = jnp.where(lane_ids == spot, sign * roll_to(extra[step], spot), straight)
+            opposite = jnp.where(lane_ids == spot, sign * roll_to(against, spot), opposite)
+    mirror_ref[...] = straight + flipped(opposite)
+    backs = [block(step, 1) for step in range(steps)]
+    for step in range(0, steps, 2):
+        both = jnp.concatenate([facing(backs, step), facing(backs, step + 1)], axis=1)
+        both = flipped(both)
+        weight_ref[step] = block(step, 0) + both[:, :lanes]
+        weight_ref[step + 1] = block(step + 1, 0) + both[:, lanes:]
+
+
+def roll_to(cells, spot):
+    return pltpu.roll(cells, spot, 1) if spot else cells
 
 
 def filtered(values, dirty, weights):
@@ -694,42 +739,68 @@
     size = length // steps
     width = weights.shape[1]
     f32 = jnp.float32
-    pick, place, flip = [jnp.asarray(table) for table in weight_tables(length, count)]
+    pick, place, flip = [jnp.asarray(table) for table in weight_tables(length, count, steps)]
     there, back = [jnp.asarray(table) for table in row_tables(length, count)]
-    down, up = [jnp.asarray(table) for table in column_tables(length, count, steps)]
+    down, up, turns = [jnp.asarray(table) for table in column_tables(length, count, steps)]
     shape = lambda *dims: jax.ShapeDtypeStruct(dims, f32)
-    packs = length * width // (count * lanes) // (length // count)
-    packs = pick.shape[0] // width
+    packs = lanes * count // width
     depth = length // packs
-
-    sent = whole_call(weight_pick_body, shape(count, depth, lanes), [], "weight_pick", 6)(
-        weights.reshape(packs, depth, width), pick
-    )
+    half = height // 2
+    vmem = pl.BlockSpec(memory_space=pltpu.VMEM)
+    smem = pl.BlockSpec(memory_space=pltpu.SMEM)
+    me = jnp.reshape(lax.axis_index("rows"), (1,)).astype(jnp.int32)
+
+    thick = depth // 2
+    sent = pl.pallas_call(
+        weight_pick_body,
+        grid=(2,),
+        in_specs=[
+            pl.BlockSpec((packs, thick, width), lambda i: (0, i, 0)),
+            pl.BlockSpec((width, width), lambda i: (0, 0)),
+        ],
+        out_specs=pl.BlockSpec((count, thick, lanes), lambda i: (0, i, 0)),
+        out_shape=shape(count, depth, lanes),
+        compiler_params=pltpu.CompilerParams(vmem_limit_bytes=vmem_bytes),
+        name="weight_pick",
+        cost_estimate=busy(4),
+    )(weights.reshape(packs, depth, width), pick)
     sent = lax.all_to_all(sent, "rows", 0, 0, tiled=True)
-    ahead = whole_call(
+    ahead = pl.pallas_call(
         functools.partial(row_forward_body, steps),
-        shape(count, 2, height, lanes),
-        [pltpu.VMEM((2, count, height, 2 * lanes), jnp.bfloat16)],
-        "row_forward",
-        6,
-    )(values, there)
-    ahead = lax.all_to_all(ahead, "rows", 0, 0, tiled=True)
+        in_specs=[smem, vmem, vmem],
+        out_specs=[vmem] * count,
+        out_shape=[shape(2, height, lanes)] * count,
+        scratch_shapes=[pltpu.VMEM((2, count, height, 2 * lanes), jnp.bfloat16)],
+        compiler_params=pltpu.CompilerParams(vmem_limit_bytes=vmem_bytes),
+        name="row_forward",
+        cost_estimate=busy(6),
+    )(me, values, there)
+    ahead = [ahead[0]] + [
+        lax.ppermute(ahead[turn], "rows", [(i, i ^ turn) for i in range(count)])
+        for turn in range(1, count)
+    ]
     mine = jnp.where(lax.axis_index("rows") == 0, place[0], place[1])
     weight, mirror = whole_call(
         weight_place_body,
-        [shape(steps, size, lanes)] * 2,
-        [pltpu.VMEM((steps, size, 2 * lanes), f32)],
+        [shape(steps, size, lanes), shape(size, lanes)],
+        [],
         "weight_place",
         10,
     )(sent, mine, flip)
-    half = height // 2
-    edge, core = whole_call(
-        functools.partial(column_body, steps),
-        [shape(count, 2, half, lanes)] * 2,
-        [pltpu.VMEM((2, steps, size, lanes), f32)] * 2,
-        "column_filter",
-        12,
-    )(ahead, down, up, weight, mirror, flip)
+    edge, core = pl.pallas_call(
+        functools.partial(column_body, steps, count),
+        in_specs=[smem] + [vmem] * (count + 6),
+        out_specs=[vmem] * 2,
+        out_shape=[shape(count, 2, half, lanes)] * 2,
+        scratch_shapes=[
+            pltpu.VMEM((2 * size, steps * lanes), f32),
+            pltpu.VMEM((2, steps, size, lanes), f32),
+            pltpu.VMEM((2, steps, size, lanes), f32),
+        ],
+        compiler_params=pltpu.CompilerParams(vmem_limit_bytes=vmem_bytes),
+        name="column_filter",
+        cost_estimate=busy(10),
+    )(me, *ahead, down, up, turns, weight, mirror, flip)
     edge = lax.all_to_all(edge, "rows", 0, 0, tiled=True)
     core = lax.all_to_all(core, "rows", 0, 0, tiled=True)
     chans = lax.axis_size("chan")

time: 253 us -> 242 us (0.957)
  waiting for transfers between devices: 91 us -> 79.9 us
  Pallas kernels: 74.7 us -> 72 us
    ppermute x0 -> x7, waiting for transfers between devices: none -> 21.5 us  [filtered(): lax.ppermute(ahead[turn], 'rows', [(i, i ^ turn) for i in range(count)])]
    all_to_all x1, waiting for transfers between devices: 21 us -> 0.01 us  [filtered(): sent = lax.all_to_all(sent, 'rows', 0, 0, tiled=True)]
    all_to_all x1 -> x0, waiting for transfers between devices: 12.6 us -> none  [filtered(): ahead = lax.all_to_all(ahead, 'rows', 0, 0, tiled=True)]
    ppermute x0 -> x7, starting transfers between devices: none -> 6.81 us  [filtered(): lax.ppermute(ahead[turn], 'rows', [(i, i ^ turn) for i in range(count)])]
    all_to_all x1 -> x0, starting transfers between devices: 4.53 us -> none  [filtered(): ahead = lax.all_to_all(ahead, 'rows', 0, 0, tiled=True)]
    pallas_call x4, Pallas kernels: 34.1 us -> 31.4 us  [the longest x1 11.2 us: filtered(): pl.pallas_call(functools.partial(column_body, steps, count), in_specs=[sm...]
  transfers between devices with their start and end apart: 24 -> 30, of which waited for: 16 -> 16; matrix products, arithmetic and copies ran while one was open for 3% -> 4% of each run, Pallas kernels for 15% -> 16%
where the time goes in v3:
time: 242 us; the launch traced here: 240 us
  waiting for transfers between devices  79.9 us (33%)
  Pallas kernels  72 us (30%)
  starting transfers between devices  53 us (22%)
  blocking collectives  19.6 us (8%)
  local copies, waits for them, and re-layouts  9.34 us (4%)
  other arithmetic  5.33 us (2%)
    ppermute x12, waiting for transfers between devices, over_chans(): lax.ppermute(pieces[turn], 'chan', [(i, i ^ turn) for i in range(chans)])  44 us
    ppermute x12, starting transfers between devices, over_chans(): lax.ppermute(pieces[turn], 'chan', [(i, i ^ turn) for i in range(chans)])  22.1 us
    pallas_call x2, Pallas kernels, starlet(): pl.pallas_call(functools.partial(starlet_body, chans, spans, fills), in_s...  21.9 us
    ppermute x7, waiting for transfers between devices, filtered(): lax.ppermute(ahead[turn], 'rows', [(i, i ^ turn) for i in range(count)])  21.5 us
    all_to_all x1, blocking collectives, filtered(): edge = lax.all_to_all(edge, 'rows', 0, 0, tiled=True)  19.6 us
    ppermute x7, starting transfers between devices, max_over(): lax.ppermute(cells, axis, [(i, i ^ distance) for i in range(count)])  11.4 us
    pallas_call x1, Pallas kernels, filtered(): pl.pallas_call(functools.partial(column_body, steps, count), in_specs=[sm...  11.2 us
    pallas_call x1, Pallas kernels, filtered(): whole_call(weight_place_body, [shape(steps, size, lanes), shape(size, lan...  10.3 us
  transfers between devices with their start and end apart: 30, of which 16 were waited for; matrix products, arithmetic and copies ran while one was open for 4% of the time, Pallas kernels for 16%

profile of v3, /device:TPU:0, one launch (start us, length us, event | category | flops | bytes accessed | tf_op | source)
XLA Modules:
  0.0 240.2 jit_solution(1358568300247531824)
XLA Ops:
  0.6 4.5 %weight_pick.1 = f32[8,512,128]{2,1,0:T(8,128)} custom-call(f32[4,512,256]{2,1,0:T(8,128)} %bitcast.67, bf16[256,256]{1,0:T(8,128)(2,1)} %constant.53.clone.pick_ref), custom_call_target="tpu_custom_call" | custom-call | bytes 14000000 | tf_op jit(solution)/shard_map/weight_pick/pallas_call | solution.py:754
  5.1 5.2 %all-to-all-start = ((f32[8,512,128]{2,1,0:T(8,128)}), f32[8,512,128]{2,1,0:T(8,128)S(1)}, u32[]{:S(2)}, u32[]{:S(2)}) async-start(f32[8,512,128]{2,1,0:T(8,128)} %weight_pick.1), calls=%async_computation | async-start | bytes 4194304 | tf_op jit(solution)/shard_map/all_to_all | solution.py:767
  10.3 5.4 %row_forward.1 = (f32[2,256,128]{2,1,0:T(8,128)}, f32[2,256,128]{2,1,0:T(8,128)}, f32[2,256,128]{2,1,0:T(8,128)}, f32[2,256,128]{2,1,0:T(8,128)}, f32[2,256,128]...) custom-call(s32[1]{0:T(128)} %bitcast.5.me_ref, f32[256,2048]{1,0:T(8,128)} %bitcast.61, ...), custom_call_target="tpu_custom_call" | custom-call | bytes 21000000 | tf_op jit(solution)/shard_map/row_forward/pallas_call | solution.py:768
  16.2 1.7 collective-permute-start.1
  17.9 1.7 collective-permute-start.3
  19.7 2.6 %collective-permute-start.5 = (f32[2,256,128]{2,1,0:T(8,128)}, f32[2,256,128]{2,1,0:T(8,128)}, u32[]{:S(2)}, u32[]{:S(2)}) collective-permute-start(f32[2,256,128]{2,1,0:T(8,128)} %get-tuple-element.52), channel_id=1, source_target_pairs={{0,6},{1,7},{2,4},{3,5},{4,2},{5,3},{6,0},{7,1},{8,14},{9,15},{10,... | collective-permute-start | bytes 786440 | tf_op jit(solution)/shard_map/ppermute | solution.py:779
  22.3 19.9 %collective-permute-done.1.refs_2_ = f32[2,256,128]{2,1,0:T(8,128)S(1)} collective-permute-done((f32[2,256,128]{2,1,0:T(8,128)}, f32[2,256,128]{2,1,0:T(8,128)S(1)}, u32[]{:S(2)}, u32[]{:S(2)}) %collective-permute-start.1) | collective-permute-done | bytes 262176 | tf_op jit(solution)/shard_map/ppermute | solution.py:779
  42.4 3.3 %select_bitcast_fusion.place_ref = bf16[1024,1152]{1,0:T(8,128)(2,1)} fusion(bf16[1,1024,1152]{2,1,0:T(8,128)(2,1)} %constant.64, bf16[1,1024,1152]{2,1,0:T(8,128)(2,1)} %constant.65, pred[]{:T(512)} %eq.15), kind=kLoop, calls=%fused_computation | loop fusion | flops 1179648 | bytes 7077889 | tf_op jit(solution)/shard_map/jit(_where)/select_n | solution.py:782
  45.8 1.3 copy-done
  47.1 10.3 %weight_place.1 = (f32[16,128,128]{2,1,0:T(8,128)}, f32[128,128]{1,0:T(8,128)}) custom-call(f32[8,512,128]{2,1,0:T(8,128)} %copy-done, bf16[1024,1152]{1,0:T(8,128)(2,1)} %select_bitcast_fusion.place_ref, bf16[128,128]{1,0:T(8,128)(2,1)} %constant.55.clone.flip_ref.refs_13_), custom_call_target="tpu_custom_call" | custom-call | bytes 35000000 | tf_op jit(solution)/shard_map/weight_place/pallas_call | solution.py:783
  57.4 1.7 collective-permute-done.6.refs_7_
  59.1 11.2 %column_filter.1 = (f32[8,2,128,128]{3,2,1,0:T(8,128)}, f32[8,2,128,128]{3,2,1,0:T(8,128)}) custom-call(s32[1]{0:T(128)} %bitcast.5.me_ref, f32[2,256,128]{2,1,0:T(8,128)} %get-tuple-element.46.refs_0_, f32[2,256,128]{2,1,0:T(8,128)} %copy-done.12, f32[2,256,128]{2,1,0:T(8,128)} %copy-done.13, f32[2,256,128]{2,1,0:T(8,128)} %copy-done.14, ...), custom_call_target="tpu_custom_call" | custom-call | bytes 35000000 | tf_op jit(solution)/shard_map/column_filter/pallas_call | solution.py:790
  70.3 19.6 %all_to_all.15.in_ref = f32[8,2,128,128]{3,2,1,0:T(8,128)} all-to-all(f32[8,2,128,128]{3,2,1,0:T(8,128)} %get-tuple-element.56), channel_id=1, replica_groups=mesh['chan'=4,'rows'=8] {'rows'}, dimensions={0} | all-to-all | bytes 2097152 | tf_op jit(solution)/shard_map/all_to_all | solution.py:804
  89.8 3.7 %all-to-all-start.2 = ((f32[8,2,128,128]{3,2,1,0:T(8,128)}), f32[8,2,128,128]{3,2,1,0:T(8,128)S(1)}, u32[]{:S(2)}, u32[]{:S(2)}) async-start(f32[8,2,128,128]{3,2,1,0:T(8,128)} %get-tuple-element.58), calls=%async_computation.2 | async-start | bytes 2097152 | tf_op jit(solution)/shard_map/all_to_all | solution.py:805
  93.6 4.5 %row_inverse.2 = (f32[256,2048]{1,0:T(8,128)}, f32[4,136,512]{2,1,0:T(8,128)}) custom-call(f32[8,2,128,128]{3,2,1,0:T(8,128)} %all_to_all.15.in_ref, bf16[8,2,256,256]{3,2,1,0:T(8,128)(2,1)} %constant.57.clone.table_ref, f32[256,2048]{1,0:T(8,128)} %bitcast.62, f32[256,2048]{1,0:T(8,128)} %bitcast.64, f32[256,2048]{1,0:T(8,128)} %bitcast.65), custom_call_target="tpu_custom_call" | custom-call | bytes 17500000 | tf_op jit(solution)/shard_map/row_inverse/pallas_call | solution.py:813
  98.1 1.3 dynamic-slice_bitcast_fusion.4
  99.4 1.6 collective-permute-start.7
  101.1 2.6 %collective-permute-start.8 = (f32[136,512]{1,0:T(8,128)S(1)}, f32[136,512]{1,0:T(8,128)S(1)}, u32[]{:S(2)}, u32[]{:S(2)}) collective-permute-start(f32[136,512]{1,0:T(8,128)S(1)} %get-tuple-element.95), channel_id=1, source_target_pairs={{0,16},{8,24},{16,0},{24,8},{1,17},{9,25},{17,1},{25,9},{2,18},{10... | collective-permute-start | bytes 835592 | tf_op jit(solution)/shard_map/ppermute | solution.py:840
  104.5 4.3 %all-to-all-done.2.in_ref = f32[8,2,128,128]{3,2,1,0:T(8,128)S(1)} async-done(((f32[8,2,128,128]{3,2,1,0:T(8,128)}), f32[8,2,128,128]{3,2,1,0:T(8,128)S(1)}, u32[]{:S(2)}, u32[]{:S(2)}) %all-to-all-start.2) | async-done | bytes 1048608 | tf_op jit(solution)/shard_map/all_to_all | solution.py:805
  109.8 4.5 %row_inverse.3 = (f32[256,2048]{1,0:T(8,128)}, f32[4,136,512]{2,1,0:T(8,128)}) custom-call(f32[8,2,128,128]{3,2,1,0:T(8,128)} %copy-done.1, bf16[8,2,256,256]{3,2,1,0:T(8,128)(2,1)} %constant.57.clone.table_ref, f32[256,2048]{1,0:T(8,128)} %bitcast.63, f32[256,2048]{1,0:T(8,128)} %bitcast.66, ...), custom_call_target="tpu_custom_call", output_to_operand_aliasing={{0}: (4, {})} | custom-call | bytes 17500000 | tf_op jit(solution)/shard_map/row_inverse/pallas_call | solution.py:813
  114.3 2.0 dynamic-slice_bitcast_fusion
  116.3 7.2 %collective-permute-done.8.refs_2_ = f32[136,512]{1,0:T(8,128)S(1)} collective-permute-done((f32[136,512]{1,0:T(8,128)S(1)}, f32[136,512]{1,0:T(8,128)S(1)}, u32[]{:S(2)}, u32[]{:S(2)}) %collective-permute-start.8) | collective-permute-done | bytes 278560 | tf_op jit(solution)/shard_map/ppermute | solution.py:840
  123.6 1.3 collective-permute-start.11
  124.9 5.6 %collective-permute-start.12 = (f32[136,512]{1,0:T(8,128)S(1)}, f32[136,512]{1,0:T(8,128)S(1)}, u32[]{:S(2)}, u32[]{:S(2)}) collective-permute-start(f32[136,512]{1,0:T(8,128)S(1)} %get-tuple-element.68), channel_id=1, source_target_pairs={{0,8},{8,0},{16,24},{24,16},{1,9},{9,1},{17,25},{25,17},{2,10},{10... | collective-permute-start | bytes 835592 | tf_op jit(solution)/shard_map/ppermute | solution.py:840
  131.6 1.4 collective-permute-start.14
  133.0 2.5 %collective-permute-start.10 = (f32[4,24,512]{2,1,0:T(8,128)S(1)}, f32[4,24,512]{2,1,0:T(8,128)S(1)}, u32[]{:S(2)}, u32[]{:S(2)}) collective-permute-start(f32[4,24,512]{2,1,0:T(8,128)S(1)} %pad_maximum_fusion), channel_id=1, source_target_pairs={{0,1},{1,2},{2,3},{3,4},{4,5},{5,6},{6,7},{8,9},{9,10},{10,11},{11... | collective-permute-start | bytes 589832 | tf_op jit(solution)/shard_map/ppermute | solution.py:859
  137.2 9.2 %starlet.2 = (f32[4,4,96,512]{3,2,1,0:T(8,128)}, f32[3,8,128]{2,1,0:T(8,128)}) custom-call(s32[4]{0:T(128)} %add_convert_fusion.ends_ref, f32[136,512]{1,0:T(8,128)} %copy-done.2, f32[136,512]{1,0:T(8,128)} %copy-done.3, f32[136,512]{1,0:T(8,128)} %copy-done.4, f32[136,512]{1,0:T(8,128)} %copy-done.5, f32[24,512]{1,0:T(8,128)} %get-tuple-element.105.refs_4_, ...), custom_call_target="tpu_custom_call" | custom-call | bytes 42000000 | tf_op jit(solution)/shard_map/starlet/pallas_call | solution.py:872
  146.5 6.4 %collective-permute-done.13.refs_6_ = f32[136,512]{1,0:T(8,128)S(1)} collective-permute-done((f32[136,512]{1,0:T(8,128)S(1)}, f32[136,512]{1,0:T(8,128)S(1)}, u32[]{:S(2)}, u32[]{:S(2)}) %collective-permute-start.13) | collective-permute-done | bytes 278560 | tf_op jit(solution)/shard_map/ppermute | solution.py:840
  154.3 12.6 %starlet.3 = (f32[4,4,160,512]{3,2,1,0:T(8,128)}, f32[3,8,128]{2,1,0:T(8,128)}) custom-call(s32[4]{0:T(128)} %add_convert_fusion.ends_ref, f32[136,512]{1,0:T(8,128)} %copy-done.2, f32[136,512]{1,0:T(8,128)} %copy-done.3, f32[136,512]{1,0:T(8,128)} %copy-done.4, f32[136,512]{1,0:T(8,128)} %copy-done.5, f32[136,512]{1,0:T(8,128)} %get-tuple-element.67.refs_4_, ...), custom_call_target="tpu_custom_call" | custom-call | bytes 42000000 | tf_op jit(solution)/shard_map/starlet/pallas_call | solution.py:872
  167.7 1.2 collective-permute-done.15
  168.9 2.3 collective-permute-start.16
  171.1 1.5 collective-permute-start.17
  172.8 2.0 collective-permute-done.17
  174.8 2.4 collective-permute-done.18
  177.2 5.1 %collective-permute-start.19 = (f32[3,8,128]{2,1,0:T(8,128)S(1)}, f32[3,8,128]{2,1,0:T(8,128)S(1)}, u32[]{:S(2)}, u32[]{:S(2)}) collective-permute-start(f32[3,8,128]{2,1,0:T(8,128)S(1)} %maximum_maximum_fusion.1), channel_id=1, source_target_pairs={{0,8},{8,0},{16,24},{24,16},{1,9},{9,1},{17,25},{25,17},{2,10},{10... | collective-permute-start | bytes 36872 | tf_op jit(solution)/shard_map/ppermute | solution.py:125
  183.4 1.4 collective-permute-start.21
  184.8 2.1 collective-permute-done.20
  186.9 2.0 collective-permute-done.21
  189.5 2.9 %shrink.2 = (f32[96,512]{1,0:T(8,128)}, f32[96,512]{1,0:T(8,128)}, f32[96,512]{1,0:T(8,128)}, f32[96,512]{1,0:T(8,128)}) custom-call(f32[4,4,96,512]{3,2,1,0:T(8,128)} %get-tuple-element.65.detail_ref, f32[3,8,128]{2,1,0:T(8,128)} %maximum_maximum_fusion.peak_ref), custom_call_target="tpu_custom_call" | custom-call | bytes 10500000 | tf_op jit(solution)/shard_map/shrink/pallas_call | solution.py:920
  192.6 1.8 collective-permute-start.23
  194.4 2.4 %collective-permute-start.24 = (f32[96,512]{1,0:T(8,128)}, f32[96,512]{1,0:T(8,128)S(1)}, u32[]{:S(2)}, u32[]{:S(2)}) collective-permute-start(f32[96,512]{1,0:T(8,128)} %get-tuple-element.75), channel_id=1, source_target_pairs={{0,24},{8,16},{16,8},{24,0},{1,25},{9,17},{17,9},{25,1},{2,26},{10... | collective-permute-start | bytes 589832 | tf_op jit(solution)/shard_map/ppermute | solution.py:840
  196.8 3.9 %shrink.3 = (f32[160,512]{1,0:T(8,128)}, f32[160,512]{1,0:T(8,128)}, f32[160,512]{1,0:T(8,128)}, f32[160,512]{1,0:T(8,128)}) custom-call(f32[4,4,160,512]{3,2,1,0:T(8,128)} %get-tuple-element.76.detail_ref, f32[3,8,128]{2,1,0:T(8,128)} %maximum_maximum_fusion.peak_ref), custom_call_target="tpu_custom_call" | custom-call | bytes 10500000 | tf_op jit(solution)/shard_map/shrink/pallas_call | solution.py:920
  201.8 6.1 %collective-permute-done.23.refs_2_ = f32[96,512]{1,0:T(8,128)S(1)} collective-permute-done((f32[96,512]{1,0:T(8,128)}, f32[96,512]{1,0:T(8,128)S(1)}, u32[]{:S(2)}, u32[]{:S(2)}) %collective-permute-start.23) | collective-permute-done | bytes 196640 | tf_op jit(solution)/shard_map/ppermute | solution.py:840
  207.8 2.8 %collective-permute-start.25 = (f32[160,512]{1,0:T(8,128)}, f32[160,512]{1,0:T(8,128)S(1)}, u32[]{:S(2)}, u32[]{:S(2)}) collective-permute-start(f32[160,512]{1,0:T(8,128)} %get-tuple-element.86), channel_id=1, source_target_pairs={{0,8},{8,0},{16,24},{24,16},{1,9},{9,1},{17,25},{25,17},{2,10},{10... | collective-permute-start | bytes 983048 | tf_op jit(solution)/shard_map/ppermute | solution.py:840
  210.7 2.4 collective-permute-start.27
  213.0 8.8 %collective-permute-done.25.refs_5_ = f32[160,512]{1,0:T(8,128)S(1)} collective-permute-done((f32[160,512]{1,0:T(8,128)}, f32[160,512]{1,0:T(8,128)S(1)}, u32[]{:S(2)}, u32[]{:S(2)}) %collective-permute-start.25) | collective-permute-done | bytes 327712 | tf_op jit(solution)/shard_map/ppermute | solution.py:840
  221.8 14.4 %collective-permute-done.26.refs_6_ = f32[160,512]{1,0:T(8,128)S(1)} collective-permute-done((f32[160,512]{1,0:T(8,128)}, f32[160,512]{1,0:T(8,128)S(1)}, u32[]{:S(2)}, u32[]{:S(2)}) %collective-permute-start.26) | collective-permute-done | bytes 327712 | tf_op jit(solution)/shard_map/ppermute | solution.py:840
  237.1 3.0 %join.1 = f32[256,2048]{1,0:T(8,128)} custom-call(s32[1]{0:T(128)} %bitcast.me_ref, f32[96,512]{1,0:T(8,128)} %get-tuple-element.81.refs_0_, f32[96,512]{1,0:T(8,128)} %copy-done.17, f32[96,512]{1,0:T(8,128)} %copy-done.18, f32[96,512]{1,0:T(8,128)} %copy-done.19, f32[160,512]{1,0:T(8,128)} %get-tuple-element.85.refs_4_, f32[160,512]{1,0:T(8,128)} %copy-done.6, ...), custom_call_target="tpu_custom_call" | custom-call | bytes 14000000 | tf_op jit(solution)/shard_map/join/pallas_call | solution.py:937
  (90 shorter events, 11.8 us)
Async XLA Ops:
  5.1 40.6 %all-to-all-start = ((f32[8,512,128]{2,1,0:T(8,128)}), f32[8,512,128]{2,1,0:T(8,128)S(1)}, u32[]{:S(2)}, u32[]{:S(2)}) async-start(f32[8,512,128]{2,1,0:T(8,128)} %weight_pick.1), calls=%async_computation | async-start | bytes 4194304 | tf_op jit(solution)/shard_map/all_to_all | solution.py:767
  15.7 4.0 %collective-permute-start = (f32[2,256,128]{2,1,0:T(8,128)}, f32[2,256,128]{2,1,0:T(8,128)S(1)}, u32[]{:S(2)}, u32[]{:S(2)}) collective-permute-start(f32[2,256,128]{2,1,0:T(8,128)} %get-tuple-element.47), channel_id=1, source_target_pairs={{0,1},{1,0},{2,3},{3,2},{4,5},{5,4},{6,7},{7,6},{8,9},{9,8},{10,11... | collective-permute-start | bytes 786440 | tf_op jit(solution)/shard_map/ppermute | solution.py:779
  16.2 25.9 %collective-permute-start.1 = (f32[2,256,128]{2,1,0:T(8,128)}, f32[2,256,128]{2,1,0:T(8,128)S(1)}, u32[]{:S(2)}, u32[]{:S(2)}) collective-permute-start(f32[2,256,128]{2,1,0:T(8,128)} %get-tuple-element.48), channel_id=1, source_target_pairs={{0,2},{1,3},{2,0},{3,1},{4,6},{5,7},{6,4},{7,5},{8,10},{9,11},{10,... | collective-permute-start | bytes 786440 | tf_op jit(solution)/shard_map/ppermute | solution.py:779
  17.9 39.5 %collective-permute-start.2 = (f32[2,256,128]{2,1,0:T(8,128)}, f32[2,256,128]{2,1,0:T(8,128)S(1)}, u32[]{:S(2)}, u32[]{:S(2)}) collective-permute-start(f32[2,256,128]{2,1,0:T(8,128)} %get-tuple-element.49), channel_id=1, source_target_pairs={{0,3},{1,2},{2,1},{3,0},{4,7},{5,6},{6,5},{7,4},{8,11},{9,10},{10,... | collective-permute-start | bytes 786440 | tf_op jit(solution)/shard_map/ppermute | solution.py:779
  17.9 39.5 %collective-permute-start.3 = (f32[2,256,128]{2,1,0:T(8,128)}, f32[2,256,128]{2,1,0:T(8,128)S(1)}, u32[]{:S(2)}, u32[]{:S(2)}) collective-permute-start(f32[2,256,128]{2,1,0:T(8,128)} %get-tuple-element.50), channel_id=1, source_target_pairs={{0,4},{1,5},{2,6},{3,7},{4,0},{5,1},{6,2},{7,3},{8,12},{9,13},{10,... | collective-permute-start | bytes 786440 | tf_op jit(solution)/shard_map/ppermute | solution.py:779
  19.6 37.8 %collective-permute-start.4 = (f32[2,256,128]{2,1,0:T(8,128)}, f32[2,256,128]{2,1,0:T(8,128)S(1)}, u32[]{:S(2)}, u32[]{:S(2)}) collective-permute-start(f32[2,256,128]{2,1,0:T(8,128)} %get-tuple-element.51), channel_id=1, source_target_pairs={{0,5},{1,4},{2,7},{3,6},{4,1},{5,0},{6,3},{7,2},{8,13},{9,12},{10,... | collective-permute-start | bytes 786440 | tf_op jit(solution)/shard_map/ppermute | solution.py:779
  19.7 26.0 %copy-start.12 = (f32[2,256,128]{2,1,0:T(8,128)}, f32[2,256,128]{2,1,0:T(8,128)S(1)}, u32[]{:S(2)}) copy-start(f32[2,256,128]{2,1,0:T(8,128)S(1)} %collective-permute-done.refs_1_) | copy-start | bytes 786436
  19.7 37.7 %collective-permute-start.5 = (f32[2,256,128]{2,1,0:T(8,128)}, f32[2,256,128]{2,1,0:T(8,128)}, u32[]{:S(2)}, u32[]{:S(2)}) collective-permute-start(f32[2,256,128]{2,1,0:T(8,128)} %get-tuple-element.52), channel_id=1, source_target_pairs={{0,6},{1,7},{2,4},{3,5},{4,2},{5,3},{6,0},{7,1},{8,14},{9,15},{10,... | collective-permute-start | bytes 786440 | tf_op jit(solution)/shard_map/ppermute | solution.py:779
  42.2 3.6 %copy-start.13 = (f32[2,256,128]{2,1,0:T(8,128)}, f32[2,256,128]{2,1,0:T(8,128)S(1)}, u32[]{:S(2)}) copy-start(f32[2,256,128]{2,1,0:T(8,128)S(1)} %collective-permute-done.1.refs_2_) | copy-start | bytes 786436
  42.2 16.9 %collective-permute-start.6 = (f32[2,256,128]{2,1,0:T(8,128)}, f32[2,256,128]{2,1,0:T(8,128)}, u32[]{:S(2)}, u32[]{:S(2)}) collective-permute-start(f32[2,256,128]{2,1,0:T(8,128)} %get-tuple-element.53), channel_id=1, source_target_pairs={{0,7},{1,6},{2,5},{3,4},{4,3},{5,2},{6,1},{7,0},{8,15},{9,14},{10,... | collective-permute-start | bytes 786440 | tf_op jit(solution)/shard_map/ppermute | solution.py:779
  45.8 1.3 copy-start
  57.4 1.7 copy-start.14
  57.4 1.7 copy-start.15
  57.4 1.7 copy-start.16
  89.8 18.9 %all-to-all-start.2 = ((f32[8,2,128,128]{3,2,1,0:T(8,128)}), f32[8,2,128,128]{3,2,1,0:T(8,128)S(1)}, u32[]{:S(2)}, u32[]{:S(2)}) async-start(f32[8,2,128,128]{3,2,1,0:T(8,128)} %get-tuple-element.58), calls=%async_computation.2 | async-start | bytes 2097152 | tf_op jit(solution)/shard_map/all_to_all | solution.py:805
  99.4 24.2 %copy-start.2 = (f32[136,512]{1,0:T(8,128)}, f32[136,512]{1,0:T(8,128)S(1)}, u32[]{:S(2)}) copy-start(f32[136,512]{1,0:T(8,128)S(1)} %get-tuple-element.61.refs_0_) | copy-start | bytes 835588
  99.4 16.8 %collective-permute-start.7 = (f32[136,512]{1,0:T(8,128)S(1)}, f32[136,512]{1,0:T(8,128)S(1)}, u32[]{:S(2)}, u32[]{:S(2)}) collective-permute-start(f32[136,512]{1,0:T(8,128)S(1)} %get-tuple-element.96), channel_id=1, source_target_pairs={{0,8},{8,0},{16,24},{24,16},{1,9},{9,1},{17,25},{25,17},{2,10},{10... | collective-permute-start | bytes 835592 | tf_op jit(solution)/shard_map/ppermute | solution.py:840
  101.1 22.4 %collective-permute-start.8 = (f32[136,512]{1,0:T(8,128)S(1)}, f32[136,512]{1,0:T(8,128)S(1)}, u32[]{:S(2)}, u32[]{:S(2)}) collective-permute-start(f32[136,512]{1,0:T(8,128)S(1)} %get-tuple-element.95), channel_id=1, source_target_pairs={{0,16},{8,24},{16,0},{24,8},{1,17},{9,25},{17,1},{25,9},{2,18},{10... | collective-permute-start | bytes 835592 | tf_op jit(solution)/shard_map/ppermute | solution.py:840
  103.7 19.8 %collective-permute-start.9 = (f32[136,512]{1,0:T(8,128)S(1)}, f32[136,512]{1,0:T(8,128)S(1)}, u32[]{:S(2)}, u32[]{:S(2)}) collective-permute-start(f32[136,512]{1,0:T(8,128)S(1)} %get-tuple-element.94), channel_id=1, source_target_pairs={{0,24},{8,16},{16,8},{24,0},{1,25},{9,17},{17,9},{25,1},{2,26},{10... | collective-permute-start | bytes 835592 | tf_op jit(solution)/shard_map/ppermute | solution.py:840
  108.8 1.0 copy-start.1
  116.3 21.0 %copy-start.3 = (f32[136,512]{1,0:T(8,128)}, f32[136,512]{1,0:T(8,128)S(1)}, u32[]{:S(2)}) copy-start(f32[136,512]{1,0:T(8,128)S(1)} %collective-permute-done.7.refs_1_) | copy-start | bytes 835588
  123.4 13.8 %copy-start.4 = (f32[136,512]{1,0:T(8,128)}, f32[136,512]{1,0:T(8,128)S(1)}, u32[]{:S(2)}) copy-start(f32[136,512]{1,0:T(8,128)S(1)} %collective-permute-done.8.refs_2_) | copy-start | bytes 835588
  123.4 13.8 %copy-start.5 = (f32[136,512]{1,0:T(8,128)}, f32[136,512]{1,0:T(8,128)S(1)}, u32[]{:S(2)}) copy-start(f32[136,512]{1,0:T(8,128)S(1)} %collective-permute-done.9.refs_3_) | copy-start | bytes 835588
  123.6 11.9 %collective-permute-start.11 = (f32[4,24,512]{2,1,0:T(8,128)S(1)}, f32[4,24,512]{2,1,0:T(8,128)S(1)}, u32[]{:S(2)}, u32[]{:S(2)}) collective-permute-start(f32[4,24,512]{2,1,0:T(8,128)S(1)} %pad_maximum_fusion.1), channel_id=1, source_target_pairs={{1,0},{2,1},{3,2},{4,3},{5,4},{6,5},{7,6},{9,8},{10,9},{11,10},{12... | collective-permute-start | bytes 589832 | tf_op jit(solution)/shard_map/ppermute | solution.py:860
  124.9 21.5 %collective-permute-start.12 = (f32[136,512]{1,0:T(8,128)S(1)}, f32[136,512]{1,0:T(8,128)S(1)}, u32[]{:S(2)}, u32[]{:S(2)}) collective-permute-start(f32[136,512]{1,0:T(8,128)S(1)} %get-tuple-element.68), channel_id=1, source_target_pairs={{0,8},{8,0},{16,24},{24,16},{1,9},{9,1},{17,25},{25,17},{2,10},{10... | collective-permute-start | bytes 835592 | tf_op jit(solution)/shard_map/ppermute | solution.py:840
  130.5 22.4 %collective-permute-start.13 = (f32[136,512]{1,0:T(8,128)S(1)}, f32[136,512]{1,0:T(8,128)S(1)}, u32[]{:S(2)}, u32[]{:S(2)}) collective-permute-start(f32[136,512]{1,0:T(8,128)S(1)} %get-tuple-element.69), channel_id=1, source_target_pairs={{0,16},{8,24},{16,0},{24,8},{1,17},{9,25},{17,1},{25,9},{2,18},{10... | collective-permute-start | bytes 835592 | tf_op jit(solution)/shard_map/ppermute | solution.py:840
  131.6 21.3 %collective-permute-start.14 = (f32[136,512]{1,0:T(8,128)S(1)}, f32[136,512]{1,0:T(8,128)S(1)}, u32[]{:S(2)}, u32[]{:S(2)}) collective-permute-start(f32[136,512]{1,0:T(8,128)S(1)} %get-tuple-element.70), channel_id=1, source_target_pairs={{0,24},{8,16},{16,8},{24,0},{1,25},{9,17},{17,9},{25,1},{2,26},{10... | collective-permute-start | bytes 835592 | tf_op jit(solution)/shard_map/ppermute | solution.py:840
  133.0 3.5 %collective-permute-start.10 = (f32[4,24,512]{2,1,0:T(8,128)S(1)}, f32[4,24,512]{2,1,0:T(8,128)S(1)}, u32[]{:S(2)}, u32[]{:S(2)}) collective-permute-start(f32[4,24,512]{2,1,0:T(8,128)S(1)} %pad_maximum_fusion), channel_id=1, source_target_pairs={{0,1},{1,2},{2,3},{3,4},{4,5},{5,6},{6,7},{8,9},{9,10},{10,11},{11... | collective-permute-start | bytes 589832 | tf_op jit(solution)/shard_map/ppermute | solution.py:859
  146.5 20.5 %copy-start.20 = (f32[3,8,128]{2,1,0:T(8,128)S(1)}, f32[3,8,128]{2,1,0:T(8,128)}, u32[]{:S(2)}) copy-start(f32[3,8,128]{2,1,0:T(8,128)} %get-tuple-element.66) | copy-start | bytes 36868
  146.5 6.4 %copy-start.9 = (f32[136,512]{1,0:T(8,128)}, f32[136,512]{1,0:T(8,128)S(1)}, u32[]{:S(2)}) copy-start(f32[136,512]{1,0:T(8,128)S(1)} %collective-permute-done.12.refs_5_) | copy-start | bytes 835588
  167.7 1.2 collective-permute-start.15
  168.9 3.9 %collective-permute-start.16 = (f32[3,8,128]{2,1,0:T(8,128)S(1)}, f32[3,8,128]{2,1,0:T(8,128)S(1)}, u32[]{:S(2)}, u32[]{:S(2)}) collective-permute-start(f32[3,8,128]{2,1,0:T(8,128)S(1)} %max.25), channel_id=1, source_target_pairs={{0,2},{1,3},{2,0},{3,1},{4,6},{5,7},{6,4},{7,5},{8,10},{9,11},{10,... | collective-permute-start | bytes 36872 | tf_op jit(solution)/shard_map/ppermute | solution.py:125
  171.1 3.7 %collective-permute-start.17 = (f32[3,8,128]{2,1,0:T(8,128)S(1)}, f32[3,8,128]{2,1,0:T(8,128)S(1)}, u32[]{:S(2)}, u32[]{:S(2)}) collective-permute-start(f32[3,8,128]{2,1,0:T(8,128)S(1)} %max.25), channel_id=1, source_target_pairs={{0,4},{1,5},{2,6},{3,7},{4,0},{5,1},{6,2},{7,3},{8,12},{9,13},{10,... | collective-permute-start | bytes 36872 | tf_op jit(solution)/shard_map/ppermute | solution.py:125
  172.6 4.6 %collective-permute-start.18 = (f32[3,8,128]{2,1,0:T(8,128)S(1)}, f32[3,8,128]{2,1,0:T(8,128)S(1)}, u32[]{:S(2)}, u32[]{:S(2)}) collective-permute-start(f32[3,8,128]{2,1,0:T(8,128)S(1)} %max.25), channel_id=1, source_target_pairs={{0,6},{1,7},{2,4},{3,5},{4,2},{5,3},{6,0},{7,1},{8,14},{9,15},{10,... | collective-permute-start | bytes 36872 | tf_op jit(solution)/shard_map/ppermute | solution.py:125
  177.2 7.6 %collective-permute-start.19 = (f32[3,8,128]{2,1,0:T(8,128)S(1)}, f32[3,8,128]{2,1,0:T(8,128)S(1)}, u32[]{:S(2)}, u32[]{:S(2)}) collective-permute-start(f32[3,8,128]{2,1,0:T(8,128)S(1)} %maximum_maximum_fusion.1), channel_id=1, source_target_pairs={{0,8},{8,0},{16,24},{24,16},{1,9},{9,1},{17,25},{25,17},{2,10},{10... | collective-permute-start | bytes 36872 | tf_op jit(solution)/shard_map/ppermute | solution.py:125
  182.3 4.6 %collective-permute-start.20 = (f32[3,8,128]{2,1,0:T(8,128)S(1)}, f32[3,8,128]{2,1,0:T(8,128)S(1)}, u32[]{:S(2)}, u32[]{:S(2)}) collective-permute-start(f32[3,8,128]{2,1,0:T(8,128)S(1)} %maximum_maximum_fusion.1), channel_id=1, source_target_pairs={{0,16},{8,24},{16,0},{24,8},{1,17},{9,25},{17,1},{25,9},{2,18},{10... | collective-permute-start | bytes 36872 | tf_op jit(solution)/shard_map/ppermute | solution.py:125
  183.4 5.5 %collective-permute-start.21 = (f32[3,8,128]{2,1,0:T(8,128)S(1)}, f32[3,8,128]{2,1,0:T(8,128)S(1)}, u32[]{:S(2)}, u32[]{:S(2)}) collective-permute-start(f32[3,8,128]{2,1,0:T(8,128)S(1)} %maximum_maximum_fusion.1), channel_id=1, source_target_pairs={{0,24},{8,16},{16,8},{24,0},{1,25},{9,17},{17,9},{25,1},{2,26},{10... | collective-permute-start | bytes 36872 | tf_op jit(solution)/shard_map/ppermute | solution.py:125
  192.4 9.4 %collective-permute-start.22 = (f32[96,512]{1,0:T(8,128)}, f32[96,512]{1,0:T(8,128)S(1)}, u32[]{:S(2)}, u32[]{:S(2)}) collective-permute-start(f32[96,512]{1,0:T(8,128)} %get-tuple-element.73), channel_id=1, source_target_pairs={{0,8},{8,0},{16,24},{24,16},{1,9},{9,1},{17,25},{25,17},{2,10},{10... | collective-permute-start | bytes 589832 | tf_op jit(solution)/shard_map/ppermute | solution.py:840
  192.6 15.3 %collective-permute-start.23 = (f32[96,512]{1,0:T(8,128)}, f32[96,512]{1,0:T(8,128)S(1)}, u32[]{:S(2)}, u32[]{:S(2)}) collective-permute-start(f32[96,512]{1,0:T(8,128)} %get-tuple-element.74), channel_id=1, source_target_pairs={{0,16},{8,24},{16,0},{24,8},{1,17},{9,25},{17,1},{25,9},{2,18},{10... | collective-permute-start | bytes 589832 | tf_op jit(solution)/shard_map/ppermute | solution.py:840
  194.4 13.5 %collective-permute-start.24 = (f32[96,512]{1,0:T(8,128)}, f32[96,512]{1,0:T(8,128)S(1)}, u32[]{:S(2)}, u32[]{:S(2)}) collective-permute-start(f32[96,512]{1,0:T(8,128)} %get-tuple-element.75), channel_id=1, source_target_pairs={{0,24},{8,16},{16,8},{24,0},{1,25},{9,17},{17,9},{25,1},{2,26},{10... | collective-permute-start | bytes 589832 | tf_op jit(solution)/shard_map/ppermute | solution.py:840
  201.8 34.5 %copy-start.17 = (f32[96,512]{1,0:T(8,128)}, f32[96,512]{1,0:T(8,128)S(1)}, u32[]{:S(2)}) copy-start(f32[96,512]{1,0:T(8,128)S(1)} %collective-permute-done.22.refs_1_) | copy-start | bytes 589828
  207.8 28.4 %copy-start.18 = (f32[96,512]{1,0:T(8,128)}, f32[96,512]{1,0:T(8,128)S(1)}, u32[]{:S(2)}) copy-start(f32[96,512]{1,0:T(8,128)S(1)} %collective-permute-done.23.refs_2_) | copy-start | bytes 589828
  207.8 28.4 %copy-start.19 = (f32[96,512]{1,0:T(8,128)}, f32[96,512]{1,0:T(8,128)S(1)}, u32[]{:S(2)}) copy-start(f32[96,512]{1,0:T(8,128)S(1)} %collective-permute-done.24.refs_3_) | copy-start | bytes 589828
  207.8 14.0 %collective-permute-start.25 = (f32[160,512]{1,0:T(8,128)}, f32[160,512]{1,0:T(8,128)S(1)}, u32[]{:S(2)}, u32[]{:S(2)}) collective-permute-start(f32[160,512]{1,0:T(8,128)} %get-tuple-element.86), channel_id=1, source_target_pairs={{0,8},{8,0},{16,24},{24,16},{1,9},{9,1},{17,25},{25,17},{2,10},{10... | collective-permute-start | bytes 983048 | tf_op jit(solution)/shard_map/ppermute | solution.py:840
  210.7 25.6 %collective-permute-start.26 = (f32[160,512]{1,0:T(8,128)}, f32[160,512]{1,0:T(8,128)S(1)}, u32[]{:S(2)}, u32[]{:S(2)}) collective-permute-start(f32[160,512]{1,0:T(8,128)} %get-tuple-element.87), channel_id=1, source_target_pairs={{0,16},{8,24},{16,0},{24,8},{1,17},{9,25},{17,1},{25,9},{2,18},{10... | collective-permute-start | bytes 983048 | tf_op jit(solution)/shard_map/ppermute | solution.py:840
  210.7 25.6 %collective-permute-start.27 = (f32[160,512]{1,0:T(8,128)}, f32[160,512]{1,0:T(8,128)S(1)}, u32[]{:S(2)}, u32[]{:S(2)}) collective-permute-start(f32[160,512]{1,0:T(8,128)} %get-tuple-element.88), channel_id=1, source_target_pairs={{0,24},{8,16},{16,8},{24,0},{1,25},{9,17},{17,9},{25,1},{2,26},{10... | collective-permute-start | bytes 983048 | tf_op jit(solution)/shard_map/ppermute | solution.py:840
  221.8 14.5 %copy-start.6 = (f32[160,512]{1,0:T(8,128)}, f32[160,512]{1,0:T(8,128)S(1)}, u32[]{:S(2)}) copy-start(f32[160,512]{1,0:T(8,128)S(1)} %collective-permute-done.25.refs_5_) | copy-start | bytes 983044
  236.3 0.9 copy-start.8
  (3 other events, 2.2 us)

commit v4 on v3

--- a/solution.py
+++ b/solution.py
@@ -16,7 +16,7 @@
 inner_length = 128
 highest = lax.Precision.HIGHEST
 lane_count = 128
-vmem_bytes = 56 * 1024 * 1024
+mebibyte = 1024 * 1024
 rim = 16
 halo_rows = 16
 unroll = 2
@@ -364,7 +364,7 @@
         body,
         out_shape=out_shapes,
         scratch_shapes=scratch,
-        compiler_params=pltpu.CompilerParams(vmem_limit_bytes=vmem_bytes),
+        compiler_params=pltpu.CompilerParams(vmem_limit_bytes=24 * mebibyte),
         name=name,
         cost_estimate=busy(microseconds),
     )
@@ -397,11 +397,10 @@
             out_ref[1, spread, :] = done[start : start + 8, lanes:]
 
 
-def row_inverse_body(
-    steps, in_ref, table_ref, est_ref, dirty_ref, old_ref, res_ref, half_ref, held
-):
-    del old_ref
-    groups, _, chunk, lanes = in_ref.shape
+def row_inverse_body(steps, groups, me_ref, *refs):
+    in_refs = refs[:groups]
+    table_ref, est_ref, dirty_ref, _, res_ref, half_ref, held = refs[groups:]
+    _, chunk, lanes = in_refs[0].shape
     parts, _, wide = half_ref.shape
     each = chunk // steps
     block = est_ref.shape[0]
@@ -409,16 +408,12 @@
 
     @pl.when(turn == 0)
     def _():
-        for group in range(groups):
+        for partner, in_ref in enumerate(in_refs):
+            group = me_ref[0] ^ partner
             halves = []
             for part in range(2):
                 pieces = [
-                    in_ref[
-                        group,
-                        part,
-                        pl.ds(start % steps * each + start // steps, 8, stride=each),
-                        :,
-                    ]
+                    in_ref[part, pl.ds(start % steps * each + start // steps, 8, stride=each), :]
                     for start in range(0, chunk, 8)
                 ]
                 halves.append(jnp.concatenate(pieces, axis=0))
@@ -465,7 +460,7 @@
                 half_ref[part, pl.ds(chunk, 8), where] = done
 
 
-def starlet_body(chans, spans, fills, ends_ref, *refs):
+def starlet_body(chans, spans, fills, ends_ref, before_ref, *refs):
     sources, (detail_ref, peak_ref, ping, pong) = refs[:-4], refs[-4:]
     part = detail_ref.shape[3]
     lanes = lane_count
@@ -535,8 +530,8 @@
                 step(blocks - 1 - i, None)
             peaks[level] = lax.fori_loop(skirt, blocks - skirt, step, peaks[level], unroll=unroll)
     for level in range(3):
-        most = peaks[level][:, :lanes]
-        for t in range(1, tiles):
+        most = before_ref[level]
+        for t in range(tiles):
             most = jnp.maximum(most, peaks[level][:, t * lanes : (t + 1) * lanes])
         peak_ref[level] = most
 
@@ -582,7 +577,7 @@
 def column_body(steps, count, me_ref, *refs):
     in_refs = refs[:count]
     there_ref, back_ref, turn_ref, weight_ref, mirror_ref, flip_ref = refs[count : count + 6]
-    edge_ref, core_ref, gathered, held, made = refs[count + 6 :]
+    out_refs, (gathered, held, made, ready) = refs[count + 6 : 3 * count + 6], refs[3 * count + 6 :]
     _, height, lanes = in_refs[0].shape
     each = height // steps
     size = each * count
@@ -653,13 +648,15 @@
         high, low = split(jnp.concatenate(block, axis=0))
         done = dot(back_ref[0], high) + dot(back_ref[1], high) + dot(back_ref[0], low)
         for k in range(2):
-            rows = pl.ds((step + k) * half, half)
-            columns = slice(k * lanes, (k + 1) * lanes)
-            for part in range(2):
-                for target in range(count):
-                    start = part * size + target * each
-                    edge_ref[target, part, rows, :] = done[start : start + half, columns]
-                    core_ref[target, part, rows, :] = done[start + half : start + each, columns]
+            ready[step + k] = done[:, k * lanes : (k + 1) * lanes]
+    for turn in range(count):
+        target = me_ref[0] ^ turn
+        for part in range(2):
+            for inner in range(2):
+                start = pl.multiple_of(part * size + target * each + inner * half, 8)
+                for step in range(steps):
+                    rows = pl.ds(step * half, half)
+                    out_refs[inner * count + turn][part, rows, :] = ready[step, pl.ds(start, half), :]
 
 
 def weight_pick_body(w_ref, pick_ref, out_ref):
@@ -760,7 +757,7 @@
         ],
         out_specs=pl.BlockSpec((count, thick, lanes), lambda i: (0, i, 0)),
         out_shape=shape(count, depth, lanes),
-        compiler_params=pltpu.CompilerParams(vmem_limit_bytes=vmem_bytes),
+        compiler_params=pltpu.CompilerParams(vmem_limit_bytes=56 * mebibyte),
         name="weight_pick",
         cost_estimate=busy(4),
     )(weights.reshape(packs, depth, width), pick)
@@ -771,14 +768,18 @@
         out_specs=[vmem] * count,
         out_shape=[shape(2, height, lanes)] * count,
         scratch_shapes=[pltpu.VMEM((2, count, height, 2 * lanes), jnp.bfloat16)],
-        compiler_params=pltpu.CompilerParams(vmem_limit_bytes=vmem_bytes),
+        compiler_params=pltpu.CompilerParams(vmem_limit_bytes=56 * mebibyte),
         name="row_forward",
         cost_estimate=busy(6),
     )(me, values, there)
-    ahead = [ahead[0]] + [
-        lax.ppermute(ahead[turn], "rows", [(i, i ^ turn) for i in range(count)])
-        for turn in range(1, count)
-    ]
+
+    def over_rows(pieces):
+        return [pieces[0]] + [
+            lax.ppermute(pieces[turn], "rows", [(i, i ^ turn) for i in range(count)])
+            for turn in range(1, count)
+        ]
+
+    ahead = over_rows(ahead)
     mine = jnp.where(lax.axis_index("rows") == 0, place[0], place[1])
     weight, mirror = whole_call(
         weight_place_body,
@@ -787,22 +788,23 @@
         "weight_place",
         10,
     )(sent, mine, flip)
-    edge, core = pl.pallas_call(
+    behind = pl.pallas_call(
         functools.partial(column_body, steps, count),
         in_specs=[smem] + [vmem] * (count + 6),
-        out_specs=[vmem] * 2,
-        out_shape=[shape(count, 2, half, lanes)] * 2,
+        out_specs=[vmem] * (2 * count),
+        out_shape=[shape(2, half, lanes)] * (2 * count),
         scratch_shapes=[
             pltpu.VMEM((2 * size, steps * lanes), f32),
             pltpu.VMEM((2, steps, size, lanes), f32),
             pltpu.VMEM((2, steps, size, lanes), f32),
+            pltpu.VMEM((steps, 2 * size, lanes), f32),
         ],
-        compiler_params=pltpu.CompilerParams(vmem_limit_bytes=vmem_bytes),
+        compiler_params=pltpu.CompilerParams(vmem_limit_bytes=24 * mebibyte),
         name="column_filter",
         cost_estimate=busy(10),
     )(me, *ahead, down, up, turns, weight, mirror, flip)
-    edge = lax.all_to_all(edge, "rows", 0, 0, tiled=True)
-    core = lax.all_to_all(core, "rows", 0, 0, tiled=True)
+    edge, core = over_rows(behind[:count]), behind[count:]
+    core = over_rows(core)
     chans = lax.axis_size("chan")
     part = length // chans
     quarter = height // 4
@@ -811,10 +813,11 @@
         rows_spec = pl.BlockSpec((quarter, length), lambda i: (blocks[0] + i * blocks[1], 0))
         whole = lambda *dims: pl.BlockSpec(dims, lambda i: (0,) * len(dims))
         return pl.pallas_call(
-            functools.partial(row_inverse_body, steps),
+            functools.partial(row_inverse_body, steps, count),
             grid=(2,),
-            in_specs=[
-                whole(*cells.shape),
+            in_specs=[smem]
+            + [whole(2, half, lanes)] * count
+            + [
                 whole(*back.shape),
                 rows_spec,
                 rows_spec,
@@ -823,11 +826,11 @@
             out_specs=[rows_spec, whole(chans, half + 8, part)],
             out_shape=[shape(height, length), shape(chans, half + 8, part)],
             scratch_shapes=[pltpu.VMEM((count, half, 2 * lanes), f32)],
-            input_output_aliases={4: 0} if old is not dirty else {},
-            compiler_params=pltpu.CompilerParams(vmem_limit_bytes=vmem_bytes),
+            input_output_aliases={count + 4: 0} if old is not dirty else {},
+            compiler_params=pltpu.CompilerParams(vmem_limit_bytes=56 * mebibyte),
             name="row_inverse",
         cost_estimate=busy(5),
-        )(cells, back, values, dirty, old)
+        )(me, *cells, back, values, dirty, old)
 
     def pieces_for(cells):
         me = lax.axis_index("chan")
@@ -848,8 +851,8 @@
     residual, outer = row_inverse(edge, dirty, (0, 3))
     outer = over_chans(pieces_for(outer))
     residual, inner = row_inverse(core, residual, (1, 1))
-    outer, inner = in_order(outer, pieces_for(inner))
-    inner = over_chans(inner)
+    inner = over_chans(pieces_for(inner))
+    outer, (inner[1],) = in_order(outer, [inner[1]])
     ahead_pairs = [(i, i + 1) for i in range(count - 1)]
     back_pairs = [(i + 1, i) for i in range(count - 1)]
     last = jnp.stack([cells[half - halo_rows :] for cells in outer])
@@ -864,27 +867,27 @@
     at_end = jnp.stack(
         [chan_id == 0, chan_id == chans - 1, row_id == 0, row_id == count - 1]
     ).astype(jnp.int32)
-    vmem = pl.BlockSpec(memory_space=pltpu.VMEM)
-
-    def starlet(sources, rows, spans, fills, microseconds):
+
+    def starlet(sources, before, rows, spans, fills, microseconds):
         extent = max(fill[0] + fill[3] for fill in fills) + 16
         cells = pltpu.VMEM((chans, extent, part + lanes), f32)
         return pl.pallas_call(
             functools.partial(starlet_body, chans, spans, fills),
-            in_specs=[pl.BlockSpec(memory_space=pltpu.SMEM)] + [vmem] * len(sources),
+            in_specs=[smem] + [vmem] * (1 + len(sources)),
             out_specs=[vmem] * 2,
             out_shape=[shape(chans, 4, rows, part), shape(3, 8, lanes)],
             scratch_shapes=[cells, cells],
-            compiler_params=pltpu.CompilerParams(vmem_limit_bytes=vmem_bytes),
+            compiler_params=pltpu.CompilerParams(vmem_limit_bytes=20 * mebibyte),
             name="starlet",
             cost_estimate=busy(microseconds),
-        )(at_end, *sources)
+        )(at_end, before, *sources)
 
     reach = quarter + halo_rows
     most = quarter - halo_rows
     skirt = halo_rows // 8
     outer_details, outer_peaks = starlet(
         outer + above + below,
+        jnp.zeros((3, 8, lanes), f32),
         2 * most,
         (
             (0, reach // 8, 0, True, False),
@@ -898,8 +901,9 @@
         ),
         12,
     )
-    inner_details, inner_peaks = starlet(
+    inner_details, peaks = starlet(
         outer + inner,
+        outer_peaks,
         half + 2 * halo_rows,
         ((0, half // 8 + 4 * skirt, 0, False, False),),
         (
@@ -909,7 +913,6 @@
         ),
         12,
     )
-    peaks = jnp.maximum(outer_peaks, inner_peaks)
     peaks = max_over(peaks, "rows", range(1, 2))
     peaks = max_over(peaks, "rows", range(2, count, 2))
     peaks = max_over(peaks, "chan", range(1, chans))
@@ -926,7 +929,7 @@
             ],
             out_specs=[pl.BlockSpec((thick, part), lambda i: (i, 0))] * chans,
             out_shape=[shape(rows, part)] * chans,
-            compiler_params=pltpu.CompilerParams(vmem_limit_bytes=vmem_bytes),
+            compiler_params=pltpu.CompilerParams(vmem_limit_bytes=14 * mebibyte),
             name="shrink",
             cost_estimate=busy(3),
         )(details, peaks)
@@ -939,7 +942,7 @@
         in_specs=[pl.BlockSpec(memory_space=pltpu.SMEM)] + [vmem] * (2 * chans),
         out_specs=vmem,
         out_shape=shape(height, length),
-        compiler_params=pltpu.CompilerParams(vmem_limit_bytes=vmem_bytes),
+        compiler_params=pltpu.CompilerParams(vmem_limit_bytes=12 * mebibyte),
         name="join",
         cost_estimate=busy(4),
     )(jnp.reshape(chan_id, (1,)).astype(jnp.int32), *outer, *inner)

time: 242 us -> 222 us (0.917)
  blocking collectives: 19.6 us -> 0 us
  Pallas kernels: 72 us -> 57.2 us
  waiting for transfers between devices: 79.9 us -> 91.8 us
  starting transfers between devices: 53 us -> 62.1 us
  local copies, waits for them, and re-layouts: 9.34 us -> 5.37 us
  other arithmetic: 5.33 us -> 2.07 us
    all_to_all x1 -> x0, blocking collectives: 19.6 us -> none  [filtered(): edge = lax.all_to_all(edge, 'rows', 0, 0, tiled=True)]
    ppermute x7 -> x21, waiting for transfers between devices: 21.5 us -> 34.8 us  [over_rows(): lax.ppermute(pieces[turn], 'rows', [(i, i ^ turn) for i in range(count)])]
    ppermute x7 -> x21, starting transfers between devices: 6.81 us -> 18.6 us  [over_rows(): lax.ppermute(pieces[turn], 'rows', [(i, i ^ turn) for i in range(count)])]
    pallas_call x2, Pallas kernels: 21.9 us -> 16.1 us  [starlet(): pl.pallas_call(functools.partial(starlet_body, chans, spans, fills), in_s...]
    ppermute x12, starting transfers between devices: 22.1 us -> 27.4 us  [over_chans(): lax.ppermute(pieces[turn], 'chan', [(i, i ^ turn) for i in range(chans)])]
    all_to_all x1 -> x0, waiting for transfers between devices: 4.26 us -> none  [filtered(): core = lax.all_to_all(core, 'rows', 0, 0, tiled=True)]
    pallas_call x2, Pallas kernels: 6.74 us -> 2.58 us  [shrink(): pl.pallas_call(functools.partial(shrink_body, chans), grid=(2,), in_specs...]
    all_to_all x1 -> x0, starting transfers between devices: 3.74 us -> none  [filtered(): core = lax.all_to_all(core, 'rows', 0, 0, tiled=True)]
  transfers between devices with their start and end apart: 30 -> 43, of which waited for: 16 -> 21; matrix products, arithmetic and copies ran while one was open for 4% -> 2% of each run, Pallas kernels for 16% -> 14%
where the time goes in v4:
time: 222 us; the launch traced here: 220 us
  waiting for transfers between devices  91.8 us (41%)
  starting transfers between devices  62.1 us (28%)
  Pallas kernels  57.2 us (26%)
  local copies, waits for them, and re-layouts  5.37 us (2%)
    ppermute x12, waiting for transfers between devices, over_chans(): lax.ppermute(pieces[turn], 'chan', [(i, i ^ turn) for i in range(chans)])  46.8 us
    ppermute x21, waiting for transfers between devices, over_rows(): lax.ppermute(pieces[turn], 'rows', [(i, i ^ turn) for i in range(count)])  34.8 us
    ppermute x12, starting transfers between devices, over_chans(): lax.ppermute(pieces[turn], 'chan', [(i, i ^ turn) for i in range(chans)])  27.4 us
    ppermute x21, starting transfers between devices, over_rows(): lax.ppermute(pieces[turn], 'rows', [(i, i ^ turn) for i in range(count)])  18.6 us
    pallas_call x2, Pallas kernels, starlet(): pl.pallas_call(functools.partial(starlet_body, chans, spans, fills), in_s...  16.1 us
    pallas_call x1, Pallas kernels, filtered(): pl.pallas_call(functools.partial(column_body, steps, count), in_specs=[sm...  9.27 us
    pallas_call x2, Pallas kernels, row_inverse(): pl.pallas_call(functools.partial(row_inverse_body, steps, count), grid=(2...  9.19 us
    pallas_call x1, Pallas kernels, filtered(): whole_call(weight_place_body, [shape(steps, size, lanes), shape(size, lan...  8.69 us
  transfers between devices with their start and end apart: 43, of which 21 were waited for; matrix products, arithmetic and copies ran while one was open for 2% of the time, Pallas kernels for 14%

profile of v4, /device:TPU:0, one launch (start us, length us, event | category | flops | bytes accessed | tf_op | source)
XLA Modules:
  0.0 219.6 jit_solution(14338985929484858136)
XLA Ops:
  0.6 4.5 %weight_pick.1 = f32[8,512,128]{2,1,0:T(8,128)} custom-call(f32[4,512,256]{2,1,0:T(8,128)} %bitcast.68, bf16[256,256]{1,0:T(8,128)(2,1)} %constant.55.clone.pick_ref), custom_call_target="tpu_custom_call" | custom-call | bytes 14000000 | tf_op jit(solution)/shard_map/weight_pick/pallas_call | solution.py:751
  5.1 5.2 %all-to-all-start = ((f32[8,512,128]{2,1,0:T(8,128)}), f32[8,512,128]{2,1,0:T(8,128)}, u32[]{:S(2)}, u32[]{:S(2)}) async-start(f32[8,512,128]{2,1,0:T(8,128)} %weight_pick.1), calls=%async_computation | async-start | bytes 4194304 | tf_op jit(solution)/shard_map/all_to_all | solution.py:764
  10.3 5.4 %row_forward.1 = (f32[2,256,128]{2,1,0:T(8,128)}, f32[2,256,128]{2,1,0:T(8,128)}, f32[2,256,128]{2,1,0:T(8,128)}, f32[2,256,128]{2,1,0:T(8,128)}, f32[2,256,128]...) custom-call(s32[1]{0:T(128)} %bitcast.5.me_ref, f32[256,2048]{1,0:T(8,128)} %bitcast.64, ...), custom_call_target="tpu_custom_call" | custom-call | bytes 21000000 | tf_op jit(solution)/shard_map/row_forward/pallas_call | solution.py:765
  16.2 1.7 collective-permute-start.1
  17.9 1.7 collective-permute-start.3
  19.7 2.5 %collective-permute-start.5 = (f32[2,256,128]{2,1,0:T(8,128)}, f32[2,256,128]{2,1,0:T(8,128)}, u32[]{:S(2)}, u32[]{:S(2)}) collective-permute-start(f32[2,256,128]{2,1,0:T(8,128)} %get-tuple-element.63), channel_id=1, source_target_pairs={{0,6},{1,7},{2,4},{3,5},{4,2},{5,3},{6,0},{7,1},{8,14},{9,15},{10,... | collective-permute-start | bytes 786440 | tf_op jit(solution)/shard_map/ppermute | solution.py:778
  22.3 19.9 %collective-permute-done.1.refs_2_ = f32[2,256,128]{2,1,0:T(8,128)S(1)} collective-permute-done((f32[2,256,128]{2,1,0:T(8,128)}, f32[2,256,128]{2,1,0:T(8,128)S(1)}, u32[]{:S(2)}, u32[]{:S(2)}) %collective-permute-start.1) | collective-permute-done | bytes 262176 | tf_op jit(solution)/shard_map/ppermute | solution.py:778
  43.2 1.9 select_bitcast_fusion.place_ref
  45.2 8.7 %weight_place.1 = (f32[16,128,128]{2,1,0:T(8,128)S(1)}, f32[128,128]{1,0:T(8,128)S(1)}) custom-call(f32[8,512,128]{2,1,0:T(8,128)} %all-to-all-done.in_ref, bf16[1024,1152]{1,0:T(8,128)(2,1)S(1)} %select_bitcast_fusion.place_ref, bf16[128,128]{1,0:T(8,128)(2,1)S(1)} %copy-done.7), custom_call_target="tpu_custom_call" | custom-call | bytes 35000000 | tf_op jit(solution)/shard_map/weight_place/pallas_call | solution.py:784
  54.5 4.5 %collective-permute-done.6.refs_7_ = f32[2,256,128]{2,1,0:T(8,128)} collective-permute-done((f32[2,256,128]{2,1,0:T(8,128)}, f32[2,256,128]{2,1,0:T(8,128)}, u32[]{:S(2)}, u32[]{:S(2)}) %collective-permute-start.6) | collective-permute-done | bytes 262176 | tf_op jit(solution)/shard_map/ppermute | solution.py:778
  59.0 9.3 %column_filter.1 = (f32[2,128,128]{2,1,0:T(8,128)S(1)}, f32[2,128,128]{2,1,0:T(8,128)S(1)}, f32[2,128,128]{2,1,0:T(8,128)S(1)}, f32[2,128,128]{2,1,0:T(8,128)S(1...) custom-call(s32[1]{0:T(128)} %bitcast.5.me_ref, ...), custom_call_target="tpu_custom_call" | custom-call | bytes 35000000 | tf_op jit(solution)/shard_map/column_filter/pallas_call | solution.py:791
  72.1 1.4 collective-permute-start.11
  74.0 2.3 %collective-permute-done.8.refs_2_ = f32[2,128,128]{2,1,0:T(8,128)S(1)} collective-permute-done((f32[2,128,128]{2,1,0:T(8,128)S(1)}, f32[2,128,128]{2,1,0:T(8,128)S(1)}, u32[]{:S(2)}, u32[]{:S(2)}) %collective-permute-start.8) | collective-permute-done | bytes 131104 | tf_op jit(solution)/shard_map/ppermute | solution.py:778
  76.3 1.2 collective-permute-done.9.refs_3_
  77.6 1.7 collective-permute-start.17
  79.8 5.8 %collective-permute-done.11.refs_5_ = f32[2,128,128]{2,1,0:T(8,128)S(1)} collective-permute-done((f32[2,128,128]{2,1,0:T(8,128)S(1)}, f32[2,128,128]{2,1,0:T(8,128)S(1)}, u32[]{:S(2)}, u32[]{:S(2)}) %collective-permute-start.11) | collective-permute-done | bytes 131104 | tf_op jit(solution)/shard_map/ppermute | solution.py:778
  87.7 4.7 %row_inverse.2 = (f32[256,2048]{1,0:T(8,128)}, f32[4,136,512]{2,1,0:T(8,128)}) custom-call(s32[1]{0:T(128)} %bitcast.5.me_ref, f32[2,128,128]{2,1,0:T(8,128)} %copy-done.6, f32[2,128,128]{2,1,0:T(8,128)} %copy-done.11, f32[2,128,128]{2,1,0:T(8,128)} %copy-done.12, f32[2,128,128]{2,1,0:T(8,128)} %copy-done.13, f32[2,128,128]{2,1,0:T(8,128)} %copy-done.14, ...), custom_call_target="tpu_custom_call" | custom-call | bytes 17500000 | tf_op jit(solution)/shard_map/row_inverse/pallas_call | solution.py:815
  92.4 1.9 collective-permute-start.22
  95.5 1.3 dynamic-slice_bitcast_fusion.4
  96.8 4.2 %collective-permute-start.16 = (f32[136,512]{1,0:T(8,128)S(1)}, f32[136,512]{1,0:T(8,128)S(1)}, u32[]{:S(2)}, u32[]{:S(2)}) collective-permute-start(f32[136,512]{1,0:T(8,128)S(1)} %get-tuple-element.116), channel_id=1, source_target_pairs={{0,24},{8,16},{16,8},{24,0},{1,25},{9,17},{17,9},{25,1},{2,26},{10... | collective-permute-start | bytes 835592 | tf_op jit(solution)/shard_map/ppermute | solution.py:843
  102.7 4.5 %row_inverse.3 = (f32[256,2048]{1,0:T(8,128)}, f32[4,136,512]{2,1,0:T(8,128)}) custom-call(s32[1]{0:T(128)} %bitcast.5.me_ref, f32[2,128,128]{2,1,0:T(8,128)} %copy-done.5, f32[2,128,128]{2,1,0:T(8,128)} %copy-done.9, f32[2,128,128]{2,1,0:T(8,128)} %copy-done.10, f32[2,128,128]{2,1,0:T(8,128)} %copy-done.17, ...), custom_call_target="tpu_custom_call", output_to_operand_aliasing={{0}: (12, {})} | custom-call | bytes 17500000 | tf_op jit(solution)/shard_map/row_inverse/pallas_call | solution.py:815
  107.2 1.3 dynamic-slice_bitcast_fusion
  108.5 2.2 collective-permute-start.24
  110.8 2.5 %collective-permute-start.28 = (f32[136,512]{1,0:T(8,128)S(1)}, f32[136,512]{1,0:T(8,128)S(1)}, u32[]{:S(2)}, u32[]{:S(2)}) collective-permute-start(f32[136,512]{1,0:T(8,128)S(1)} %get-tuple-element.112), channel_id=1, source_target_pairs={{0,24},{8,16},{16,8},{24,0},{1,25},{9,17},{17,9},{25,1},{2,26},{10... | collective-permute-start | bytes 835592 | tf_op jit(solution)/shard_map/ppermute | solution.py:843
  113.3 8.2 %collective-permute-start.27 = (f32[136,512]{1,0:T(8,128)S(1)}, f32[136,512]{1,0:T(8,128)S(1)}, u32[]{:S(2)}, u32[]{:S(2)}) collective-permute-start(f32[136,512]{1,0:T(8,128)S(1)} %get-tuple-element.113), channel_id=1, source_target_pairs={{0,16},{8,24},{16,0},{24,8},{1,17},{9,25},{17,1},{25,9},{2,18},{10... | collective-permute-start | bytes 835592 | tf_op jit(solution)/shard_map/ppermute | solution.py:843
  121.5 4.9 %collective-permute-done.15.refs_2_ = f32[136,512]{1,0:T(8,128)S(1)} collective-permute-done((f32[136,512]{1,0:T(8,128)S(1)}, f32[136,512]{1,0:T(8,128)S(1)}, u32[]{:S(2)}, u32[]{:S(2)}) %collective-permute-start.15) | collective-permute-done | bytes 278560 | tf_op jit(solution)/shard_map/ppermute | solution.py:843
  126.6 1.7 collective-permute-start.25
  128.4 1.3 collective-permute-start.26
  129.7 3.3 %collective-permute-done.26 = f32[4,24,512]{2,1,0:T(8,128)S(1)} collective-permute-done((f32[4,24,512]{2,1,0:T(8,128)S(1)}, f32[4,24,512]{2,1,0:T(8,128)S(1)}, u32[]{:S(2)}, u32[]{:S(2)}) %collective-permute-start.26) | collective-permute-done | bytes 196640 | tf_op jit(solution)/shard_map/ppermute | solution.py:863
  133.0 6.8 %starlet.2 = (f32[4,4,96,512]{3,2,1,0:T(8,128)S(1)}, f32[3,8,128]{2,1,0:T(8,128)S(1)}) custom-call(s32[4]{0:T(128)S(1)} %add_convert_fusion.ends_ref, f32[3,8,128]{2,1,0:T(8,128)S(1)} %broadcast_in_dim.9.before_ref, f32[136,512]{1,0:T(8,128)S(1)} %get-tuple-element.86.refs_0_, f32[136,512]{1,0:T(8,128)S(1)} %collective-permute-done.14.refs_1_, ...), custom_call_target="tpu_custom_call" | custom-call | bytes 42000000 | tf_op jit(solution)/shard_map/starlet/pallas_call | solution.py:874
  139.9 9.0 %collective-permute-done.27.refs_6_ = f32[136,512]{1,0:T(8,128)S(1)} collective-permute-done((f32[136,512]{1,0:T(8,128)S(1)}, f32[136,512]{1,0:T(8,128)S(1)}, u32[]{:S(2)}, u32[]{:S(2)}) %collective-permute-start.27) | collective-permute-done | bytes 278560 | tf_op jit(solution)/shard_map/ppermute | solution.py:843
  148.9 9.3 %starlet.3 = (f32[4,4,160,512]{3,2,1,0:T(8,128)S(1)}, f32[3,8,128]{2,1,0:T(8,128)S(1)}) custom-call(s32[4]{0:T(128)S(1)} %add_convert_fusion.ends_ref, f32[3,8,128]{2,1,0:T(8,128)S(1)} %get-tuple-element.91.before_ref, f32[136,512]{1,0:T(8,128)S(1)} %get-tuple-element.86.refs_0_, f32[136,512]{1,0:T(8,128)S(1)} %collective-permute-done.14.refs_1_, ...), custom_call_target="tpu_custom_call" | custom-call | bytes 42000000 | tf_op jit(solution)/shard_map/starlet/pallas_call | solution.py:874
  158.2 1.2 collective-permute-done.29
  159.4 1.9 collective-permute-start.32
  162.9 1.2 collective-permute-done.32
  166.1 2.5 %collective-permute-start.35 = (f32[3,8,128]{2,1,0:T(8,128)S(1)}, f32[3,8,128]{2,1,0:T(8,128)S(1)}, u32[]{:S(2)}, u32[]{:S(2)}) collective-permute-start(f32[3,8,128]{2,1,0:T(8,128)S(1)} %maximum_maximum_fusion.1), channel_id=1, source_target_pairs={{0,24},{8,16},{16,8},{24,0},{1,25},{9,17},{17,9},{25,1},{2,26},{10... | collective-permute-start | bytes 36872 | tf_op jit(solution)/shard_map/ppermute | solution.py:125
  168.5 1.9 collective-permute-start.33
  170.4 1.2 collective-permute-done.35
  171.7 1.5 collective-permute-done.34
  176.2 2.3 %collective-permute-start.38 = (f32[96,512]{1,0:T(8,128)S(1)}, f32[96,512]{1,0:T(8,128)S(1)}, u32[]{:S(2)}, u32[]{:S(2)}) collective-permute-start(f32[96,512]{1,0:T(8,128)S(1)} %get-tuple-element.97), channel_id=1, source_target_pairs={{0,24},{8,16},{16,8},{24,0},{1,25},{9,17},{17,9},{25,1},{2,26},{10... | collective-permute-start | bytes 589832 | tf_op jit(solution)/shard_map/ppermute | solution.py:843
  178.5 1.6 shrink.3
  180.2 1.7 collective-permute-done.36.refs_1_
  181.9 8.0 %collective-permute-done.37.refs_2_ = f32[96,512]{1,0:T(8,128)S(1)} collective-permute-done((f32[96,512]{1,0:T(8,128)S(1)}, f32[96,512]{1,0:T(8,128)S(1)}, u32[]{:S(2)}, u32[]{:S(2)}) %collective-permute-start.37) | collective-permute-done | bytes 196640 | tf_op jit(solution)/shard_map/ppermute | solution.py:843
  189.9 2.7 %collective-permute-start.39 = (f32[160,512]{1,0:T(8,128)S(1)}, f32[160,512]{1,0:T(8,128)S(1)}, u32[]{:S(2)}, u32[]{:S(2)}) collective-permute-start(f32[160,512]{1,0:T(8,128)S(1)} %get-tuple-element.108), channel_id=1, source_target_pairs={{0,8},{8,0},{16,24},{24,16},{1,9},{9,1},{17,25},{25,17},{2,10},{10... | collective-permute-start | bytes 983048 | tf_op jit(solution)/shard_map/ppermute | solution.py:843
  193.7 1.5 collective-permute-start.41
  195.2 8.7 %collective-permute-done.39.refs_5_ = f32[160,512]{1,0:T(8,128)S(1)} collective-permute-done((f32[160,512]{1,0:T(8,128)S(1)}, f32[160,512]{1,0:T(8,128)S(1)}, u32[]{:S(2)}, u32[]{:S(2)}) %collective-permute-start.39) | collective-permute-done | bytes 327712 | tf_op jit(solution)/shard_map/ppermute | solution.py:843
  203.9 14.3 %collective-permute-done.40.refs_6_ = f32[160,512]{1,0:T(8,128)S(1)} collective-permute-done((f32[160,512]{1,0:T(8,128)S(1)}, f32[160,512]{1,0:T(8,128)S(1)}, u32[]{:S(2)}, u32[]{:S(2)}) %collective-permute-start.40) | collective-permute-done | bytes 327712 | tf_op jit(solution)/shard_map/ppermute | solution.py:843
  218.2 1.5 join.1
  (119 shorter events, 20.1 us)
Async XLA Ops:
  5.1 40.1 %all-to-all-start = ((f32[8,512,128]{2,1,0:T(8,128)}), f32[8,512,128]{2,1,0:T(8,128)}, u32[]{:S(2)}, u32[]{:S(2)}) async-start(f32[8,512,128]{2,1,0:T(8,128)} %weight_pick.1), calls=%async_computation | async-start | bytes 4194304 | tf_op jit(solution)/shard_map/all_to_all | solution.py:764
  15.7 4.0 %collective-permute-start = (f32[2,256,128]{2,1,0:T(8,128)}, f32[2,256,128]{2,1,0:T(8,128)S(1)}, u32[]{:S(2)}, u32[]{:S(2)}) collective-permute-start(f32[2,256,128]{2,1,0:T(8,128)} %get-tuple-element.58), channel_id=1, source_target_pairs={{0,1},{1,0},{2,3},{3,2},{4,5},{5,4},{6,7},{7,6},{8,9},{9,8},{10,11... | collective-permute-start | bytes 786440 | tf_op jit(solution)/shard_map/ppermute | solution.py:778
  16.2 26.0 %collective-permute-start.1 = (f32[2,256,128]{2,1,0:T(8,128)}, f32[2,256,128]{2,1,0:T(8,128)S(1)}, u32[]{:S(2)}, u32[]{:S(2)}) collective-permute-start(f32[2,256,128]{2,1,0:T(8,128)} %get-tuple-element.59), channel_id=1, source_target_pairs={{0,2},{1,3},{2,0},{3,1},{4,6},{5,7},{6,4},{7,5},{8,10},{9,11},{10,... | collective-permute-start | bytes 786440 | tf_op jit(solution)/shard_map/ppermute | solution.py:778
  17.9 36.0 %collective-permute-start.2 = (f32[2,256,128]{2,1,0:T(8,128)}, f32[2,256,128]{2,1,0:T(8,128)}, u32[]{:S(2)}, u32[]{:S(2)}) collective-permute-start(f32[2,256,128]{2,1,0:T(8,128)} %get-tuple-element.60), channel_id=1, source_target_pairs={{0,3},{1,2},{2,1},{3,0},{4,7},{5,6},{6,5},{7,4},{8,11},{9,10},{10,... | collective-permute-start | bytes 786440 | tf_op jit(solution)/shard_map/ppermute | solution.py:778
  17.9 36.0 %collective-permute-start.3 = (f32[2,256,128]{2,1,0:T(8,128)}, f32[2,256,128]{2,1,0:T(8,128)}, u32[]{:S(2)}, u32[]{:S(2)}) collective-permute-start(f32[2,256,128]{2,1,0:T(8,128)} %get-tuple-element.61), channel_id=1, source_target_pairs={{0,4},{1,5},{2,6},{3,7},{4,0},{5,1},{6,2},{7,3},{8,12},{9,13},{10,... | collective-permute-start | bytes 786440 | tf_op jit(solution)/shard_map/ppermute | solution.py:778
  19.7 34.3 %collective-permute-start.4 = (f32[2,256,128]{2,1,0:T(8,128)}, f32[2,256,128]{2,1,0:T(8,128)}, u32[]{:S(2)}, u32[]{:S(2)}) collective-permute-start(f32[2,256,128]{2,1,0:T(8,128)} %get-tuple-element.62), channel_id=1, source_target_pairs={{0,5},{1,4},{2,7},{3,6},{4,1},{5,0},{6,3},{7,2},{8,13},{9,12},{10,... | collective-permute-start | bytes 786440 | tf_op jit(solution)/shard_map/ppermute | solution.py:778
  19.7 34.7 %collective-permute-start.5 = (f32[2,256,128]{2,1,0:T(8,128)}, f32[2,256,128]{2,1,0:T(8,128)}, u32[]{:S(2)}, u32[]{:S(2)}) collective-permute-start(f32[2,256,128]{2,1,0:T(8,128)} %get-tuple-element.63), channel_id=1, source_target_pairs={{0,6},{1,7},{2,4},{3,5},{4,2},{5,3},{6,0},{7,1},{8,14},{9,15},{10,... | collective-permute-start | bytes 786440 | tf_op jit(solution)/shard_map/ppermute | solution.py:778
  42.9 16.2 %collective-permute-start.6 = (f32[2,256,128]{2,1,0:T(8,128)}, f32[2,256,128]{2,1,0:T(8,128)}, u32[]{:S(2)}, u32[]{:S(2)}) collective-permute-start(f32[2,256,128]{2,1,0:T(8,128)} %get-tuple-element.64), channel_id=1, source_target_pairs={{0,7},{1,6},{2,5},{3,4},{4,3},{5,2},{6,1},{7,0},{8,15},{9,14},{10,... | collective-permute-start | bytes 786440 | tf_op jit(solution)/shard_map/ppermute | solution.py:778
  45.1 13.9 %copy-start = (bf16[2,256,256]{2,1,0:T(8,128)(2,1)S(1)}, bf16[2,256,256]{2,1,0:T(8,128)(2,1)}, u32[]{:S(2)}) copy-start(bf16[2,256,256]{2,1,0:T(8,128)(2,1)} %constant.61.clone.refs_9_) | copy-start | bytes 786436
  45.1 13.9 %copy-start.1 = (bf16[2,256,256]{2,1,0:T(8,128)(2,1)S(1)}, bf16[2,256,256]{2,1,0:T(8,128)(2,1)}, u32[]{:S(2)}) copy-start(bf16[2,256,256]{2,1,0:T(8,128)(2,1)} %constant.60.clone.refs_8_) | copy-start | bytes 786436
  45.2 13.9 %copy-start.2 = (f32[2,256,128]{2,1,0:T(8,128)S(1)}, f32[2,256,128]{2,1,0:T(8,128)}, u32[]{:S(2)}) copy-start(f32[2,256,128]{2,1,0:T(8,128)} %get-tuple-element.57.refs_0_) | copy-start | bytes 786436
  45.2 13.8 %copy-start.4 = (f32[2,256,128]{2,1,0:T(8,128)S(1)}, f32[2,256,128]{2,1,0:T(8,128)}, u32[]{:S(2)}) copy-start(f32[2,256,128]{2,1,0:T(8,128)} %copy-done.3) | copy-start | bytes 786436
  69.6 3.9 %collective-permute-start.7 = (f32[2,128,128]{2,1,0:T(8,128)S(1)}, f32[2,128,128]{2,1,0:T(8,128)S(1)}, u32[]{:S(2)}, u32[]{:S(2)}) collective-permute-start(f32[2,128,128]{2,1,0:T(8,128)S(1)} %get-tuple-element.68), channel_id=1, source_target_pairs={{0,1},{1,0},{2,3},{3,2},{4,5},{5,4},{6,7},{7,6},{8,9},{9,8},{10,11... | collective-permute-start | bytes 393224 | tf_op jit(solution)/shard_map/ppermute | solution.py:778
  70.0 6.3 %collective-permute-start.8 = (f32[2,128,128]{2,1,0:T(8,128)S(1)}, f32[2,128,128]{2,1,0:T(8,128)S(1)}, u32[]{:S(2)}, u32[]{:S(2)}) collective-permute-start(f32[2,128,128]{2,1,0:T(8,128)S(1)} %get-tuple-element.69), channel_id=1, source_target_pairs={{0,2},{1,3},{2,0},{3,1},{4,6},{5,7},{6,4},{7,5},{8,10},{9,11},{10,... | collective-permute-start | bytes 393224 | tf_op jit(solution)/shard_map/ppermute | solution.py:778
  70.5 7.0 %collective-permute-start.9 = (f32[2,128,128]{2,1,0:T(8,128)S(1)}, f32[2,128,128]{2,1,0:T(8,128)S(1)}, u32[]{:S(2)}, u32[]{:S(2)}) collective-permute-start(f32[2,128,128]{2,1,0:T(8,128)S(1)} %get-tuple-element.70), channel_id=1, source_target_pairs={{0,3},{1,2},{2,1},{3,0},{4,7},{5,6},{6,5},{7,4},{8,11},{9,10},{10,... | collective-permute-start | bytes 393224 | tf_op jit(solution)/shard_map/ppermute | solution.py:778
  71.5 7.8 %collective-permute-start.10 = (f32[2,128,128]{2,1,0:T(8,128)S(1)}, f32[2,128,128]{2,1,0:T(8,128)S(1)}, u32[]{:S(2)}, u32[]{:S(2)}) collective-permute-start(f32[2,128,128]{2,1,0:T(8,128)S(1)} %get-tuple-element.71), channel_id=1, source_target_pairs={{0,4},{1,5},{2,6},{3,7},{4,0},{5,1},{6,2},{7,3},{8,12},{9,13},{10,... | collective-permute-start | bytes 393224 | tf_op jit(solution)/shard_map/ppermute | solution.py:778
  72.1 13.5 %collective-permute-start.11 = (f32[2,128,128]{2,1,0:T(8,128)S(1)}, f32[2,128,128]{2,1,0:T(8,128)S(1)}, u32[]{:S(2)}, u32[]{:S(2)}) collective-permute-start(f32[2,128,128]{2,1,0:T(8,128)S(1)} %get-tuple-element.72), channel_id=1, source_target_pairs={{0,5},{1,4},{2,7},{3,6},{4,1},{5,0},{6,3},{7,2},{8,13},{9,12},{10,... | collective-permute-start | bytes 393224 | tf_op jit(solution)/shard_map/ppermute | solution.py:778
  73.5 14.2 %copy-start.11 = (f32[2,128,128]{2,1,0:T(8,128)}, f32[2,128,128]{2,1,0:T(8,128)S(1)}, u32[]{:S(2)}) copy-start(f32[2,128,128]{2,1,0:T(8,128)S(1)} %collective-permute-done.7.refs_1_) | copy-start | bytes 393220
  73.5 12.8 %collective-permute-start.12 = (f32[2,128,128]{2,1,0:T(8,128)S(1)}, f32[2,128,128]{2,1,0:T(8,128)S(1)}, u32[]{:S(2)}, u32[]{:S(2)}) collective-permute-start(f32[2,128,128]{2,1,0:T(8,128)S(1)} %get-tuple-element.73), channel_id=1, source_target_pairs={{0,6},{1,7},{2,4},{3,5},{4,2},{5,3},{6,0},{7,1},{8,14},{9,15},{10,... | collective-permute-start | bytes 393224 | tf_op jit(solution)/shard_map/ppermute | solution.py:778
  76.3 10.4 %collective-permute-start.13 = (f32[2,128,128]{2,1,0:T(8,128)S(1)}, f32[2,128,128]{2,1,0:T(8,128)S(1)}, u32[]{:S(2)}, u32[]{:S(2)}) collective-permute-start(f32[2,128,128]{2,1,0:T(8,128)S(1)} %get-tuple-element.74), channel_id=1, source_target_pairs={{0,7},{1,6},{2,5},{3,4},{4,3},{5,2},{6,1},{7,0},{8,15},{9,14},{10,... | collective-permute-start | bytes 393224 | tf_op jit(solution)/shard_map/ppermute | solution.py:778
  77.6 14.8 %collective-permute-start.17 = (f32[2,128,128]{2,1,0:T(8,128)S(1)}, f32[2,128,128]{2,1,0:T(8,128)S(1)}, u32[]{:S(2)}, u32[]{:S(2)}) collective-permute-start(f32[2,128,128]{2,1,0:T(8,128)S(1)} %get-tuple-element.77), channel_id=1, source_target_pairs={{0,1},{1,0},{2,3},{3,2},{4,5},{5,4},{6,7},{7,6},{8,9},{9,8},{10,11... | collective-permute-start | bytes 393224 | tf_op jit(solution)/shard_map/ppermute | solution.py:778
  79.3 15.1 %collective-permute-start.18 = (f32[2,128,128]{2,1,0:T(8,128)S(1)}, f32[2,128,128]{2,1,0:T(8,128)S(1)}, u32[]{:S(2)}, u32[]{:S(2)}) collective-permute-start(f32[2,128,128]{2,1,0:T(8,128)S(1)} %get-tuple-element.78), channel_id=1, source_target_pairs={{0,2},{1,3},{2,0},{3,1},{4,6},{5,7},{6,4},{7,5},{8,10},{9,11},{10,... | collective-permute-start | bytes 393224 | tf_op jit(solution)/shard_map/ppermute | solution.py:778
  85.6 11.2 %collective-permute-start.19 = (f32[2,128,128]{2,1,0:T(8,128)S(1)}, f32[2,128,128]{2,1,0:T(8,128)S(1)}, u32[]{:S(2)}, u32[]{:S(2)}) collective-permute-start(f32[2,128,128]{2,1,0:T(8,128)S(1)} %get-tuple-element.79), channel_id=1, source_target_pairs={{0,3},{1,2},{2,1},{3,0},{4,7},{5,6},{6,5},{7,4},{8,11},{9,10},{10,... | collective-permute-start | bytes 393224 | tf_op jit(solution)/shard_map/ppermute | solution.py:778
  86.2 14.8 %collective-permute-start.20 = (f32[2,128,128]{2,1,0:T(8,128)S(1)}, f32[2,128,128]{2,1,0:T(8,128)S(1)}, u32[]{:S(2)}, u32[]{:S(2)}) collective-permute-start(f32[2,128,128]{2,1,0:T(8,128)S(1)} %get-tuple-element.80), channel_id=1, source_target_pairs={{0,4},{1,5},{2,6},{3,7},{4,0},{5,1},{6,2},{7,3},{8,12},{9,13},{10,... | collective-permute-start | bytes 393224 | tf_op jit(solution)/shard_map/ppermute | solution.py:778
  86.8 14.3 %collective-permute-start.21 = (f32[2,128,128]{2,1,0:T(8,128)S(1)}, f32[2,128,128]{2,1,0:T(8,128)S(1)}, u32[]{:S(2)}, u32[]{:S(2)}) collective-permute-start(f32[2,128,128]{2,1,0:T(8,128)S(1)} %get-tuple-element.81), channel_id=1, source_target_pairs={{0,5},{1,4},{2,7},{3,6},{4,1},{5,0},{6,3},{7,2},{8,13},{9,12},{10,... | collective-permute-start | bytes 393224 | tf_op jit(solution)/shard_map/ppermute | solution.py:778
  92.4 9.3 %collective-permute-start.22 = (f32[2,128,128]{2,1,0:T(8,128)S(1)}, f32[2,128,128]{2,1,0:T(8,128)S(1)}, u32[]{:S(2)}, u32[]{:S(2)}) collective-permute-start(f32[2,128,128]{2,1,0:T(8,128)S(1)} %get-tuple-element.82), channel_id=1, source_target_pairs={{0,6},{1,7},{2,4},{3,5},{4,2},{5,3},{6,0},{7,1},{8,14},{9,15},{10,... | collective-permute-start | bytes 393224 | tf_op jit(solution)/shard_map/ppermute | solution.py:778
  94.4 7.7 %collective-permute-start.23 = (f32[2,128,128]{2,1,0:T(8,128)S(1)}, f32[2,128,128]{2,1,0:T(8,128)S(1)}, u32[]{:S(2)}, u32[]{:S(2)}) collective-permute-start(f32[2,128,128]{2,1,0:T(8,128)S(1)} %get-tuple-element.83), channel_id=1, source_target_pairs={{0,7},{1,6},{2,5},{3,4},{4,3},{5,2},{6,1},{7,0},{8,15},{9,14},{10,... | collective-permute-start | bytes 393224 | tf_op jit(solution)/shard_map/ppermute | solution.py:778
  96.8 16.5 %collective-permute-start.16 = (f32[136,512]{1,0:T(8,128)S(1)}, f32[136,512]{1,0:T(8,128)S(1)}, u32[]{:S(2)}, u32[]{:S(2)}) collective-permute-start(f32[136,512]{1,0:T(8,128)S(1)} %get-tuple-element.116), channel_id=1, source_target_pairs={{0,24},{8,16},{16,8},{24,0},{1,25},{9,17},{17,9},{25,1},{2,26},{10... | collective-permute-start | bytes 835592 | tf_op jit(solution)/shard_map/ppermute | solution.py:843
  101.0 25.4 %collective-permute-start.15 = (f32[136,512]{1,0:T(8,128)S(1)}, f32[136,512]{1,0:T(8,128)S(1)}, u32[]{:S(2)}, u32[]{:S(2)}) collective-permute-start(f32[136,512]{1,0:T(8,128)S(1)} %get-tuple-element.117), channel_id=1, source_target_pairs={{0,16},{8,24},{16,0},{24,8},{1,17},{9,25},{17,1},{25,9},{2,18},{10... | collective-permute-start | bytes 835592 | tf_op jit(solution)/shard_map/ppermute | solution.py:843
  101.0 25.4 %collective-permute-start.14 = (f32[136,512]{1,0:T(8,128)S(1)}, f32[136,512]{1,0:T(8,128)S(1)}, u32[]{:S(2)}, u32[]{:S(2)}) collective-permute-start(f32[136,512]{1,0:T(8,128)S(1)} %get-tuple-element.118), channel_id=1, source_target_pairs={{0,8},{8,0},{16,24},{24,16},{1,9},{9,1},{17,25},{25,17},{2,10},{10... | collective-permute-start | bytes 835592 | tf_op jit(solution)/shard_map/ppermute | solution.py:843
  108.5 17.9 %collective-permute-start.24 = (f32[136,512]{1,0:T(8,128)S(1)}, f32[136,512]{1,0:T(8,128)S(1)}, u32[]{:S(2)}, u32[]{:S(2)}) collective-permute-start(f32[136,512]{1,0:T(8,128)S(1)} %get-tuple-element.115), channel_id=1, source_target_pairs={{0,8},{8,0},{16,24},{24,16},{1,9},{9,1},{17,25},{25,17},{2,10},{10... | collective-permute-start | bytes 835592 | tf_op jit(solution)/shard_map/ppermute | solution.py:843
  110.8 29.1 %collective-permute-start.28 = (f32[136,512]{1,0:T(8,128)S(1)}, f32[136,512]{1,0:T(8,128)S(1)}, u32[]{:S(2)}, u32[]{:S(2)}) collective-permute-start(f32[136,512]{1,0:T(8,128)S(1)} %get-tuple-element.112), channel_id=1, source_target_pairs={{0,24},{8,16},{16,8},{24,0},{1,25},{9,17},{17,9},{25,1},{2,26},{10... | collective-permute-start | bytes 835592 | tf_op jit(solution)/shard_map/ppermute | solution.py:843
  113.3 35.6 %collective-permute-start.27 = (f32[136,512]{1,0:T(8,128)S(1)}, f32[136,512]{1,0:T(8,128)S(1)}, u32[]{:S(2)}, u32[]{:S(2)}) collective-permute-start(f32[136,512]{1,0:T(8,128)S(1)} %get-tuple-element.113), channel_id=1, source_target_pairs={{0,16},{8,24},{16,0},{24,8},{1,17},{9,25},{17,1},{25,9},{2,18},{10... | collective-permute-start | bytes 835592 | tf_op jit(solution)/shard_map/ppermute | solution.py:843
  126.6 3.1 %collective-permute-start.25 = (f32[4,24,512]{2,1,0:T(8,128)S(1)}, f32[4,24,512]{2,1,0:T(8,128)S(1)}, u32[]{:S(2)}, u32[]{:S(2)}) collective-permute-start(f32[4,24,512]{2,1,0:T(8,128)S(1)} %pad_maximum_fusion), channel_id=1, source_target_pairs={{0,1},{1,2},{2,3},{3,4},{4,5},{5,6},{6,7},{8,9},{9,10},{10,11},{11... | collective-permute-start | bytes 589832 | tf_op jit(solution)/shard_map/ppermute | solution.py:862
  128.4 4.6 %collective-permute-start.26 = (f32[4,24,512]{2,1,0:T(8,128)S(1)}, f32[4,24,512]{2,1,0:T(8,128)S(1)}, u32[]{:S(2)}, u32[]{:S(2)}) collective-permute-start(f32[4,24,512]{2,1,0:T(8,128)S(1)} %pad_maximum_fusion.1), channel_id=1, source_target_pairs={{1,0},{2,1},{3,2},{4,3},{5,4},{6,5},{7,6},{9,8},{10,9},{11,10},{12... | collective-permute-start | bytes 589832 | tf_op jit(solution)/shard_map/ppermute | solution.py:863
  158.2 1.2 collective-permute-start.29
  159.4 4.6 %collective-permute-start.32 = (f32[3,8,128]{2,1,0:T(8,128)S(1)}, f32[3,8,128]{2,1,0:T(8,128)S(1)}, u32[]{:S(2)}, u32[]{:S(2)}) collective-permute-start(f32[3,8,128]{2,1,0:T(8,128)S(1)} %max.21), channel_id=1, source_target_pairs={{0,6},{1,7},{2,4},{3,5},{4,2},{5,3},{6,0},{7,1},{8,14},{9,15},{10,... | collective-permute-start | bytes 36872 | tf_op jit(solution)/shard_map/ppermute | solution.py:125
  161.3 3.7 %collective-permute-start.31 = (f32[3,8,128]{2,1,0:T(8,128)S(1)}, f32[3,8,128]{2,1,0:T(8,128)S(1)}, u32[]{:S(2)}, u32[]{:S(2)}) collective-permute-start(f32[3,8,128]{2,1,0:T(8,128)S(1)} %max.21), channel_id=1, source_target_pairs={{0,4},{1,5},{2,6},{3,7},{4,0},{5,1},{6,2},{7,3},{8,12},{9,13},{10,... | collective-permute-start | bytes 36872 | tf_op jit(solution)/shard_map/ppermute | solution.py:125
  162.4 3.7 %collective-permute-start.30 = (f32[3,8,128]{2,1,0:T(8,128)S(1)}, f32[3,8,128]{2,1,0:T(8,128)S(1)}, u32[]{:S(2)}, u32[]{:S(2)}) collective-permute-start(f32[3,8,128]{2,1,0:T(8,128)S(1)} %max.21), channel_id=1, source_target_pairs={{0,2},{1,3},{2,0},{3,1},{4,6},{5,7},{6,4},{7,5},{8,10},{9,11},{10,... | collective-permute-start | bytes 36872 | tf_op jit(solution)/shard_map/ppermute | solution.py:125
  166.1 5.6 %collective-permute-start.35 = (f32[3,8,128]{2,1,0:T(8,128)S(1)}, f32[3,8,128]{2,1,0:T(8,128)S(1)}, u32[]{:S(2)}, u32[]{:S(2)}) collective-permute-start(f32[3,8,128]{2,1,0:T(8,128)S(1)} %maximum_maximum_fusion.1), channel_id=1, source_target_pairs={{0,24},{8,16},{16,8},{24,0},{1,25},{9,17},{17,9},{25,1},{2,26},{10... | collective-permute-start | bytes 36872 | tf_op jit(solution)/shard_map/ppermute | solution.py:125
  168.5 4.6 %collective-permute-start.34 = (f32[3,8,128]{2,1,0:T(8,128)S(1)}, f32[3,8,128]{2,1,0:T(8,128)S(1)}, u32[]{:S(2)}, u32[]{:S(2)}) collective-permute-start(f32[3,8,128]{2,1,0:T(8,128)S(1)} %maximum_maximum_fusion.1), channel_id=1, source_target_pairs={{0,16},{8,24},{16,0},{24,8},{1,17},{9,25},{17,1},{25,9},{2,18},{10... | collective-permute-start | bytes 36872 | tf_op jit(solution)/shard_map/ppermute | solution.py:125
  168.5 4.6 %collective-permute-start.33 = (f32[3,8,128]{2,1,0:T(8,128)S(1)}, f32[3,8,128]{2,1,0:T(8,128)S(1)}, u32[]{:S(2)}, u32[]{:S(2)}) collective-permute-start(f32[3,8,128]{2,1,0:T(8,128)S(1)} %maximum_maximum_fusion.1), channel_id=1, source_target_pairs={{0,8},{8,0},{16,24},{24,16},{1,9},{9,1},{17,25},{25,17},{2,10},{10... | collective-permute-start | bytes 36872 | tf_op jit(solution)/shard_map/ppermute | solution.py:125
  174.1 7.8 %collective-permute-start.36 = (f32[96,512]{1,0:T(8,128)S(1)}, f32[96,512]{1,0:T(8,128)S(1)}, u32[]{:S(2)}, u32[]{:S(2)}) collective-permute-start(f32[96,512]{1,0:T(8,128)S(1)} %get-tuple-element.95), channel_id=1, source_target_pairs={{0,8},{8,0},{16,24},{24,16},{1,9},{9,1},{17,25},{25,17},{2,10},{10... | collective-permute-start | bytes 589832 | tf_op jit(solution)/shard_map/ppermute | solution.py:843
  175.2 14.8 %collective-permute-start.37 = (f32[96,512]{1,0:T(8,128)S(1)}, f32[96,512]{1,0:T(8,128)S(1)}, u32[]{:S(2)}, u32[]{:S(2)}) collective-permute-start(f32[96,512]{1,0:T(8,128)S(1)} %get-tuple-element.96), channel_id=1, source_target_pairs={{0,16},{8,24},{16,0},{24,8},{1,17},{9,25},{17,1},{25,9},{2,18},{10... | collective-permute-start | bytes 589832 | tf_op jit(solution)/shard_map/ppermute | solution.py:843
  176.2 13.7 %collective-permute-start.38 = (f32[96,512]{1,0:T(8,128)S(1)}, f32[96,512]{1,0:T(8,128)S(1)}, u32[]{:S(2)}, u32[]{:S(2)}) collective-permute-start(f32[96,512]{1,0:T(8,128)S(1)} %get-tuple-element.97), channel_id=1, source_target_pairs={{0,24},{8,16},{16,8},{24,0},{1,25},{9,17},{17,9},{25,1},{2,26},{10... | collective-permute-start | bytes 589832 | tf_op jit(solution)/shard_map/ppermute | solution.py:843
  189.9 14.0 %collective-permute-start.39 = (f32[160,512]{1,0:T(8,128)S(1)}, f32[160,512]{1,0:T(8,128)S(1)}, u32[]{:S(2)}, u32[]{:S(2)}) collective-permute-start(f32[160,512]{1,0:T(8,128)S(1)} %get-tuple-element.108), channel_id=1, source_target_pairs={{0,8},{8,0},{16,24},{24,16},{1,9},{9,1},{17,25},{25,17},{2,10},{10... | collective-permute-start | bytes 983048 | tf_op jit(solution)/shard_map/ppermute | solution.py:843
  192.6 25.6 %collective-permute-start.40 = (f32[160,512]{1,0:T(8,128)S(1)}, f32[160,512]{1,0:T(8,128)S(1)}, u32[]{:S(2)}, u32[]{:S(2)}) collective-permute-start(f32[160,512]{1,0:T(8,128)S(1)} %get-tuple-element.109), channel_id=1, source_target_pairs={{0,16},{8,24},{16,0},{24,8},{1,17},{9,25},{17,1},{25,9},{2,18},{10... | collective-permute-start | bytes 983048 | tf_op jit(solution)/shard_map/ppermute | solution.py:843
  193.7 24.5 %collective-permute-start.41 = (f32[160,512]{1,0:T(8,128)S(1)}, f32[160,512]{1,0:T(8,128)S(1)}, u32[]{:S(2)}, u32[]{:S(2)}) collective-permute-start(f32[160,512]{1,0:T(8,128)S(1)} %get-tuple-element.110), channel_id=1, source_target_pairs={{0,24},{8,16},{16,8},{24,0},{1,25},{9,17},{17,9},{25,1},{2,26},{10... | collective-permute-start | bytes 983048 | tf_op jit(solution)/shard_map/ppermute | solution.py:843
  (18 other events, 78.7 us)

commit v5 on v4

--- a/solution.py
+++ b/solution.py
@@ -19,7 +19,6 @@
 mebibyte = 1024 * 1024
 rim = 16
 halo_rows = 16
-unroll = 2
 
 
 def with_halo(cells, sides, width):
@@ -528,7 +527,9 @@
             for i in range(level, skirt):
                 step(i, None)
                 step(blocks - 1 - i, None)
-            peaks[level] = lax.fori_loop(skirt, blocks - skirt, step, peaks[level], unroll=unroll)
+            peaks[level] = lax.fori_loop(
+                skirt, blocks - skirt, step, peaks[level], unroll=(blocks - 2 * skirt) // 2
+            )
     for level in range(3):
         most = before_ref[level]
         for t in range(tiles):
@@ -612,7 +613,7 @@
             held[1, step, rows, :] = pair[1]
         return carry
 
-    lax.fori_loop(0, size // 8, forward, 0)
+    lax.fori_loop(0, size // 8, forward, 0, unroll=4)
     lane_ids = lax.broadcasted_iota(jnp.int32, (size, lanes), 1)
     lone = jnp.zeros((size, lanes), jnp.float32)
     for step in range(steps):
@@ -639,7 +640,7 @@
             made[1, step, rows, :] = pair[1]
         return carry
 
-    lax.fori_loop(0, size // 8, backward, 0)
+    lax.fori_loop(0, size // 8, backward, 0, unroll=4)
     half = each // 2
     for step in range(0, steps, 2):
         block = [

time: 222 us -> 219 us (0.986)
  Pallas kernels: 57.2 us -> 53.4 us
where the time goes in v5:
time: 219 us; the launch traced here: 216 us
  waiting for transfers between devices  92.3 us (42%)
  starting transfers between devices  62 us (28%)
  Pallas kernels  53.4 us (24%)
  local copies, waits for them, and re-layouts  5.37 us (2%)
    ppermute x12, waiting for transfers between devices, over_chans(): lax.ppermute(pieces[turn], 'chan', [(i, i ^ turn) for i in range(chans)])  47.2 us
    ppermute x21, waiting for transfers between devices, over_rows(): lax.ppermute(pieces[turn], 'rows', [(i, i ^ turn) for i in range(count)])  34.8 us
    ppermute x12, starting transfers between devices, over_chans(): lax.ppermute(pieces[turn], 'chan', [(i, i ^ turn) for i in range(chans)])  27.4 us
    ppermute x21, starting transfers between devices, over_rows(): lax.ppermute(pieces[turn], 'rows', [(i, i ^ turn) for i in range(count)])  18.5 us
    pallas_call x2, Pallas kernels, starlet(): pl.pallas_call(functools.partial(starlet_body, chans, spans, fills), in_s...  14.1 us
    pallas_call x2, Pallas kernels, row_inverse(): pl.pallas_call(functools.partial(row_inverse_body, steps, count), grid=(2...  9.01 us
    pallas_call x1, Pallas kernels, filtered(): whole_call(weight_place_body, [shape(steps, size, lanes), shape(size, lan...  8.69 us
    ppermute x7, starting transfers between devices, max_over(): lax.ppermute(cells, axis, [(i, i ^ distance) for i in range(count)])  7.95 us
  transfers between devices with their start and end apart: 43, of which 21 were waited for; matrix products, arithmetic and copies ran while one was open for 2% of the time, Pallas kernels for 14%

profile of v5, /device:TPU:0, one launch (start us, length us, event | category | flops | bytes accessed | tf_op | source)
XLA Modules:
  0.0 216.3 jit_solution(18159094465798728019)
XLA Ops:
  0.6 4.5 %weight_pick.1 = f32[8,512,128]{2,1,0:T(8,128)} custom-call(f32[4,512,256]{2,1,0:T(8,128)} %bitcast.68, bf16[256,256]{1,0:T(8,128)(2,1)} %constant.55.clone.pick_ref), custom_call_target="tpu_custom_call" | custom-call | bytes 14000000 | tf_op jit(solution)/shard_map/weight_pick/pallas_call | solution.py:752
  5.1 5.2 %all-to-all-start = ((f32[8,512,128]{2,1,0:T(8,128)}), f32[8,512,128]{2,1,0:T(8,128)}, u32[]{:S(2)}, u32[]{:S(2)}) async-start(f32[8,512,128]{2,1,0:T(8,128)} %weight_pick.1), calls=%async_computation | async-start | bytes 4194304 | tf_op jit(solution)/shard_map/all_to_all | solution.py:765
  10.3 5.4 %row_forward.1 = (f32[2,256,128]{2,1,0:T(8,128)}, f32[2,256,128]{2,1,0:T(8,128)}, f32[2,256,128]{2,1,0:T(8,128)}, f32[2,256,128]{2,1,0:T(8,128)}, f32[2,256,128]...) custom-call(s32[1]{0:T(128)} %bitcast.5.me_ref, f32[256,2048]{1,0:T(8,128)} %bitcast.64, ...), custom_call_target="tpu_custom_call" | custom-call | bytes 21000000 | tf_op jit(solution)/shard_map/row_forward/pallas_call | solution.py:766
  16.2 1.7 collective-permute-start.1
  17.9 1.7 collective-permute-start.3
  19.7 2.5 %collective-permute-start.5 = (f32[2,256,128]{2,1,0:T(8,128)}, f32[2,256,128]{2,1,0:T(8,128)}, u32[]{:S(2)}, u32[]{:S(2)}) collective-permute-start(f32[2,256,128]{2,1,0:T(8,128)} %get-tuple-element.63), channel_id=1, source_target_pairs={{0,6},{1,7},{2,4},{3,5},{4,2},{5,3},{6,0},{7,1},{8,14},{9,15},{10,... | collective-permute-start | bytes 786440 | tf_op jit(solution)/shard_map/ppermute | solution.py:779
  22.3 19.9 %collective-permute-done.1.refs_2_ = f32[2,256,128]{2,1,0:T(8,128)S(1)} collective-permute-done((f32[2,256,128]{2,1,0:T(8,128)}, f32[2,256,128]{2,1,0:T(8,128)S(1)}, u32[]{:S(2)}, u32[]{:S(2)}) %collective-permute-start.1) | collective-permute-done | bytes 262176 | tf_op jit(solution)/shard_map/ppermute | solution.py:779
  43.2 1.9 select_bitcast_fusion.place_ref
  45.2 8.7 %weight_place.1 = (f32[16,128,128]{2,1,0:T(8,128)S(1)}, f32[128,128]{1,0:T(8,128)S(1)}) custom-call(f32[8,512,128]{2,1,0:T(8,128)} %all-to-all-done.in_ref, bf16[1024,1152]{1,0:T(8,128)(2,1)S(1)} %select_bitcast_fusion.place_ref, bf16[128,128]{1,0:T(8,128)(2,1)S(1)} %copy-done.7), custom_call_target="tpu_custom_call" | custom-call | bytes 35000000 | tf_op jit(solution)/shard_map/weight_place/pallas_call | solution.py:785
  54.5 4.5 %collective-permute-done.6.refs_7_ = f32[2,256,128]{2,1,0:T(8,128)} collective-permute-done((f32[2,256,128]{2,1,0:T(8,128)}, f32[2,256,128]{2,1,0:T(8,128)}, u32[]{:S(2)}, u32[]{:S(2)}) %collective-permute-start.6) | collective-permute-done | bytes 262176 | tf_op jit(solution)/shard_map/ppermute | solution.py:779
  59.0 7.6 %column_filter.1 = (f32[2,128,128]{2,1,0:T(8,128)S(1)}, f32[2,128,128]{2,1,0:T(8,128)S(1)}, f32[2,128,128]{2,1,0:T(8,128)S(1)}, f32[2,128,128]{2,1,0:T(8,128)S(1...) custom-call(s32[1]{0:T(128)} %bitcast.5.me_ref, ...), custom_call_target="tpu_custom_call" | custom-call | bytes 35000000 | tf_op jit(solution)/shard_map/column_filter/pallas_call | solution.py:792
  70.5 1.4 collective-permute-start.11
  72.3 2.4 %collective-permute-done.8.refs_2_ = f32[2,128,128]{2,1,0:T(8,128)S(1)} collective-permute-done((f32[2,128,128]{2,1,0:T(8,128)S(1)}, f32[2,128,128]{2,1,0:T(8,128)S(1)}, u32[]{:S(2)}, u32[]{:S(2)}) %collective-permute-start.8) | collective-permute-done | bytes 131104 | tf_op jit(solution)/shard_map/ppermute | solution.py:779
  74.7 1.2 collective-permute-done.9.refs_3_
  75.9 1.7 collective-permute-start.17
  78.2 5.8 %collective-permute-done.11.refs_5_ = f32[2,128,128]{2,1,0:T(8,128)S(1)} collective-permute-done((f32[2,128,128]{2,1,0:T(8,128)S(1)}, f32[2,128,128]{2,1,0:T(8,128)S(1)}, u32[]{:S(2)}, u32[]{:S(2)}) %collective-permute-start.11) | collective-permute-done | bytes 131104 | tf_op jit(solution)/shard_map/ppermute | solution.py:779
  86.1 4.5 %row_inverse.2 = (f32[256,2048]{1,0:T(8,128)}, f32[4,136,512]{2,1,0:T(8,128)}) custom-call(s32[1]{0:T(128)} %bitcast.5.me_ref, f32[2,128,128]{2,1,0:T(8,128)} %copy-done.6, f32[2,128,128]{2,1,0:T(8,128)} %copy-done.11, f32[2,128,128]{2,1,0:T(8,128)} %copy-done.12, f32[2,128,128]{2,1,0:T(8,128)} %copy-done.13, f32[2,128,128]{2,1,0:T(8,128)} %copy-done.14, ...), custom_call_target="tpu_custom_call" | custom-call | bytes 17500000 | tf_op jit(solution)/shard_map/row_inverse/pallas_call | solution.py:816
  90.6 2.1 collective-permute-start.22
  93.7 1.3 dynamic-slice_bitcast_fusion.4
  95.0 4.2 %collective-permute-start.16 = (f32[136,512]{1,0:T(8,128)S(1)}, f32[136,512]{1,0:T(8,128)S(1)}, u32[]{:S(2)}, u32[]{:S(2)}) collective-permute-start(f32[136,512]{1,0:T(8,128)S(1)} %get-tuple-element.116), channel_id=1, source_target_pairs={{0,24},{8,16},{16,8},{24,0},{1,25},{9,17},{17,9},{25,1},{2,26},{10... | collective-permute-start | bytes 835592 | tf_op jit(solution)/shard_map/ppermute | solution.py:844
  100.9 4.5 %row_inverse.3 = (f32[256,2048]{1,0:T(8,128)}, f32[4,136,512]{2,1,0:T(8,128)}) custom-call(s32[1]{0:T(128)} %bitcast.5.me_ref, f32[2,128,128]{2,1,0:T(8,128)} %copy-done.5, f32[2,128,128]{2,1,0:T(8,128)} %copy-done.9, f32[2,128,128]{2,1,0:T(8,128)} %copy-done.10, f32[2,128,128]{2,1,0:T(8,128)} %copy-done.17, ...), custom_call_target="tpu_custom_call", output_to_operand_aliasing={{0}: (12, {})} | custom-call | bytes 17500000 | tf_op jit(solution)/shard_map/row_inverse/pallas_call | solution.py:816
  105.4 1.3 dynamic-slice_bitcast_fusion
  106.7 2.2 %collective-permute-start.24 = (f32[136,512]{1,0:T(8,128)S(1)}, f32[136,512]{1,0:T(8,128)S(1)}, u32[]{:S(2)}, u32[]{:S(2)}) collective-permute-start(f32[136,512]{1,0:T(8,128)S(1)} %get-tuple-element.115), channel_id=1, source_target_pairs={{0,8},{8,0},{16,24},{24,16},{1,9},{9,1},{17,25},{25,17},{2,10},{10... | collective-permute-start | bytes 835592 | tf_op jit(solution)/shard_map/ppermute | solution.py:844
  109.0 2.5 %collective-permute-start.28 = (f32[136,512]{1,0:T(8,128)S(1)}, f32[136,512]{1,0:T(8,128)S(1)}, u32[]{:S(2)}, u32[]{:S(2)}) collective-permute-start(f32[136,512]{1,0:T(8,128)S(1)} %get-tuple-element.112), channel_id=1, source_target_pairs={{0,24},{8,16},{16,8},{24,0},{1,25},{9,17},{17,9},{25,1},{2,26},{10... | collective-permute-start | bytes 835592 | tf_op jit(solution)/shard_map/ppermute | solution.py:844
  111.5 8.2 %collective-permute-start.27 = (f32[136,512]{1,0:T(8,128)S(1)}, f32[136,512]{1,0:T(8,128)S(1)}, u32[]{:S(2)}, u32[]{:S(2)}) collective-permute-start(f32[136,512]{1,0:T(8,128)S(1)} %get-tuple-element.113), channel_id=1, source_target_pairs={{0,16},{8,24},{16,0},{24,8},{1,17},{9,25},{17,1},{25,9},{2,18},{10... | collective-permute-start | bytes 835592 | tf_op jit(solution)/shard_map/ppermute | solution.py:844
  119.6 4.9 %collective-permute-done.15.refs_2_ = f32[136,512]{1,0:T(8,128)S(1)} collective-permute-done((f32[136,512]{1,0:T(8,128)S(1)}, f32[136,512]{1,0:T(8,128)S(1)}, u32[]{:S(2)}, u32[]{:S(2)}) %collective-permute-start.15) | collective-permute-done | bytes 278560 | tf_op jit(solution)/shard_map/ppermute | solution.py:844
  124.8 1.7 collective-permute-start.25
  126.6 1.3 collective-permute-start.26
  127.9 3.3 %collective-permute-done.26 = f32[4,24,512]{2,1,0:T(8,128)S(1)} collective-permute-done((f32[4,24,512]{2,1,0:T(8,128)S(1)}, f32[4,24,512]{2,1,0:T(8,128)S(1)}, u32[]{:S(2)}, u32[]{:S(2)}) %collective-permute-start.26) | collective-permute-done | bytes 196640 | tf_op jit(solution)/shard_map/ppermute | solution.py:864
  131.2 6.4 %starlet.2 = (f32[4,4,96,512]{3,2,1,0:T(8,128)S(1)}, f32[3,8,128]{2,1,0:T(8,128)S(1)}) custom-call(s32[4]{0:T(128)S(1)} %add_convert_fusion.ends_ref, f32[3,8,128]{2,1,0:T(8,128)S(1)} %broadcast_in_dim.9.before_ref, f32[136,512]{1,0:T(8,128)S(1)} %get-tuple-element.86.refs_0_, f32[136,512]{1,0:T(8,128)S(1)} %collective-permute-done.14.refs_1_, ...), custom_call_target="tpu_custom_call" | custom-call | bytes 42000000 | tf_op jit(solution)/shard_map/starlet/pallas_call | solution.py:875
  137.7 9.4 %collective-permute-done.27.refs_6_ = f32[136,512]{1,0:T(8,128)S(1)} collective-permute-done((f32[136,512]{1,0:T(8,128)S(1)}, f32[136,512]{1,0:T(8,128)S(1)}, u32[]{:S(2)}, u32[]{:S(2)}) %collective-permute-start.27) | collective-permute-done | bytes 278560 | tf_op jit(solution)/shard_map/ppermute | solution.py:844
  147.1 7.7 %starlet.3 = (f32[4,4,160,512]{3,2,1,0:T(8,128)S(1)}, f32[3,8,128]{2,1,0:T(8,128)S(1)}) custom-call(s32[4]{0:T(128)S(1)} %add_convert_fusion.ends_ref, f32[3,8,128]{2,1,0:T(8,128)S(1)} %get-tuple-element.91.before_ref, f32[136,512]{1,0:T(8,128)S(1)} %get-tuple-element.86.refs_0_, f32[136,512]{1,0:T(8,128)S(1)} %collective-permute-done.14.refs_1_, ...), custom_call_target="tpu_custom_call" | custom-call | bytes 42000000 | tf_op jit(solution)/shard_map/starlet/pallas_call | solution.py:875
  154.9 1.2 collective-permute-done.29
  156.0 2.1 collective-permute-start.32
  160.6 1.2 collective-permute-done.31
  162.7 2.5 %collective-permute-start.35 = (f32[3,8,128]{2,1,0:T(8,128)S(1)}, f32[3,8,128]{2,1,0:T(8,128)S(1)}, u32[]{:S(2)}, u32[]{:S(2)}) collective-permute-start(f32[3,8,128]{2,1,0:T(8,128)S(1)} %maximum_maximum_fusion.1), channel_id=1, source_target_pairs={{0,24},{8,16},{16,8},{24,0},{1,25},{9,17},{17,9},{25,1},{2,26},{10... | collective-permute-start | bytes 36872 | tf_op jit(solution)/shard_map/ppermute | solution.py:124
  165.2 1.9 collective-permute-start.33
  167.1 1.2 collective-permute-done.35
  168.3 1.5 collective-permute-done.34
  172.9 2.3 %collective-permute-start.38 = (f32[96,512]{1,0:T(8,128)S(1)}, f32[96,512]{1,0:T(8,128)S(1)}, u32[]{:S(2)}, u32[]{:S(2)}) collective-permute-start(f32[96,512]{1,0:T(8,128)S(1)} %get-tuple-element.97), channel_id=1, source_target_pairs={{0,24},{8,16},{16,8},{24,0},{1,25},{9,17},{17,9},{25,1},{2,26},{10... | collective-permute-start | bytes 589832 | tf_op jit(solution)/shard_map/ppermute | solution.py:844
  175.2 1.6 shrink.3
  176.8 1.7 collective-permute-done.36.refs_1_
  178.5 8.0 %collective-permute-done.37.refs_2_ = f32[96,512]{1,0:T(8,128)S(1)} collective-permute-done((f32[96,512]{1,0:T(8,128)S(1)}, f32[96,512]{1,0:T(8,128)S(1)}, u32[]{:S(2)}, u32[]{:S(2)}) %collective-permute-start.37) | collective-permute-done | bytes 196640 | tf_op jit(solution)/shard_map/ppermute | solution.py:844
  186.5 2.7 %collective-permute-start.39 = (f32[160,512]{1,0:T(8,128)S(1)}, f32[160,512]{1,0:T(8,128)S(1)}, u32[]{:S(2)}, u32[]{:S(2)}) collective-permute-start(f32[160,512]{1,0:T(8,128)S(1)} %get-tuple-element.108), channel_id=1, source_target_pairs={{0,8},{8,0},{16,24},{24,16},{1,9},{9,1},{17,25},{25,17},{2,10},{10... | collective-permute-start | bytes 983048 | tf_op jit(solution)/shard_map/ppermute | solution.py:844
  190.3 1.5 collective-permute-start.41
  191.8 8.7 %collective-permute-done.39.refs_5_ = f32[160,512]{1,0:T(8,128)S(1)} collective-permute-done((f32[160,512]{1,0:T(8,128)S(1)}, f32[160,512]{1,0:T(8,128)S(1)}, u32[]{:S(2)}, u32[]{:S(2)}) %collective-permute-start.39) | collective-permute-done | bytes 327712 | tf_op jit(solution)/shard_map/ppermute | solution.py:844
  200.5 14.3 %collective-permute-done.40.refs_6_ = f32[160,512]{1,0:T(8,128)S(1)} collective-permute-done((f32[160,512]{1,0:T(8,128)S(1)}, f32[160,512]{1,0:T(8,128)S(1)}, u32[]{:S(2)}, u32[]{:S(2)}) %collective-permute-start.40) | collective-permute-done | bytes 327712 | tf_op jit(solution)/shard_map/ppermute | solution.py:844
  214.8 1.5 join.1
  (119 shorter events, 19.7 us)
Async XLA Ops:
  5.1 40.1 %all-to-all-start = ((f32[8,512,128]{2,1,0:T(8,128)}), f32[8,512,128]{2,1,0:T(8,128)}, u32[]{:S(2)}, u32[]{:S(2)}) async-start(f32[8,512,128]{2,1,0:T(8,128)} %weight_pick.1), calls=%async_computation | async-start | bytes 4194304 | tf_op jit(solution)/shard_map/all_to_all | solution.py:765
  15.7 4.0 %collective-permute-start = (f32[2,256,128]{2,1,0:T(8,128)}, f32[2,256,128]{2,1,0:T(8,128)S(1)}, u32[]{:S(2)}, u32[]{:S(2)}) collective-permute-start(f32[2,256,128]{2,1,0:T(8,128)} %get-tuple-element.58), channel_id=1, source_target_pairs={{0,1},{1,0},{2,3},{3,2},{4,5},{5,4},{6,7},{7,6},{8,9},{9,8},{10,11... | collective-permute-start | bytes 786440 | tf_op jit(solution)/shard_map/ppermute | solution.py:779
  16.2 26.0 %collective-permute-start.1 = (f32[2,256,128]{2,1,0:T(8,128)}, f32[2,256,128]{2,1,0:T(8,128)S(1)}, u32[]{:S(2)}, u32[]{:S(2)}) collective-permute-start(f32[2,256,128]{2,1,0:T(8,128)} %get-tuple-element.59), channel_id=1, source_target_pairs={{0,2},{1,3},{2,0},{3,1},{4,6},{5,7},{6,4},{7,5},{8,10},{9,11},{10,... | collective-permute-start | bytes 786440 | tf_op jit(solution)/shard_map/ppermute | solution.py:779
  17.9 36.0 %collective-permute-start.2 = (f32[2,256,128]{2,1,0:T(8,128)}, f32[2,256,128]{2,1,0:T(8,128)}, u32[]{:S(2)}, u32[]{:S(2)}) collective-permute-start(f32[2,256,128]{2,1,0:T(8,128)} %get-tuple-element.60), channel_id=1, source_target_pairs={{0,3},{1,2},{2,1},{3,0},{4,7},{5,6},{6,5},{7,4},{8,11},{9,10},{10,... | collective-permute-start | bytes 786440 | tf_op jit(solution)/shard_map/ppermute | solution.py:779
  17.9 36.0 %collective-permute-start.3 = (f32[2,256,128]{2,1,0:T(8,128)}, f32[2,256,128]{2,1,0:T(8,128)}, u32[]{:S(2)}, u32[]{:S(2)}) collective-permute-start(f32[2,256,128]{2,1,0:T(8,128)} %get-tuple-element.61), channel_id=1, source_target_pairs={{0,4},{1,5},{2,6},{3,7},{4,0},{5,1},{6,2},{7,3},{8,12},{9,13},{10,... | collective-permute-start | bytes 786440 | tf_op jit(solution)/shard_map/ppermute | solution.py:779
  19.7 34.3 %collective-permute-start.4 = (f32[2,256,128]{2,1,0:T(8,128)}, f32[2,256,128]{2,1,0:T(8,128)}, u32[]{:S(2)}, u32[]{:S(2)}) collective-permute-start(f32[2,256,128]{2,1,0:T(8,128)} %get-tuple-element.62), channel_id=1, source_target_pairs={{0,5},{1,4},{2,7},{3,6},{4,1},{5,0},{6,3},{7,2},{8,13},{9,12},{10,... | collective-permute-start | bytes 786440 | tf_op jit(solution)/shard_map/ppermute | solution.py:779
  19.7 34.7 %collective-permute-start.5 = (f32[2,256,128]{2,1,0:T(8,128)}, f32[2,256,128]{2,1,0:T(8,128)}, u32[]{:S(2)}, u32[]{:S(2)}) collective-permute-start(f32[2,256,128]{2,1,0:T(8,128)} %get-tuple-element.63), channel_id=1, source_target_pairs={{0,6},{1,7},{2,4},{3,5},{4,2},{5,3},{6,0},{7,1},{8,14},{9,15},{10,... | collective-permute-start | bytes 786440 | tf_op jit(solution)/shard_map/ppermute | solution.py:779
  42.9 16.2 %collective-permute-start.6 = (f32[2,256,128]{2,1,0:T(8,128)}, f32[2,256,128]{2,1,0:T(8,128)}, u32[]{:S(2)}, u32[]{:S(2)}) collective-permute-start(f32[2,256,128]{2,1,0:T(8,128)} %get-tuple-element.64), channel_id=1, source_target_pairs={{0,7},{1,6},{2,5},{3,4},{4,3},{5,2},{6,1},{7,0},{8,15},{9,14},{10,... | collective-permute-start | bytes 786440 | tf_op jit(solution)/shard_map/ppermute | solution.py:779
  45.1 13.9 %copy-start = (bf16[2,256,256]{2,1,0:T(8,128)(2,1)S(1)}, bf16[2,256,256]{2,1,0:T(8,128)(2,1)}, u32[]{:S(2)}) copy-start(bf16[2,256,256]{2,1,0:T(8,128)(2,1)} %constant.61.clone.refs_9_) | copy-start | bytes 786436
  45.1 13.9 %copy-start.1 = (bf16[2,256,256]{2,1,0:T(8,128)(2,1)S(1)}, bf16[2,256,256]{2,1,0:T(8,128)(2,1)}, u32[]{:S(2)}) copy-start(bf16[2,256,256]{2,1,0:T(8,128)(2,1)} %constant.60.clone.refs_8_) | copy-start | bytes 786436
  45.2 13.9 %copy-start.2 = (f32[2,256,128]{2,1,0:T(8,128)S(1)}, f32[2,256,128]{2,1,0:T(8,128)}, u32[]{:S(2)}) copy-start(f32[2,256,128]{2,1,0:T(8,128)} %get-tuple-element.57.refs_0_) | copy-start | bytes 786436
  45.2 13.8 %copy-start.4 = (f32[2,256,128]{2,1,0:T(8,128)S(1)}, f32[2,256,128]{2,1,0:T(8,128)}, u32[]{:S(2)}) copy-start(f32[2,256,128]{2,1,0:T(8,128)} %copy-done.3) | copy-start | bytes 786436
  68.0 3.9 %collective-permute-start.7 = (f32[2,128,128]{2,1,0:T(8,128)S(1)}, f32[2,128,128]{2,1,0:T(8,128)S(1)}, u32[]{:S(2)}, u32[]{:S(2)}) collective-permute-start(f32[2,128,128]{2,1,0:T(8,128)S(1)} %get-tuple-element.68), channel_id=1, source_target_pairs={{0,1},{1,0},{2,3},{3,2},{4,5},{5,4},{6,7},{7,6},{8,9},{9,8},{10,11... | collective-permute-start | bytes 393224 | tf_op jit(solution)/shard_map/ppermute | solution.py:779
  68.4 6.3 %collective-permute-start.8 = (f32[2,128,128]{2,1,0:T(8,128)S(1)}, f32[2,128,128]{2,1,0:T(8,128)S(1)}, u32[]{:S(2)}, u32[]{:S(2)}) collective-permute-start(f32[2,128,128]{2,1,0:T(8,128)S(1)} %get-tuple-element.69), channel_id=1, source_target_pairs={{0,2},{1,3},{2,0},{3,1},{4,6},{5,7},{6,4},{7,5},{8,10},{9,11},{10,... | collective-permute-start | bytes 393224 | tf_op jit(solution)/shard_map/ppermute | solution.py:779
  68.9 7.0 %collective-permute-start.9 = (f32[2,128,128]{2,1,0:T(8,128)S(1)}, f32[2,128,128]{2,1,0:T(8,128)S(1)}, u32[]{:S(2)}, u32[]{:S(2)}) collective-permute-start(f32[2,128,128]{2,1,0:T(8,128)S(1)} %get-tuple-element.70), channel_id=1, source_target_pairs={{0,3},{1,2},{2,1},{3,0},{4,7},{5,6},{6,5},{7,4},{8,11},{9,10},{10,... | collective-permute-start | bytes 393224 | tf_op jit(solution)/shard_map/ppermute | solution.py:779
  69.9 7.8 %collective-permute-start.10 = (f32[2,128,128]{2,1,0:T(8,128)S(1)}, f32[2,128,128]{2,1,0:T(8,128)S(1)}, u32[]{:S(2)}, u32[]{:S(2)}) collective-permute-start(f32[2,128,128]{2,1,0:T(8,128)S(1)} %get-tuple-element.71), channel_id=1, source_target_pairs={{0,4},{1,5},{2,6},{3,7},{4,0},{5,1},{6,2},{7,3},{8,12},{9,13},{10,... | collective-permute-start | bytes 393224 | tf_op jit(solution)/shard_map/ppermute | solution.py:779
  70.5 13.5 %collective-permute-start.11 = (f32[2,128,128]{2,1,0:T(8,128)S(1)}, f32[2,128,128]{2,1,0:T(8,128)S(1)}, u32[]{:S(2)}, u32[]{:S(2)}) collective-permute-start(f32[2,128,128]{2,1,0:T(8,128)S(1)} %get-tuple-element.72), channel_id=1, source_target_pairs={{0,5},{1,4},{2,7},{3,6},{4,1},{5,0},{6,3},{7,2},{8,13},{9,12},{10,... | collective-permute-start | bytes 393224 | tf_op jit(solution)/shard_map/ppermute | solution.py:779
  71.9 14.2 %copy-start.11 = (f32[2,128,128]{2,1,0:T(8,128)}, f32[2,128,128]{2,1,0:T(8,128)S(1)}, u32[]{:S(2)}) copy-start(f32[2,128,128]{2,1,0:T(8,128)S(1)} %collective-permute-done.7.refs_1_) | copy-start | bytes 393220
  71.9 12.8 %collective-permute-start.12 = (f32[2,128,128]{2,1,0:T(8,128)S(1)}, f32[2,128,128]{2,1,0:T(8,128)S(1)}, u32[]{:S(2)}, u32[]{:S(2)}) collective-permute-start(f32[2,128,128]{2,1,0:T(8,128)S(1)} %get-tuple-element.73), channel_id=1, source_target_pairs={{0,6},{1,7},{2,4},{3,5},{4,2},{5,3},{6,0},{7,1},{8,14},{9,15},{10,... | collective-permute-start | bytes 393224 | tf_op jit(solution)/shard_map/ppermute | solution.py:779
  74.7 10.4 %collective-permute-start.13 = (f32[2,128,128]{2,1,0:T(8,128)S(1)}, f32[2,128,128]{2,1,0:T(8,128)S(1)}, u32[]{:S(2)}, u32[]{:S(2)}) collective-permute-start(f32[2,128,128]{2,1,0:T(8,128)S(1)} %get-tuple-element.74), channel_id=1, source_target_pairs={{0,7},{1,6},{2,5},{3,4},{4,3},{5,2},{6,1},{7,0},{8,15},{9,14},{10,... | collective-permute-start | bytes 393224 | tf_op jit(solution)/shard_map/ppermute | solution.py:779
  75.9 14.7 %collective-permute-start.17 = (f32[2,128,128]{2,1,0:T(8,128)S(1)}, f32[2,128,128]{2,1,0:T(8,128)S(1)}, u32[]{:S(2)}, u32[]{:S(2)}) collective-permute-start(f32[2,128,128]{2,1,0:T(8,128)S(1)} %get-tuple-element.77), channel_id=1, source_target_pairs={{0,1},{1,0},{2,3},{3,2},{4,5},{5,4},{6,7},{7,6},{8,9},{9,8},{10,11... | collective-permute-start | bytes 393224 | tf_op jit(solution)/shard_map/ppermute | solution.py:779
  77.6 15.1 %collective-permute-start.18 = (f32[2,128,128]{2,1,0:T(8,128)S(1)}, f32[2,128,128]{2,1,0:T(8,128)S(1)}, u32[]{:S(2)}, u32[]{:S(2)}) collective-permute-start(f32[2,128,128]{2,1,0:T(8,128)S(1)} %get-tuple-element.78), channel_id=1, source_target_pairs={{0,2},{1,3},{2,0},{3,1},{4,6},{5,7},{6,4},{7,5},{8,10},{9,11},{10,... | collective-permute-start | bytes 393224 | tf_op jit(solution)/shard_map/ppermute | solution.py:779
  84.0 11.0 %collective-permute-start.19 = (f32[2,128,128]{2,1,0:T(8,128)S(1)}, f32[2,128,128]{2,1,0:T(8,128)S(1)}, u32[]{:S(2)}, u32[]{:S(2)}) collective-permute-start(f32[2,128,128]{2,1,0:T(8,128)S(1)} %get-tuple-element.79), channel_id=1, source_target_pairs={{0,3},{1,2},{2,1},{3,0},{4,7},{5,6},{6,5},{7,4},{8,11},{9,10},{10,... | collective-permute-start | bytes 393224 | tf_op jit(solution)/shard_map/ppermute | solution.py:779
  84.6 14.6 %collective-permute-start.20 = (f32[2,128,128]{2,1,0:T(8,128)S(1)}, f32[2,128,128]{2,1,0:T(8,128)S(1)}, u32[]{:S(2)}, u32[]{:S(2)}) collective-permute-start(f32[2,128,128]{2,1,0:T(8,128)S(1)} %get-tuple-element.80), channel_id=1, source_target_pairs={{0,4},{1,5},{2,6},{3,7},{4,0},{5,1},{6,2},{7,3},{8,12},{9,13},{10,... | collective-permute-start | bytes 393224 | tf_op jit(solution)/shard_map/ppermute | solution.py:779
  85.1 14.1 %collective-permute-start.21 = (f32[2,128,128]{2,1,0:T(8,128)S(1)}, f32[2,128,128]{2,1,0:T(8,128)S(1)}, u32[]{:S(2)}, u32[]{:S(2)}) collective-permute-start(f32[2,128,128]{2,1,0:T(8,128)S(1)} %get-tuple-element.81), channel_id=1, source_target_pairs={{0,5},{1,4},{2,7},{3,6},{4,1},{5,0},{6,3},{7,2},{8,13},{9,12},{10,... | collective-permute-start | bytes 393224 | tf_op jit(solution)/shard_map/ppermute | solution.py:779
  90.6 9.3 %collective-permute-start.22 = (f32[2,128,128]{2,1,0:T(8,128)S(1)}, f32[2,128,128]{2,1,0:T(8,128)S(1)}, u32[]{:S(2)}, u32[]{:S(2)}) collective-permute-start(f32[2,128,128]{2,1,0:T(8,128)S(1)} %get-tuple-element.82), channel_id=1, source_target_pairs={{0,6},{1,7},{2,4},{3,5},{4,2},{5,3},{6,0},{7,1},{8,14},{9,15},{10,... | collective-permute-start | bytes 393224 | tf_op jit(solution)/shard_map/ppermute | solution.py:779
  92.7 7.5 %collective-permute-start.23 = (f32[2,128,128]{2,1,0:T(8,128)S(1)}, f32[2,128,128]{2,1,0:T(8,128)S(1)}, u32[]{:S(2)}, u32[]{:S(2)}) collective-permute-start(f32[2,128,128]{2,1,0:T(8,128)S(1)} %get-tuple-element.83), channel_id=1, source_target_pairs={{0,7},{1,6},{2,5},{3,4},{4,3},{5,2},{6,1},{7,0},{8,15},{9,14},{10,... | collective-permute-start | bytes 393224 | tf_op jit(solution)/shard_map/ppermute | solution.py:779
  95.0 16.5 %collective-permute-start.16 = (f32[136,512]{1,0:T(8,128)S(1)}, f32[136,512]{1,0:T(8,128)S(1)}, u32[]{:S(2)}, u32[]{:S(2)}) collective-permute-start(f32[136,512]{1,0:T(8,128)S(1)} %get-tuple-element.116), channel_id=1, source_target_pairs={{0,24},{8,16},{16,8},{24,0},{1,25},{9,17},{17,9},{25,1},{2,26},{10... | collective-permute-start | bytes 835592 | tf_op jit(solution)/shard_map/ppermute | solution.py:844
  99.2 25.4 %collective-permute-start.15 = (f32[136,512]{1,0:T(8,128)S(1)}, f32[136,512]{1,0:T(8,128)S(1)}, u32[]{:S(2)}, u32[]{:S(2)}) collective-permute-start(f32[136,512]{1,0:T(8,128)S(1)} %get-tuple-element.117), channel_id=1, source_target_pairs={{0,16},{8,24},{16,0},{24,8},{1,17},{9,25},{17,1},{25,9},{2,18},{10... | collective-permute-start | bytes 835592 | tf_op jit(solution)/shard_map/ppermute | solution.py:844
  99.2 25.4 %collective-permute-start.14 = (f32[136,512]{1,0:T(8,128)S(1)}, f32[136,512]{1,0:T(8,128)S(1)}, u32[]{:S(2)}, u32[]{:S(2)}) collective-permute-start(f32[136,512]{1,0:T(8,128)S(1)} %get-tuple-element.118), channel_id=1, source_target_pairs={{0,8},{8,0},{16,24},{24,16},{1,9},{9,1},{17,25},{25,17},{2,10},{10... | collective-permute-start | bytes 835592 | tf_op jit(solution)/shard_map/ppermute | solution.py:844
  106.7 18.0 %collective-permute-start.24 = (f32[136,512]{1,0:T(8,128)S(1)}, f32[136,512]{1,0:T(8,128)S(1)}, u32[]{:S(2)}, u32[]{:S(2)}) collective-permute-start(f32[136,512]{1,0:T(8,128)S(1)} %get-tuple-element.115), channel_id=1, source_target_pairs={{0,8},{8,0},{16,24},{24,16},{1,9},{9,1},{17,25},{25,17},{2,10},{10... | collective-permute-start | bytes 835592 | tf_op jit(solution)/shard_map/ppermute | solution.py:844
  109.0 28.7 %collective-permute-start.28 = (f32[136,512]{1,0:T(8,128)S(1)}, f32[136,512]{1,0:T(8,128)S(1)}, u32[]{:S(2)}, u32[]{:S(2)}) collective-permute-start(f32[136,512]{1,0:T(8,128)S(1)} %get-tuple-element.112), channel_id=1, source_target_pairs={{0,24},{8,16},{16,8},{24,0},{1,25},{9,17},{17,9},{25,1},{2,26},{10... | collective-permute-start | bytes 835592 | tf_op jit(solution)/shard_map/ppermute | solution.py:844
  111.5 35.6 %collective-permute-start.27 = (f32[136,512]{1,0:T(8,128)S(1)}, f32[136,512]{1,0:T(8,128)S(1)}, u32[]{:S(2)}, u32[]{:S(2)}) collective-permute-start(f32[136,512]{1,0:T(8,128)S(1)} %get-tuple-element.113), channel_id=1, source_target_pairs={{0,16},{8,24},{16,0},{24,8},{1,17},{9,25},{17,1},{25,9},{2,18},{10... | collective-permute-start | bytes 835592 | tf_op jit(solution)/shard_map/ppermute | solution.py:844
  124.8 3.1 %collective-permute-start.25 = (f32[4,24,512]{2,1,0:T(8,128)S(1)}, f32[4,24,512]{2,1,0:T(8,128)S(1)}, u32[]{:S(2)}, u32[]{:S(2)}) collective-permute-start(f32[4,24,512]{2,1,0:T(8,128)S(1)} %pad_maximum_fusion), channel_id=1, source_target_pairs={{0,1},{1,2},{2,3},{3,4},{4,5},{5,6},{6,7},{8,9},{9,10},{10,11},{11... | collective-permute-start | bytes 589832 | tf_op jit(solution)/shard_map/ppermute | solution.py:863
  126.6 4.6 %collective-permute-start.26 = (f32[4,24,512]{2,1,0:T(8,128)S(1)}, f32[4,24,512]{2,1,0:T(8,128)S(1)}, u32[]{:S(2)}, u32[]{:S(2)}) collective-permute-start(f32[4,24,512]{2,1,0:T(8,128)S(1)} %pad_maximum_fusion.1), channel_id=1, source_target_pairs={{1,0},{2,1},{3,2},{4,3},{5,4},{6,5},{7,6},{9,8},{10,9},{11,10},{12... | collective-permute-start | bytes 589832 | tf_op jit(solution)/shard_map/ppermute | solution.py:864
  154.8 1.2 collective-permute-start.29
  156.0 4.6 %collective-permute-start.32 = (f32[3,8,128]{2,1,0:T(8,128)S(1)}, f32[3,8,128]{2,1,0:T(8,128)S(1)}, u32[]{:S(2)}, u32[]{:S(2)}) collective-permute-start(f32[3,8,128]{2,1,0:T(8,128)S(1)} %max.21), channel_id=1, source_target_pairs={{0,6},{1,7},{2,4},{3,5},{4,2},{5,3},{6,0},{7,1},{8,14},{9,15},{10,... | collective-permute-start | bytes 36872 | tf_op jit(solution)/shard_map/ppermute | solution.py:124
  158.1 3.7 %collective-permute-start.31 = (f32[3,8,128]{2,1,0:T(8,128)S(1)}, f32[3,8,128]{2,1,0:T(8,128)S(1)}, u32[]{:S(2)}, u32[]{:S(2)}) collective-permute-start(f32[3,8,128]{2,1,0:T(8,128)S(1)} %max.21), channel_id=1, source_target_pairs={{0,4},{1,5},{2,6},{3,7},{4,0},{5,1},{6,2},{7,3},{8,12},{9,13},{10,... | collective-permute-start | bytes 36872 | tf_op jit(solution)/shard_map/ppermute | solution.py:124
  159.0 3.7 %collective-permute-start.30 = (f32[3,8,128]{2,1,0:T(8,128)S(1)}, f32[3,8,128]{2,1,0:T(8,128)S(1)}, u32[]{:S(2)}, u32[]{:S(2)}) collective-permute-start(f32[3,8,128]{2,1,0:T(8,128)S(1)} %max.21), channel_id=1, source_target_pairs={{0,2},{1,3},{2,0},{3,1},{4,6},{5,7},{6,4},{7,5},{8,10},{9,11},{10,... | collective-permute-start | bytes 36872 | tf_op jit(solution)/shard_map/ppermute | solution.py:124
  162.7 5.6 %collective-permute-start.35 = (f32[3,8,128]{2,1,0:T(8,128)S(1)}, f32[3,8,128]{2,1,0:T(8,128)S(1)}, u32[]{:S(2)}, u32[]{:S(2)}) collective-permute-start(f32[3,8,128]{2,1,0:T(8,128)S(1)} %maximum_maximum_fusion.1), channel_id=1, source_target_pairs={{0,24},{8,16},{16,8},{24,0},{1,25},{9,17},{17,9},{25,1},{2,26},{10... | collective-permute-start | bytes 36872 | tf_op jit(solution)/shard_map/ppermute | solution.py:124
  165.2 4.6 %collective-permute-start.34 = (f32[3,8,128]{2,1,0:T(8,128)S(1)}, f32[3,8,128]{2,1,0:T(8,128)S(1)}, u32[]{:S(2)}, u32[]{:S(2)}) collective-permute-start(f32[3,8,128]{2,1,0:T(8,128)S(1)} %maximum_maximum_fusion.1), channel_id=1, source_target_pairs={{0,16},{8,24},{16,0},{24,8},{1,17},{9,25},{17,1},{25,9},{2,18},{10... | collective-permute-start | bytes 36872 | tf_op jit(solution)/shard_map/ppermute | solution.py:124
  165.2 4.6 %collective-permute-start.33 = (f32[3,8,128]{2,1,0:T(8,128)S(1)}, f32[3,8,128]{2,1,0:T(8,128)S(1)}, u32[]{:S(2)}, u32[]{:S(2)}) collective-permute-start(f32[3,8,128]{2,1,0:T(8,128)S(1)} %maximum_maximum_fusion.1), channel_id=1, source_target_pairs={{0,8},{8,0},{16,24},{24,16},{1,9},{9,1},{17,25},{25,17},{2,10},{10... | collective-permute-start | bytes 36872 | tf_op jit(solution)/shard_map/ppermute | solution.py:124
  170.7 7.8 %collective-permute-start.36 = (f32[96,512]{1,0:T(8,128)S(1)}, f32[96,512]{1,0:T(8,128)S(1)}, u32[]{:S(2)}, u32[]{:S(2)}) collective-permute-start(f32[96,512]{1,0:T(8,128)S(1)} %get-tuple-element.95), channel_id=1, source_target_pairs={{0,8},{8,0},{16,24},{24,16},{1,9},{9,1},{17,25},{25,17},{2,10},{10... | collective-permute-start | bytes 589832 | tf_op jit(solution)/shard_map/ppermute | solution.py:844
  171.8 14.8 %collective-permute-start.37 = (f32[96,512]{1,0:T(8,128)S(1)}, f32[96,512]{1,0:T(8,128)S(1)}, u32[]{:S(2)}, u32[]{:S(2)}) collective-permute-start(f32[96,512]{1,0:T(8,128)S(1)} %get-tuple-element.96), channel_id=1, source_target_pairs={{0,16},{8,24},{16,0},{24,8},{1,17},{9,25},{17,1},{25,9},{2,18},{10... | collective-permute-start | bytes 589832 | tf_op jit(solution)/shard_map/ppermute | solution.py:844
  172.9 13.7 %collective-permute-start.38 = (f32[96,512]{1,0:T(8,128)S(1)}, f32[96,512]{1,0:T(8,128)S(1)}, u32[]{:S(2)}, u32[]{:S(2)}) collective-permute-start(f32[96,512]{1,0:T(8,128)S(1)} %get-tuple-element.97), channel_id=1, source_target_pairs={{0,24},{8,16},{16,8},{24,0},{1,25},{9,17},{17,9},{25,1},{2,26},{10... | collective-permute-start | bytes 589832 | tf_op jit(solution)/shard_map/ppermute | solution.py:844
  186.5 13.9 %collective-permute-start.39 = (f32[160,512]{1,0:T(8,128)S(1)}, f32[160,512]{1,0:T(8,128)S(1)}, u32[]{:S(2)}, u32[]{:S(2)}) collective-permute-start(f32[160,512]{1,0:T(8,128)S(1)} %get-tuple-element.108), channel_id=1, source_target_pairs={{0,8},{8,0},{16,24},{24,16},{1,9},{9,1},{17,25},{25,17},{2,10},{10... | collective-permute-start | bytes 983048 | tf_op jit(solution)/shard_map/ppermute | solution.py:844
  189.2 25.6 %collective-permute-start.40 = (f32[160,512]{1,0:T(8,128)S(1)}, f32[160,512]{1,0:T(8,128)S(1)}, u32[]{:S(2)}, u32[]{:S(2)}) collective-permute-start(f32[160,512]{1,0:T(8,128)S(1)} %get-tuple-element.109), channel_id=1, source_target_pairs={{0,16},{8,24},{16,0},{24,8},{1,17},{9,25},{17,1},{25,9},{2,18},{10... | collective-permute-start | bytes 983048 | tf_op jit(solution)/shard_map/ppermute | solution.py:844
  190.3 24.5 %collective-permute-start.41 = (f32[160,512]{1,0:T(8,128)S(1)}, f32[160,512]{1,0:T(8,128)S(1)}, u32[]{:S(2)}, u32[]{:S(2)}) collective-permute-start(f32[160,512]{1,0:T(8,128)S(1)} %get-tuple-element.110), channel_id=1, source_target_pairs={{0,24},{8,16},{16,8},{24,0},{1,25},{9,17},{17,9},{25,1},{2,26},{10... | collective-permute-start | bytes 983048 | tf_op jit(solution)/shard_map/ppermute | solution.py:844
  (18 other events, 78.5 us)

commit v6 on v5

--- a/solution.py
+++ b/solution.py
@@ -262,8 +262,8 @@
     half = lanes // 2
     spots = np.arange(lanes)
     there, back = [], []
-    for group in range(count):
-        columns = group_columns(length, count, group)
+    for group in range(2):
+        columns = group_columns(length, count, 0) if group == 0 else radix * spots
         angles = 2.0 * np.pi * (np.outer(spots, columns) % length) / length
         cosine, sine = np.cos(angles), np.sin(angles)
         ahead = np.zeros((2, lanes, 2, lanes))
@@ -284,7 +284,9 @@
             behind[1, 0, 0] = (-1.0) ** spots
         there.append(ahead.reshape(2 * lanes, 2 * lanes))
         back.append(behind.reshape(2 * lanes, 2 * lanes) / float(length) ** 2)
-    return split_table(np.stack(there)), split_table(np.stack(back))
+    angles = 2.0 * np.pi * np.outer(np.arange(count), spots) / length
+    turns = np.stack([np.cos(angles), np.sin(angles)]).astype(np.float32)
+    return split_table(np.stack(there)), split_table(np.stack(back)), turns
 
 
 def column_tables(length, count, steps):
@@ -369,7 +371,17 @@
     )
 
 
-def row_forward_body(steps, me_ref, x_ref, table_ref, *refs):
+def spun(pairs, spin_ref, sign):
+    out = [pairs[0]]
+    for group in range(1, len(pairs)):
+        real, imag = pairs[group]
+        cosine = jnp.broadcast_to(spin_ref[0, pl.ds(group, 1), :], real.shape)
+        sine = sign * jnp.broadcast_to(spin_ref[1, pl.ds(group, 1), :], real.shape)
+        out.append((real * cosine - imag * sine, imag * cosine + real * sine))
+    return out
+
+
+def row_forward_body(steps, me_ref, x_ref, table_ref, spin_ref, *refs):
     out_refs, held = refs[:-1], refs[-1]
     groups = len(out_refs)
     _, height, lanes = out_refs[0].shape
@@ -379,16 +391,18 @@
         tiles = [x_ref[rows, pl.ds(lanes * t, lanes)] for t in range(2 * groups)]
         pairs = real_dft(tiles)
         pairs = [(pairs[0][0], pairs[groups][0])] + pairs[1:groups]
+        pairs = spun(pairs, spin_ref, -1.0)
         for group in range(groups):
             high, low = split(jnp.concatenate(pairs[group], axis=1))
             held[0, group, rows, :] = high
             held[1, group, rows, :] = low
     for turn, out_ref in enumerate(out_refs):
         group = me_ref[0] ^ turn
+        kind = jnp.minimum(group, 1)
         done = (
-            dot(held[0, group], table_ref[group, 0])
-            + dot(held[1, group], table_ref[group, 0])
-            + dot(held[0, group], table_ref[group, 1])
+            dot(held[0, group], table_ref[kind, 0])
+            + dot(held[1, group], table_ref[kind, 0])
+            + dot(held[0, group], table_ref[kind, 1])
         )
         for start in range(0, height, 8):
             spread = pl.ds(start % steps * each + start // steps, 8, stride=each)
@@ -398,7 +412,7 @@
 
 def row_inverse_body(steps, groups, me_ref, *refs):
     in_refs = refs[:groups]
-    table_ref, est_ref, dirty_ref, _, res_ref, half_ref, held = refs[groups:]
+    table_ref, spin_ref, est_ref, dirty_ref, _, res_ref, half_ref, held = refs[groups:]
     _, chunk, lanes = in_refs[0].shape
     parts, _, wide = half_ref.shape
     each = chunk // steps
@@ -409,6 +423,7 @@
     def _():
         for partner, in_ref in enumerate(in_refs):
             group = me_ref[0] ^ partner
+            kind = jnp.minimum(group, 1)
             halves = []
             for part in range(2):
                 pieces = [
@@ -418,9 +433,9 @@
                 halves.append(jnp.concatenate(pieces, axis=0))
             high, low = split(jnp.concatenate(halves, axis=1))
             held[group] = (
-                dot(high, table_ref[group, 0])
-                + dot(low, table_ref[group, 0])
-                + dot(high, table_ref[group, 1])
+                dot(high, table_ref[kind, 0])
+                + dot(low, table_ref[kind, 0])
+                + dot(high, table_ref[kind, 1])
             )
 
     per = wide // lanes
@@ -433,6 +448,7 @@
             (held[group, chunk_rows, pl.ds(0, lanes)], held[group, chunk_rows, pl.ds(lanes, lanes)])
             for group in range(groups)
         ]
+        pairs = spun(pairs, spin_ref, 1.0)
         pairs = [(pairs[0][0], None)] + pairs[1:] + [(pairs[0][1], None)]
         tiles = real_inverse_dft(pairs)
         for t in range(2 * groups):
@@ -738,7 +754,7 @@
     width = weights.shape[1]
     f32 = jnp.float32
     pick, place, flip = [jnp.asarray(table) for table in weight_tables(length, count, steps)]
-    there, back = [jnp.asarray(table) for table in row_tables(length, count)]
+    there, back, spins = [jnp.asarray(table) for table in row_tables(length, count)]
     down, up, turns = [jnp.asarray(table) for table in column_tables(length, count, steps)]
     shape = lambda *dims: jax.ShapeDtypeStruct(dims, f32)
     packs = lanes * count // width
@@ -765,14 +781,14 @@
     sent = lax.all_to_all(sent, "rows", 0, 0, tiled=True)
     ahead = pl.pallas_call(
         functools.partial(row_forward_body, steps),
-        in_specs=[smem, vmem, vmem],
+        in_specs=[smem, vmem, vmem, vmem],
         out_specs=[vmem] * count,
         out_shape=[shape(2, height, lanes)] * count,
         scratch_shapes=[pltpu.VMEM((2, count, height, 2 * lanes), jnp.bfloat16)],
         compiler_params=pltpu.CompilerParams(vmem_limit_bytes=56 * mebibyte),
         name="row_forward",
         cost_estimate=busy(6),
-    )(me, values, there)
+    )(me, values, there, spins)
 
     def over_rows(pieces):
         return [pieces[0]] + [
@@ -820,6 +836,7 @@
             + [whole(2, half, lanes)] * count
             + [
                 whole(*back.shape),
+                whole(*spins.shape),
                 rows_spec,
                 rows_spec,
                 pl.BlockSpec(memory_space=pl.ANY),
@@ -827,11 +844,11 @@
             out_specs=[rows_spec, whole(chans, half + 8, part)],
             out_shape=[shape(height, length), shape(chans, half + 8, part)],
             scratch_shapes=[pltpu.VMEM((count, half, 2 * lanes), f32)],
-            input_output_aliases={count + 4: 0} if old is not dirty else {},
+            input_output_aliases={count + 5: 0} if old is not dirty else {},
             compiler_params=pltpu.CompilerParams(vmem_limit_bytes=56 * mebibyte),
             name="row_inverse",
         cost_estimate=busy(5),
-        )(me, *cells, back, values, dirty, old)
+        )(me, *cells, back, spins, values, dirty, old)
 
     def pieces_for(cells):
         me = lax.axis_index("chan")

time: 219 us -> 218 us (level)
  no operation moved by 1% of the time
where the time goes in v6:
time: 218 us; the launch traced here: 216 us
  waiting for transfers between devices  92.5 us (42%)
  starting transfers between devices  62.4 us (29%)
  Pallas kernels  52.4 us (24%)
  local copies, waits for them, and re-layouts  5.37 us (2%)
    ppermute x12, waiting for transfers between devices, over_chans(): lax.ppermute(pieces[turn], 'chan', [(i, i ^ turn) for i in range(chans)])  47.2 us
    ppermute x21, waiting for transfers between devices, over_rows(): lax.ppermute(pieces[turn], 'rows', [(i, i ^ turn) for i in range(count)])  35 us
    ppermute x12, starting transfers between devices, over_chans(): lax.ppermute(pieces[turn], 'chan', [(i, i ^ turn) for i in range(chans)])  27.8 us
    ppermute x21, starting transfers between devices, over_rows(): lax.ppermute(pieces[turn], 'rows', [(i, i ^ turn) for i in range(count)])  18.5 us
    pallas_call x2, Pallas kernels, starlet(): pl.pallas_call(functools.partial(starlet_body, chans, spans, fills), in_s...  14.1 us
    pallas_call x1, Pallas kernels, filtered(): whole_call(weight_place_body, [shape(steps, size, lanes), shape(size, lan...  8.69 us
    pallas_call x2, Pallas kernels, row_inverse(): pl.pallas_call(functools.partial(row_inverse_body, steps, count), grid=(2...  8.2 us
    ppermute x7, starting transfers between devices, max_over(): lax.ppermute(cells, axis, [(i, i ^ distance) for i in range(count)])  7.95 us
  transfers between devices with their start and end apart: 43, of which 21 were waited for; matrix products, arithmetic and copies ran while one was open for 2% of the time, Pallas kernels for 14%

profile of v6, /device:TPU:0, one launch (start us, length us, event | category | flops | bytes accessed | tf_op | source)
XLA Modules:
  0.0 215.9 jit_solution(1859069226394995570)
XLA Ops:
  0.6 4.5 %weight_pick.1 = f32[8,512,128]{2,1,0:T(8,128)} custom-call(f32[4,512,256]{2,1,0:T(8,128)} %bitcast.68, bf16[256,256]{1,0:T(8,128)(2,1)} %constant.57.clone.pick_ref), custom_call_target="tpu_custom_call" | custom-call | bytes 14000000 | tf_op jit(solution)/shard_map/weight_pick/pallas_call | solution.py:768
  5.1 5.2 %all-to-all-start = ((f32[8,512,128]{2,1,0:T(8,128)}), f32[8,512,128]{2,1,0:T(8,128)}, u32[]{:S(2)}, u32[]{:S(2)}) async-start(f32[8,512,128]{2,1,0:T(8,128)} %weight_pick.1), calls=%async_computation | async-start | bytes 4194304 | tf_op jit(solution)/shard_map/all_to_all | solution.py:781
  10.3 5.2 %row_forward.1 = (f32[2,256,128]{2,1,0:T(8,128)}, f32[2,256,128]{2,1,0:T(8,128)}, f32[2,256,128]{2,1,0:T(8,128)}, f32[2,256,128]{2,1,0:T(8,128)}, f32[2,256,128]...) custom-call(s32[1]{0:T(128)} %bitcast.5.me_ref, f32[256,2048]{1,0:T(8,128)} %bitcast.64, ...), custom_call_target="tpu_custom_call" | custom-call | bytes 21000000 | tf_op jit(solution)/shard_map/row_forward/pallas_call | solution.py:782
  16.0 1.7 collective-permute-start.1
  17.7 1.7 collective-permute-start.3
  19.5 2.5 %collective-permute-start.5 = (f32[2,256,128]{2,1,0:T(8,128)}, f32[2,256,128]{2,1,0:T(8,128)}, u32[]{:S(2)}, u32[]{:S(2)}) collective-permute-start(f32[2,256,128]{2,1,0:T(8,128)} %get-tuple-element.63), channel_id=1, source_target_pairs={{0,6},{1,7},{2,4},{3,5},{4,2},{5,3},{6,0},{7,1},{8,14},{9,15},{10,... | collective-permute-start | bytes 786440 | tf_op jit(solution)/shard_map/ppermute | solution.py:795
  22.0 20.1 %collective-permute-done.1.refs_2_ = f32[2,256,128]{2,1,0:T(8,128)S(1)} collective-permute-done((f32[2,256,128]{2,1,0:T(8,128)}, f32[2,256,128]{2,1,0:T(8,128)S(1)}, u32[]{:S(2)}, u32[]{:S(2)}) %collective-permute-start.1) | collective-permute-done | bytes 262176 | tf_op jit(solution)/shard_map/ppermute | solution.py:795
  43.2 1.9 select_bitcast_fusion.place_ref
  45.2 8.7 %weight_place.1 = (f32[16,128,128]{2,1,0:T(8,128)S(1)}, f32[128,128]{1,0:T(8,128)S(1)}) custom-call(f32[8,512,128]{2,1,0:T(8,128)} %all-to-all-done.in_ref, bf16[1024,1152]{1,0:T(8,128)(2,1)S(1)} %select_bitcast_fusion.place_ref, bf16[128,128]{1,0:T(8,128)(2,1)S(1)} %copy-done.7), custom_call_target="tpu_custom_call" | custom-call | bytes 35000000 | tf_op jit(solution)/shard_map/weight_place/pallas_call | solution.py:801
  54.5 4.5 %collective-permute-done.6.refs_7_ = f32[2,256,128]{2,1,0:T(8,128)} collective-permute-done((f32[2,256,128]{2,1,0:T(8,128)}, f32[2,256,128]{2,1,0:T(8,128)}, u32[]{:S(2)}, u32[]{:S(2)}) %collective-permute-start.6) | collective-permute-done | bytes 262176 | tf_op jit(solution)/shard_map/ppermute | solution.py:795
  59.0 7.6 %column_filter.1 = (f32[2,128,128]{2,1,0:T(8,128)S(1)}, f32[2,128,128]{2,1,0:T(8,128)S(1)}, f32[2,128,128]{2,1,0:T(8,128)S(1)}, f32[2,128,128]{2,1,0:T(8,128)S(1...) custom-call(s32[1]{0:T(128)} %bitcast.5.me_ref, ...), custom_call_target="tpu_custom_call" | custom-call | bytes 35000000 | tf_op jit(solution)/shard_map/column_filter/pallas_call | solution.py:808
  70.5 1.4 collective-permute-start.11
  72.3 2.4 %collective-permute-done.8.refs_2_ = f32[2,128,128]{2,1,0:T(8,128)S(1)} collective-permute-done((f32[2,128,128]{2,1,0:T(8,128)S(1)}, f32[2,128,128]{2,1,0:T(8,128)S(1)}, u32[]{:S(2)}, u32[]{:S(2)}) %collective-permute-start.8) | collective-permute-done | bytes 131104 | tf_op jit(solution)/shard_map/ppermute | solution.py:795
  74.7 1.2 collective-permute-done.9.refs_3_
  75.9 1.7 collective-permute-start.17
  78.2 5.8 %collective-permute-done.11.refs_5_ = f32[2,128,128]{2,1,0:T(8,128)S(1)} collective-permute-done((f32[2,128,128]{2,1,0:T(8,128)S(1)}, f32[2,128,128]{2,1,0:T(8,128)S(1)}, u32[]{:S(2)}, u32[]{:S(2)}) %collective-permute-start.11) | collective-permute-done | bytes 131104 | tf_op jit(solution)/shard_map/ppermute | solution.py:795
  86.1 4.1 %row_inverse.2 = (f32[256,2048]{1,0:T(8,128)}, f32[4,136,512]{2,1,0:T(8,128)}) custom-call(s32[1]{0:T(128)} %bitcast.5.me_ref, f32[2,128,128]{2,1,0:T(8,128)} %copy-done.6, f32[2,128,128]{2,1,0:T(8,128)} %copy-done.11, f32[2,128,128]{2,1,0:T(8,128)} %copy-done.12, f32[2,128,128]{2,1,0:T(8,128)} %copy-done.13, f32[2,128,128]{2,1,0:T(8,128)} %copy-done.14, ...), custom_call_target="tpu_custom_call" | custom-call | bytes 17500000 | tf_op jit(solution)/shard_map/row_inverse/pallas_call | solution.py:832
  90.2 2.1 collective-permute-start.22
  93.3 1.3 dynamic-slice_bitcast_fusion.4
  94.6 4.2 %collective-permute-start.16 = (f32[136,512]{1,0:T(8,128)S(1)}, f32[136,512]{1,0:T(8,128)S(1)}, u32[]{:S(2)}, u32[]{:S(2)}) collective-permute-start(f32[136,512]{1,0:T(8,128)S(1)} %get-tuple-element.116), channel_id=1, source_target_pairs={{0,24},{8,16},{16,8},{24,0},{1,25},{9,17},{17,9},{25,1},{2,26},{10... | collective-permute-start | bytes 835592 | tf_op jit(solution)/shard_map/ppermute | solution.py:861
  100.5 4.1 %row_inverse.3 = (f32[256,2048]{1,0:T(8,128)}, f32[4,136,512]{2,1,0:T(8,128)}) custom-call(s32[1]{0:T(128)} %bitcast.5.me_ref, f32[2,128,128]{2,1,0:T(8,128)} %copy-done.5, f32[2,128,128]{2,1,0:T(8,128)} %copy-done.9, f32[2,128,128]{2,1,0:T(8,128)} %copy-done.10, f32[2,128,128]{2,1,0:T(8,128)} %copy-done.17, ...), custom_call_target="tpu_custom_call", output_to_operand_aliasing={{0}: (13, {})} | custom-call | bytes 17500000 | tf_op jit(solution)/shard_map/row_inverse/pallas_call | solution.py:832
  104.6 1.3 dynamic-slice_bitcast_fusion
  105.9 2.2 %collective-permute-start.24 = (f32[136,512]{1,0:T(8,128)S(1)}, f32[136,512]{1,0:T(8,128)S(1)}, u32[]{:S(2)}, u32[]{:S(2)}) collective-permute-start(f32[136,512]{1,0:T(8,128)S(1)} %get-tuple-element.115), channel_id=1, source_target_pairs={{0,8},{8,0},{16,24},{24,16},{1,9},{9,1},{17,25},{25,17},{2,10},{10... | collective-permute-start | bytes 835592 | tf_op jit(solution)/shard_map/ppermute | solution.py:861
  108.2 2.5 %collective-permute-start.28 = (f32[136,512]{1,0:T(8,128)S(1)}, f32[136,512]{1,0:T(8,128)S(1)}, u32[]{:S(2)}, u32[]{:S(2)}) collective-permute-start(f32[136,512]{1,0:T(8,128)S(1)} %get-tuple-element.112), channel_id=1, source_target_pairs={{0,24},{8,16},{16,8},{24,0},{1,25},{9,17},{17,9},{25,1},{2,26},{10... | collective-permute-start | bytes 835592 | tf_op jit(solution)/shard_map/ppermute | solution.py:861
  110.7 8.6 %collective-permute-start.27 = (f32[136,512]{1,0:T(8,128)S(1)}, f32[136,512]{1,0:T(8,128)S(1)}, u32[]{:S(2)}, u32[]{:S(2)}) collective-permute-start(f32[136,512]{1,0:T(8,128)S(1)} %get-tuple-element.113), channel_id=1, source_target_pairs={{0,16},{8,24},{16,0},{24,8},{1,17},{9,25},{17,1},{25,9},{2,18},{10... | collective-permute-start | bytes 835592 | tf_op jit(solution)/shard_map/ppermute | solution.py:861
  119.3 5.0 %collective-permute-done.15.refs_2_ = f32[136,512]{1,0:T(8,128)S(1)} collective-permute-done((f32[136,512]{1,0:T(8,128)S(1)}, f32[136,512]{1,0:T(8,128)S(1)}, u32[]{:S(2)}, u32[]{:S(2)}) %collective-permute-start.15) | collective-permute-done | bytes 278560 | tf_op jit(solution)/shard_map/ppermute | solution.py:861
  124.4 1.7 collective-permute-start.25
  126.2 1.3 collective-permute-start.26
  127.5 3.3 %collective-permute-done.26 = f32[4,24,512]{2,1,0:T(8,128)S(1)} collective-permute-done((f32[4,24,512]{2,1,0:T(8,128)S(1)}, f32[4,24,512]{2,1,0:T(8,128)S(1)}, u32[]{:S(2)}, u32[]{:S(2)}) %collective-permute-start.26) | collective-permute-done | bytes 196640 | tf_op jit(solution)/shard_map/ppermute | solution.py:881
  130.9 6.4 %starlet.2 = (f32[4,4,96,512]{3,2,1,0:T(8,128)S(1)}, f32[3,8,128]{2,1,0:T(8,128)S(1)}) custom-call(s32[4]{0:T(128)S(1)} %add_convert_fusion.ends_ref, f32[3,8,128]{2,1,0:T(8,128)S(1)} %broadcast_in_dim.9.before_ref, f32[136,512]{1,0:T(8,128)S(1)} %get-tuple-element.86.refs_0_, f32[136,512]{1,0:T(8,128)S(1)} %collective-permute-done.14.refs_1_, ...), custom_call_target="tpu_custom_call" | custom-call | bytes 42000000 | tf_op jit(solution)/shard_map/starlet/pallas_call | solution.py:892
  137.3 9.4 %collective-permute-done.27.refs_6_ = f32[136,512]{1,0:T(8,128)S(1)} collective-permute-done((f32[136,512]{1,0:T(8,128)S(1)}, f32[136,512]{1,0:T(8,128)S(1)}, u32[]{:S(2)}, u32[]{:S(2)}) %collective-permute-start.27) | collective-permute-done | bytes 278560 | tf_op jit(solution)/shard_map/ppermute | solution.py:861
  146.7 7.7 %starlet.3 = (f32[4,4,160,512]{3,2,1,0:T(8,128)S(1)}, f32[3,8,128]{2,1,0:T(8,128)S(1)}) custom-call(s32[4]{0:T(128)S(1)} %add_convert_fusion.ends_ref, f32[3,8,128]{2,1,0:T(8,128)S(1)} %get-tuple-element.91.before_ref, f32[136,512]{1,0:T(8,128)S(1)} %get-tuple-element.86.refs_0_, f32[136,512]{1,0:T(8,128)S(1)} %collective-permute-done.14.refs_1_, ...), custom_call_target="tpu_custom_call" | custom-call | bytes 42000000 | tf_op jit(solution)/shard_map/starlet/pallas_call | solution.py:892
  154.5 1.2 collective-permute-done.29
  155.7 2.1 collective-permute-start.32
  160.3 1.2 collective-permute-done.31
  162.3 2.5 %collective-permute-start.35 = (f32[3,8,128]{2,1,0:T(8,128)S(1)}, f32[3,8,128]{2,1,0:T(8,128)S(1)}, u32[]{:S(2)}, u32[]{:S(2)}) collective-permute-start(f32[3,8,128]{2,1,0:T(8,128)S(1)} %maximum_maximum_fusion.1), channel_id=1, source_target_pairs={{0,24},{8,16},{16,8},{24,0},{1,25},{9,17},{17,9},{25,1},{2,26},{10... | collective-permute-start | bytes 36872 | tf_op jit(solution)/shard_map/ppermute | solution.py:124
  164.8 1.9 collective-permute-start.33
  166.7 1.2 collective-permute-done.35
  167.9 1.5 collective-permute-done.34
  172.5 2.3 %collective-permute-start.38 = (f32[96,512]{1,0:T(8,128)S(1)}, f32[96,512]{1,0:T(8,128)S(1)}, u32[]{:S(2)}, u32[]{:S(2)}) collective-permute-start(f32[96,512]{1,0:T(8,128)S(1)} %get-tuple-element.97), channel_id=1, source_target_pairs={{0,24},{8,16},{16,8},{24,0},{1,25},{9,17},{17,9},{25,1},{2,26},{10... | collective-permute-start | bytes 589832 | tf_op jit(solution)/shard_map/ppermute | solution.py:861
  174.8 1.6 shrink.3
  176.4 1.7 collective-permute-done.36.refs_1_
  178.2 8.0 %collective-permute-done.37.refs_2_ = f32[96,512]{1,0:T(8,128)S(1)} collective-permute-done((f32[96,512]{1,0:T(8,128)S(1)}, f32[96,512]{1,0:T(8,128)S(1)}, u32[]{:S(2)}, u32[]{:S(2)}) %collective-permute-start.37) | collective-permute-done | bytes 196640 | tf_op jit(solution)/shard_map/ppermute | solution.py:861
  186.2 2.7 %collective-permute-start.39 = (f32[160,512]{1,0:T(8,128)S(1)}, f32[160,512]{1,0:T(8,128)S(1)}, u32[]{:S(2)}, u32[]{:S(2)}) collective-permute-start(f32[160,512]{1,0:T(8,128)S(1)} %get-tuple-element.108), channel_id=1, source_target_pairs={{0,8},{8,0},{16,24},{24,16},{1,9},{9,1},{17,25},{25,17},{2,10},{10... | collective-permute-start | bytes 983048 | tf_op jit(solution)/shard_map/ppermute | solution.py:861
  189.9 1.5 collective-permute-start.41
  191.4 8.7 %collective-permute-done.39.refs_5_ = f32[160,512]{1,0:T(8,128)S(1)} collective-permute-done((f32[160,512]{1,0:T(8,128)S(1)}, f32[160,512]{1,0:T(8,128)S(1)}, u32[]{:S(2)}, u32[]{:S(2)}) %collective-permute-start.39) | collective-permute-done | bytes 327712 | tf_op jit(solution)/shard_map/ppermute | solution.py:861
  200.1 14.3 %collective-permute-done.40.refs_6_ = f32[160,512]{1,0:T(8,128)S(1)} collective-permute-done((f32[160,512]{1,0:T(8,128)S(1)}, f32[160,512]{1,0:T(8,128)S(1)}, u32[]{:S(2)}, u32[]{:S(2)}) %collective-permute-start.40) | collective-permute-done | bytes 327712 | tf_op jit(solution)/shard_map/ppermute | solution.py:861
  214.4 1.5 join.1
  (119 shorter events, 19.6 us)
Async XLA Ops:
  5.1 40.1 %all-to-all-start = ((f32[8,512,128]{2,1,0:T(8,128)}), f32[8,512,128]{2,1,0:T(8,128)}, u32[]{:S(2)}, u32[]{:S(2)}) async-start(f32[8,512,128]{2,1,0:T(8,128)} %weight_pick.1), calls=%async_computation | async-start | bytes 4194304 | tf_op jit(solution)/shard_map/all_to_all | solution.py:781
  15.5 4.0 %collective-permute-start = (f32[2,256,128]{2,1,0:T(8,128)}, f32[2,256,128]{2,1,0:T(8,128)S(1)}, u32[]{:S(2)}, u32[]{:S(2)}) collective-permute-start(f32[2,256,128]{2,1,0:T(8,128)} %get-tuple-element.58), channel_id=1, source_target_pairs={{0,1},{1,0},{2,3},{3,2},{4,5},{5,4},{6,7},{7,6},{8,9},{9,8},{10,11... | collective-permute-start | bytes 786440 | tf_op jit(solution)/shard_map/ppermute | solution.py:795
  16.0 26.2 %collective-permute-start.1 = (f32[2,256,128]{2,1,0:T(8,128)}, f32[2,256,128]{2,1,0:T(8,128)S(1)}, u32[]{:S(2)}, u32[]{:S(2)}) collective-permute-start(f32[2,256,128]{2,1,0:T(8,128)} %get-tuple-element.59), channel_id=1, source_target_pairs={{0,2},{1,3},{2,0},{3,1},{4,6},{5,7},{6,4},{7,5},{8,10},{9,11},{10,... | collective-permute-start | bytes 786440 | tf_op jit(solution)/shard_map/ppermute | solution.py:795
  17.6 36.3 %collective-permute-start.2 = (f32[2,256,128]{2,1,0:T(8,128)}, f32[2,256,128]{2,1,0:T(8,128)}, u32[]{:S(2)}, u32[]{:S(2)}) collective-permute-start(f32[2,256,128]{2,1,0:T(8,128)} %get-tuple-element.60), channel_id=1, source_target_pairs={{0,3},{1,2},{2,1},{3,0},{4,7},{5,6},{6,5},{7,4},{8,11},{9,10},{10,... | collective-permute-start | bytes 786440 | tf_op jit(solution)/shard_map/ppermute | solution.py:795
  17.7 36.2 %collective-permute-start.3 = (f32[2,256,128]{2,1,0:T(8,128)}, f32[2,256,128]{2,1,0:T(8,128)}, u32[]{:S(2)}, u32[]{:S(2)}) collective-permute-start(f32[2,256,128]{2,1,0:T(8,128)} %get-tuple-element.61), channel_id=1, source_target_pairs={{0,4},{1,5},{2,6},{3,7},{4,0},{5,1},{6,2},{7,3},{8,12},{9,13},{10,... | collective-permute-start | bytes 786440 | tf_op jit(solution)/shard_map/ppermute | solution.py:795
  19.4 34.5 %collective-permute-start.4 = (f32[2,256,128]{2,1,0:T(8,128)}, f32[2,256,128]{2,1,0:T(8,128)}, u32[]{:S(2)}, u32[]{:S(2)}) collective-permute-start(f32[2,256,128]{2,1,0:T(8,128)} %get-tuple-element.62), channel_id=1, source_target_pairs={{0,5},{1,4},{2,7},{3,6},{4,1},{5,0},{6,3},{7,2},{8,13},{9,12},{10,... | collective-permute-start | bytes 786440 | tf_op jit(solution)/shard_map/ppermute | solution.py:795
  19.5 35.0 %collective-permute-start.5 = (f32[2,256,128]{2,1,0:T(8,128)}, f32[2,256,128]{2,1,0:T(8,128)}, u32[]{:S(2)}, u32[]{:S(2)}) collective-permute-start(f32[2,256,128]{2,1,0:T(8,128)} %get-tuple-element.63), channel_id=1, source_target_pairs={{0,6},{1,7},{2,4},{3,5},{4,2},{5,3},{6,0},{7,1},{8,14},{9,15},{10,... | collective-permute-start | bytes 786440 | tf_op jit(solution)/shard_map/ppermute | solution.py:795
  42.9 16.2 %collective-permute-start.6 = (f32[2,256,128]{2,1,0:T(8,128)}, f32[2,256,128]{2,1,0:T(8,128)}, u32[]{:S(2)}, u32[]{:S(2)}) collective-permute-start(f32[2,256,128]{2,1,0:T(8,128)} %get-tuple-element.64), channel_id=1, source_target_pairs={{0,7},{1,6},{2,5},{3,4},{4,3},{5,2},{6,1},{7,0},{8,15},{9,14},{10,... | collective-permute-start | bytes 786440 | tf_op jit(solution)/shard_map/ppermute | solution.py:795
  45.1 13.9 %copy-start = (bf16[2,256,256]{2,1,0:T(8,128)(2,1)S(1)}, bf16[2,256,256]{2,1,0:T(8,128)(2,1)}, u32[]{:S(2)}) copy-start(bf16[2,256,256]{2,1,0:T(8,128)(2,1)} %constant.64.clone.refs_9_) | copy-start | bytes 786436
  45.1 13.9 %copy-start.1 = (bf16[2,256,256]{2,1,0:T(8,128)(2,1)S(1)}, bf16[2,256,256]{2,1,0:T(8,128)(2,1)}, u32[]{:S(2)}) copy-start(bf16[2,256,256]{2,1,0:T(8,128)(2,1)} %constant.63.clone.refs_8_) | copy-start | bytes 786436
  45.2 13.9 %copy-start.2 = (f32[2,256,128]{2,1,0:T(8,128)S(1)}, f32[2,256,128]{2,1,0:T(8,128)}, u32[]{:S(2)}) copy-start(f32[2,256,128]{2,1,0:T(8,128)} %get-tuple-element.57.refs_0_) | copy-start | bytes 786436
  45.2 13.8 %copy-start.4 = (f32[2,256,128]{2,1,0:T(8,128)S(1)}, f32[2,256,128]{2,1,0:T(8,128)}, u32[]{:S(2)}) copy-start(f32[2,256,128]{2,1,0:T(8,128)} %copy-done.3) | copy-start | bytes 786436
  68.0 3.9 %collective-permute-start.7 = (f32[2,128,128]{2,1,0:T(8,128)S(1)}, f32[2,128,128]{2,1,0:T(8,128)S(1)}, u32[]{:S(2)}, u32[]{:S(2)}) collective-permute-start(f32[2,128,128]{2,1,0:T(8,128)S(1)} %get-tuple-element.68), channel_id=1, source_target_pairs={{0,1},{1,0},{2,3},{3,2},{4,5},{5,4},{6,7},{7,6},{8,9},{9,8},{10,11... | collective-permute-start | bytes 393224 | tf_op jit(solution)/shard_map/ppermute | solution.py:795
  68.4 6.3 %collective-permute-start.8 = (f32[2,128,128]{2,1,0:T(8,128)S(1)}, f32[2,128,128]{2,1,0:T(8,128)S(1)}, u32[]{:S(2)}, u32[]{:S(2)}) collective-permute-start(f32[2,128,128]{2,1,0:T(8,128)S(1)} %get-tuple-element.69), channel_id=1, source_target_pairs={{0,2},{1,3},{2,0},{3,1},{4,6},{5,7},{6,4},{7,5},{8,10},{9,11},{10,... | collective-permute-start | bytes 393224 | tf_op jit(solution)/shard_map/ppermute | solution.py:795
  68.9 7.0 %collective-permute-start.9 = (f32[2,128,128]{2,1,0:T(8,128)S(1)}, f32[2,128,128]{2,1,0:T(8,128)S(1)}, u32[]{:S(2)}, u32[]{:S(2)}) collective-permute-start(f32[2,128,128]{2,1,0:T(8,128)S(1)} %get-tuple-element.70), channel_id=1, source_target_pairs={{0,3},{1,2},{2,1},{3,0},{4,7},{5,6},{6,5},{7,4},{8,11},{9,10},{10,... | collective-permute-start | bytes 393224 | tf_op jit(solution)/shard_map/ppermute | solution.py:795
  69.9 7.8 %collective-permute-start.10 = (f32[2,128,128]{2,1,0:T(8,128)S(1)}, f32[2,128,128]{2,1,0:T(8,128)S(1)}, u32[]{:S(2)}, u32[]{:S(2)}) collective-permute-start(f32[2,128,128]{2,1,0:T(8,128)S(1)} %get-tuple-element.71), channel_id=1, source_target_pairs={{0,4},{1,5},{2,6},{3,7},{4,0},{5,1},{6,2},{7,3},{8,12},{9,13},{10,... | collective-permute-start | bytes 393224 | tf_op jit(solution)/shard_map/ppermute | solution.py:795
  70.5 13.5 %collective-permute-start.11 = (f32[2,128,128]{2,1,0:T(8,128)S(1)}, f32[2,128,128]{2,1,0:T(8,128)S(1)}, u32[]{:S(2)}, u32[]{:S(2)}) collective-permute-start(f32[2,128,128]{2,1,0:T(8,128)S(1)} %get-tuple-element.72), channel_id=1, source_target_pairs={{0,5},{1,4},{2,7},{3,6},{4,1},{5,0},{6,3},{7,2},{8,13},{9,12},{10,... | collective-permute-start | bytes 393224 | tf_op jit(solution)/shard_map/ppermute | solution.py:795
  71.9 14.2 %copy-start.11 = (f32[2,128,128]{2,1,0:T(8,128)}, f32[2,128,128]{2,1,0:T(8,128)S(1)}, u32[]{:S(2)}) copy-start(f32[2,128,128]{2,1,0:T(8,128)S(1)} %collective-permute-done.7.refs_1_) | copy-start | bytes 393220
  71.9 12.8 %collective-permute-start.12 = (f32[2,128,128]{2,1,0:T(8,128)S(1)}, f32[2,128,128]{2,1,0:T(8,128)S(1)}, u32[]{:S(2)}, u32[]{:S(2)}) collective-permute-start(f32[2,128,128]{2,1,0:T(8,128)S(1)} %get-tuple-element.73), channel_id=1, source_target_pairs={{0,6},{1,7},{2,4},{3,5},{4,2},{5,3},{6,0},{7,1},{8,14},{9,15},{10,... | collective-permute-start | bytes 393224 | tf_op jit(solution)/shard_map/ppermute | solution.py:795
  74.7 10.4 %collective-permute-start.13 = (f32[2,128,128]{2,1,0:T(8,128)S(1)}, f32[2,128,128]{2,1,0:T(8,128)S(1)}, u32[]{:S(2)}, u32[]{:S(2)}) collective-permute-start(f32[2,128,128]{2,1,0:T(8,128)S(1)} %get-tuple-element.74), channel_id=1, source_target_pairs={{0,7},{1,6},{2,5},{3,4},{4,3},{5,2},{6,1},{7,0},{8,15},{9,14},{10,... | collective-permute-start | bytes 393224 | tf_op jit(solution)/shard_map/ppermute | solution.py:795
  75.9 14.3 %collective-permute-start.17 = (f32[2,128,128]{2,1,0:T(8,128)S(1)}, f32[2,128,128]{2,1,0:T(8,128)S(1)}, u32[]{:S(2)}, u32[]{:S(2)}) collective-permute-start(f32[2,128,128]{2,1,0:T(8,128)S(1)} %get-tuple-element.77), channel_id=1, source_target_pairs={{0,1},{1,0},{2,3},{3,2},{4,5},{5,4},{6,7},{7,6},{8,9},{9,8},{10,11... | collective-permute-start | bytes 393224 | tf_op jit(solution)/shard_map/ppermute | solution.py:795
  77.6 14.7 %collective-permute-start.18 = (f32[2,128,128]{2,1,0:T(8,128)S(1)}, f32[2,128,128]{2,1,0:T(8,128)S(1)}, u32[]{:S(2)}, u32[]{:S(2)}) collective-permute-start(f32[2,128,128]{2,1,0:T(8,128)S(1)} %get-tuple-element.78), channel_id=1, source_target_pairs={{0,2},{1,3},{2,0},{3,1},{4,6},{5,7},{6,4},{7,5},{8,10},{9,11},{10,... | collective-permute-start | bytes 393224 | tf_op jit(solution)/shard_map/ppermute | solution.py:795
  84.0 10.6 %collective-permute-start.19 = (f32[2,128,128]{2,1,0:T(8,128)S(1)}, f32[2,128,128]{2,1,0:T(8,128)S(1)}, u32[]{:S(2)}, u32[]{:S(2)}) collective-permute-start(f32[2,128,128]{2,1,0:T(8,128)S(1)} %get-tuple-element.79), channel_id=1, source_target_pairs={{0,3},{1,2},{2,1},{3,0},{4,7},{5,6},{6,5},{7,4},{8,11},{9,10},{10,... | collective-permute-start | bytes 393224 | tf_op jit(solution)/shard_map/ppermute | solution.py:795
  84.6 14.2 %collective-permute-start.20 = (f32[2,128,128]{2,1,0:T(8,128)S(1)}, f32[2,128,128]{2,1,0:T(8,128)S(1)}, u32[]{:S(2)}, u32[]{:S(2)}) collective-permute-start(f32[2,128,128]{2,1,0:T(8,128)S(1)} %get-tuple-element.80), channel_id=1, source_target_pairs={{0,4},{1,5},{2,6},{3,7},{4,0},{5,1},{6,2},{7,3},{8,12},{9,13},{10,... | collective-permute-start | bytes 393224 | tf_op jit(solution)/shard_map/ppermute | solution.py:795
  85.1 13.8 %collective-permute-start.21 = (f32[2,128,128]{2,1,0:T(8,128)S(1)}, f32[2,128,128]{2,1,0:T(8,128)S(1)}, u32[]{:S(2)}, u32[]{:S(2)}) collective-permute-start(f32[2,128,128]{2,1,0:T(8,128)S(1)} %get-tuple-element.81), channel_id=1, source_target_pairs={{0,5},{1,4},{2,7},{3,6},{4,1},{5,0},{6,3},{7,2},{8,13},{9,12},{10,... | collective-permute-start | bytes 393224 | tf_op jit(solution)/shard_map/ppermute | solution.py:795
  90.2 9.3 %collective-permute-start.22 = (f32[2,128,128]{2,1,0:T(8,128)S(1)}, f32[2,128,128]{2,1,0:T(8,128)S(1)}, u32[]{:S(2)}, u32[]{:S(2)}) collective-permute-start(f32[2,128,128]{2,1,0:T(8,128)S(1)} %get-tuple-element.82), channel_id=1, source_target_pairs={{0,6},{1,7},{2,4},{3,5},{4,2},{5,3},{6,0},{7,1},{8,14},{9,15},{10,... | collective-permute-start | bytes 393224 | tf_op jit(solution)/shard_map/ppermute | solution.py:795
  92.4 7.5 %collective-permute-start.23 = (f32[2,128,128]{2,1,0:T(8,128)S(1)}, f32[2,128,128]{2,1,0:T(8,128)S(1)}, u32[]{:S(2)}, u32[]{:S(2)}) collective-permute-start(f32[2,128,128]{2,1,0:T(8,128)S(1)} %get-tuple-element.83), channel_id=1, source_target_pairs={{0,7},{1,6},{2,5},{3,4},{4,3},{5,2},{6,1},{7,0},{8,15},{9,14},{10,... | collective-permute-start | bytes 393224 | tf_op jit(solution)/shard_map/ppermute | solution.py:795
  94.6 16.1 %collective-permute-start.16 = (f32[136,512]{1,0:T(8,128)S(1)}, f32[136,512]{1,0:T(8,128)S(1)}, u32[]{:S(2)}, u32[]{:S(2)}) collective-permute-start(f32[136,512]{1,0:T(8,128)S(1)} %get-tuple-element.116), channel_id=1, source_target_pairs={{0,24},{8,16},{16,8},{24,0},{1,25},{9,17},{17,9},{25,1},{2,26},{10... | collective-permute-start | bytes 835592 | tf_op jit(solution)/shard_map/ppermute | solution.py:861
  98.8 25.4 %collective-permute-start.15 = (f32[136,512]{1,0:T(8,128)S(1)}, f32[136,512]{1,0:T(8,128)S(1)}, u32[]{:S(2)}, u32[]{:S(2)}) collective-permute-start(f32[136,512]{1,0:T(8,128)S(1)} %get-tuple-element.117), channel_id=1, source_target_pairs={{0,16},{8,24},{16,0},{24,8},{1,17},{9,25},{17,1},{25,9},{2,18},{10... | collective-permute-start | bytes 835592 | tf_op jit(solution)/shard_map/ppermute | solution.py:861
  98.9 25.4 %collective-permute-start.14 = (f32[136,512]{1,0:T(8,128)S(1)}, f32[136,512]{1,0:T(8,128)S(1)}, u32[]{:S(2)}, u32[]{:S(2)}) collective-permute-start(f32[136,512]{1,0:T(8,128)S(1)} %get-tuple-element.118), channel_id=1, source_target_pairs={{0,8},{8,0},{16,24},{24,16},{1,9},{9,1},{17,25},{25,17},{2,10},{10... | collective-permute-start | bytes 835592 | tf_op jit(solution)/shard_map/ppermute | solution.py:861
  105.9 18.4 %collective-permute-start.24 = (f32[136,512]{1,0:T(8,128)S(1)}, f32[136,512]{1,0:T(8,128)S(1)}, u32[]{:S(2)}, u32[]{:S(2)}) collective-permute-start(f32[136,512]{1,0:T(8,128)S(1)} %get-tuple-element.115), channel_id=1, source_target_pairs={{0,8},{8,0},{16,24},{24,16},{1,9},{9,1},{17,25},{25,17},{2,10},{10... | collective-permute-start | bytes 835592 | tf_op jit(solution)/shard_map/ppermute | solution.py:861
  108.2 29.1 %collective-permute-start.28 = (f32[136,512]{1,0:T(8,128)S(1)}, f32[136,512]{1,0:T(8,128)S(1)}, u32[]{:S(2)}, u32[]{:S(2)}) collective-permute-start(f32[136,512]{1,0:T(8,128)S(1)} %get-tuple-element.112), channel_id=1, source_target_pairs={{0,24},{8,16},{16,8},{24,0},{1,25},{9,17},{17,9},{25,1},{2,26},{10... | collective-permute-start | bytes 835592 | tf_op jit(solution)/shard_map/ppermute | solution.py:861
  110.7 36.0 %collective-permute-start.27 = (f32[136,512]{1,0:T(8,128)S(1)}, f32[136,512]{1,0:T(8,128)S(1)}, u32[]{:S(2)}, u32[]{:S(2)}) collective-permute-start(f32[136,512]{1,0:T(8,128)S(1)} %get-tuple-element.113), channel_id=1, source_target_pairs={{0,16},{8,24},{16,0},{24,8},{1,17},{9,25},{17,1},{25,9},{2,18},{10... | collective-permute-start | bytes 835592 | tf_op jit(solution)/shard_map/ppermute | solution.py:861
  124.4 3.1 %collective-permute-start.25 = (f32[4,24,512]{2,1,0:T(8,128)S(1)}, f32[4,24,512]{2,1,0:T(8,128)S(1)}, u32[]{:S(2)}, u32[]{:S(2)}) collective-permute-start(f32[4,24,512]{2,1,0:T(8,128)S(1)} %pad_maximum_fusion), channel_id=1, source_target_pairs={{0,1},{1,2},{2,3},{3,4},{4,5},{5,6},{6,7},{8,9},{9,10},{10,11},{11... | collective-permute-start | bytes 589832 | tf_op jit(solution)/shard_map/ppermute | solution.py:880
  126.2 4.6 %collective-permute-start.26 = (f32[4,24,512]{2,1,0:T(8,128)S(1)}, f32[4,24,512]{2,1,0:T(8,128)S(1)}, u32[]{:S(2)}, u32[]{:S(2)}) collective-permute-start(f32[4,24,512]{2,1,0:T(8,128)S(1)} %pad_maximum_fusion.1), channel_id=1, source_target_pairs={{1,0},{2,1},{3,2},{4,3},{5,4},{6,5},{7,6},{9,8},{10,9},{11,10},{12... | collective-permute-start | bytes 589832 | tf_op jit(solution)/shard_map/ppermute | solution.py:881
  154.4 1.2 collective-permute-start.29
  155.7 4.6 %collective-permute-start.32 = (f32[3,8,128]{2,1,0:T(8,128)S(1)}, f32[3,8,128]{2,1,0:T(8,128)S(1)}, u32[]{:S(2)}, u32[]{:S(2)}) collective-permute-start(f32[3,8,128]{2,1,0:T(8,128)S(1)} %max.21), channel_id=1, source_target_pairs={{0,6},{1,7},{2,4},{3,5},{4,2},{5,3},{6,0},{7,1},{8,14},{9,15},{10,... | collective-permute-start | bytes 36872 | tf_op jit(solution)/shard_map/ppermute | solution.py:124
  157.7 3.7 %collective-permute-start.31 = (f32[3,8,128]{2,1,0:T(8,128)S(1)}, f32[3,8,128]{2,1,0:T(8,128)S(1)}, u32[]{:S(2)}, u32[]{:S(2)}) collective-permute-start(f32[3,8,128]{2,1,0:T(8,128)S(1)} %max.21), channel_id=1, source_target_pairs={{0,4},{1,5},{2,6},{3,7},{4,0},{5,1},{6,2},{7,3},{8,12},{9,13},{10,... | collective-permute-start | bytes 36872 | tf_op jit(solution)/shard_map/ppermute | solution.py:124
  158.6 3.7 %collective-permute-start.30 = (f32[3,8,128]{2,1,0:T(8,128)S(1)}, f32[3,8,128]{2,1,0:T(8,128)S(1)}, u32[]{:S(2)}, u32[]{:S(2)}) collective-permute-start(f32[3,8,128]{2,1,0:T(8,128)S(1)} %max.21), channel_id=1, source_target_pairs={{0,2},{1,3},{2,0},{3,1},{4,6},{5,7},{6,4},{7,5},{8,10},{9,11},{10,... | collective-permute-start | bytes 36872 | tf_op jit(solution)/shard_map/ppermute | solution.py:124
  162.3 5.6 %collective-permute-start.35 = (f32[3,8,128]{2,1,0:T(8,128)S(1)}, f32[3,8,128]{2,1,0:T(8,128)S(1)}, u32[]{:S(2)}, u32[]{:S(2)}) collective-permute-start(f32[3,8,128]{2,1,0:T(8,128)S(1)} %maximum_maximum_fusion.1), channel_id=1, source_target_pairs={{0,24},{8,16},{16,8},{24,0},{1,25},{9,17},{17,9},{25,1},{2,26},{10... | collective-permute-start | bytes 36872 | tf_op jit(solution)/shard_map/ppermute | solution.py:124
  164.8 4.6 %collective-permute-start.34 = (f32[3,8,128]{2,1,0:T(8,128)S(1)}, f32[3,8,128]{2,1,0:T(8,128)S(1)}, u32[]{:S(2)}, u32[]{:S(2)}) collective-permute-start(f32[3,8,128]{2,1,0:T(8,128)S(1)} %maximum_maximum_fusion.1), channel_id=1, source_target_pairs={{0,16},{8,24},{16,0},{24,8},{1,17},{9,25},{17,1},{25,9},{2,18},{10... | collective-permute-start | bytes 36872 | tf_op jit(solution)/shard_map/ppermute | solution.py:124
  164.8 4.6 %collective-permute-start.33 = (f32[3,8,128]{2,1,0:T(8,128)S(1)}, f32[3,8,128]{2,1,0:T(8,128)S(1)}, u32[]{:S(2)}, u32[]{:S(2)}) collective-permute-start(f32[3,8,128]{2,1,0:T(8,128)S(1)} %maximum_maximum_fusion.1), channel_id=1, source_target_pairs={{0,8},{8,0},{16,24},{24,16},{1,9},{9,1},{17,25},{25,17},{2,10},{10... | collective-permute-start | bytes 36872 | tf_op jit(solution)/shard_map/ppermute | solution.py:124
  170.3 7.8 %collective-permute-start.36 = (f32[96,512]{1,0:T(8,128)S(1)}, f32[96,512]{1,0:T(8,128)S(1)}, u32[]{:S(2)}, u32[]{:S(2)}) collective-permute-start(f32[96,512]{1,0:T(8,128)S(1)} %get-tuple-element.95), channel_id=1, source_target_pairs={{0,8},{8,0},{16,24},{24,16},{1,9},{9,1},{17,25},{25,17},{2,10},{10... | collective-permute-start | bytes 589832 | tf_op jit(solution)/shard_map/ppermute | solution.py:861
  171.4 14.7 %collective-permute-start.37 = (f32[96,512]{1,0:T(8,128)S(1)}, f32[96,512]{1,0:T(8,128)S(1)}, u32[]{:S(2)}, u32[]{:S(2)}) collective-permute-start(f32[96,512]{1,0:T(8,128)S(1)} %get-tuple-element.96), channel_id=1, source_target_pairs={{0,16},{8,24},{16,0},{24,8},{1,17},{9,25},{17,1},{25,9},{2,18},{10... | collective-permute-start | bytes 589832 | tf_op jit(solution)/shard_map/ppermute | solution.py:861
  172.5 13.7 %collective-permute-start.38 = (f32[96,512]{1,0:T(8,128)S(1)}, f32[96,512]{1,0:T(8,128)S(1)}, u32[]{:S(2)}, u32[]{:S(2)}) collective-permute-start(f32[96,512]{1,0:T(8,128)S(1)} %get-tuple-element.97), channel_id=1, source_target_pairs={{0,24},{8,16},{16,8},{24,0},{1,25},{9,17},{17,9},{25,1},{2,26},{10... | collective-permute-start | bytes 589832 | tf_op jit(solution)/shard_map/ppermute | solution.py:861
  186.2 13.9 %collective-permute-start.39 = (f32[160,512]{1,0:T(8,128)S(1)}, f32[160,512]{1,0:T(8,128)S(1)}, u32[]{:S(2)}, u32[]{:S(2)}) collective-permute-start(f32[160,512]{1,0:T(8,128)S(1)} %get-tuple-element.108), channel_id=1, source_target_pairs={{0,8},{8,0},{16,24},{24,16},{1,9},{9,1},{17,25},{25,17},{2,10},{10... | collective-permute-start | bytes 983048 | tf_op jit(solution)/shard_map/ppermute | solution.py:861
  188.8 25.6 %collective-permute-start.40 = (f32[160,512]{1,0:T(8,128)S(1)}, f32[160,512]{1,0:T(8,128)S(1)}, u32[]{:S(2)}, u32[]{:S(2)}) collective-permute-start(f32[160,512]{1,0:T(8,128)S(1)} %get-tuple-element.109), channel_id=1, source_target_pairs={{0,16},{8,24},{16,0},{24,8},{1,17},{9,25},{17,1},{25,9},{2,18},{10... | collective-permute-start | bytes 983048 | tf_op jit(solution)/shard_map/ppermute | solution.py:861
  189.9 24.5 %collective-permute-start.41 = (f32[160,512]{1,0:T(8,128)S(1)}, f32[160,512]{1,0:T(8,128)S(1)}, u32[]{:S(2)}, u32[]{:S(2)}) collective-permute-start(f32[160,512]{1,0:T(8,128)S(1)} %get-tuple-element.110), channel_id=1, source_target_pairs={{0,24},{8,16},{16,8},{24,0},{1,25},{9,17},{17,9},{25,1},{2,26},{10... | collective-permute-start | bytes 983048 | tf_op jit(solution)/shard_map/ppermute | solution.py:861
  (18 other events, 78.5 us)

commit v7 on v6

--- a/solution.py
+++ b/solution.py
@@ -554,21 +554,25 @@
 
 
 def shrink_body(chans, detail_ref, peak_ref, *out_refs):
-    factors = []
-    for level in range(3):
-        energy = 0.0
+    thresholds = [
+        fractions[level] * jnp.sqrt(jnp.max(peak_ref[level], keepdims=True)) for level in range(3)
+    ]
+    for start in range(0, out_refs[0].shape[0], 16):
+        rows = pl.ds(start, 16)
+        factors = []
+        for level in range(3):
+            energy = 0.0
+            for chan in range(chans):
+                detail = detail_ref[chan, level, rows, :]
+                energy = energy + detail * detail
+            energy = jnp.sqrt(energy)
+            threshold = jnp.broadcast_to(thresholds[level], energy.shape)
+            factors.append(1.0 - threshold / jnp.maximum(energy, threshold))
         for chan in range(chans):
-            detail = detail_ref[chan, level]
-            energy = energy + detail * detail
-        energy = jnp.sqrt(energy)
-        threshold = fractions[level] * jnp.sqrt(jnp.max(peak_ref[level], keepdims=True))
-        threshold = jnp.broadcast_to(threshold, energy.shape)
-        factors.append(1.0 - threshold / jnp.maximum(energy, threshold))
-    for chan in range(chans):
-        total = detail_ref[chan, 3]
-        for level in range(3):
-            total = total + factors[level] * detail_ref[chan, level]
-        out_refs[chan][...] = total
+            total = detail_ref[chan, 3, rows, :]
+            for level in range(3):
+                total = total + factors[level] * detail_ref[chan, level, rows, :]
+            out_refs[chan][rows, :] = total
 
 
 def join_body(me_ref, *refs):
@@ -629,7 +633,7 @@
             held[1, step, rows, :] = pair[1]
         return carry
 
-    lax.fori_loop(0, size // 8, forward, 0, unroll=4)
+    lax.fori_loop(0, size // 8, forward, 0, unroll=8)
     lane_ids = lax.broadcasted_iota(jnp.int32, (size, lanes), 1)
     lone = jnp.zeros((size, lanes), jnp.float32)
     for step in range(steps):
@@ -656,7 +660,7 @@
             made[1, step, rows, :] = pair[1]
         return carry
 
-    lax.fori_loop(0, size // 8, backward, 0, unroll=4)
+    lax.fori_loop(0, size // 8, backward, 0, unroll=8)
     half = each // 2
     for step in range(0, steps, 2):
         block = [
@@ -826,7 +830,7 @@
     part = length // chans
     quarter = height // 4
 
-    def row_inverse(cells, old, blocks):
+    def row_inverse(cells, old, blocks, microseconds):
         rows_spec = pl.BlockSpec((quarter, length), lambda i: (blocks[0] + i * blocks[1], 0))
         whole = lambda *dims: pl.BlockSpec(dims, lambda i: (0,) * len(dims))
         return pl.pallas_call(
@@ -847,7 +851,7 @@
             input_output_aliases={count + 5: 0} if old is not dirty else {},
             compiler_params=pltpu.CompilerParams(vmem_limit_bytes=56 * mebibyte),
             name="row_inverse",
-        cost_estimate=busy(5),
+        cost_estimate=busy(microseconds),
         )(me, *cells, back, spins, values, dirty, old)
 
     def pieces_for(cells):
@@ -866,9 +870,9 @@
         both = lax.optimization_barrier((*earlier, *later))
         return list(both[: len(earlier)]), list(both[len(earlier) :])
 
-    residual, outer = row_inverse(edge, dirty, (0, 3))
+    residual, outer = row_inverse(edge, dirty, (0, 3), 20)
     outer = over_chans(pieces_for(outer))
-    residual, inner = row_inverse(core, residual, (1, 1))
+    residual, inner = row_inverse(core, residual, (1, 1), 5)
     inner = over_chans(pieces_for(inner))
     outer, (inner[1],) = in_order(outer, [inner[1]])
     ahead_pairs = [(i, i + 1) for i in range(count - 1)]
@@ -937,15 +941,10 @@
 
     def shrink(details):
         rows = details.shape[2]
-        thick = rows // 2
         return pl.pallas_call(
             functools.partial(shrink_body, chans),
-            grid=(2,),
-            in_specs=[
-                pl.BlockSpec((chans, 4, thick, part), lambda i: (0, 0, i, 0)),
-                pl.BlockSpec((3, 8, lanes), lambda i: (0, 0, 0)),
-            ],
-            out_specs=[pl.BlockSpec((thick, part), lambda i: (i, 0))] * chans,
+            in_specs=[vmem, vmem],
+            out_specs=[vmem] * chans,
             out_shape=[shape(rows, part)] * chans,
             compiler_params=pltpu.CompilerParams(vmem_limit_bytes=14 * mebibyte),
             name="shrink",

time: 218 us -> 218 us (level)
  no operation moved by 1% of the time
where the time goes in v7:
time: 218 us; the launch traced here: 215 us
  waiting for transfers between devices  93.2 us (43%)
  starting transfers between devices  62.5 us (29%)
  Pallas kernels  51.2 us (23%)
  local copies, waits for them, and re-layouts  5.37 us (2%)
    ppermute x12, waiting for transfers between devices, over_chans(): lax.ppermute(pieces[turn], 'chan', [(i, i ^ turn) for i in range(chans)])  47.8 us
    ppermute x21, waiting for transfers between devices, over_rows(): lax.ppermute(pieces[turn], 'rows', [(i, i ^ turn) for i in range(count)])  35 us
    ppermute x12, starting transfers between devices, over_chans(): lax.ppermute(pieces[turn], 'chan', [(i, i ^ turn) for i in range(chans)])  27.8 us
    ppermute x21, starting transfers between devices, over_rows(): lax.ppermute(pieces[turn], 'rows', [(i, i ^ turn) for i in range(count)])  18.5 us
    pallas_call x2, Pallas kernels, starlet(): pl.pallas_call(functools.partial(starlet_body, chans, spans, fills), in_s...  14.1 us
    pallas_call x1, Pallas kernels, filtered(): whole_call(weight_place_body, [shape(steps, size, lanes), shape(size, lan...  8.69 us
    pallas_call x2, Pallas kernels, row_inverse(): pl.pallas_call(functools.partial(row_inverse_body, steps, count), grid=(2...  8.2 us
    ppermute x7, starting transfers between devices, max_over(): lax.ppermute(cells, axis, [(i, i ^ distance) for i in range(count)])  7.95 us
  transfers between devices with their start and end apart: 43, of which 21 were waited for; matrix products, arithmetic and copies ran while one was open for 2% of the time, Pallas kernels for 14%

profile of v7, /device:TPU:0, one launch (start us, length us, event | category | flops | bytes accessed | tf_op | source)
XLA Modules:
  0.0 215.4 jit_solution(17528770684611599628)
XLA Ops:
  0.6 4.5 %weight_pick.1 = f32[8,512,128]{2,1,0:T(8,128)} custom-call(f32[4,512,256]{2,1,0:T(8,128)} %bitcast.68, bf16[256,256]{1,0:T(8,128)(2,1)} %constant.57.clone.pick_ref), custom_call_target="tpu_custom_call" | custom-call | bytes 14000000 | tf_op jit(solution)/shard_map/weight_pick/pallas_call | solution.py:772
  5.1 5.2 %all-to-all-start = ((f32[8,512,128]{2,1,0:T(8,128)}), f32[8,512,128]{2,1,0:T(8,128)}, u32[]{:S(2)}, u32[]{:S(2)}) async-start(f32[8,512,128]{2,1,0:T(8,128)} %weight_pick.1), calls=%async_computation | async-start | bytes 4194304 | tf_op jit(solution)/shard_map/all_to_all | solution.py:785
  10.3 5.2 %row_forward.1 = (f32[2,256,128]{2,1,0:T(8,128)}, f32[2,256,128]{2,1,0:T(8,128)}, f32[2,256,128]{2,1,0:T(8,128)}, f32[2,256,128]{2,1,0:T(8,128)}, f32[2,256,128]...) custom-call(s32[1]{0:T(128)} %bitcast.5.me_ref, f32[256,2048]{1,0:T(8,128)} %bitcast.64, ...), custom_call_target="tpu_custom_call" | custom-call | bytes 21000000 | tf_op jit(solution)/shard_map/row_forward/pallas_call | solution.py:786
  16.0 1.7 collective-permute-start.1
  17.7 1.7 collective-permute-start.3
  19.5 2.5 %collective-permute-start.5 = (f32[2,256,128]{2,1,0:T(8,128)}, f32[2,256,128]{2,1,0:T(8,128)}, u32[]{:S(2)}, u32[]{:S(2)}) collective-permute-start(f32[2,256,128]{2,1,0:T(8,128)} %get-tuple-element.63), channel_id=1, source_target_pairs={{0,6},{1,7},{2,4},{3,5},{4,2},{5,3},{6,0},{7,1},{8,14},{9,15},{10,... | collective-permute-start | bytes 786440 | tf_op jit(solution)/shard_map/ppermute | solution.py:799
  22.0 20.1 %collective-permute-done.1.refs_2_ = f32[2,256,128]{2,1,0:T(8,128)S(1)} collective-permute-done((f32[2,256,128]{2,1,0:T(8,128)}, f32[2,256,128]{2,1,0:T(8,128)S(1)}, u32[]{:S(2)}, u32[]{:S(2)}) %collective-permute-start.1) | collective-permute-done | bytes 262176 | tf_op jit(solution)/shard_map/ppermute | solution.py:799
  43.2 1.9 select_bitcast_fusion.place_ref
  45.2 8.7 %weight_place.1 = (f32[16,128,128]{2,1,0:T(8,128)S(1)}, f32[128,128]{1,0:T(8,128)S(1)}) custom-call(f32[8,512,128]{2,1,0:T(8,128)} %all-to-all-done.in_ref, bf16[1024,1152]{1,0:T(8,128)(2,1)S(1)} %select_bitcast_fusion.place_ref, bf16[128,128]{1,0:T(8,128)(2,1)S(1)} %copy-done.7), custom_call_target="tpu_custom_call" | custom-call | bytes 35000000 | tf_op jit(solution)/shard_map/weight_place/pallas_call | solution.py:805
  54.5 4.5 %collective-permute-done.6.refs_7_ = f32[2,256,128]{2,1,0:T(8,128)} collective-permute-done((f32[2,256,128]{2,1,0:T(8,128)}, f32[2,256,128]{2,1,0:T(8,128)}, u32[]{:S(2)}, u32[]{:S(2)}) %collective-permute-start.6) | collective-permute-done | bytes 262176 | tf_op jit(solution)/shard_map/ppermute | solution.py:799
  59.0 7.4 %column_filter.1 = (f32[2,128,128]{2,1,0:T(8,128)S(1)}, f32[2,128,128]{2,1,0:T(8,128)S(1)}, f32[2,128,128]{2,1,0:T(8,128)S(1)}, f32[2,128,128]{2,1,0:T(8,128)S(1...) custom-call(s32[1]{0:T(128)} %bitcast.5.me_ref, ...), custom_call_target="tpu_custom_call" | custom-call | bytes 35000000 | tf_op jit(solution)/shard_map/column_filter/pallas_call | solution.py:812
  70.3 1.4 collective-permute-start.11
  72.1 2.4 %collective-permute-done.8.refs_2_ = f32[2,128,128]{2,1,0:T(8,128)S(1)} collective-permute-done((f32[2,128,128]{2,1,0:T(8,128)S(1)}, f32[2,128,128]{2,1,0:T(8,128)S(1)}, u32[]{:S(2)}, u32[]{:S(2)}) %collective-permute-start.8) | collective-permute-done | bytes 131104 | tf_op jit(solution)/shard_map/ppermute | solution.py:799
  74.5 1.2 collective-permute-done.9.refs_3_
  75.7 1.7 collective-permute-start.17
  78.0 5.8 %collective-permute-done.11.refs_5_ = f32[2,128,128]{2,1,0:T(8,128)S(1)} collective-permute-done((f32[2,128,128]{2,1,0:T(8,128)S(1)}, f32[2,128,128]{2,1,0:T(8,128)S(1)}, u32[]{:S(2)}, u32[]{:S(2)}) %collective-permute-start.11) | collective-permute-done | bytes 131104 | tf_op jit(solution)/shard_map/ppermute | solution.py:799
  85.9 4.1 %row_inverse.2 = (f32[256,2048]{1,0:T(8,128)}, f32[4,136,512]{2,1,0:T(8,128)}) custom-call(s32[1]{0:T(128)} %bitcast.5.me_ref, f32[2,128,128]{2,1,0:T(8,128)} %copy-done.6, f32[2,128,128]{2,1,0:T(8,128)} %copy-done.11, f32[2,128,128]{2,1,0:T(8,128)} %copy-done.12, f32[2,128,128]{2,1,0:T(8,128)} %copy-done.13, f32[2,128,128]{2,1,0:T(8,128)} %copy-done.14, ...), custom_call_target="tpu_custom_call" | custom-call | bytes 70000000 | tf_op jit(solution)/shard_map/row_inverse/pallas_call | solution.py:836
  90.1 2.1 collective-permute-start.22
  93.1 1.3 dynamic-slice_bitcast_fusion.4
  94.4 4.2 %collective-permute-start.16 = (f32[136,512]{1,0:T(8,128)S(1)}, f32[136,512]{1,0:T(8,128)S(1)}, u32[]{:S(2)}, u32[]{:S(2)}) collective-permute-start(f32[136,512]{1,0:T(8,128)S(1)} %get-tuple-element.116), channel_id=1, source_target_pairs={{0,24},{8,16},{16,8},{24,0},{1,25},{9,17},{17,9},{25,1},{2,26},{10... | collective-permute-start | bytes 835592 | tf_op jit(solution)/shard_map/ppermute | solution.py:865
  100.3 4.1 %row_inverse.3 = (f32[256,2048]{1,0:T(8,128)}, f32[4,136,512]{2,1,0:T(8,128)}) custom-call(s32[1]{0:T(128)} %bitcast.5.me_ref, f32[2,128,128]{2,1,0:T(8,128)} %copy-done.5, f32[2,128,128]{2,1,0:T(8,128)} %copy-done.9, f32[2,128,128]{2,1,0:T(8,128)} %copy-done.10, f32[2,128,128]{2,1,0:T(8,128)} %copy-done.17, ...), custom_call_target="tpu_custom_call", output_to_operand_aliasing={{0}: (13, {})} | custom-call | bytes 17500000 | tf_op jit(solution)/shard_map/row_inverse/pallas_call | solution.py:836
  104.4 1.3 dynamic-slice_bitcast_fusion
  105.7 2.2 %collective-permute-start.24 = (f32[136,512]{1,0:T(8,128)S(1)}, f32[136,512]{1,0:T(8,128)S(1)}, u32[]{:S(2)}, u32[]{:S(2)}) collective-permute-start(f32[136,512]{1,0:T(8,128)S(1)} %get-tuple-element.115), channel_id=1, source_target_pairs={{0,8},{8,0},{16,24},{24,16},{1,9},{9,1},{17,25},{25,17},{2,10},{10... | collective-permute-start | bytes 835592 | tf_op jit(solution)/shard_map/ppermute | solution.py:865
  108.0 2.5 %collective-permute-start.28 = (f32[136,512]{1,0:T(8,128)S(1)}, f32[136,512]{1,0:T(8,128)S(1)}, u32[]{:S(2)}, u32[]{:S(2)}) collective-permute-start(f32[136,512]{1,0:T(8,128)S(1)} %get-tuple-element.112), channel_id=1, source_target_pairs={{0,24},{8,16},{16,8},{24,0},{1,25},{9,17},{17,9},{25,1},{2,26},{10... | collective-permute-start | bytes 835592 | tf_op jit(solution)/shard_map/ppermute | solution.py:865
  110.5 8.6 %collective-permute-start.27 = (f32[136,512]{1,0:T(8,128)S(1)}, f32[136,512]{1,0:T(8,128)S(1)}, u32[]{:S(2)}, u32[]{:S(2)}) collective-permute-start(f32[136,512]{1,0:T(8,128)S(1)} %get-tuple-element.113), channel_id=1, source_target_pairs={{0,16},{8,24},{16,0},{24,8},{1,17},{9,25},{17,1},{25,9},{2,18},{10... | collective-permute-start | bytes 835592 | tf_op jit(solution)/shard_map/ppermute | solution.py:865
  119.1 4.9 %collective-permute-done.15.refs_2_ = f32[136,512]{1,0:T(8,128)S(1)} collective-permute-done((f32[136,512]{1,0:T(8,128)S(1)}, f32[136,512]{1,0:T(8,128)S(1)}, u32[]{:S(2)}, u32[]{:S(2)}) %collective-permute-start.15) | collective-permute-done | bytes 278560 | tf_op jit(solution)/shard_map/ppermute | solution.py:865
  124.2 1.7 collective-permute-start.25
  126.0 1.3 collective-permute-start.26
  127.3 3.3 %collective-permute-done.26 = f32[4,24,512]{2,1,0:T(8,128)S(1)} collective-permute-done((f32[4,24,512]{2,1,0:T(8,128)S(1)}, f32[4,24,512]{2,1,0:T(8,128)S(1)}, u32[]{:S(2)}, u32[]{:S(2)}) %collective-permute-start.26) | collective-permute-done | bytes 196640 | tf_op jit(solution)/shard_map/ppermute | solution.py:885
  130.7 6.4 %starlet.2 = (f32[4,4,96,512]{3,2,1,0:T(8,128)S(1)}, f32[3,8,128]{2,1,0:T(8,128)S(1)}) custom-call(s32[4]{0:T(128)S(1)} %add_convert_fusion.ends_ref, f32[3,8,128]{2,1,0:T(8,128)S(1)} %broadcast_in_dim.9.before_ref, f32[136,512]{1,0:T(8,128)S(1)} %get-tuple-element.86.refs_0_, f32[136,512]{1,0:T(8,128)S(1)} %collective-permute-done.14.refs_1_, ...), custom_call_target="tpu_custom_call" | custom-call | bytes 42000000 | tf_op jit(solution)/shard_map/starlet/pallas_call | solution.py:896
  137.1 9.4 %collective-permute-done.27.refs_6_ = f32[136,512]{1,0:T(8,128)S(1)} collective-permute-done((f32[136,512]{1,0:T(8,128)S(1)}, f32[136,512]{1,0:T(8,128)S(1)}, u32[]{:S(2)}, u32[]{:S(2)}) %collective-permute-start.27) | collective-permute-done | bytes 278560 | tf_op jit(solution)/shard_map/ppermute | solution.py:865
  146.5 7.7 %starlet.3 = (f32[4,4,160,512]{3,2,1,0:T(8,128)S(1)}, f32[3,8,128]{2,1,0:T(8,128)S(1)}) custom-call(s32[4]{0:T(128)S(1)} %add_convert_fusion.ends_ref, f32[3,8,128]{2,1,0:T(8,128)S(1)} %get-tuple-element.91.before_ref, f32[136,512]{1,0:T(8,128)S(1)} %get-tuple-element.86.refs_0_, f32[136,512]{1,0:T(8,128)S(1)} %collective-permute-done.14.refs_1_, ...), custom_call_target="tpu_custom_call" | custom-call | bytes 42000000 | tf_op jit(solution)/shard_map/starlet/pallas_call | solution.py:896
  154.3 1.2 collective-permute-done.29
  155.5 2.1 collective-permute-start.32
  160.1 1.2 collective-permute-done.31
  162.1 2.5 %collective-permute-start.35 = (f32[3,8,128]{2,1,0:T(8,128)S(1)}, f32[3,8,128]{2,1,0:T(8,128)S(1)}, u32[]{:S(2)}, u32[]{:S(2)}) collective-permute-start(f32[3,8,128]{2,1,0:T(8,128)S(1)} %maximum_maximum_fusion.1), channel_id=1, source_target_pairs={{0,24},{8,16},{16,8},{24,0},{1,25},{9,17},{17,9},{25,1},{2,26},{10... | collective-permute-start | bytes 36872 | tf_op jit(solution)/shard_map/ppermute | solution.py:124
  164.6 1.9 collective-permute-start.33
  166.5 1.2 collective-permute-done.35
  167.7 1.5 collective-permute-done.34
  172.0 2.3 %collective-permute-start.38 = (f32[96,512]{1,0:T(8,128)S(1)}, f32[96,512]{1,0:T(8,128)S(1)}, u32[]{:S(2)}, u32[]{:S(2)}) collective-permute-start(f32[96,512]{1,0:T(8,128)S(1)} %get-tuple-element.97), channel_id=1, source_target_pairs={{0,24},{8,16},{16,8},{24,0},{1,25},{9,17},{17,9},{25,1},{2,26},{10... | collective-permute-start | bytes 589832 | tf_op jit(solution)/shard_map/ppermute | solution.py:865
  175.2 2.4 %collective-permute-done.36.refs_1_ = f32[96,512]{1,0:T(8,128)S(1)} collective-permute-done((f32[96,512]{1,0:T(8,128)S(1)}, f32[96,512]{1,0:T(8,128)S(1)}, u32[]{:S(2)}, u32[]{:S(2)}) %collective-permute-start.36) | collective-permute-done | bytes 196640 | tf_op jit(solution)/shard_map/ppermute | solution.py:865
  177.6 8.0 %collective-permute-done.37.refs_2_ = f32[96,512]{1,0:T(8,128)S(1)} collective-permute-done((f32[96,512]{1,0:T(8,128)S(1)}, f32[96,512]{1,0:T(8,128)S(1)}, u32[]{:S(2)}, u32[]{:S(2)}) %collective-permute-start.37) | collective-permute-done | bytes 196640 | tf_op jit(solution)/shard_map/ppermute | solution.py:865
  185.7 2.7 %collective-permute-start.39 = (f32[160,512]{1,0:T(8,128)S(1)}, f32[160,512]{1,0:T(8,128)S(1)}, u32[]{:S(2)}, u32[]{:S(2)}) collective-permute-start(f32[160,512]{1,0:T(8,128)S(1)} %get-tuple-element.108), channel_id=1, source_target_pairs={{0,8},{8,0},{16,24},{24,16},{1,9},{9,1},{17,25},{25,17},{2,10},{10... | collective-permute-start | bytes 983048 | tf_op jit(solution)/shard_map/ppermute | solution.py:865
  188.3 1.1 collective-permute-start.40
  189.4 1.5 collective-permute-start.41
  190.9 8.8 %collective-permute-done.39.refs_5_ = f32[160,512]{1,0:T(8,128)S(1)} collective-permute-done((f32[160,512]{1,0:T(8,128)S(1)}, f32[160,512]{1,0:T(8,128)S(1)}, u32[]{:S(2)}, u32[]{:S(2)}) %collective-permute-start.39) | collective-permute-done | bytes 327712 | tf_op jit(solution)/shard_map/ppermute | solution.py:865
  199.7 14.3 %collective-permute-done.40.refs_6_ = f32[160,512]{1,0:T(8,128)S(1)} collective-permute-done((f32[160,512]{1,0:T(8,128)S(1)}, f32[160,512]{1,0:T(8,128)S(1)}, u32[]{:S(2)}, u32[]{:S(2)}) %collective-permute-start.40) | collective-permute-done | bytes 327712 | tf_op jit(solution)/shard_map/ppermute | solution.py:865
  213.9 1.5 join.1
  (119 shorter events, 19.2 us)
Async XLA Ops:
  5.1 40.1 %all-to-all-start = ((f32[8,512,128]{2,1,0:T(8,128)}), f32[8,512,128]{2,1,0:T(8,128)}, u32[]{:S(2)}, u32[]{:S(2)}) async-start(f32[8,512,128]{2,1,0:T(8,128)} %weight_pick.1), calls=%async_computation | async-start | bytes 4194304 | tf_op jit(solution)/shard_map/all_to_all | solution.py:785
  15.5 4.0 %collective-permute-start = (f32[2,256,128]{2,1,0:T(8,128)}, f32[2,256,128]{2,1,0:T(8,128)S(1)}, u32[]{:S(2)}, u32[]{:S(2)}) collective-permute-start(f32[2,256,128]{2,1,0:T(8,128)} %get-tuple-element.58), channel_id=1, source_target_pairs={{0,1},{1,0},{2,3},{3,2},{4,5},{5,4},{6,7},{7,6},{8,9},{9,8},{10,11... | collective-permute-start | bytes 786440 | tf_op jit(solution)/shard_map/ppermute | solution.py:799
  16.0 26.2 %collective-permute-start.1 = (f32[2,256,128]{2,1,0:T(8,128)}, f32[2,256,128]{2,1,0:T(8,128)S(1)}, u32[]{:S(2)}, u32[]{:S(2)}) collective-permute-start(f32[2,256,128]{2,1,0:T(8,128)} %get-tuple-element.59), channel_id=1, source_target_pairs={{0,2},{1,3},{2,0},{3,1},{4,6},{5,7},{6,4},{7,5},{8,10},{9,11},{10,... | collective-permute-start | bytes 786440 | tf_op jit(solution)/shard_map/ppermute | solution.py:799
  17.6 36.3 %collective-permute-start.2 = (f32[2,256,128]{2,1,0:T(8,128)}, f32[2,256,128]{2,1,0:T(8,128)}, u32[]{:S(2)}, u32[]{:S(2)}) collective-permute-start(f32[2,256,128]{2,1,0:T(8,128)} %get-tuple-element.60), channel_id=1, source_target_pairs={{0,3},{1,2},{2,1},{3,0},{4,7},{5,6},{6,5},{7,4},{8,11},{9,10},{10,... | collective-permute-start | bytes 786440 | tf_op jit(solution)/shard_map/ppermute | solution.py:799
  17.7 36.2 %collective-permute-start.3 = (f32[2,256,128]{2,1,0:T(8,128)}, f32[2,256,128]{2,1,0:T(8,128)}, u32[]{:S(2)}, u32[]{:S(2)}) collective-permute-start(f32[2,256,128]{2,1,0:T(8,128)} %get-tuple-element.61), channel_id=1, source_target_pairs={{0,4},{1,5},{2,6},{3,7},{4,0},{5,1},{6,2},{7,3},{8,12},{9,13},{10,... | collective-permute-start | bytes 786440 | tf_op jit(solution)/shard_map/ppermute | solution.py:799
  19.4 34.5 %collective-permute-start.4 = (f32[2,256,128]{2,1,0:T(8,128)}, f32[2,256,128]{2,1,0:T(8,128)}, u32[]{:S(2)}, u32[]{:S(2)}) collective-permute-start(f32[2,256,128]{2,1,0:T(8,128)} %get-tuple-element.62), channel_id=1, source_target_pairs={{0,5},{1,4},{2,7},{3,6},{4,1},{5,0},{6,3},{7,2},{8,13},{9,12},{10,... | collective-permute-start | bytes 786440 | tf_op jit(solution)/shard_map/ppermute | solution.py:799
  19.5 35.0 %collective-permute-start.5 = (f32[2,256,128]{2,1,0:T(8,128)}, f32[2,256,128]{2,1,0:T(8,128)}, u32[]{:S(2)}, u32[]{:S(2)}) collective-permute-start(f32[2,256,128]{2,1,0:T(8,128)} %get-tuple-element.63), channel_id=1, source_target_pairs={{0,6},{1,7},{2,4},{3,5},{4,2},{5,3},{6,0},{7,1},{8,14},{9,15},{10,... | collective-permute-start | bytes 786440 | tf_op jit(solution)/shard_map/ppermute | solution.py:799
  42.9 16.2 %collective-permute-start.6 = (f32[2,256,128]{2,1,0:T(8,128)}, f32[2,256,128]{2,1,0:T(8,128)}, u32[]{:S(2)}, u32[]{:S(2)}) collective-permute-start(f32[2,256,128]{2,1,0:T(8,128)} %get-tuple-element.64), channel_id=1, source_target_pairs={{0,7},{1,6},{2,5},{3,4},{4,3},{5,2},{6,1},{7,0},{8,15},{9,14},{10,... | collective-permute-start | bytes 786440 | tf_op jit(solution)/shard_map/ppermute | solution.py:799
  45.1 13.9 %copy-start = (bf16[2,256,256]{2,1,0:T(8,128)(2,1)S(1)}, bf16[2,256,256]{2,1,0:T(8,128)(2,1)}, u32[]{:S(2)}) copy-start(bf16[2,256,256]{2,1,0:T(8,128)(2,1)} %constant.64.clone.refs_9_) | copy-start | bytes 786436
  45.1 13.9 %copy-start.1 = (bf16[2,256,256]{2,1,0:T(8,128)(2,1)S(1)}, bf16[2,256,256]{2,1,0:T(8,128)(2,1)}, u32[]{:S(2)}) copy-start(bf16[2,256,256]{2,1,0:T(8,128)(2,1)} %constant.63.clone.refs_8_) | copy-start | bytes 786436
  45.2 13.9 %copy-start.2 = (f32[2,256,128]{2,1,0:T(8,128)S(1)}, f32[2,256,128]{2,1,0:T(8,128)}, u32[]{:S(2)}) copy-start(f32[2,256,128]{2,1,0:T(8,128)} %get-tuple-element.57.refs_0_) | copy-start | bytes 786436
  45.2 13.8 %copy-start.4 = (f32[2,256,128]{2,1,0:T(8,128)S(1)}, f32[2,256,128]{2,1,0:T(8,128)}, u32[]{:S(2)}) copy-start(f32[2,256,128]{2,1,0:T(8,128)} %copy-done.3) | copy-start | bytes 786436
  67.8 3.9 %collective-permute-start.7 = (f32[2,128,128]{2,1,0:T(8,128)S(1)}, f32[2,128,128]{2,1,0:T(8,128)S(1)}, u32[]{:S(2)}, u32[]{:S(2)}) collective-permute-start(f32[2,128,128]{2,1,0:T(8,128)S(1)} %get-tuple-element.68), channel_id=1, source_target_pairs={{0,1},{1,0},{2,3},{3,2},{4,5},{5,4},{6,7},{7,6},{8,9},{9,8},{10,11... | collective-permute-start | bytes 393224 | tf_op jit(solution)/shard_map/ppermute | solution.py:799
  68.2 6.3 %collective-permute-start.8 = (f32[2,128,128]{2,1,0:T(8,128)S(1)}, f32[2,128,128]{2,1,0:T(8,128)S(1)}, u32[]{:S(2)}, u32[]{:S(2)}) collective-permute-start(f32[2,128,128]{2,1,0:T(8,128)S(1)} %get-tuple-element.69), channel_id=1, source_target_pairs={{0,2},{1,3},{2,0},{3,1},{4,6},{5,7},{6,4},{7,5},{8,10},{9,11},{10,... | collective-permute-start | bytes 393224 | tf_op jit(solution)/shard_map/ppermute | solution.py:799
  68.7 7.0 %collective-permute-start.9 = (f32[2,128,128]{2,1,0:T(8,128)S(1)}, f32[2,128,128]{2,1,0:T(8,128)S(1)}, u32[]{:S(2)}, u32[]{:S(2)}) collective-permute-start(f32[2,128,128]{2,1,0:T(8,128)S(1)} %get-tuple-element.70), channel_id=1, source_target_pairs={{0,3},{1,2},{2,1},{3,0},{4,7},{5,6},{6,5},{7,4},{8,11},{9,10},{10,... | collective-permute-start | bytes 393224 | tf_op jit(solution)/shard_map/ppermute | solution.py:799
  69.7 7.8 %collective-permute-start.10 = (f32[2,128,128]{2,1,0:T(8,128)S(1)}, f32[2,128,128]{2,1,0:T(8,128)S(1)}, u32[]{:S(2)}, u32[]{:S(2)}) collective-permute-start(f32[2,128,128]{2,1,0:T(8,128)S(1)} %get-tuple-element.71), channel_id=1, source_target_pairs={{0,4},{1,5},{2,6},{3,7},{4,0},{5,1},{6,2},{7,3},{8,12},{9,13},{10,... | collective-permute-start | bytes 393224 | tf_op jit(solution)/shard_map/ppermute | solution.py:799
  70.3 13.5 %collective-permute-start.11 = (f32[2,128,128]{2,1,0:T(8,128)S(1)}, f32[2,128,128]{2,1,0:T(8,128)S(1)}, u32[]{:S(2)}, u32[]{:S(2)}) collective-permute-start(f32[2,128,128]{2,1,0:T(8,128)S(1)} %get-tuple-element.72), channel_id=1, source_target_pairs={{0,5},{1,4},{2,7},{3,6},{4,1},{5,0},{6,3},{7,2},{8,13},{9,12},{10,... | collective-permute-start | bytes 393224 | tf_op jit(solution)/shard_map/ppermute | solution.py:799
  71.7 14.2 %copy-start.11 = (f32[2,128,128]{2,1,0:T(8,128)}, f32[2,128,128]{2,1,0:T(8,128)S(1)}, u32[]{:S(2)}) copy-start(f32[2,128,128]{2,1,0:T(8,128)S(1)} %collective-permute-done.7.refs_1_) | copy-start | bytes 393220
  71.7 12.8 %collective-permute-start.12 = (f32[2,128,128]{2,1,0:T(8,128)S(1)}, f32[2,128,128]{2,1,0:T(8,128)S(1)}, u32[]{:S(2)}, u32[]{:S(2)}) collective-permute-start(f32[2,128,128]{2,1,0:T(8,128)S(1)} %get-tuple-element.73), channel_id=1, source_target_pairs={{0,6},{1,7},{2,4},{3,5},{4,2},{5,3},{6,0},{7,1},{8,14},{9,15},{10,... | collective-permute-start | bytes 393224 | tf_op jit(solution)/shard_map/ppermute | solution.py:799
  74.5 10.4 %collective-permute-start.13 = (f32[2,128,128]{2,1,0:T(8,128)S(1)}, f32[2,128,128]{2,1,0:T(8,128)S(1)}, u32[]{:S(2)}, u32[]{:S(2)}) collective-permute-start(f32[2,128,128]{2,1,0:T(8,128)S(1)} %get-tuple-element.74), channel_id=1, source_target_pairs={{0,7},{1,6},{2,5},{3,4},{4,3},{5,2},{6,1},{7,0},{8,15},{9,14},{10,... | collective-permute-start | bytes 393224 | tf_op jit(solution)/shard_map/ppermute | solution.py:799
  75.7 14.3 %collective-permute-start.17 = (f32[2,128,128]{2,1,0:T(8,128)S(1)}, f32[2,128,128]{2,1,0:T(8,128)S(1)}, u32[]{:S(2)}, u32[]{:S(2)}) collective-permute-start(f32[2,128,128]{2,1,0:T(8,128)S(1)} %get-tuple-element.77), channel_id=1, source_target_pairs={{0,1},{1,0},{2,3},{3,2},{4,5},{5,4},{6,7},{7,6},{8,9},{9,8},{10,11... | collective-permute-start | bytes 393224 | tf_op jit(solution)/shard_map/ppermute | solution.py:799
  77.4 14.7 %collective-permute-start.18 = (f32[2,128,128]{2,1,0:T(8,128)S(1)}, f32[2,128,128]{2,1,0:T(8,128)S(1)}, u32[]{:S(2)}, u32[]{:S(2)}) collective-permute-start(f32[2,128,128]{2,1,0:T(8,128)S(1)} %get-tuple-element.78), channel_id=1, source_target_pairs={{0,2},{1,3},{2,0},{3,1},{4,6},{5,7},{6,4},{7,5},{8,10},{9,11},{10,... | collective-permute-start | bytes 393224 | tf_op jit(solution)/shard_map/ppermute | solution.py:799
  83.8 10.6 %collective-permute-start.19 = (f32[2,128,128]{2,1,0:T(8,128)S(1)}, f32[2,128,128]{2,1,0:T(8,128)S(1)}, u32[]{:S(2)}, u32[]{:S(2)}) collective-permute-start(f32[2,128,128]{2,1,0:T(8,128)S(1)} %get-tuple-element.79), channel_id=1, source_target_pairs={{0,3},{1,2},{2,1},{3,0},{4,7},{5,6},{6,5},{7,4},{8,11},{9,10},{10,... | collective-permute-start | bytes 393224 | tf_op jit(solution)/shard_map/ppermute | solution.py:799
  84.4 14.2 %collective-permute-start.20 = (f32[2,128,128]{2,1,0:T(8,128)S(1)}, f32[2,128,128]{2,1,0:T(8,128)S(1)}, u32[]{:S(2)}, u32[]{:S(2)}) collective-permute-start(f32[2,128,128]{2,1,0:T(8,128)S(1)} %get-tuple-element.80), channel_id=1, source_target_pairs={{0,4},{1,5},{2,6},{3,7},{4,0},{5,1},{6,2},{7,3},{8,12},{9,13},{10,... | collective-permute-start | bytes 393224 | tf_op jit(solution)/shard_map/ppermute | solution.py:799
  84.9 13.8 %collective-permute-start.21 = (f32[2,128,128]{2,1,0:T(8,128)S(1)}, f32[2,128,128]{2,1,0:T(8,128)S(1)}, u32[]{:S(2)}, u32[]{:S(2)}) collective-permute-start(f32[2,128,128]{2,1,0:T(8,128)S(1)} %get-tuple-element.81), channel_id=1, source_target_pairs={{0,5},{1,4},{2,7},{3,6},{4,1},{5,0},{6,3},{7,2},{8,13},{9,12},{10,... | collective-permute-start | bytes 393224 | tf_op jit(solution)/shard_map/ppermute | solution.py:799
  90.1 9.3 %collective-permute-start.22 = (f32[2,128,128]{2,1,0:T(8,128)S(1)}, f32[2,128,128]{2,1,0:T(8,128)S(1)}, u32[]{:S(2)}, u32[]{:S(2)}) collective-permute-start(f32[2,128,128]{2,1,0:T(8,128)S(1)} %get-tuple-element.82), channel_id=1, source_target_pairs={{0,6},{1,7},{2,4},{3,5},{4,2},{5,3},{6,0},{7,1},{8,14},{9,15},{10,... | collective-permute-start | bytes 393224 | tf_op jit(solution)/shard_map/ppermute | solution.py:799
  92.2 7.5 %collective-permute-start.23 = (f32[2,128,128]{2,1,0:T(8,128)S(1)}, f32[2,128,128]{2,1,0:T(8,128)S(1)}, u32[]{:S(2)}, u32[]{:S(2)}) collective-permute-start(f32[2,128,128]{2,1,0:T(8,128)S(1)} %get-tuple-element.83), channel_id=1, source_target_pairs={{0,7},{1,6},{2,5},{3,4},{4,3},{5,2},{6,1},{7,0},{8,15},{9,14},{10,... | collective-permute-start | bytes 393224 | tf_op jit(solution)/shard_map/ppermute | solution.py:799
  94.4 16.1 %collective-permute-start.16 = (f32[136,512]{1,0:T(8,128)S(1)}, f32[136,512]{1,0:T(8,128)S(1)}, u32[]{:S(2)}, u32[]{:S(2)}) collective-permute-start(f32[136,512]{1,0:T(8,128)S(1)} %get-tuple-element.116), channel_id=1, source_target_pairs={{0,24},{8,16},{16,8},{24,0},{1,25},{9,17},{17,9},{25,1},{2,26},{10... | collective-permute-start | bytes 835592 | tf_op jit(solution)/shard_map/ppermute | solution.py:865
  98.6 25.4 %collective-permute-start.15 = (f32[136,512]{1,0:T(8,128)S(1)}, f32[136,512]{1,0:T(8,128)S(1)}, u32[]{:S(2)}, u32[]{:S(2)}) collective-permute-start(f32[136,512]{1,0:T(8,128)S(1)} %get-tuple-element.117), channel_id=1, source_target_pairs={{0,16},{8,24},{16,0},{24,8},{1,17},{9,25},{17,1},{25,9},{2,18},{10... | collective-permute-start | bytes 835592 | tf_op jit(solution)/shard_map/ppermute | solution.py:865
  98.7 25.4 %collective-permute-start.14 = (f32[136,512]{1,0:T(8,128)S(1)}, f32[136,512]{1,0:T(8,128)S(1)}, u32[]{:S(2)}, u32[]{:S(2)}) collective-permute-start(f32[136,512]{1,0:T(8,128)S(1)} %get-tuple-element.118), channel_id=1, source_target_pairs={{0,8},{8,0},{16,24},{24,16},{1,9},{9,1},{17,25},{25,17},{2,10},{10... | collective-permute-start | bytes 835592 | tf_op jit(solution)/shard_map/ppermute | solution.py:865
  105.7 18.4 %collective-permute-start.24 = (f32[136,512]{1,0:T(8,128)S(1)}, f32[136,512]{1,0:T(8,128)S(1)}, u32[]{:S(2)}, u32[]{:S(2)}) collective-permute-start(f32[136,512]{1,0:T(8,128)S(1)} %get-tuple-element.115), channel_id=1, source_target_pairs={{0,8},{8,0},{16,24},{24,16},{1,9},{9,1},{17,25},{25,17},{2,10},{10... | collective-permute-start | bytes 835592 | tf_op jit(solution)/shard_map/ppermute | solution.py:865
  108.0 29.1 %collective-permute-start.28 = (f32[136,512]{1,0:T(8,128)S(1)}, f32[136,512]{1,0:T(8,128)S(1)}, u32[]{:S(2)}, u32[]{:S(2)}) collective-permute-start(f32[136,512]{1,0:T(8,128)S(1)} %get-tuple-element.112), channel_id=1, source_target_pairs={{0,24},{8,16},{16,8},{24,0},{1,25},{9,17},{17,9},{25,1},{2,26},{10... | collective-permute-start | bytes 835592 | tf_op jit(solution)/shard_map/ppermute | solution.py:865
  110.5 36.0 %collective-permute-start.27 = (f32[136,512]{1,0:T(8,128)S(1)}, f32[136,512]{1,0:T(8,128)S(1)}, u32[]{:S(2)}, u32[]{:S(2)}) collective-permute-start(f32[136,512]{1,0:T(8,128)S(1)} %get-tuple-element.113), channel_id=1, source_target_pairs={{0,16},{8,24},{16,0},{24,8},{1,17},{9,25},{17,1},{25,9},{2,18},{10... | collective-permute-start | bytes 835592 | tf_op jit(solution)/shard_map/ppermute | solution.py:865
  124.2 3.1 %collective-permute-start.25 = (f32[4,24,512]{2,1,0:T(8,128)S(1)}, f32[4,24,512]{2,1,0:T(8,128)S(1)}, u32[]{:S(2)}, u32[]{:S(2)}) collective-permute-start(f32[4,24,512]{2,1,0:T(8,128)S(1)} %pad_maximum_fusion), channel_id=1, source_target_pairs={{0,1},{1,2},{2,3},{3,4},{4,5},{5,6},{6,7},{8,9},{9,10},{10,11},{11... | collective-permute-start | bytes 589832 | tf_op jit(solution)/shard_map/ppermute | solution.py:884
  126.0 4.6 %collective-permute-start.26 = (f32[4,24,512]{2,1,0:T(8,128)S(1)}, f32[4,24,512]{2,1,0:T(8,128)S(1)}, u32[]{:S(2)}, u32[]{:S(2)}) collective-permute-start(f32[4,24,512]{2,1,0:T(8,128)S(1)} %pad_maximum_fusion.1), channel_id=1, source_target_pairs={{1,0},{2,1},{3,2},{4,3},{5,4},{6,5},{7,6},{9,8},{10,9},{11,10},{12... | collective-permute-start | bytes 589832 | tf_op jit(solution)/shard_map/ppermute | solution.py:885
  154.2 1.2 collective-permute-start.29
  155.5 4.6 %collective-permute-start.32 = (f32[3,8,128]{2,1,0:T(8,128)S(1)}, f32[3,8,128]{2,1,0:T(8,128)S(1)}, u32[]{:S(2)}, u32[]{:S(2)}) collective-permute-start(f32[3,8,128]{2,1,0:T(8,128)S(1)} %max.21), channel_id=1, source_target_pairs={{0,6},{1,7},{2,4},{3,5},{4,2},{5,3},{6,0},{7,1},{8,14},{9,15},{10,... | collective-permute-start | bytes 36872 | tf_op jit(solution)/shard_map/ppermute | solution.py:124
  157.6 3.7 %collective-permute-start.31 = (f32[3,8,128]{2,1,0:T(8,128)S(1)}, f32[3,8,128]{2,1,0:T(8,128)S(1)}, u32[]{:S(2)}, u32[]{:S(2)}) collective-permute-start(f32[3,8,128]{2,1,0:T(8,128)S(1)} %max.21), channel_id=1, source_target_pairs={{0,4},{1,5},{2,6},{3,7},{4,0},{5,1},{6,2},{7,3},{8,12},{9,13},{10,... | collective-permute-start | bytes 36872 | tf_op jit(solution)/shard_map/ppermute | solution.py:124
  158.4 3.7 %collective-permute-start.30 = (f32[3,8,128]{2,1,0:T(8,128)S(1)}, f32[3,8,128]{2,1,0:T(8,128)S(1)}, u32[]{:S(2)}, u32[]{:S(2)}) collective-permute-start(f32[3,8,128]{2,1,0:T(8,128)S(1)} %max.21), channel_id=1, source_target_pairs={{0,2},{1,3},{2,0},{3,1},{4,6},{5,7},{6,4},{7,5},{8,10},{9,11},{10,... | collective-permute-start | bytes 36872 | tf_op jit(solution)/shard_map/ppermute | solution.py:124
  162.1 5.6 %collective-permute-start.35 = (f32[3,8,128]{2,1,0:T(8,128)S(1)}, f32[3,8,128]{2,1,0:T(8,128)S(1)}, u32[]{:S(2)}, u32[]{:S(2)}) collective-permute-start(f32[3,8,128]{2,1,0:T(8,128)S(1)} %maximum_maximum_fusion.1), channel_id=1, source_target_pairs={{0,24},{8,16},{16,8},{24,0},{1,25},{9,17},{17,9},{25,1},{2,26},{10... | collective-permute-start | bytes 36872 | tf_op jit(solution)/shard_map/ppermute | solution.py:124
  164.6 4.6 %collective-permute-start.34 = (f32[3,8,128]{2,1,0:T(8,128)S(1)}, f32[3,8,128]{2,1,0:T(8,128)S(1)}, u32[]{:S(2)}, u32[]{:S(2)}) collective-permute-start(f32[3,8,128]{2,1,0:T(8,128)S(1)} %maximum_maximum_fusion.1), channel_id=1, source_target_pairs={{0,16},{8,24},{16,0},{24,8},{1,17},{9,25},{17,1},{25,9},{2,18},{10... | collective-permute-start | bytes 36872 | tf_op jit(solution)/shard_map/ppermute | solution.py:124
  164.6 4.6 %collective-permute-start.33 = (f32[3,8,128]{2,1,0:T(8,128)S(1)}, f32[3,8,128]{2,1,0:T(8,128)S(1)}, u32[]{:S(2)}, u32[]{:S(2)}) collective-permute-start(f32[3,8,128]{2,1,0:T(8,128)S(1)} %maximum_maximum_fusion.1), channel_id=1, source_target_pairs={{0,8},{8,0},{16,24},{24,16},{1,9},{9,1},{17,25},{25,17},{2,10},{10... | collective-permute-start | bytes 36872 | tf_op jit(solution)/shard_map/ppermute | solution.py:124
  169.8 7.8 %collective-permute-start.36 = (f32[96,512]{1,0:T(8,128)S(1)}, f32[96,512]{1,0:T(8,128)S(1)}, u32[]{:S(2)}, u32[]{:S(2)}) collective-permute-start(f32[96,512]{1,0:T(8,128)S(1)} %get-tuple-element.95), channel_id=1, source_target_pairs={{0,8},{8,0},{16,24},{24,16},{1,9},{9,1},{17,25},{25,17},{2,10},{10... | collective-permute-start | bytes 589832 | tf_op jit(solution)/shard_map/ppermute | solution.py:865
  170.9 14.7 %collective-permute-start.37 = (f32[96,512]{1,0:T(8,128)S(1)}, f32[96,512]{1,0:T(8,128)S(1)}, u32[]{:S(2)}, u32[]{:S(2)}) collective-permute-start(f32[96,512]{1,0:T(8,128)S(1)} %get-tuple-element.96), channel_id=1, source_target_pairs={{0,16},{8,24},{16,0},{24,8},{1,17},{9,25},{17,1},{25,9},{2,18},{10... | collective-permute-start | bytes 589832 | tf_op jit(solution)/shard_map/ppermute | solution.py:865
  172.0 13.7 %collective-permute-start.38 = (f32[96,512]{1,0:T(8,128)S(1)}, f32[96,512]{1,0:T(8,128)S(1)}, u32[]{:S(2)}, u32[]{:S(2)}) collective-permute-start(f32[96,512]{1,0:T(8,128)S(1)} %get-tuple-element.97), channel_id=1, source_target_pairs={{0,24},{8,16},{16,8},{24,0},{1,25},{9,17},{17,9},{25,1},{2,26},{10... | collective-permute-start | bytes 589832 | tf_op jit(solution)/shard_map/ppermute | solution.py:865
  185.7 14.0 %collective-permute-start.39 = (f32[160,512]{1,0:T(8,128)S(1)}, f32[160,512]{1,0:T(8,128)S(1)}, u32[]{:S(2)}, u32[]{:S(2)}) collective-permute-start(f32[160,512]{1,0:T(8,128)S(1)} %get-tuple-element.108), channel_id=1, source_target_pairs={{0,8},{8,0},{16,24},{24,16},{1,9},{9,1},{17,25},{25,17},{2,10},{10... | collective-permute-start | bytes 983048 | tf_op jit(solution)/shard_map/ppermute | solution.py:865
  188.3 25.6 %collective-permute-start.40 = (f32[160,512]{1,0:T(8,128)S(1)}, f32[160,512]{1,0:T(8,128)S(1)}, u32[]{:S(2)}, u32[]{:S(2)}) collective-permute-start(f32[160,512]{1,0:T(8,128)S(1)} %get-tuple-element.109), channel_id=1, source_target_pairs={{0,16},{8,24},{16,0},{24,8},{1,17},{9,25},{17,1},{25,9},{2,18},{10... | collective-permute-start | bytes 983048 | tf_op jit(solution)/shard_map/ppermute | solution.py:865
  189.4 24.5 %collective-permute-start.41 = (f32[160,512]{1,0:T(8,128)S(1)}, f32[160,512]{1,0:T(8,128)S(1)}, u32[]{:S(2)}, u32[]{:S(2)}) collective-permute-start(f32[160,512]{1,0:T(8,128)S(1)} %get-tuple-element.110), channel_id=1, source_target_pairs={{0,24},{8,16},{16,8},{24,0},{1,25},{9,17},{17,9},{25,1},{2,26},{10... | collective-permute-start | bytes 983048 | tf_op jit(solution)/shard_map/ppermute | solution.py:865
  (18 other events, 78.5 us)
